TPU v7x, 128 devices: a whole 4x4x4 slice. The times are simulated.
128 devices in a mesh: group: 2 (over z_hi), fsdp: 64 (over y, x, z_lo, core).
Axes of the slice: x: 4, y: 4, z: 4 (z_hi: 2, z_lo: 2; z = z_hi * 2 + z_lo), core: 2. Of those that a mesh axis runs over, the one named last changes fastest.
Arguments:
- latent_noise: float32 [64, 256, 64], P('fsdp'), may hold values from -6 to 6
- fresh_noise: float32 [64, 256, 64], P('fsdp'), may hold values from -6 to 6
- text_states: bfloat16 [64, 128, 1536], P('fsdp'), may hold values from -6 to 6
- step_index: int32 [64], P('fsdp'), may hold values from 0 to 999
- base_qkv: bfloat16 [1536, 4608], P('fsdp'), may hold values from -0.30618622 to 0.30618622
- latent_in: bfloat16 [64, 1536], replicated, may hold values from -0.75 to 0.75
- modulation: float32 [1536], replicated, may hold values from -3 to 3
- velocity_out: bfloat16 [1536, 64], replicated, may hold values from -0.15625 to 0.15625
- gen_down: bfloat16 [1536, 192], P('fsdp'), may hold values from -0.00015258789 to 0.00015258789
- gen_up: bfloat16 [3, 64, 1536], P(None, None, 'fsdp'), may hold values from -0.0007324219 to 0.0007324219
- critic_down: bfloat16 [1536, 192], P('fsdp'), may hold values from -0.15625 to 0.15625
- critic_up: bfloat16 [3, 64, 1536], P(None, None, 'fsdp'), may hold values from -0.75 to 0.75
Outputs:
- sample_out: float32 [64, 256, 64], P('fsdp')
- grad_down: float32 [2, 1536, 192], P('group', 'fsdp')
- grad_up: float32 [2, 3, 64, 1536], P('group', None, None, 'fsdp')
All inputs are finite; a program needn't handle non-finite values. Where the computation divides by a largest or mean magnitude, that divisor is 1e-20 or more.
Results may differ from a plain program's by a relative error of at most 0.014.
Values may be sent and summed in bfloat16 or wider, within the bound.
No kernel may reach another device: no remote copies, remote signals or barrier semaphores. Data moves between devices by JAX's collectives and lax.ppermute only.
A program may use at most 128 MiB of HBM per device.

v0:
```python
import jax
import jax.numpy as jnp
from jax import lax
from jax.sharding import PartitionSpec as P

HEADS = 12
HD = 128
CH = 64
RANK = 64
NSTEPS = 1000
IMG = 256
TXT = 128


def spread_2(array, axis, root):
    mine = lax.axis_index(axis) == root
    return lax.psum(jnp.where(mine, array, jnp.zeros_like(array)), axis)


def normalize(values):
    return values * lax.rsqrt(jnp.mean(values * values, axis=-1, keepdims=True) + 1e-06)


def embed_tokens(latent, prompt_states, noise_level, latent_in, modulation):
    hidden = jnp.dot(latent.astype(jnp.bfloat16), latent_in, preferred_element_type=jnp.float32)
    picture = (normalize(hidden) * (1.0 + noise_level * modulation)).astype(jnp.bfloat16)
    prompt = normalize(prompt_states.astype(jnp.float32)).astype(jnp.bfloat16)
    return jnp.concatenate([prompt, picture], axis=0)


def attend(queries, key_rows, value_rows):
    query_count = queries.shape[0]
    key_count = key_rows.shape[0]
    query_heads = queries.astype(jnp.float32).reshape(query_count, HEADS, HD)
    key_heads = key_rows.astype(jnp.float32).reshape(key_count, HEADS, HD)
    value_heads = value_rows.astype(jnp.float32).reshape(key_count, HEADS, HD)
    scores = jnp.einsum("qhd,khd->hqk", query_heads, key_heads) * HD ** (-0.5)
    largest = jnp.max(scores, axis=-1, keepdims=True)
    weights = jnp.exp(scores - largest)
    shares = (weights / jnp.sum(weights, axis=-1, keepdims=True)).astype(jnp.bfloat16)
    shares = lax.optimization_barrier(shares).astype(jnp.float32)
    attended = jnp.einsum("hqk,khd->qhd", shares, value_heads)
    return attended.reshape(query_count, HEADS * HD)


def adapter_out(reduced, up_map):
    return jnp.concatenate(
        [
            jnp.dot(
                reduced[:, block * RANK : (block + 1) * RANK],
                up_map[block],
                preferred_element_type=jnp.float32,
            )
            for block in range(3)
        ],
        axis=1,
    )


def split_heads(qkv):
    head_span = HEADS * HD
    return (qkv[TXT:, :head_span], qkv[:, head_span : 2 * head_span], qkv[:, 2 * head_span :])


def readout(qkv, velocity_out):
    queries, key_rows, value_rows = split_heads(qkv)
    attended = attend(queries, key_rows, value_rows)
    return jnp.dot(attended.astype(jnp.bfloat16), velocity_out, preferred_element_type=jnp.float32)


def adapter_grads(tokens, reduced, qkv, up_map, cotangent, velocity_out):
    head_span = HEADS * HD
    upstream = jnp.dot(
        cotangent.astype(jnp.bfloat16), velocity_out.T, preferred_element_type=jnp.float32
    )
    queries, key_rows, value_rows = split_heads(qkv)
    unused, backward = jax.vjp(attend, queries, key_rows, value_rows)
    grad_query, grad_key, grad_value = backward(upstream)
    text_zeros = jnp.zeros((TXT, head_span), grad_query.dtype)
    grad_qkv = jnp.concatenate(
        [jnp.concatenate([text_zeros, grad_query], axis=0), grad_key, grad_value], axis=1
    )
    grad_upmap = jnp.stack(
        [
            jnp.dot(
                reduced[:, block * RANK : (block + 1) * RANK].T,
                grad_qkv[:, block * head_span : (block + 1) * head_span],
                preferred_element_type=jnp.float32,
            )
            for block in range(3)
        ]
    )
    grad_reduced = jnp.concatenate(
        [
            jnp.dot(
                grad_qkv[:, block * head_span : (block + 1) * head_span],
                up_map[block].T,
                preferred_element_type=jnp.float32,
            )
            for block in range(3)
        ],
        axis=1,
    ).astype(jnp.bfloat16)
    grad_downmap = jnp.dot(tokens.T, grad_reduced, preferred_element_type=jnp.float32)
    return (grad_downmap, grad_upmap)


def fold_project(tokens, weights, down_map):
    base_part = jnp.dot(
        tokens,
        lax.all_gather(weights, "fsdp", axis=0, tiled=True),
        preferred_element_type=jnp.float32,
    )
    reduced = jnp.dot(
        tokens,
        lax.all_gather(down_map, "fsdp", axis=0, tiled=True),
        preferred_element_type=jnp.float32,
    )
    return (base_part, reduced.astype(jnp.bfloat16))


def per_device(
    latent_noise,
    fresh_noise,
    text_states,
    step_index,
    base_qkv,
    latent_in,
    modulation,
    velocity_out,
    gen_down,
    gen_up,
    critic_down,
    critic_up,
):
    group_index = lax.axis_index("group")
    leading = group_index == 0
    noise_start = latent_noise[0]
    fresh = fresh_noise[0]
    prompt_states = text_states[0]
    noise_level = (step_index[0] + 1).astype(jnp.float32) / NSTEPS
    upmap_gen, upmap_critic = (
        lax.all_gather(gen_up, "fsdp", axis=2, tiled=True),
        lax.all_gather(critic_up, "fsdp", axis=2, tiled=True),
    )
    tokens_gen = embed_tokens(noise_start, prompt_states, 1.0, latent_in, modulation)
    base_gen, reduced_gen = fold_project(tokens_gen, base_qkv, gen_down)
    qkv_gen = (base_gen + adapter_out(reduced_gen, upmap_gen)).astype(jnp.bfloat16)
    sample = noise_start - readout(qkv_gen, velocity_out)
    noised = (1.0 - noise_level) * sample + noise_level * fresh
    tokens_score = embed_tokens(noised, prompt_states, noise_level, latent_in, modulation)
    base_score, reduced_critic = fold_project(tokens_score, base_qkv, critic_down)
    switch = (group_index == 1).astype(jnp.float32)
    qkv_score = (base_score + switch * adapter_out(reduced_critic, upmap_critic)).astype(
        jnp.bfloat16
    )
    own_velocity = readout(qkv_score, velocity_out)
    velocity_fake = spread_2(own_velocity.astype(jnp.bfloat16), "group", 1).astype(
        own_velocity.dtype
    )
    clean_real = noised - noise_level * own_velocity
    clean_fake = noised - noise_level * velocity_fake
    spread = jnp.mean(jnp.abs(sample - clean_real)) + 1e-05
    cot_gen = -(clean_fake - clean_real) / spread
    cot_critic = 2.0 * (velocity_fake - (fresh - sample)) / (IMG * CH)
    tokens_role = jnp.where(leading, tokens_gen, tokens_score)
    reduced_role = jnp.where(leading, reduced_gen, reduced_critic)
    qkv_role = jnp.where(leading, qkv_gen, qkv_score)
    upmap_role = jnp.where(leading, upmap_gen, upmap_critic)
    cot_role = jnp.where(leading, cot_gen, cot_critic)
    grad_downmap, grad_upmap = adapter_grads(
        tokens_role, reduced_role, qkv_role, upmap_role, cot_role, velocity_out
    )
    share_down, share_up = (
        lax.psum_scatter(grad_downmap, "fsdp", scatter_dimension=0, tiled=True),
        lax.psum_scatter(grad_upmap, "fsdp", scatter_dimension=2, tiled=True),
    )
    return (sample[None], share_down[None], share_up[None])


def solution(mesh):
    in_specs = (
        P("fsdp", None, None),
        P("fsdp", None, None),
        P("fsdp", None, None),
        P("fsdp"),
        P("fsdp", None),
        P(),
        P(),
        P(),
        P("fsdp", None),
        P(None, None, "fsdp"),
        P("fsdp", None),
        P(None, None, "fsdp"),
    )
    out_specs = (P("fsdp", None, None), P("group", "fsdp", None), P("group", None, None, "fsdp"))
    return jax.shard_map(
        per_device, mesh=mesh, in_specs=in_specs, out_specs=out_specs, check_vma=False
    )
```

profile of v0, /device:TPU:0, one launch (start us, length us, event | category | flops | bytes accessed | tf_op | source)
XLA Modules:
  0.0 1309.7 jit_solution(18314242343687159196)
XLA Ops:
  8.7 1.2 fusion.36
  9.8 1.3 multiply_reduce_fusion.4
  11.2 85.4 %all_gather.17 = bf16[1536,192]{1,0:T(8,128)(2,1)S(1)} all-gather(bf16[24,192]{1,0:T(8,128)(2,1)S(1)} %copy-done.29), channel_id=1, replica_groups=mesh['group'=2,'fsdp'=64] {'fsdp'}, dimensions={0}, use_global_device_ids=true | all-gather | bytes 599040 | tf_op jit(solution)/shard_map/all_gather | solution.py:116
  97.6 84.0 %all_gather.19 = bf16[1536,192]{1,0:T(8,128)(2,1)} all-gather(bf16[24,192]{1,0:T(8,128)(2,1)S(1)} %copy-done.30), channel_id=1, replica_groups=mesh['group'=2,'fsdp'=64] {'fsdp'}, dimensions={0}, use_global_device_ids=true | all-gather | bytes 599040 | tf_op jit(solution)/shard_map/all_gather | solution.py:116
  181.6 80.9 %all_gather.18 = bf16[3,64,1536]{1,2,0:T(8,128)(2,1)S(1)} all-gather(bf16[3,64,24]{1,2,0:T(8,128)(2,1)S(1)} %copy-done.27), channel_id=1, replica_groups=mesh['group'=2,'fsdp'=64] {'fsdp'}, dimensions={2}, use_global_device_ids=true | all-gather | bytes 599040 | tf_op jit(solution)/shard_map/all_gather | solution.py:143
  262.5 79.6 %all_gather.20 = bf16[3,64,1536]{1,2,0:T(8,128)(2,1)S(1)} all-gather(bf16[3,64,24]{1,2,0:T(8,128)(2,1)S(1)} %copy-done.28), channel_id=1, replica_groups=mesh['group'=2,'fsdp'=64] {'fsdp'}, dimensions={2}, use_global_device_ids=true | all-gather | bytes 599040 | tf_op jit(solution)/shard_map/all_gather | solution.py:144
  342.1 1.9 fusion.41
  344.0 1.9 fusion.42
  345.9 2.0 fusion.43
  347.9 12.4 fusion.2
  360.4 1.7 copy-done.7
  362.1 1.6 fusion.102
  363.9 1.7 copy.50
  365.6 2.4 copy.48
  368.0 3.8 fusion.103
  371.9 2.8 divide_convert_fusion.2
  377.2 1.3 broadcast_select_fusion.2
  378.4 2.0 fusion.38
  380.4 2.0 fusion.39
  382.4 1.9 fusion.40
  384.3 14.3 %broadcast_select_fusion = (bf16[384,4608]{1,0:T(8,128)(2,1)S(1)}, bf16[384,4608]{1,0:T(8,128)(2,1)}) fusion(bf16[384,4608]{1,0:T(8,128)(2,1)} %copy-done.7, pred[]{:T(512)S(6)} %eq.6, f32[384,1536]{1,0:T(8,128)} %fusion.38, f32[384,1536]{1,0:T(8,128)} %fusion.39, f32[384,1536]{1,0:T(8,128)} %fusion.40, f32[]{:T(128)S(6)} %convert_element_type.145, ...), kind=kOutput, calls=%fused_computation.27 | convolution fusion | flops 5448794112 | bytes 33030148 | tf_op jit(solution)/shard_map/dot_general | solution.py:109
  398.7 1.0 slice.127
  399.7 1.0 copy-done.8
  400.7 2.1 slice.124
  402.8 4.1 fusion.100
  406.9 1.4 copy.62
  408.3 1.4 copy.59
  409.7 2.4 copy.54
  412.1 1.7 copy.63
  413.8 2.4 copy.53
  416.2 1.4 copy.55
  417.6 5.4 fusion.104
  423.0 2.8 divide_convert_fusion.1
  426.7 0.9 convert_select_fusion
  428.2 12.9 psum.7
  441.7 1.2 fusion.73
  443.7 0.9 multiply_reduce_fusion
  444.6 1.4 fusion.24
  446.1 3.6 convert_reduce_fusion
  449.7 2.9 fusion.98
  452.6 1.5 fusion.26
  454.2 1.5 fusion.25
  458.0 1.2 pad_maximum_fusion.2
  459.2 3.9 copy.66
  463.2 1.4 broadcast_select_fusion.1
  466.1 1.8 fusion.30
  469.2 543.7 %all-reduce.4.cloned.1.call-done = f32[3,64,1536]{1,0,2:T(4,128)} async-done(((f32[3,64,1536]{1,0,2:T(4,128)}), f32[3,64,1536]{1,0,2:T(4,128)}) %all-reduce.4.cloned.1.call-update) | async-done | bytes 1179664
  1014.3 288.8 %reduce-scatter.2.cloned.1.call-done = f32[24,192]{1,0:T(8,128)} async-done(((f32[1536,192]{1,0:T(8,128)}), f32[24,192]{1,0:T(8,128)}) %reduce-scatter.2.cloned.1.call-update) | async-done | bytes 18448 | tf_op jit(solution)/shard_map/reduce_scatter | solution.py:175
  (100 shorter events, 12.7 us)
Async XLA Ops:
  7.2 2.7 copy-start
  7.2 89.4 %copy-start.10 = (bf16[1,128,1536]{2,1,0:T(8,128)(2,1)S(1)}, bf16[1,128,1536]{2,1,0:T(8,128)(2,1)}, u32[]{:S(2)}) copy-start(bf16[1,128,1536]{2,1,0:T(8,128)(2,1)} %param.14) | copy-start | bytes 1179652
  7.2 4.0 copy-start.31
  7.2 4.0 copy-start.29
  7.2 340.7 %all-gather.2.cloned.1.call-start = ((), (), s32[]{:S(2)}) async-start(), calls=%async_computation.1 | async-start | bytes 14376960 | tf_op jit(solution)/shard_map/all_gather | solution.py:111
  7.9 1004.9 %all-reduce.4.cloned.1.call-start = ((), (), s32[]{:S(2)}) async-start(), calls=%async_computation.3 | async-start | bytes 6291456
  96.7 251.2 %copy-start.20 = (bf16[128,1536]{1,0:T(8,128)(2,1)}, bf16[128,1536]{1,0:T(8,128)(2,1)S(1)}, u32[]{:S(2)}) copy-start(bf16[128,1536]{1,0:T(8,128)(2,1)S(1)} %fusion.37) | copy-start | bytes 1179652
  96.7 0.9 copy-start.30
  96.9 251.0 %copy-start.14 = (bf16[256,1536]{1,0:T(8,128)(2,1)}, bf16[256,1536]{1,0:T(8,128)(2,1)S(1)}, u32[]{:S(2)}) copy-start(bf16[256,1536]{1,0:T(8,128)(2,1)S(1)} %multiply_convert_fusion.1) | copy-start | bytes 2359300
  97.0 84.6 %copy-start.27 = (bf16[3,64,24]{1,2,0:T(8,128)(2,1)S(1)}, bf16[3,64,24]{1,2,0:T(8,128)(2,1)}, u32[]{:S(2)}) copy-start(bf16[3,64,24]{1,2,0:T(8,128)(2,1)} %param.21) | copy-start | bytes 27652
  97.0 165.6 %copy-start.28 = (bf16[3,64,24]{1,2,0:T(8,128)(2,1)S(1)}, bf16[3,64,24]{1,2,0:T(8,128)(2,1)}, u32[]{:S(2)}) copy-start(bf16[3,64,24]{1,2,0:T(8,128)(2,1)} %param.23) | copy-start | bytes 27652
  97.6 248.3 %copy-start.25 = (bf16[384,192]{0,1:T(8,128)(2,1)}, bf16[384,192]{0,1:T(8,128)(2,1)S(1)}, u32[]{:S(2)}) copy-start(bf16[384,192]{0,1:T(8,128)(2,1)S(1)} %convolution_convert_fusion.5) | copy-start | bytes 442372
  262.5 83.4 %copy-start.2 = (bf16[3,64,1536]{1,2,0:T(8,128)(2,1)}, bf16[3,64,1536]{1,2,0:T(8,128)(2,1)S(1)}, u32[]{:S(2)}) copy-start(bf16[3,64,1536]{1,2,0:T(8,128)(2,1)S(1)} %all_gather.18) | copy-start | bytes 1769476
  342.1 40.3 %copy-start.3 = (bf16[3,64,1536]{1,2,0:T(8,128)(2,1)}, bf16[3,64,1536]{1,2,0:T(8,128)(2,1)S(1)}, u32[]{:S(2)}) copy-start(bf16[3,64,1536]{1,2,0:T(8,128)(2,1)S(1)} %all_gather.20) | copy-start | bytes 1769476
  360.3 1.8 copy-start.7
  371.9 2.8 copy-start.6
  374.7 0.9 copy-start.9
  374.7 0.9 copy-start.23
  374.7 1.2 copy-start.18
  375.9 2.6 copy-start.11
  375.9 1.2 copy-start.13
  375.9 1.2 copy-start.21
  375.9 1.3 copy-start.26
  377.2 7.1 copy-start.16
  398.7 2.0 copy-start.8
  423.0 2.8 copy-start.5
  425.8 1.8 copy-start.12
  425.8 1.8 copy-start.19
  426.7 16.2 %copy-start.4 = (bf16[384,1536]{0,1:T(8,128)(2,1)S(1)}, bf16[384,1536]{0,1:T(8,128)(2,1)}, u32[]{:S(2)}) copy-start(bf16[384,1536]{0,1:T(8,128)(2,1)} %copy.59) | copy-start | bytes 3538948
  455.7 0.9 copy-start.24
  463.2 840.0 %reduce-scatter.2.cloned.1.call-start = ((), (), s32[]{:S(2)}) async-start(), calls=%async_computation.2 | async-start | bytes 1597440 | tf_op jit(solution)/shard_map/reduce_scatter | solution.py:175
  464.6 1.1 copy-start.15
  464.7 1.4 copy-start.17
  464.7 1.5 copy-start.22
  465.4 837.8 %copy-start.1 = (bf16[64,1536]{1,0:T(8,128)(2,1)S(1)}, bf16[64,1536]{1,0:T(8,128)(2,1)}, u32[]{:S(2)}) copy-start(bf16[64,1536]{1,0:T(8,128)(2,1)} %param.17) | copy-start | bytes 589828
  466.1 1.8 copy-start.32
Sparse Core Ops, SparseCore 0:
  9.8 123.4 all-gather.1
  463.3 549.5 all-reduce.3
  1015.9 287.1 reduce-scatter.1
where the time goes:
time: 1310 us
  waiting for transfers between devices  833 us (64%)
  blocking collectives  343 us (26%)
  matrix products  64.8 us (5%)
  local copies, waits for them, and re-layouts  34 us (3%)
  other arithmetic  18.5 us (1%)
  between operations  16.2 us (1%)
    unnamed x4, waiting for transfers between devices  544 us
    reduce_scatter x1, waiting for transfers between devices, per_device(): lax.psum_scatter(grad_downmap, 'fsdp', scatter_dimension=0, tiled=True)  289 us
    all_gather x2, blocking collectives, fold_project(): lax.all_gather(down_map, 'fsdp', axis=0, tiled=True)  169 us
    all_gather x1, blocking collectives, per_device(): lax.all_gather(gen_up, 'fsdp', axis=2, tiled=True)  80.9 us
    all_gather x1, blocking collectives, per_device(): lax.all_gather(critic_up, 'fsdp', axis=2, tiled=True)  79.6 us
    dot_general x2, matrix products, fold_project(): jnp.dot(tokens, lax.all_gather(weights, 'fsdp', axis=0, tiled=True), pref...  26.7 us
  transfers between devices with their start and end apart: 3, of which 2 were waited for; matrix products, arithmetic and copies ran while one was open for 1% of the time, Pallas kernels for 0%

commit v1 on v0

v1 whole, which is shorter than its diff:
```python
import jax
import jax.numpy as jnp
from jax import lax
from jax.experimental import pallas as pl
from jax.experimental.pallas import tpu as pltpu
from jax.sharding import PartitionSpec as P

HEADS = 12
HD = 128
CH = 64
RANK = 64
NSTEPS = 1000
IMG = 256
TXT = 128
ROWS = TXT + IMG
HW = HEADS * HD
CHUNK = 512
BF = jnp.bfloat16
F32 = jnp.float32
SCALE = HD ** (-0.5)


def dot(left, right, left_dim=1, right_dim=0):
    dims = (((left_dim,), (right_dim,)), ((), ()))
    return lax.dot_general(left, right, dims, preferred_element_type=F32)


def high_low(values):
    high = values.astype(BF)
    return high, (values - high.astype(F32)).astype(BF)


def forward_kernel(
    flag_ref,
    sigma_ref,
    latent_ref,
    fresh_ref,
    prompt_ref,
    latent_in_ref,
    modulation_ref,
    velocity_out_ref,
    fold_ref,
    text_ref,
    gen_down_ref,
    gen_up_ref,
    role_down_ref,
    role_up_ref,
    sample_ref,
    velocity_ref,
    q_ref,
    k_ref,
    v_ref,
    weights_ref,
    inverse_ref,
    attended_ref,
    reduced_ref,
    picture_ref,
    stacked,
    q_now,
    k_now,
    v_now,
    attended_now,
):
    flag = flag_ref[0, 0]
    sigma = sigma_ref[0, 0]

    def readout(latent, noise_level, down_ref, up_ref, switch, save):
        narrow = latent.astype(BF)
        hidden = dot(narrow, latent_in_ref[...])
        inverse_rms = lax.rsqrt(jnp.mean(hidden * hidden, axis=-1, keepdims=True) + 1e-06)
        picture = (hidden * inverse_rms * (1.0 + noise_level * modulation_ref[...])).astype(BF)
        reduced_picture = dot(picture, down_ref[...]).astype(BF)
        reduced_prompt = dot(prompt_ref[...], down_ref[:, RANK:]).astype(BF)

        @save
        def _():
            picture_ref[...] = picture
            reduced_ref[TXT:, :] = reduced_picture
            reduced_ref[:TXT, :RANK] = jnp.zeros((TXT, RANK), BF)
            reduced_ref[:TXT, RANK:] = reduced_prompt

        if switch is not None:
            reduced_picture = reduced_picture * switch.astype(BF)
            reduced_prompt = reduced_prompt * switch.astype(BF)
        scaled_high, scaled_low = high_low(narrow.astype(F32) * inverse_rms)
        for block, now in enumerate((q_now, k_now, v_now)):
            rank_span = slice(block * RANK, (block + 1) * RANK)
            left = jnp.concatenate(
                [scaled_high, scaled_low, scaled_high, reduced_picture[:, rank_span]], axis=1
            )
            for start in range(0, HW, CHUNK):
                own = slice(start, start + CHUNK)
                wide = slice(block * HW + start, block * HW + start + CHUNK)
                fold = fold_ref[:CH, wide] + noise_level * fold_ref[CH:, wide]
                fold_high, fold_low = high_low(fold)
                stacked[:CH, :] = fold_high
                stacked[CH : 2 * CH, :] = fold_high
                stacked[2 * CH : 3 * CH, :] = fold_low
                stacked[3 * CH :, :] = up_ref[rank_span, own]
                picture_part = dot(left, stacked[...]).astype(BF)
                if block == 0:
                    now[:, own] = picture_part
                else:
                    now[TXT:, own] = picture_part
                    prompt_span = slice((block - 1) * RANK, block * RANK)
                    text_span = slice((block - 1) * HW + start, (block - 1) * HW + start + CHUNK)
                    adapter = dot(reduced_prompt[:, prompt_span], up_ref[rank_span, own])
                    now[:TXT, own] = (text_ref[:, text_span] + adapter).astype(BF)

        def head(index, carry):
            span = pl.ds(pl.multiple_of(index * HD, HD), HD)
            queries, keys, values = q_now[:, span], k_now[:, span], v_now[:, span]
            scores = dot(queries, keys, 1, 1) * SCALE
            largest = jnp.max(scores, axis=-1, keepdims=True)
            weights = jnp.exp(scores - largest)
            inverse = 1.0 / jnp.sum(weights, axis=-1, keepdims=True)
            weights = weights.astype(BF)
            attended = (dot(weights, values) * inverse).astype(BF)
            attended_now[:, span] = attended

            @save
            def _():
                q_ref[:, span] = queries
                k_ref[:, span] = keys
                v_ref[:, span] = values
                attended_ref[:, span] = attended
                weights_ref[index] = weights
                inverse_ref[index] = inverse

            return carry

        lax.fori_loop(0, HEADS, head, 0, unroll=2)
        return dot(attended_now[...], velocity_out_ref[...])

    latent = latent_ref[...]
    sample = latent - readout(latent, 1.0, gen_down_ref, gen_up_ref, None, lambda f: f())
    sample_ref[...] = sample
    noised = (1.0 - sigma) * sample + sigma * fresh_ref[...]
    velocity_ref[...] = readout(
        noised, sigma, role_down_ref, role_up_ref, flag.astype(F32), pl.when(flag == 1)
    )


def backward_kernel(
    flag_ref,
    sigma_ref,
    sample_ref,
    fresh_ref,
    own_ref,
    fake_ref,
    prompt_ref,
    velocity_out_ref,
    role_up_ref,
    q_ref,
    k_ref,
    v_ref,
    weights_ref,
    inverse_ref,
    attended_ref,
    reduced_ref,
    picture_ref,
    grads_ref,
    grad_q,
    grad_k,
    grad_v,
):
    flag = flag_ref[0, 0]
    sigma = sigma_ref[0, 0]
    sample = sample_ref[...]
    own = own_ref[...]
    noised = (1.0 - sigma) * sample + sigma * fresh_ref[...]
    clean_real = noised - sigma * own
    clean_fake = noised - sigma * fake_ref[...].astype(F32)
    distance = jnp.sum(jnp.sum(jnp.abs(sample - clean_real), axis=1, keepdims=True), axis=0, keepdims=True)
    spread = distance * (1.0 / (IMG * CH)) + 1e-05
    cot_gen = -(clean_fake - clean_real) / spread
    cot_critic = 2.0 * (own - (fresh_ref[...] - sample)) / (IMG * CH)
    cotangent = jnp.where(flag == 0, cot_gen, cot_critic).astype(BF)

    def head(index, carry):
        span = pl.ds(pl.multiple_of(index * HD, HD), HD)
        queries, keys, values = q_ref[:, span], k_ref[:, span], v_ref[:, span]
        weights = weights_ref[index]
        upstream = dot(cotangent, velocity_out_ref[span, :], 1, 1) * inverse_ref[index]
        inner = jnp.sum(upstream * attended_ref[:, span].astype(F32), axis=-1, keepdims=True)
        upstream = upstream.astype(BF)
        grad_v[:, span] = dot(weights, upstream, 0, 0).astype(BF)
        grad_weights = dot(upstream, values, 1, 1)
        grad_scores = (weights.astype(F32) * (grad_weights - inner) * SCALE).astype(BF)
        grad_q[:, span] = dot(grad_scores, keys).astype(BF)
        grad_k[:, span] = dot(grad_scores, queries, 0, 0).astype(BF)
        return carry

    lax.fori_loop(0, HEADS, head, 0, unroll=2)
    spans = [slice(block * RANK, (block + 1) * RANK) for block in range(3)]
    reduced_q = dot(grad_q[...], role_up_ref[spans[0], :], 1, 1).astype(BF)
    reduced_k = dot(grad_k[...], role_up_ref[spans[1], :], 1, 1).astype(BF)
    reduced_v = dot(grad_v[...], role_up_ref[spans[2], :], 1, 1).astype(BF)
    reduced_kv = jnp.concatenate([reduced_k, reduced_v], axis=1)
    down_q = dot(reduced_q, picture_ref[...], 0, 0)
    down_kv = dot(reduced_kv[:TXT], prompt_ref[...], 0, 0) + dot(reduced_kv[TXT:], picture_ref[...], 0, 0)
    up_q = dot(reduced_ref[TXT:, spans[0]], grad_q[...], 0, 0)
    up_k = dot(reduced_ref[:, spans[1]], grad_k[...], 0, 0)
    up_v = dot(reduced_ref[:, spans[2]], grad_v[...], 0, 0)
    grads = jnp.concatenate([down_q, down_kv, up_q, up_k, up_v], axis=0)
    grads_ref[...] = grads.T.astype(BF)


def vmem():
    return pl.BlockSpec(memory_space=pltpu.VMEM)


def smem():
    return pl.BlockSpec(memory_space=pltpu.SMEM)


def run_forward(*operands):
    shape = jax.ShapeDtypeStruct
    return pl.pallas_call(
        forward_kernel,
        out_shape=(
            shape((IMG, CH), F32),
            shape((IMG, CH), F32),
            shape((IMG, HW), BF),
            shape((ROWS, HW), BF),
            shape((ROWS, HW), BF),
            shape((HEADS, IMG, ROWS), BF),
            shape((HEADS, IMG, 1), F32),
            shape((IMG, HW), BF),
            shape((ROWS, 3 * RANK), BF),
            shape((IMG, HW), BF),
        ),
        in_specs=[smem()] * 2 + [vmem()] * (len(operands) - 2),
        out_specs=tuple([vmem()] * 10),
        scratch_shapes=[
            pltpu.VMEM((4 * CH, CHUNK), BF),
            pltpu.VMEM((IMG, HW), BF),
            pltpu.VMEM((ROWS, HW), BF),
            pltpu.VMEM((ROWS, HW), BF),
            pltpu.VMEM((IMG, HW), BF),
        ],
        compiler_params=pltpu.CompilerParams(vmem_limit_bytes=48 * 2**20),
        name="forward",
    )(*operands)


def run_backward(*operands):
    return pl.pallas_call(
        backward_kernel,
        out_shape=jax.ShapeDtypeStruct((HW, 6 * RANK), BF),
        in_specs=[smem()] * 2 + [vmem()] * (len(operands) - 2),
        out_specs=vmem(),
        scratch_shapes=[
            pltpu.VMEM((IMG, HW), BF),
            pltpu.VMEM((ROWS, HW), BF),
            pltpu.VMEM((ROWS, HW), BF),
        ],
        compiler_params=pltpu.CompilerParams(vmem_limit_bytes=48 * 2**20),
        name="backward",
    )(*operands)


def per_device(
    latent_noise,
    fresh_noise,
    text_states,
    step_index,
    base_qkv,
    latent_in,
    modulation,
    velocity_out,
    gen_down,
    gen_up,
    critic_down,
    critic_up,
):
    devices = lax.axis_size("fsdp")
    group_index = lax.axis_index("group")
    leading = group_index == 0
    flag = group_index.astype(jnp.int32).reshape(1, 1)
    sigma = ((step_index + 1).astype(F32) / NSTEPS).reshape(1, 1)
    shard = base_qkv.shape[0]

    weights = lax.all_gather(base_qkv, "fsdp", axis=0, tiled=True)
    role_down = jnp.where(leading, gen_down, critic_down)
    role_up = jnp.where(leading, gen_up, critic_up)
    rows = jnp.concatenate(
        [
            gen_down,
            role_down,
            gen_up.reshape(3 * RANK, shard).T,
            role_up.reshape(3 * RANK, shard).T,
        ],
        axis=1,
    )
    adapters = lax.all_to_all(jnp.broadcast_to(rows[None], (devices,) + rows.shape), "fsdp", 0, 0)
    adapters = adapters.reshape(devices * shard, 12 * RANK)
    gen_down_full = adapters[:, : 3 * RANK]
    role_down_full = adapters[:, 3 * RANK : 6 * RANK]
    ups = adapters[:, 6 * RANK :].T
    gen_up_full, role_up_full = ups[: 3 * RANK], ups[3 * RANK :]

    states = text_states[0].astype(F32)
    prompt = (
        states * lax.rsqrt(jnp.mean(states * states, axis=-1, keepdims=True) + 1e-06)
    ).astype(BF)
    scaled_in = (latent_in.astype(F32) * modulation).astype(BF)
    fold = dot(jnp.concatenate([latent_in, scaled_in], axis=0), weights)
    text = dot(prompt, weights[:, HW:])

    sample, own_velocity, *saved = run_forward(
        flag,
        sigma,
        latent_noise[0],
        fresh_noise[0],
        prompt,
        latent_in,
        modulation.reshape(1, HW),
        velocity_out,
        fold,
        text,
        gen_down_full,
        gen_up_full,
        role_down_full,
        role_up_full,
    )
    fake_velocity = lax.ppermute(own_velocity.astype(BF), "group", [(1, 0)])
    grads = run_backward(
        flag,
        sigma,
        sample,
        fresh_noise[0],
        own_velocity,
        fake_velocity,
        prompt,
        velocity_out,
        role_up_full,
        *saved,
    )
    shares = lax.all_to_all(grads.reshape(devices, shard, 6 * RANK), "fsdp", 0, 0)
    share = jnp.sum(shares.astype(F32), axis=0)
    share_down = share[:, : 3 * RANK]
    share_up = share[:, 3 * RANK :].T.reshape(3, RANK, shard)
    return (sample[None], share_down[None], share_up[None])


def solution(mesh):
    in_specs = (
        P("fsdp", None, None),
        P("fsdp", None, None),
        P("fsdp", None, None),
        P("fsdp"),
        P("fsdp", None),
        P(),
        P(),
        P(),
        P("fsdp", None),
        P(None, None, "fsdp"),
        P("fsdp", None),
        P(None, None, "fsdp"),
    )
    out_specs = (P("fsdp", None, None), P("group", "fsdp", None), P("group", None, None, "fsdp"))
    return jax.shard_map(
        per_device, mesh=mesh, in_specs=in_specs, out_specs=out_specs, check_vma=False
    )
```

time: 1310 us -> 244 us (0.19)
  waiting for transfers between devices: 833 us -> 150 us
  blocking collectives: 343 us -> 0 us
  matrix products: 64.8 us -> 11.2 us
  Pallas kernels: 0 us -> 32.2 us
  local copies, waits for them, and re-layouts: 34 us -> 13.2 us
  starting transfers between devices: 0.12 us -> 17.6 us
  other arithmetic: 18.5 us -> 2.78 us
    unnamed x4 -> x1, waiting for transfers between devices: 544 us -> 0.68 us
    all_gather x4 -> x0, blocking collectives: 330 us -> none  [the longest x2 169 us: fold_project(): lax.all_gather(down_map, 'fsdp', axis=0, tiled=True)]
    reduce_scatter x1 -> x0, waiting for transfers between devices: 289 us -> none  [per_device(): lax.psum_scatter(grad_downmap, 'fsdp', scatter_dimension=0, tiled=True)]
    all_gather x1, waiting for transfers between devices: 0.01 us -> 85.5 us  [per_device(): weights = lax.all_gather(base_qkv, 'fsdp', axis=0, tiled=True)]
    all_to_all x0 -> x2, waiting for transfers between devices: none -> 57.7 us  [the longest x1 39 us: per_device(): lax.all_to_all(jnp.broadcast_to(rows[None], (devices,) + rows.shape), 'fs...]
    dot_general x29 -> x2, matrix products: 55.6 us -> 11.2 us  [dot(): return lax.dot_general(left, right, dims, preferred_element_type=F32)]
    pallas_call x0 -> x2, Pallas kernels: none -> 32.2 us  [the longest x1 19.4 us: run_forward(): pl.pallas_call(forward_kernel, out_shape=(shape((IMG, CH), F32), shape((I...]
    slice x14 -> x3, local copies, waits for them, and re-layouts: 24 us -> 5.48 us  [the longest x1 2.76 us: per_device(): role_down_full = adapters[:, 3 * RANK:6 * RANK]]
  transfers between devices with their start and end apart: 3 -> 4, of which waited for: 2 -> 4; matrix products, arithmetic and copies ran while one was open for 1% -> 5% of each run, Pallas kernels for 0% -> 0%
where the time goes in v1:
time: 244 us; the launch traced here: 242 us
  waiting for transfers between devices  150 us (61%)
  Pallas kernels  32.2 us (13%)
  starting transfers between devices  17.6 us (7%)
  between operations  14.8 us (6%)
  local copies, waits for them, and re-layouts  13.2 us (5%)
  matrix products  11.2 us (5%)
  other arithmetic  2.78 us (1%)
    all_gather x1, waiting for transfers between devices, per_device(): weights = lax.all_gather(base_qkv, 'fsdp', axis=0, tiled=True)  85.5 us
    all_to_all x1, waiting for transfers between devices, per_device(): lax.all_to_all(jnp.broadcast_to(rows[None], (devices,) + rows.shape), 'fs...  39 us
    pallas_call x1, Pallas kernels, run_forward(): pl.pallas_call(forward_kernel, out_shape=(shape((IMG, CH), F32), shape((I...  19.4 us
    all_to_all x1, waiting for transfers between devices, per_device(): lax.all_to_all(grads.reshape(devices, shard, 6 * RANK), 'fsdp', 0, 0)  18.8 us
    pallas_call x1, Pallas kernels, run_backward(): pl.pallas_call(backward_kernel, out_shape=jax.ShapeDtypeStruct((HW, 6 * R...  12.7 us
    dot_general x2, matrix products, dot(): return lax.dot_general(left, right, dims, preferred_element_type=F32)  11.2 us
    all_to_all x1, starting transfers between devices, per_device(): lax.all_to_all(jnp.broadcast_to(rows[None], (devices,) + rows.shape), 'fs...  9.75 us
    all_to_all x1, starting transfers between devices, per_device(): lax.all_to_all(grads.reshape(devices, shard, 6 * RANK), 'fsdp', 0, 0)  6.35 us
  transfers between devices with their start and end apart: 4, of which 4 were waited for; matrix products, arithmetic and copies ran while one was open for 5% of the time, Pallas kernels for 0%

profile of v1, /device:TPU:0, one launch (start us, length us, event | category | flops | bytes accessed | tf_op | source)
XLA Modules:
  0.0 242.0 jit_solution(60807753623583800)
XLA Ops:
  7.2 0.0 all-gather.2.cloned.1.call-start
  7.2 0.7 all-gather.2.cloned.1.call-update
  7.9 0.7 copy.26
  8.6 0.7 broadcast_select_fusion
  9.4 0.1 reshape.43
  9.5 0.1 reshape.42
  9.6 0.7 broadcast_select_fusion.1
  10.3 0.8 pad_maximum_fusion
  11.1 1.6 broadcast_in_dim.6
  12.7 0.0 copy-start.4
  12.7 0.0 copy-start.5
  12.7 0.0 copy-start.6
  12.7 0.0 copy-start.3
  12.7 0.0 copy-start.2
  12.7 0.0 copy-start
  12.7 9.8 %all-to-all-start = ((bf16[64,24,768]{2,1,0:T(8,128)(2,1)}), bf16[64,24,768]{2,1,0:T(8,128)(2,1)}, u32[]{:S(2)}, u32[]{:S(2)}) async-start(bf16[64,24,768]{2,1,0:T(8,128)(2,1)} %broadcast_in_dim.6), calls=%async_computation | async-start | bytes 4718592 | tf_op jit(solution)/shard_map/all_to_all | solution.py:296
  23.1 0.0 copy-done.4
  23.1 0.1 copy.24
  23.2 0.0 copy-done.5
  23.2 0.1 copy.25
  23.3 0.0 copy-done.6
  23.3 0.0 copy-done.3
  23.3 0.2 copy.29.velocity_out_ref
  23.6 0.0 copy-done.2
  23.6 0.2 fusion.2
  23.8 0.0 copy-done
  23.8 0.1 fusion.3.prompt_ref
  23.9 39.0 %all-to-all-done = bf16[64,24,768]{2,1,0:T(8,128)(2,1)} async-done(((bf16[64,24,768]{2,1,0:T(8,128)(2,1)}), bf16[64,24,768]{2,1,0:T(8,128)(2,1)}, u32[]{:S(2)}, u32[]{:S(2)}) %all-to-all-start) | async-done | bytes 2359328 | tf_op jit(solution)/shard_map/all_to_all | solution.py:296
  62.9 1.4 slice.34
  64.3 1.5 copy.33
  65.8 1.3 fusion.10
  67.1 2.8 %fusion.9 = (bf16[1536,192]{1,0:T(8,128)(2,1)}, bf16[1536,192]{1,0:T(8,128)(2,1)S(1)}) fusion(bf16[1536,768]{1,0:T(8,128)(2,1)} %bitcast.8), kind=kLoop, calls=%fused_computation.19 | loop fusion | bytes 2359296 | tf_op jit(solution)/shard_map/slice | solution.py:299
  69.9 85.5 %all-gather.2.cloned.1.call-done = bf16[1536,4608]{1,0:T(8,128)(2,1)} async-done(((bf16[24,4608]{1,0:T(8,128)(2,1)}), bf16[1536,4608]{1,0:T(8,128)(2,1)}) %all-gather.2.cloned.1.call-update) | async-done | bytes 14155792 | tf_op jit(solution)/shard_map/all_gather | solution.py:284
  155.4 0.0 copy-start.1
  155.4 8.6 %fusion.4.fold_ref = f32[128,4608]{1,0:T(8,128)} fusion(bf16[1536,4608]{1,0:T(8,128)(2,1)} %all-gather.2.cloned.1.call-done, bf16[64,1536]{1,0:T(8,128)(2,1)S(1)} %multiply_convert_fusion, bf16[64,1536]{1,0:T(8,128)(2,1)S(1)} %copy-done), kind=kOutput, calls=%fused_computation.7 | convolution fusion | flops 1812725760 | bytes 16908288 | tf_op jit(solution)/shard_map/dot_general | solution.py:25
  164.0 1.3 copy-done.1
  165.3 2.6 %fusion.text_ref = f32[128,3072]{1,0:T(8,128)} fusion(bf16[128,1536]{1,0:T(8,128)(2,1)S(1)} %fusion.3.prompt_ref, bf16[1536,4608]{1,0:T(8,128)(2,1)S(1)} %copy-done.1), kind=kOutput, calls=%fused_computation | convolution fusion | flops 1207959552 | bytes 11403264 | tf_op jit(solution)/shard_map/dot_general | solution.py:25
  167.9 19.4 %forward.1 = (f32[256,64]{1,0:T(8,128)S(1)}, f32[256,64]{1,0:T(8,128)S(1)}, bf16[256,1536]{1,0:T(8,128)(2,1)S(1)}, bf16[384,1536]{1,0:T(8,128)(2,1)}, bf16[384,1...) custom-call(s32[1,1]{1,0:T(1,128)} %bitcast.flag_ref, ...), custom_call_target="tpu_custom_call" | custom-call | tf_op jit(solution)/shard_map/forward/pallas_call | solution.py:219
  187.4 1.5 collective-permute-start
  188.8 6.2 %collective-permute-done.fake_ref = bf16[256,64]{1,0:T(8,128)(2,1)S(1)} collective-permute-done((bf16[256,64]{1,0:T(8,128)(2,1)S(1)}, bf16[256,64]{1,0:T(8,128)(2,1)S(1)}, u32[]{:S(2)}, u32[]{:S(2)}) %collective-permute-start) | collective-permute-done | bytes 32800 | tf_op jit(solution)/shard_map/ppermute | solution.py:327
  195.0 12.7 %backward.1 = bf16[1536,384]{1,0:T(8,128)(2,1)} custom-call(s32[1,1]{1,0:T(1,128)} %bitcast.flag_ref, f32[1,1]{1,0:T(1,128)} %bitcast.1.sigma_ref, f32[256,64]{1,0:T(8,128)S(1)} %get-tuple-element.13.sample_ref, f32[256,64]{1,0:T(8,128)S(1)} %bitcast.27, f32[256,64]{1,0:T(8,128)S(1)} %get-tuple-element.14.own_ref, ...), custom_call_target="tpu_custom_call" | custom-call | tf_op jit(solution)/shard_map/backward/pallas_call | solution.py:248
  207.8 6.3 %all-to-all-start.1 = ((bf16[64,24,384]{2,1,0:T(8,128)(2,1)}), bf16[64,24,384]{2,1,0:T(8,128)(2,1)S(1)}, u32[]{:S(2)}, u32[]{:S(2)}) async-start(bf16[64,24,384]{2,1,0:T(8,128)(2,1)} %bitcast.11), calls=%async_computation.1 | async-start | bytes 2359296 | tf_op jit(solution)/shard_map/all_to_all | solution.py:340
  214.1 0.7 copy.31
  214.8 18.8 %all-to-all-done.1 = bf16[64,24,384]{2,1,0:T(8,128)(2,1)S(1)} async-done(((bf16[64,24,384]{2,1,0:T(8,128)(2,1)}), bf16[64,24,384]{2,1,0:T(8,128)(2,1)S(1)}, u32[]{:S(2)}, u32[]{:S(2)}) %all-to-all-start.1) | async-done | bytes 1179680 | tf_op jit(solution)/shard_map/all_to_all | solution.py:340
  233.6 0.2 convert_reduce_fusion
  233.8 0.6 slice_bitcast_fusion
  234.4 0.1 broadcast_in_dim_reshape.3
  234.5 0.6 copy.32
  (5 shorter events, 0.1 us)
Async XLA Ops:
  7.2 148.3 %all-gather.2.cloned.1.call-start = ((), (), s32[]{:S(2)}) async-start(), calls=%async_computation.2 | async-start | bytes 14376960 | tf_op jit(solution)/shard_map/all_gather | solution.py:284
  12.7 10.4 %copy-start.4 = (f32[1,256,64]{1,2,0:T(8,128)S(1)}, f32[1,256,64]{1,2,0:T(8,128)}, u32[]{:S(2)}) copy-start(f32[1,256,64]{1,2,0:T(8,128)} %param.12) | copy-start | bytes 196612
  12.7 10.6 %copy-start.5 = (f32[1,256,64]{1,2,0:T(8,128)S(1)}, f32[1,256,64]{1,2,0:T(8,128)}, u32[]{:S(2)}) copy-start(f32[1,256,64]{1,2,0:T(8,128)} %param.13) | copy-start | bytes 196612
  12.7 10.7 %copy-start.6 = (f32[1536]{0:T(1024)S(1)}, f32[1536]{0:T(1024)}, u32[]{:S(2)}) copy-start(f32[1536]{0:T(1024)} %param.18) | copy-start | bytes 18436
  12.7 10.7 %copy-start.3 = (bf16[1536,64]{0,1:T(8,128)(2,1)S(1)}, bf16[1536,64]{0,1:T(8,128)(2,1)}, u32[]{:S(2)}) copy-start(bf16[1536,64]{0,1:T(8,128)(2,1)} %param.19) | copy-start | bytes 589828
  12.7 10.9 %copy-start.2 = (bf16[1,128,1536]{2,1,0:T(8,128)(2,1)S(1)}, bf16[1,128,1536]{2,1,0:T(8,128)(2,1)}, u32[]{:S(2)}) copy-start(bf16[1,128,1536]{2,1,0:T(8,128)(2,1)} %param.14) | copy-start | bytes 1179652
  12.7 11.1 %copy-start = (bf16[64,1536]{1,0:T(8,128)(2,1)S(1)}, bf16[64,1536]{1,0:T(8,128)(2,1)}, u32[]{:S(2)}) copy-start(bf16[64,1536]{1,0:T(8,128)(2,1)} %latent_in_ref.1) | copy-start | bytes 589828
  12.7 50.2 %all-to-all-start = ((bf16[64,24,768]{2,1,0:T(8,128)(2,1)}), bf16[64,24,768]{2,1,0:T(8,128)(2,1)}, u32[]{:S(2)}, u32[]{:S(2)}) async-start(bf16[64,24,768]{2,1,0:T(8,128)(2,1)} %broadcast_in_dim.6), calls=%async_computation | async-start | bytes 4718592 | tf_op jit(solution)/shard_map/all_to_all | solution.py:296
  155.4 9.9 %copy-start.1 = (bf16[1536,4608]{1,0:T(8,128)(2,1)S(1)}, bf16[1536,4608]{1,0:T(8,128)(2,1)}, u32[]{:S(2)}) copy-start(bf16[1536,4608]{1,0:T(8,128)(2,1)} %all-gather.2.cloned.1.call-done) | copy-start | bytes 42467332
  187.4 7.7 %collective-permute-start = (bf16[256,64]{1,0:T(8,128)(2,1)S(1)}, bf16[256,64]{1,0:T(8,128)(2,1)S(1)}, u32[]{:S(2)}, u32[]{:S(2)}) collective-permute-start(bf16[256,64]{1,0:T(8,128)(2,1)S(1)} %convert_element_type.30), channel_id=1, source_target_pairs={{64,0},{65,1},{66,2},{67,3},{68,4},{69,5},{70,6},{71,7},{72,8},{73... | collective-permute-start | bytes 98312 | tf_op jit(solution)/shard_map/ppermute | solution.py:327
  207.8 25.8 %all-to-all-start.1 = ((bf16[64,24,384]{2,1,0:T(8,128)(2,1)}), bf16[64,24,384]{2,1,0:T(8,128)(2,1)S(1)}, u32[]{:S(2)}, u32[]{:S(2)}) async-start(bf16[64,24,384]{2,1,0:T(8,128)(2,1)} %bitcast.11), calls=%async_computation.1 | async-start | bytes 2359296 | tf_op jit(solution)/shard_map/all_to_all | solution.py:340
Sparse Core Ops, SparseCore 0:
  9.7 145.6 all-gather.1

commit v2 on v1

v2 whole, which is shorter than its diff:
```python
import jax
import jax.numpy as jnp
from jax import lax
from jax.experimental import pallas as pl
from jax.experimental.pallas import tpu as pltpu
from jax.sharding import PartitionSpec as P

HEADS = 12
HD = 128
CH = 64
RANK = 64
NSTEPS = 1000
IMG = 256
TXT = 128
ROWS = TXT + IMG
HW = HEADS * HD
CHUNK = 512
QUARTER = HW // 2
SIDE = 6 * RANK
SHARE = 72
PART = 128
BF = jnp.bfloat16
F32 = jnp.float32
SCALE = HD ** (-0.5)


def dot(left, right, left_dim=1, right_dim=0):
    dims = (((left_dim,), (right_dim,)), ((), ()))
    return lax.dot_general(left, right, dims, preferred_element_type=F32)


def high_low(values):
    high = values.astype(BF)
    return high, (values - high.astype(F32)).astype(BF)


def unit_rows(values):
    values = values.astype(F32)
    return (values * lax.rsqrt(jnp.mean(values * values, axis=-1, keepdims=True) + 1e-06)).astype(BF)


def pack_kernel(
    place_ref, base_ref, gen_down_ref, gen_up_ref, critic_down_ref, critic_up_ref, packed_ref, pair
):
    group = place_ref[0]

    def both(gen_ref, critic_ref):
        gen, critic = gen_ref[...].astype(F32), critic_ref[...].astype(F32)
        return jnp.concatenate([gen, jnp.where(group == 0, gen, critic)], axis=1).astype(BF)

    for core, side in enumerate(
        (both(gen_down_ref, critic_down_ref), both(gen_up_ref, critic_up_ref))
    ):
        start = pl.multiple_of(HW + group * HW + core * QUARTER, QUARTER)
        pair[core, :, :QUARTER] = base_ref[:, pl.ds(start, QUARTER)]
        pair[core, :, QUARTER:] = side
    rows = base_ref.shape[0]
    for device in range(packed_ref.shape[0]):
        packed_ref[device, :, : QUARTER + SIDE] = pair[device % 2]
        columns = base_ref[:, device * SHARE : (device + 1) * SHARE]
        packed_ref[device, :, QUARTER + SIDE :] = jnp.concatenate(
            [columns, jnp.zeros((rows, PART - SHARE), BF)], axis=1
        )


def mix_kernel(
    text_ref,
    other_text_ref,
    latent_in_ref,
    modulation_ref,
    packed_ref,
    prompt_ref,
    own_ref,
    other_ref,
    share_ref,
    side_ref,
):
    prompt = unit_rows(text_ref[...])
    prompt_ref[...] = prompt
    side_ref[...] = packed_ref[:, QUARTER : QUARTER + SIDE]
    prompts = jnp.concatenate([prompt, unit_rows(other_text_ref[...])], axis=0)
    quarter = dot(prompts, packed_ref[:, :QUARTER]).astype(BF)
    own_ref[...] = quarter[:TXT]
    other_ref[...] = quarter[TXT:]
    scaled_in = (latent_in_ref[...].astype(F32) * modulation_ref[...]).astype(BF)
    folds = jnp.concatenate([latent_in_ref[...], scaled_in], axis=0)
    share = dot(folds, packed_ref[:, QUARTER + SIDE :]).T[:SHARE].astype(BF)
    for device in range(share_ref.shape[0]):
        share_ref[device] = share


def forward_kernel(
    place_ref,
    sigma_ref,
    latent_ref,
    fresh_ref,
    prompt_ref,
    latent_in_ref,
    modulation_ref,
    velocity_out_ref,
    fold_ref,
    text_own_ref,
    text_core_ref,
    text_group_ref,
    text_both_ref,
    side_own_ref,
    side_core_ref,
    sample_ref,
    velocity_ref,
    narrow_velocity_ref,
    q_ref,
    k_ref,
    v_ref,
    weights_ref,
    inverse_ref,
    attended_ref,
    reduced_ref,
    picture_ref,
    role_up_ref,
    stacked,
    q_now,
    k_now,
    v_now,
    attended_now,
    text,
    downs,
    ups,
):
    group, core = place_ref[0], place_ref[1]
    sigma = sigma_ref[0, 0]
    for part_ref, part_group, part_core in (
        (text_own_ref, group, core),
        (text_core_ref, group, 1 - core),
        (text_group_ref, 1 - group, core),
        (text_both_ref, 1 - group, 1 - core),
    ):
        start = pl.multiple_of(part_group * HW + part_core * QUARTER, QUARTER)
        text[:, pl.ds(start, QUARTER)] = part_ref[...]

    @pl.when(core == 0)
    def _():
        downs[...] = side_own_ref[...]
        ups[...] = side_core_ref[...]

    @pl.when(core == 1)
    def _():
        downs[...] = side_core_ref[...]
        ups[...] = side_own_ref[...]

    role_up_ref[...] = ups[:, 3 * RANK :]

    def readout(latent, noise_level, role, switch, save):
        base = role * 3 * RANK
        narrow = latent.astype(BF)
        hidden = dot(narrow, latent_in_ref[...])
        inverse_rms = lax.rsqrt(jnp.mean(hidden * hidden, axis=-1, keepdims=True) + 1e-06)
        picture = (hidden * inverse_rms * (1.0 + noise_level * modulation_ref[...])).astype(BF)
        reduced_picture = dot(picture, downs[:, base : base + 3 * RANK]).astype(BF)
        reduced_prompt = dot(prompt_ref[...], downs[:, base : base + 3 * RANK]).astype(BF)

        @save
        def _():
            picture_ref[...] = picture
            reduced_ref[TXT:, :] = reduced_picture
            reduced_ref[:TXT, :] = reduced_prompt

        if switch is not None:
            reduced_picture = reduced_picture * switch.astype(BF)
            reduced_prompt = reduced_prompt * switch.astype(BF)
        scaled_high, scaled_low = high_low(narrow.astype(F32) * inverse_rms)
        for block, now in enumerate((q_now, k_now, v_now)):
            rank_span = slice(block * RANK, (block + 1) * RANK)
            up_span = slice(base + block * RANK, base + (block + 1) * RANK)
            left = jnp.concatenate(
                [scaled_high, scaled_low, scaled_high, reduced_picture[:, rank_span]], axis=1
            )
            for start in range(0, HW, CHUNK):
                own = slice(start, start + CHUNK)
                wide = slice(block * HW + start, block * HW + start + CHUNK)
                parts = fold_ref[wide, :].astype(F32)
                fold_high, fold_low = high_low(parts[:, :CH] + noise_level * parts[:, CH:])
                up = ups[own, up_span]
                stacked[...] = jnp.concatenate([fold_high, fold_high, fold_low, up], axis=1)
                picture_part = dot(left, stacked[...], 1, 1).astype(BF)
                if block == 0:
                    now[:, own] = picture_part
                else:
                    now[TXT:, own] = picture_part
                    text_span = slice((block - 1) * HW + start, (block - 1) * HW + start + CHUNK)
                    adapter = dot(reduced_prompt[:, rank_span], up, 1, 1)
                    now[:TXT, own] = (text[:, text_span].astype(F32) + adapter).astype(BF)

        def head(index, carry):
            span = pl.ds(pl.multiple_of(index * HD, HD), HD)
            queries, keys, values = q_now[:, span], k_now[:, span], v_now[:, span]
            scores = dot(queries, keys, 1, 1) * SCALE
            largest = jnp.max(scores, axis=-1, keepdims=True)
            weights = jnp.exp(scores - largest)
            inverse = 1.0 / jnp.sum(weights, axis=-1, keepdims=True)
            weights = weights.astype(BF)
            attended = (dot(weights, values) * inverse).astype(BF)
            attended_now[:, span] = attended

            @save
            def _():
                q_ref[:, span] = queries
                k_ref[:, span] = keys
                v_ref[:, span] = values
                attended_ref[:, span] = attended
                weights_ref[index] = weights
                inverse_ref[index] = inverse

            return carry

        lax.fori_loop(0, HEADS, head, 0, unroll=2)
        return dot(attended_now[...], velocity_out_ref[...])

    latent = latent_ref[...]
    sample = latent - readout(latent, 1.0, 0, None, lambda f: f())
    sample_ref[...] = sample
    noised = (1.0 - sigma) * sample + sigma * fresh_ref[...]
    velocity = readout(noised, sigma, 1, group.astype(F32), pl.when(group == 1))
    velocity_ref[...] = velocity
    narrow_velocity_ref[...] = velocity.astype(BF)


def backward_kernel(
    place_ref,
    sigma_ref,
    sample_ref,
    fresh_ref,
    own_ref,
    fake_ref,
    prompt_ref,
    velocity_out_ref,
    role_up_ref,
    q_ref,
    k_ref,
    v_ref,
    weights_ref,
    inverse_ref,
    attended_ref,
    reduced_ref,
    picture_ref,
    grads_ref,
    grad_q,
    grad_k,
    grad_v,
):
    flag = place_ref[0]
    sigma = sigma_ref[0, 0]
    sample = sample_ref[...]
    own = own_ref[...]
    noised = (1.0 - sigma) * sample + sigma * fresh_ref[...]
    clean_real = noised - sigma * own
    clean_fake = noised - sigma * fake_ref[...].astype(F32)
    distance = jnp.sum(jnp.sum(jnp.abs(sample - clean_real), axis=1, keepdims=True), axis=0, keepdims=True)
    spread = distance * (1.0 / (IMG * CH)) + 1e-05
    cot_gen = -(clean_fake - clean_real) / spread
    cot_critic = 2.0 * (own - (fresh_ref[...] - sample)) / (IMG * CH)
    cotangent = jnp.where(flag == 0, cot_gen, cot_critic).astype(BF)

    def head(index, carry):
        span = pl.ds(pl.multiple_of(index * HD, HD), HD)
        queries, keys, values = q_ref[:, span], k_ref[:, span], v_ref[:, span]
        weights = weights_ref[index]
        upstream = dot(cotangent, velocity_out_ref[span, :], 1, 1) * inverse_ref[index]
        inner = jnp.sum(upstream * attended_ref[:, span].astype(F32), axis=-1, keepdims=True)
        upstream = upstream.astype(BF)
        grad_v[:, span] = dot(weights, upstream, 0, 0).astype(BF)
        grad_weights = dot(upstream, values, 1, 1)
        grad_scores = (weights.astype(F32) * (grad_weights - inner) * SCALE).astype(BF)
        grad_q[:, span] = dot(grad_scores, keys).astype(BF)
        grad_k[:, span] = dot(grad_scores, queries, 0, 0).astype(BF)
        return carry

    lax.fori_loop(0, HEADS, head, 0, unroll=2)
    spans = [slice(block * RANK, (block + 1) * RANK) for block in range(3)]
    reduced_q = dot(grad_q[...], role_up_ref[:, spans[0]]).astype(BF)
    reduced_k = dot(grad_k[...], role_up_ref[:, spans[1]]).astype(BF)
    reduced_v = dot(grad_v[...], role_up_ref[:, spans[2]]).astype(BF)
    reduced_kv = jnp.concatenate([reduced_k, reduced_v], axis=1)
    down_q = dot(reduced_q, picture_ref[...], 0, 0)
    down_kv = dot(reduced_kv[:TXT], prompt_ref[...], 0, 0) + dot(reduced_kv[TXT:], picture_ref[...], 0, 0)
    up_q = dot(reduced_ref[TXT:, spans[0]], grad_q[...], 0, 0)
    up_k = dot(reduced_ref[:, spans[1]], grad_k[...], 0, 0)
    up_v = dot(reduced_ref[:, spans[2]], grad_v[...], 0, 0)
    grads = jnp.concatenate([down_q, down_kv, up_q, up_k, up_v], axis=0)
    grads_ref[...] = grads.T.astype(BF)


def vmem():
    return pl.BlockSpec(memory_space=pltpu.VMEM)


def smem():
    return pl.BlockSpec(memory_space=pltpu.SMEM)


def run(kernel, name, scalars, outputs, scratch, *operands):
    shapes = tuple(jax.ShapeDtypeStruct(*output) for output in outputs)
    return pl.pallas_call(
        kernel,
        out_shape=shapes,
        in_specs=[smem()] * scalars + [vmem()] * (len(operands) - scalars),
        out_specs=tuple([vmem()] * len(outputs)),
        scratch_shapes=[pltpu.VMEM(*buffer) for buffer in scratch],
        compiler_params=pltpu.CompilerParams(vmem_limit_bytes=48 * 2**20),
        name=name,
    )(*operands)


def per_device(
    latent_noise,
    fresh_noise,
    text_states,
    step_index,
    base_qkv,
    latent_in,
    modulation,
    velocity_out,
    gen_down,
    gen_up,
    critic_down,
    critic_up,
):
    devices = lax.axis_size("fsdp")
    group = lax.axis_index("group")
    core = lax.rem(lax.axis_index("fsdp"), 2)
    place = jnp.stack([group, core]).astype(jnp.int32)
    sigma = ((step_index + 1).astype(F32) / NSTEPS).reshape(1, 1)
    shard = base_qkv.shape[0]
    cores = [(device, device ^ 1) for device in range(devices)]
    both = [
        (g * devices + device, (1 - g) * devices + (device ^ 1))
        for g in range(2)
        for device in range(devices)
    ]
    fresh = fresh_noise[0]
    text = text_states[0]
    gain = modulation.reshape(1, HW)

    other_text = lax.ppermute(text, "fsdp", cores)
    (packed,) = run(
        pack_kernel,
        "pack",
        1,
        [((devices, shard, QUARTER + SIDE + PART), BF)],
        [((2, shard, QUARTER + SIDE), BF)],
        place,
        base_qkv,
        gen_down,
        gen_up.reshape(3 * RANK, shard).T,
        critic_down,
        critic_up.reshape(3 * RANK, shard).T,
    )
    packed = lax.all_to_all(packed, "fsdp", 0, 0).reshape(HW, QUARTER + SIDE + PART)
    prompt, text_own, text_other, share, side_own = run(
        mix_kernel,
        "mix",
        0,
        [
            ((TXT, HW), BF),
            ((TXT, QUARTER), BF),
            ((TXT, QUARTER), BF),
            ((devices, SHARE, PART), BF),
            ((HW, SIDE), BF),
        ],
        [],
        text,
        other_text,
        latent_in,
        gain,
        packed,
    )
    text_core = lax.ppermute(text_other, "fsdp", cores)
    text_group = lax.ppermute(text_own, "group", [(0, 1), (1, 0)])
    text_both = lax.ppermute(text_other, ("group", "fsdp"), both)
    side_core = lax.ppermute(side_own, "fsdp", cores)
    fold = lax.all_to_all(share, "fsdp", 0, 0).reshape(devices * SHARE, PART)

    sample, velocity, narrow_velocity, *saved, role_up = run(
        forward_kernel,
        "forward",
        2,
        [
            ((IMG, CH), F32),
            ((IMG, CH), F32),
            ((IMG, CH), BF),
            ((IMG, HW), BF),
            ((ROWS, HW), BF),
            ((ROWS, HW), BF),
            ((HEADS, IMG, ROWS), BF),
            ((HEADS, IMG, 1), F32),
            ((IMG, HW), BF),
            ((ROWS, 3 * RANK), BF),
            ((IMG, HW), BF),
            ((HW, 3 * RANK), BF),
        ],
        [
            ((CHUNK, 4 * CH), BF),
            ((IMG, HW), BF),
            ((ROWS, HW), BF),
            ((ROWS, HW), BF),
            ((IMG, HW), BF),
            ((TXT, 2 * HW), BF),
            ((HW, SIDE), BF),
            ((HW, SIDE), BF),
        ],
        place,
        sigma,
        latent_noise[0],
        fresh,
        prompt,
        latent_in,
        gain,
        velocity_out,
        fold,
        text_own,
        text_core,
        text_group,
        text_both,
        side_own,
        side_core,
    )
    fake_velocity = lax.ppermute(narrow_velocity, "group", [(1, 0)])
    (grads,) = run(
        backward_kernel,
        "backward",
        2,
        [((HW, SIDE), BF)],
        [((IMG, HW), BF), ((ROWS, HW), BF), ((ROWS, HW), BF)],
        place,
        sigma,
        sample,
        fresh,
        velocity,
        fake_velocity,
        prompt,
        velocity_out,
        role_up,
        *saved,
    )
    shares = lax.all_to_all(grads.reshape(devices, shard, SIDE), "fsdp", 0, 0)
    total = jnp.sum(shares.astype(F32), axis=0)
    share_down = total[:, : 3 * RANK]
    share_up = total[:, 3 * RANK :].T.reshape(3, RANK, shard)
    return (sample[None], share_down[None], share_up[None])


def solution(mesh):
    in_specs = (
        P("fsdp", None, None),
        P("fsdp", None, None),
        P("fsdp", None, None),
        P("fsdp"),
        P("fsdp", None),
        P(),
        P(),
        P(),
        P("fsdp", None),
        P(None, None, "fsdp"),
        P("fsdp", None),
        P(None, None, "fsdp"),
    )
    out_specs = (P("fsdp", None, None), P("group", "fsdp", None), P("group", None, None, "fsdp"))
    return jax.shard_map(
        per_device, mesh=mesh, in_specs=in_specs, out_specs=out_specs, check_vma=False
    )
```

time: 244 us -> 177 us (0.73)
  waiting for transfers between devices: 150 us -> 91.5 us
  starting transfers between devices: 17.6 us -> 33.4 us
  between operations: 14.8 us -> 1.43 us
  matrix products: 11.2 us -> 0 us
  Pallas kernels: 32.2 us -> 39.2 us
  local copies, waits for them, and re-layouts: 13.2 us -> 9.45 us
  other arithmetic: 2.78 us -> 0.27 us
    all_gather x1 -> x0, waiting for transfers between devices: 85.5 us -> none  [per_device(): weights = lax.all_gather(base_qkv, 'fsdp', axis=0, tiled=True)]
    ppermute x1 -> x6, waiting for transfers between devices: 6.18 us -> 27 us  [the longest x1 16 us: per_device(): text_group = lax.ppermute(text_own, 'group', [(0, 1), (1, 0)])]
    dot_general x2 -> x0, matrix products: 11.2 us -> none  [dot(): return lax.dot_general(left, right, dims, preferred_element_type=F32)]
    all_to_all x2 -> x3, starting transfers between devices: 16.1 us -> 27.3 us  [the longest x1 9.74 us: per_device(): lax.all_to_all(packed, 'fsdp', 0, 0).reshape(HW, QUARTER + SIDE + PART)]
    pallas_call x2 -> x4, Pallas kernels: 32.2 us -> 39.2 us  [run(): pl.pallas_call(kernel, out_shape=shapes, in_specs=[smem()] * scalars + [v...]
    all_to_all x2 -> x3, waiting for transfers between devices: 57.7 us -> 64.4 us  [the longest x1 45.6 us: per_device(): lax.all_to_all(packed, 'fsdp', 0, 0).reshape(HW, QUARTER + SIDE + PART)]
    slice x3 -> x0, local copies, waits for them, and re-layouts: 5.48 us -> none  [the longest x1 2.76 us: per_device(): role_down_full = adapters[:, 3 * RANK:6 * RANK]]
    ppermute x1 -> x6, starting transfers between devices: 1.47 us -> 6.11 us  [the longest x1 3.66 us: per_device(): text_group = lax.ppermute(text_own, 'group', [(0, 1), (1, 0)])]
  transfers between devices with their start and end apart: 4 -> 9, of which waited for: 4 -> 6; matrix products, arithmetic and copies ran while one was open for 5% -> 1% of each run, Pallas kernels for 0% -> 0%
where the time goes in v2:
time: 177 us; the launch traced here: 175 us
  waiting for transfers between devices  91.5 us (52%)
  Pallas kernels  39.2 us (22%)
  starting transfers between devices  33.4 us (19%)
  local copies, waits for them, and re-layouts  9.45 us (5%)
    all_to_all x1, waiting for transfers between devices, per_device(): lax.all_to_all(packed, 'fsdp', 0, 0).reshape(HW, QUARTER + SIDE + PART)  45.6 us
    pallas_call x4, Pallas kernels, run(): pl.pallas_call(kernel, out_shape=shapes, in_specs=[smem()] * scalars + [v...  39.2 us
    all_to_all x1, waiting for transfers between devices, per_device(): shares = lax.all_to_all(grads.reshape(devices, shard, SIDE), 'fsdp', 0, 0)  18.8 us
    ppermute x1, waiting for transfers between devices, per_device(): text_group = lax.ppermute(text_own, 'group', [(0, 1), (1, 0)])  16 us
    all_to_all x1, starting transfers between devices, per_device(): lax.all_to_all(packed, 'fsdp', 0, 0).reshape(HW, QUARTER + SIDE + PART)  9.74 us
    all_to_all x1, starting transfers between devices, per_device(): fold = lax.all_to_all(share, 'fsdp', 0, 0).reshape(devices * SHARE, PART)  9.18 us
    unnamed x27, local copies, waits for them, and re-layouts  8.56 us
    all_to_all x1, starting transfers between devices, per_device(): shares = lax.all_to_all(grads.reshape(devices, shard, SIDE), 'fsdp', 0, 0)  8.36 us
  transfers between devices with their start and end apart: 9, of which 6 were waited for; matrix products, arithmetic and copies ran while one was open for 1% of the time, Pallas kernels for 0%

profile of v2, /device:TPU:0, one launch (start us, length us, event | category | flops | bytes accessed | tf_op | source)
XLA Modules:
  0.0 175.1 jit_solution(2630837090560591336)
XLA Ops:
  0.6 0.7 copy.24
  1.4 0.1 reshape.29
  1.5 0.7 copy.25
  2.2 0.1 reshape.30
  2.3 0.1 pad_add_fusion.place_ref
  2.4 0.0 copy-start.4
  2.4 0.9 copy-done.4
  3.3 0.0 copy-start.5
  3.3 0.7 copy-done.5
  4.0 0.7 copy-done.6
  4.7 1.0 pack.1
  5.7 0.0 copy-start
  5.7 1.9 %copy-done = bf16[64,24,1280]{2,1,0:T(8,128)(2,1)} copy-done((bf16[64,24,1280]{2,1,0:T(8,128)(2,1)}, bf16[64,24,1280]{2,1,0:T(8,128)(2,1)S(1)}, u32[]{:S(2)}) %copy-start) | copy-done | bytes 3932184
  7.6 9.7 %all-to-all-start = ((bf16[64,24,1280]{2,1,0:T(8,128)(2,1)}), bf16[64,24,1280]{2,1,0:T(8,128)(2,1)}, u32[]{:S(2)}, u32[]{:S(2)}) async-start(bf16[64,24,1280]{2,1,0:T(8,128)(2,1)} %copy-done), calls=%async_computation | async-start | bytes 7864320 | tf_op jit(solution)/shard_map/all_to_all | solution.py:357
  17.4 0.0 copy-done.3
  17.4 0.1 collective-permute-start
  17.5 0.0 copy-done.9
  17.5 1.7 collective-permute-done.other_text_ref
  19.2 45.6 %all-to-all-done = bf16[64,24,1280]{2,1,0:T(8,128)(2,1)} async-done(((bf16[64,24,1280]{2,1,0:T(8,128)(2,1)}), bf16[64,24,1280]{2,1,0:T(8,128)(2,1)}, u32[]{:S(2)}, u32[]{:S(2)}) %all-to-all-start) | async-done | bytes 3932192 | tf_op jit(solution)/shard_map/all_to_all | solution.py:357
  64.8 0.0 copy-done.2
  64.8 4.5 %mix.1 = (bf16[128,1536]{1,0:T(8,128)(2,1)S(1)}, bf16[128,768]{1,0:T(8,128)(2,1)S(1)}, bf16[128,768]{1,0:T(8,128)(2,1)S(1)}, bf16[64,72,128]{2,1,0:T(8,128)(2,1)}, bf16[1536,384]{1,0:T(8,128)(2,1)S(1)}) custom-call(bf16[128,1536]{1,0:T(8,128)(2,1)S(1)} %bitcast.27, bf16[128,1536]{1,0:T(8,128)(2,1)S(1)} %collective-permute-done.other_text_ref, ...), custom_call_target="tpu_custom_call" | custom-call | tf_op jit(solution)/shard_map/mix/pallas_call | solution.py:302
  69.3 0.9 collective-permute-start.4
  70.2 0.2 copy-done.1
  70.4 9.2 %all-to-all-start.1 = ((bf16[64,72,128]{2,1,0:T(8,128)(2,1)}), bf16[64,72,128]{2,1,0:T(8,128)(2,1)}, u32[]{:S(2)}, u32[]{:S(2)}) async-start(bf16[64,72,128]{2,1,0:T(8,128)(2,1)} %get-tuple-element.21), calls=%async_computation.1 | async-start | bytes 2359296 | tf_op jit(solution)/shard_map/all_to_all | solution.py:380
  79.6 3.7 %collective-permute-start.2 = (bf16[128,768]{1,0:T(8,128)(2,1)S(1)}, bf16[128,768]{1,0:T(8,128)(2,1)S(1)}, u32[]{:S(2)}, u32[]{:S(2)}) collective-permute-start(bf16[128,768]{1,0:T(8,128)(2,1)S(1)} %get-tuple-element.22.text_own_ref), channel_id=1, source_target_pairs={{0,64},{64,0},{1,65},{65,1},{2,66},{66,2},{3,67},{67,3},{4,68},{68... | collective-permute-start | bytes 589832 | tf_op jit(solution)/shard_map/ppermute | solution.py:377
  83.2 0.0 collective-permute-start.3
  83.2 0.2 collective-permute-start.1
  84.1 0.0 copy-done.7
  84.1 0.1 copy.22
  84.2 0.0 copy-done.8
  84.2 0.1 copy.23
  84.3 1.2 copy.26.velocity_out_ref
  85.5 16.0 %collective-permute-done.2.text_group_ref = bf16[128,768]{1,0:T(8,128)(2,1)S(1)} collective-permute-done((bf16[128,768]{1,0:T(8,128)(2,1)S(1)}, bf16[128,768]{1,0:T(8,128)(2,1)S(1)}, u32[]{:S(2)}, u32[]{:S(2)}) %collective-permute-start.2) | collective-permute-done | bytes 196640 | tf_op jit(solution)/shard_map/ppermute | solution.py:377
  101.4 2.8 %collective-permute-done.3.text_both_ref = bf16[128,768]{1,0:T(8,128)(2,1)S(1)} collective-permute-done((bf16[128,768]{1,0:T(8,128)(2,1)S(1)}, bf16[128,768]{1,0:T(8,128)(2,1)S(1)}, u32[]{:S(2)}, u32[]{:S(2)}) %collective-permute-start.3) | collective-permute-done | bytes 196640 | tf_op jit(solution)/shard_map/ppermute | solution.py:378
  104.2 0.0 collective-permute-done.1.text_core_ref
  104.2 0.0 all-to-all-done.1
  104.2 0.0 collective-permute-done.4.side_core_ref
  104.2 21.2 %forward.1 = (f32[256,64]{1,0:T(8,128)S(1)}, f32[256,64]{1,0:T(8,128)S(1)}, bf16[256,64]{1,0:T(8,128)(2,1)S(1)}, bf16[256,1536]{1,0:T(8,128)(2,1)S(1)}, bf16[384...) custom-call(s32[2]{0:T(128)S(1)} %pad_add_fusion.place_ref, ...), custom_call_target="tpu_custom_call" | custom-call | tf_op jit(solution)/shard_map/forward/pallas_call | solution.py:302
  125.4 1.3 collective-permute-start.5
  126.7 6.6 %collective-permute-done.5.fake_ref = bf16[256,64]{1,0:T(8,128)(2,1)S(1)} collective-permute-done((bf16[256,64]{1,0:T(8,128)(2,1)S(1)}, bf16[256,64]{1,0:T(8,128)(2,1)S(1)}, u32[]{:S(2)}, u32[]{:S(2)}) %collective-permute-start.5) | collective-permute-done | bytes 32800 | tf_op jit(solution)/shard_map/ppermute | solution.py:426
  133.3 12.5 %backward.1 = bf16[1536,384]{1,0:T(8,128)(2,1)} custom-call(s32[2]{0:T(128)S(1)} %pad_add_fusion.place_ref, f32[1,1]{1,0:T(1,128)} %bitcast.2.sigma_ref, f32[256,64]{1,0:T(8,128)S(1)} %get-tuple-element.25.sample_ref, f32[256,64]{1,0:T(8,128)S(1)} %bitcast.23, f32[256,64]{1,0:T(8,128)S(1)} %get-tuple-element.26.own_ref, ...), custom_call_target="tpu_custom_call" | custom-call | tf_op jit(solution)/shard_map/backward/pallas_call | solution.py:302
  145.8 8.4 %all-to-all-start.2 = ((bf16[64,24,384]{2,1,0:T(8,128)(2,1)}), bf16[64,24,384]{2,1,0:T(8,128)(2,1)S(1)}, u32[]{:S(2)}, u32[]{:S(2)}) async-start(bf16[64,24,384]{2,1,0:T(8,128)(2,1)} %bitcast.11), calls=%async_computation.2 | async-start | bytes 2359296 | tf_op jit(solution)/shard_map/all_to_all | solution.py:444
  154.2 0.7 copy.28
  154.9 18.8 %all-to-all-done.2 = bf16[64,24,384]{2,1,0:T(8,128)(2,1)S(1)} async-done(((bf16[64,24,384]{2,1,0:T(8,128)(2,1)}), bf16[64,24,384]{2,1,0:T(8,128)(2,1)S(1)}, u32[]{:S(2)}, u32[]{:S(2)}) %all-to-all-start.2) | async-done | bytes 1179680 | tf_op jit(solution)/shard_map/all_to_all | solution.py:444
  173.6 0.2 convert_reduce_fusion
  173.8 0.6 slice_bitcast_fusion
  174.4 0.1 broadcast_in_dim_reshape.3
  174.5 0.6 copy.29
  (8 shorter events, 0.0 us)
Async XLA Ops:
  2.4 0.9 copy-start.4
  3.3 0.7 copy-start.5
  4.0 0.7 copy-start.6
  5.7 1.9 %copy-start = (bf16[64,24,1280]{2,1,0:T(8,128)(2,1)}, bf16[64,24,1280]{2,1,0:T(8,128)(2,1)S(1)}, u32[]{:S(2)}) copy-start(bf16[64,24,1280]{2,1,0:T(8,128)(2,1)S(1)} %pack.1) | copy-start | bytes 11796484
  7.6 9.8 %copy-start.3 = (bf16[1,128,1536]{2,1,0:T(8,128)(2,1)S(1)}, bf16[1,128,1536]{2,1,0:T(8,128)(2,1)}, u32[]{:S(2)}) copy-start(bf16[1,128,1536]{2,1,0:T(8,128)(2,1)} %param.14) | copy-start | bytes 1179652
  7.6 9.9 %copy-start.9 = (f32[1536]{0:T(1024)S(1)}, f32[1536]{0:T(1024)}, u32[]{:S(2)}) copy-start(f32[1536]{0:T(1024)} %param.18) | copy-start | bytes 18436
  7.6 57.2 %copy-start.2 = (bf16[64,1536]{1,0:T(8,128)(2,1)S(1)}, bf16[64,1536]{1,0:T(8,128)(2,1)}, u32[]{:S(2)}) copy-start(bf16[64,1536]{1,0:T(8,128)(2,1)} %latent_in_ref.3) | copy-start | bytes 589828
  7.6 57.2 %all-to-all-start = ((bf16[64,24,1280]{2,1,0:T(8,128)(2,1)}), bf16[64,24,1280]{2,1,0:T(8,128)(2,1)}, u32[]{:S(2)}, u32[]{:S(2)}) async-start(bf16[64,24,1280]{2,1,0:T(8,128)(2,1)} %copy-done), calls=%async_computation | async-start | bytes 7864320 | tf_op jit(solution)/shard_map/all_to_all | solution.py:357
  17.4 1.8 %collective-permute-start = (bf16[128,1536]{1,0:T(8,128)(2,1)S(1)}, bf16[128,1536]{1,0:T(8,128)(2,1)S(1)}, u32[]{:S(2)}, u32[]{:S(2)}) collective-permute-start(bf16[128,1536]{1,0:T(8,128)(2,1)S(1)} %bitcast.26), channel_id=1, source_target_pairs={{0,1},{1,0},{2,3},{3,2},{4,5},{5,4},{6,7},{7,6},{8,9},{9,8},{10,11... | collective-permute-start | bytes 1179656 | tf_op jit(solution)/shard_map/ppermute | solution.py:343
  69.3 1.1 copy-start.1
  69.3 34.9 %collective-permute-start.4 = (bf16[1536,384]{1,0:T(8,128)(2,1)S(1)}, bf16[1536,384]{1,0:T(8,128)(2,1)}, u32[]{:S(2)}, u32[]{:S(2)}) collective-permute-start(bf16[1536,384]{1,0:T(8,128)(2,1)S(1)} %get-tuple-element.24.side_own_ref), channel_id=1, source_target_pairs={{0,1},{1,0},{2,3},{3,2},{4,5},{5,4},{6,7},{7,6},{8,9},{9,8},{10,11... | collective-permute-start | bytes 3538952 | tf_op jit(solution)/shard_map/ppermute | solution.py:379
  70.2 13.9 %copy-start.7 = (f32[1,256,64]{1,2,0:T(8,128)S(1)}, f32[1,256,64]{1,2,0:T(8,128)}, u32[]{:S(2)}) copy-start(f32[1,256,64]{1,2,0:T(8,128)} %param.12) | copy-start | bytes 196612
  70.2 14.0 %copy-start.8 = (f32[1,256,64]{1,2,0:T(8,128)S(1)}, f32[1,256,64]{1,2,0:T(8,128)}, u32[]{:S(2)}) copy-start(f32[1,256,64]{1,2,0:T(8,128)} %param.13) | copy-start | bytes 196612
  70.4 33.8 %all-to-all-start.1 = ((bf16[64,72,128]{2,1,0:T(8,128)(2,1)}), bf16[64,72,128]{2,1,0:T(8,128)(2,1)}, u32[]{:S(2)}, u32[]{:S(2)}) async-start(bf16[64,72,128]{2,1,0:T(8,128)(2,1)} %get-tuple-element.21), calls=%async_computation.1 | async-start | bytes 2359296 | tf_op jit(solution)/shard_map/all_to_all | solution.py:380
  79.6 21.9 %collective-permute-start.2 = (bf16[128,768]{1,0:T(8,128)(2,1)S(1)}, bf16[128,768]{1,0:T(8,128)(2,1)S(1)}, u32[]{:S(2)}, u32[]{:S(2)}) collective-permute-start(bf16[128,768]{1,0:T(8,128)(2,1)S(1)} %get-tuple-element.22.text_own_ref), channel_id=1, source_target_pairs={{0,64},{64,0},{1,65},{65,1},{2,66},{66,2},{3,67},{67,3},{4,68},{68... | collective-permute-start | bytes 589832 | tf_op jit(solution)/shard_map/ppermute | solution.py:377
  83.2 21.0 %collective-permute-start.3 = (bf16[128,768]{1,0:T(8,128)(2,1)S(1)}, bf16[128,768]{1,0:T(8,128)(2,1)S(1)}, u32[]{:S(2)}, u32[]{:S(2)}) collective-permute-start(bf16[128,768]{1,0:T(8,128)(2,1)S(1)} %get-tuple-element.23), channel_id=1, source_target_pairs={{0,65},{1,64},{2,67},{3,66},{4,69},{5,68},{6,71},{7,70},{8,73},{9,... | collective-permute-start | bytes 589832 | tf_op jit(solution)/shard_map/ppermute | solution.py:378
  83.2 21.0 %collective-permute-start.1 = (bf16[128,768]{1,0:T(8,128)(2,1)S(1)}, bf16[128,768]{1,0:T(8,128)(2,1)S(1)}, u32[]{:S(2)}, u32[]{:S(2)}) collective-permute-start(bf16[128,768]{1,0:T(8,128)(2,1)S(1)} %get-tuple-element.23), channel_id=1, source_target_pairs={{0,1},{1,0},{2,3},{3,2},{4,5},{5,4},{6,7},{7,6},{8,9},{9,8},{10,11... | collective-permute-start | bytes 589832 | tf_op jit(solution)/shard_map/ppermute | solution.py:376
  125.4 7.9 %collective-permute-start.5 = (bf16[256,64]{1,0:T(8,128)(2,1)S(1)}, bf16[256,64]{1,0:T(8,128)(2,1)S(1)}, u32[]{:S(2)}, u32[]{:S(2)}) collective-permute-start(bf16[256,64]{1,0:T(8,128)(2,1)S(1)} %get-tuple-element.27), channel_id=1, source_target_pairs={{64,0},{65,1},{66,2},{67,3},{68,4},{69,5},{70,6},{71,7},{72,8},{73... | collective-permute-start | bytes 98312 | tf_op jit(solution)/shard_map/ppermute | solution.py:426
  145.8 27.8 %all-to-all-start.2 = ((bf16[64,24,384]{2,1,0:T(8,128)(2,1)}), bf16[64,24,384]{2,1,0:T(8,128)(2,1)S(1)}, u32[]{:S(2)}, u32[]{:S(2)}) async-start(bf16[64,24,384]{2,1,0:T(8,128)(2,1)} %bitcast.11), calls=%async_computation.2 | async-start | bytes 2359296 | tf_op jit(solution)/shard_map/all_to_all | solution.py:444

commit v3 on v2

--- a/solution.py
+++ b/solution.py
@@ -15,10 +15,11 @@
 ROWS = TXT + IMG
 HW = HEADS * HD
 CHUNK = 512
-QUARTER = HW // 2
+EIGHTH = HW // 4
 SIDE = 6 * RANK
 SHARE = 72
 PART = 128
+MOVES = tuple((group, near) for group in range(2) for near in range(4))
 BF = jnp.bfloat16
 F32 = jnp.float32
 SCALE = HD ** (-0.5)
@@ -40,53 +41,67 @@
 
 
 def pack_kernel(
-    place_ref, base_ref, gen_down_ref, gen_up_ref, critic_down_ref, critic_up_ref, packed_ref, pair
+    place_ref,
+    base_ref,
+    gen_down_ref,
+    gen_up_ref,
+    critic_down_ref,
+    critic_up_ref,
+    packed_ref,
 ):
     group = place_ref[0]
 
-    def both(gen_ref, critic_ref):
-        gen, critic = gen_ref[...].astype(F32), critic_ref[...].astype(F32)
+    def both(gen, critic):
+        gen, critic = gen.astype(F32), critic.astype(F32)
         return jnp.concatenate([gen, jnp.where(group == 0, gen, critic)], axis=1).astype(BF)
 
-    for core, side in enumerate(
-        (both(gen_down_ref, critic_down_ref), both(gen_up_ref, critic_up_ref))
-    ):
-        start = pl.multiple_of(HW + group * HW + core * QUARTER, QUARTER)
-        pair[core, :, :QUARTER] = base_ref[:, pl.ds(start, QUARTER)]
-        pair[core, :, QUARTER:] = side
+    sides = (
+        both(gen_down_ref[...], critic_down_ref[...]),
+        both(gen_up_ref[...].T, critic_up_ref[...].T),
+    )
     rows = base_ref.shape[0]
-    for device in range(packed_ref.shape[0]):
-        packed_ref[device, :, : QUARTER + SIDE] = pair[device % 2]
-        columns = base_ref[:, device * SHARE : (device + 1) * SHARE]
-        packed_ref[device, :, QUARTER + SIDE :] = jnp.concatenate(
-            [columns, jnp.zeros((rows, PART - SHARE), BF)], axis=1
-        )
+    for near in range(4):
+        start = pl.multiple_of(HW + group * HW + near * EIGHTH, EIGHTH)
+        eighth = base_ref[:, pl.ds(start, EIGHTH)]
+        for device in range(near, packed_ref.shape[0], 4):
+            packed_ref[device, :, :EIGHTH] = eighth
+            packed_ref[device, :, EIGHTH : EIGHTH + SIDE] = sides[near % 2]
+            columns = base_ref[:, device * SHARE : (device + 1) * SHARE]
+            packed_ref[device, :, EIGHTH + SIDE :] = jnp.concatenate(
+                [columns, jnp.zeros((rows, PART - SHARE), BF)], axis=1
+            )
+
+
+def fold_kernel(latent_in_ref, modulation_ref, packed_ref, share_ref, side_ref):
+    scaled_in = (latent_in_ref[...].astype(F32) * modulation_ref[...]).astype(BF)
+    folds = jnp.concatenate([latent_in_ref[...], scaled_in], axis=0)
+    share = dot(folds, packed_ref[:, EIGHTH + SIDE :]).T[:SHARE].astype(BF)
+    for device in range(share_ref.shape[0]):
+        share_ref[device] = share
+    side_ref[...] = packed_ref[:, EIGHTH : EIGHTH + SIDE]
 
 
 def mix_kernel(
-    text_ref,
-    other_text_ref,
-    latent_in_ref,
-    modulation_ref,
+    text_0_ref,
+    text_1_ref,
+    text_2_ref,
+    text_3_ref,
     packed_ref,
     prompt_ref,
-    own_ref,
-    other_ref,
-    share_ref,
-    side_ref,
+    out_0_ref,
+    out_1_ref,
+    out_2_ref,
+    out_3_ref,
 ):
-    prompt = unit_rows(text_ref[...])
+    prompt = unit_rows(text_0_ref[...])
     prompt_ref[...] = prompt
-    side_ref[...] = packed_ref[:, QUARTER : QUARTER + SIDE]
-    prompts = jnp.concatenate([prompt, unit_rows(other_text_ref[...])], axis=0)
-    quarter = dot(prompts, packed_ref[:, :QUARTER]).astype(BF)
-    own_ref[...] = quarter[:TXT]
-    other_ref[...] = quarter[TXT:]
-    scaled_in = (latent_in_ref[...].astype(F32) * modulation_ref[...]).astype(BF)
-    folds = jnp.concatenate([latent_in_ref[...], scaled_in], axis=0)
-    share = dot(folds, packed_ref[:, QUARTER + SIDE :]).T[:SHARE].astype(BF)
-    for device in range(share_ref.shape[0]):
-        share_ref[device] = share
+    out_0_ref[...] = dot(prompt, packed_ref[:, :EIGHTH]).astype(BF)
+    for text_ref, out_ref in (
+        (text_1_ref, out_1_ref),
+        (text_2_ref, out_2_ref),
+        (text_3_ref, out_3_ref),
+    ):
+        out_ref[...] = dot(unit_rows(text_ref[...]), packed_ref[:, :EIGHTH]).astype(BF)
 
 
 def forward_kernel(
@@ -99,10 +114,14 @@
     modulation_ref,
     velocity_out_ref,
     fold_ref,
-    text_own_ref,
-    text_core_ref,
-    text_group_ref,
-    text_both_ref,
+    text_0_ref,
+    text_1_ref,
+    text_2_ref,
+    text_3_ref,
+    text_4_ref,
+    text_5_ref,
+    text_6_ref,
+    text_7_ref,
     side_own_ref,
     side_core_ref,
     sample_ref,
@@ -126,16 +145,21 @@
     downs,
     ups,
 ):
-    group, core = place_ref[0], place_ref[1]
+    group, near, core = place_ref[0], place_ref[1], place_ref[2]
     sigma = sigma_ref[0, 0]
-    for part_ref, part_group, part_core in (
-        (text_own_ref, group, core),
-        (text_core_ref, group, 1 - core),
-        (text_group_ref, 1 - group, core),
-        (text_both_ref, 1 - group, 1 - core),
-    ):
-        start = pl.multiple_of(part_group * HW + part_core * QUARTER, QUARTER)
-        text[:, pl.ds(start, QUARTER)] = part_ref[...]
+    text_refs = (
+        text_0_ref,
+        text_1_ref,
+        text_2_ref,
+        text_3_ref,
+        text_4_ref,
+        text_5_ref,
+        text_6_ref,
+        text_7_ref,
+    )
+    for (across, move), text_ref in zip(MOVES, text_refs):
+        start = (group ^ across) * HW + (near ^ move) * EIGHTH
+        text[:, pl.ds(pl.multiple_of(start, EIGHTH), EIGHTH)] = text_ref[...]
 
     @pl.when(core == 0)
     def _():
@@ -297,7 +321,7 @@
     return pl.BlockSpec(memory_space=pltpu.SMEM)
 
 
-def run(kernel, name, scalars, outputs, scratch, *operands):
+def run(kernel, name, megabytes, scalars, outputs, scratch, *operands):
     shapes = tuple(jax.ShapeDtypeStruct(*output) for output in outputs)
     return pl.pallas_call(
         kernel,
@@ -305,7 +329,7 @@
         in_specs=[smem()] * scalars + [vmem()] * (len(operands) - scalars),
         out_specs=tuple([vmem()] * len(outputs)),
         scratch_shapes=[pltpu.VMEM(*buffer) for buffer in scratch],
-        compiler_params=pltpu.CompilerParams(vmem_limit_bytes=48 * 2**20),
+        compiler_params=pltpu.CompilerParams(vmem_limit_bytes=megabytes * 2**20),
         name=name,
     )(*operands)
 
@@ -326,62 +350,72 @@
 ):
     devices = lax.axis_size("fsdp")
     group = lax.axis_index("group")
-    core = lax.rem(lax.axis_index("fsdp"), 2)
-    place = jnp.stack([group, core]).astype(jnp.int32)
+    index = lax.axis_index("fsdp")
+    place = jnp.stack([group, lax.rem(index, 4), lax.rem(index, 2)]).astype(jnp.int32)
     sigma = ((step_index + 1).astype(F32) / NSTEPS).reshape(1, 1)
     shard = base_qkv.shape[0]
-    cores = [(device, device ^ 1) for device in range(devices)]
-    both = [
-        (g * devices + device, (1 - g) * devices + (device ^ 1))
-        for g in range(2)
-        for device in range(devices)
-    ]
+
+    def move(array, across, near):
+        pairs = [
+            (g * devices + device, (g ^ across) * devices + (device ^ near))
+            for g in range(2)
+            for device in range(devices)
+        ]
+        return lax.ppermute(array, ("group", "fsdp"), pairs)
+
     fresh = fresh_noise[0]
     text = text_states[0]
     gain = modulation.reshape(1, HW)
 
-    other_text = lax.ppermute(text, "fsdp", cores)
+    texts = [text, move(text, 0, 1), move(text, 1, 2), move(text, 1, 3)]
     (packed,) = run(
         pack_kernel,
         "pack",
+        16,
         1,
-        [((devices, shard, QUARTER + SIDE + PART), BF)],
-        [((2, shard, QUARTER + SIDE), BF)],
+        [((devices, shard, EIGHTH + SIDE + PART), BF)],
+        [],
         place,
         base_qkv,
         gen_down,
-        gen_up.reshape(3 * RANK, shard).T,
+        gen_up.reshape(3 * RANK, shard),
         critic_down,
-        critic_up.reshape(3 * RANK, shard).T,
-    )
-    packed = lax.all_to_all(packed, "fsdp", 0, 0).reshape(HW, QUARTER + SIDE + PART)
-    prompt, text_own, text_other, share, side_own = run(
-        mix_kernel,
-        "mix",
+        critic_up.reshape(3 * RANK, shard),
+    )
+    packed = lax.all_to_all(packed, "fsdp", 0, 0).reshape(HW, EIGHTH + SIDE + PART)
+    packed, *texts = lax.optimization_barrier((packed, *texts))
+    share, side_own = run(
+        fold_kernel,
+        "fold",
+        16,
         0,
-        [
-            ((TXT, HW), BF),
-            ((TXT, QUARTER), BF),
-            ((TXT, QUARTER), BF),
-            ((devices, SHARE, PART), BF),
-            ((HW, SIDE), BF),
-        ],
+        [((devices, SHARE, PART), BF), ((HW, SIDE), BF)],
         [],
-        text,
-        other_text,
         latent_in,
         gain,
         packed,
     )
-    text_core = lax.ppermute(text_other, "fsdp", cores)
-    text_group = lax.ppermute(text_own, "group", [(0, 1), (1, 0)])
-    text_both = lax.ppermute(text_other, ("group", "fsdp"), both)
-    side_core = lax.ppermute(side_own, "fsdp", cores)
     fold = lax.all_to_all(share, "fsdp", 0, 0).reshape(devices * SHARE, PART)
+    side_core = move(side_own, 0, 1)
+    prompt, *parts = run(
+        mix_kernel,
+        "mix",
+        16,
+        0,
+        [((TXT, HW), BF)] + [((TXT, EIGHTH), BF)] * 4,
+        [],
+        *texts,
+        packed,
+    )
+    pieces = [
+        parts[near] if (across, near) == (0, 0) else move(parts[near], across, near)
+        for across, near in MOVES
+    ]
 
     sample, velocity, narrow_velocity, *saved, role_up = run(
         forward_kernel,
         "forward",
+        32,
         2,
         [
             ((IMG, CH), F32),
@@ -416,10 +450,7 @@
         gain,
         velocity_out,
         fold,
-        text_own,
-        text_core,
-        text_group,
-        text_both,
+        *pieces,
         side_own,
         side_core,
     )
@@ -427,6 +458,7 @@
     (grads,) = run(
         backward_kernel,
         "backward",
+        24,
         2,
         [((HW, SIDE), BF)],
         [((IMG, HW), BF), ((ROWS, HW), BF), ((ROWS, HW), BF)],

time: 177 us -> 155 us (0.88)
  waiting for transfers between devices: 91.5 us -> 65.4 us
  local copies, waits for them, and re-layouts: 9.45 us -> 17.8 us
  Pallas kernels: 39.2 us -> 33.1 us
  starting transfers between devices: 33.4 us -> 35.4 us
    all_to_all x1, waiting for transfers between devices: 45.6 us -> 12.4 us  [per_device(): lax.all_to_all(packed, 'fsdp', 0, 0).reshape(HW, EIGHTH + SIDE + PART)]
    unnamed x27 -> x37, local copies, waits for them, and re-layouts: 8.56 us -> 17.1 us
    ppermute x5 -> x11, starting transfers between devices: 4.83 us -> 12.6 us  [move(): return lax.ppermute(array, ('group', 'fsdp'), pairs)]
    ppermute x5 -> x11, waiting for transfers between devices: 20.4 us -> 27.9 us  [move(): return lax.ppermute(array, ('group', 'fsdp'), pairs)]
    pallas_call x4 -> x5, Pallas kernels: 39.2 us -> 33.1 us  [run(): pl.pallas_call(kernel, out_shape=shapes, in_specs=[smem()] * scalars + [v...]
    all_to_all x1, starting transfers between devices: 9.18 us -> 5.6 us  [per_device(): fold = lax.all_to_all(share, 'fsdp', 0, 0).reshape(devices * SHARE, PART)]
    all_to_all x1, starting transfers between devices: 8.36 us -> 6.41 us  [per_device(): shares = lax.all_to_all(grads.reshape(devices, shard, SIDE), 'fsdp', 0, 0)]
  transfers between devices with their start and end apart: 9 -> 15, of which waited for: 6 -> 8; matrix products, arithmetic and copies ran while one was open for 1% -> 2% of each run, Pallas kernels for 0% -> 1%
where the time goes in v3:
time: 155 us; the launch traced here: 153 us
  waiting for transfers between devices  65.4 us (42%)
  starting transfers between devices  35.4 us (23%)
  Pallas kernels  33.1 us (21%)
  local copies, waits for them, and re-layouts  17.8 us (11%)
    pallas_call x5, Pallas kernels, run(): pl.pallas_call(kernel, out_shape=shapes, in_specs=[smem()] * scalars + [v...  33.1 us
    ppermute x11, waiting for transfers between devices, move(): return lax.ppermute(array, ('group', 'fsdp'), pairs)  27.9 us
    all_to_all x1, waiting for transfers between devices, per_device(): shares = lax.all_to_all(grads.reshape(devices, shard, SIDE), 'fsdp', 0, 0)  18.8 us
    unnamed x37, local copies, waits for them, and re-layouts  17.1 us
    ppermute x11, starting transfers between devices, move(): return lax.ppermute(array, ('group', 'fsdp'), pairs)  12.6 us
    all_to_all x1, waiting for transfers between devices, per_device(): lax.all_to_all(packed, 'fsdp', 0, 0).reshape(HW, EIGHTH + SIDE + PART)  12.4 us
    all_to_all x1, starting transfers between devices, per_device(): lax.all_to_all(packed, 'fsdp', 0, 0).reshape(HW, EIGHTH + SIDE + PART)  9.51 us
    all_to_all x1, starting transfers between devices, per_device(): shares = lax.all_to_all(grads.reshape(devices, shard, SIDE), 'fsdp', 0, 0)  6.41 us
  transfers between devices with their start and end apart: 15, of which 8 were waited for; matrix products, arithmetic and copies ran while one was open for 2% of the time, Pallas kernels for 1%

profile of v3, /device:TPU:0, one launch (start us, length us, event | category | flops | bytes accessed | tf_op | source)
XLA Modules:
  0.0 153.4 jit_solution(18257754217713381923)
XLA Ops:
  0.6 0.8 copy.24
  1.5 0.8 copy.25
  2.3 0.1 pad_add_fusion.place_ref
  2.4 0.9 copy-done.11
  3.3 0.7 copy-done.12
  4.0 0.7 copy-done.13
  4.7 0.9 pack.1
  5.6 1.5 copy-done
  7.2 9.5 %all-to-all-start = ((bf16[64,24,896]{2,1,0:T(8,128)(2,1)}), bf16[64,24,896]{2,1,0:T(8,128)(2,1)S(1)}, u32[]{:S(2)}, u32[]{:S(2)}) async-start(bf16[64,24,896]{2,1,0:T(8,128)(2,1)} %copy-done), calls=%async_computation | async-start | bytes 5505024 | tf_op jit(solution)/shard_map/all_to_all | solution.py:385
  16.7 3.5 %collective-permute-start.2 = (bf16[128,1536]{1,0:T(8,128)(2,1)S(1)}, bf16[128,1536]{1,0:T(8,128)(2,1)S(1)}, u32[]{:S(2)}, u32[]{:S(2)}) collective-permute-start(bf16[128,1536]{1,0:T(8,128)(2,1)S(1)} %bitcast.25), channel_id=1, source_target_pairs={{0,67},{1,66},{2,65},{3,64},{4,71},{5,70},{6,69},{7,68},{8,75},{9,... | collective-permute-start | bytes 1179656 | tf_op jit(solution)/shard_map/ppermute | solution.py:364
  20.2 0.3 collective-permute-start.1
  20.6 9.1 %collective-permute-done.2.text_3_ref = bf16[128,1536]{1,0:T(8,128)(2,1)S(1)} collective-permute-done((bf16[128,1536]{1,0:T(8,128)(2,1)S(1)}, bf16[128,1536]{1,0:T(8,128)(2,1)S(1)}, u32[]{:S(2)}, u32[]{:S(2)}) %collective-permute-start.2) | collective-permute-done | bytes 393248 | tf_op jit(solution)/shard_map/ppermute | solution.py:364
  29.7 0.7 copy-done.5
  30.5 7.8 %collective-permute-done.1.text_2_ref = bf16[128,1536]{1,0:T(8,128)(2,1)S(1)} collective-permute-done((bf16[128,1536]{1,0:T(8,128)(2,1)S(1)}, bf16[128,1536]{1,0:T(8,128)(2,1)S(1)}, u32[]{:S(2)}, u32[]{:S(2)}) %collective-permute-start.1) | collective-permute-done | bytes 393248 | tf_op jit(solution)/shard_map/ppermute | solution.py:364
  38.3 0.8 copy-done.7
  39.1 0.8 copy-done.9
  39.8 12.4 %all-to-all-done = bf16[64,24,896]{2,1,0:T(8,128)(2,1)S(1)} async-done(((bf16[64,24,896]{2,1,0:T(8,128)(2,1)}), bf16[64,24,896]{2,1,0:T(8,128)(2,1)S(1)}, u32[]{:S(2)}, u32[]{:S(2)}) %all-to-all-start) | async-done | bytes 2752544 | tf_op jit(solution)/shard_map/all_to_all | solution.py:385
  52.2 1.4 fold.1
  53.6 1.0 copy-done.1
  54.7 0.4 collective-permute-start.10
  55.1 5.6 %all-to-all-start.1 = ((bf16[64,72,128]{2,1,0:T(8,128)(2,1)}), bf16[64,72,128]{2,1,0:T(8,128)(2,1)}, u32[]{:S(2)}, u32[]{:S(2)}) async-start(bf16[64,72,128]{2,1,0:T(8,128)(2,1)} %copy-done.1), calls=%async_computation.1 | async-start | bytes 2359296 | tf_op jit(solution)/shard_map/all_to_all | solution.py:398
  60.7 1.0 copy-done.4
  61.7 1.0 copy-done.6
  62.7 1.0 copy-done.8
  63.7 1.0 copy-done.10
  64.7 1.6 %mix.1 = (bf16[128,1536]{1,0:T(8,128)(2,1)S(1)}, bf16[128,384]{1,0:T(8,128)(2,1)S(1)}, bf16[128,384]{1,0:T(8,128)(2,1)S(1)}, bf16[128,384]{1,0:T(8,128)(2,1)}, bf16[128,384]{1,0:T(8,128)(2,1)S(1)}) custom-call(bf16[128,1536]{1,0:T(8,128)(2,1)S(1)} %bitcast.28, bf16[128,1536]{1,0:T(8,128)(2,1)S(1)} %copy-done.10, bf16[128,1536]{1,0:T(8,128)(2,1)S(1)} %copy-done.8, ...), custom_call_target="tpu_custom_call" | custom-call | tf_op jit(solution)/shard_map/mix/pallas_call | solution.py:326
  66.3 3.6 %collective-permute-start.6 = (bf16[128,384]{1,0:T(8,128)(2,1)S(1)}, bf16[128,384]{1,0:T(8,128)(2,1)S(1)}, u32[]{:S(2)}, u32[]{:S(2)}) collective-permute-start(bf16[128,384]{1,0:T(8,128)(2,1)S(1)} %get-tuple-element.34.text_0_ref), channel_id=1, source_target_pairs={{0,64},{1,65},{2,66},{3,67},{4,68},{5,69},{6,70},{7,71},{8,72},{9,... | collective-permute-start | bytes 294920 | tf_op jit(solution)/shard_map/ppermute | solution.py:364
  69.9 0.1 collective-permute-start.3
  70.0 3.5 %collective-permute-start.8 = (bf16[128,384]{1,0:T(8,128)(2,1)}, bf16[128,384]{1,0:T(8,128)(2,1)S(1)}, u32[]{:S(2)}, u32[]{:S(2)}) collective-permute-start(bf16[128,384]{1,0:T(8,128)(2,1)} %get-tuple-element.36), channel_id=1, source_target_pairs={{0,66},{1,67},{2,64},{3,65},{4,70},{5,71},{6,68},{7,69},{8,74},{9,... | collective-permute-start | bytes 294920 | tf_op jit(solution)/shard_map/ppermute | solution.py:364
  73.6 7.5 %collective-permute-done.6.text_4_ref = bf16[128,384]{1,0:T(8,128)(2,1)S(1)} collective-permute-done((bf16[128,384]{1,0:T(8,128)(2,1)S(1)}, bf16[128,384]{1,0:T(8,128)(2,1)S(1)}, u32[]{:S(2)}, u32[]{:S(2)}) %collective-permute-start.6) | collective-permute-done | bytes 98336 | tf_op jit(solution)/shard_map/ppermute | solution.py:364
  81.1 0.4 collective-permute-start.4
  81.4 1.8 %collective-permute-done.7.text_5_ref = bf16[128,384]{1,0:T(8,128)(2,1)S(1)} collective-permute-done((bf16[128,384]{1,0:T(8,128)(2,1)S(1)}, bf16[128,384]{1,0:T(8,128)(2,1)S(1)}, u32[]{:S(2)}, u32[]{:S(2)}) %collective-permute-start.7) | collective-permute-done | bytes 98336 | tf_op jit(solution)/shard_map/ppermute | solution.py:364
  83.2 0.6 collective-permute-start.9
  84.5 0.9 copy.22
  85.5 0.9 copy.23
  86.4 1.2 copy.26.velocity_out_ref
  87.6 1.7 %collective-permute-done.9.text_7_ref = bf16[128,384]{1,0:T(8,128)(2,1)S(1)} collective-permute-done((bf16[128,384]{1,0:T(8,128)(2,1)S(1)}, bf16[128,384]{1,0:T(8,128)(2,1)S(1)}, u32[]{:S(2)}, u32[]{:S(2)}) %collective-permute-start.9) | collective-permute-done | bytes 98336 | tf_op jit(solution)/shard_map/ppermute | solution.py:364
  89.3 18.9 %forward.1 = (f32[256,64]{1,0:T(8,128)S(1)}, f32[256,64]{1,0:T(8,128)S(1)}, bf16[256,64]{1,0:T(8,128)(2,1)S(1)}, bf16[256,1536]{1,0:T(8,128)(2,1)S(1)}, bf16[384...) custom-call(s32[3]{0:T(128)S(1)} %pad_add_fusion.place_ref, ...), custom_call_target="tpu_custom_call" | custom-call | tf_op jit(solution)/shard_map/forward/pallas_call | solution.py:326
  108.2 1.3 collective-permute-start.11
  109.5 6.4 %collective-permute-done.11.fake_ref = bf16[256,64]{1,0:T(8,128)(2,1)S(1)} collective-permute-done((bf16[256,64]{1,0:T(8,128)(2,1)S(1)}, bf16[256,64]{1,0:T(8,128)(2,1)S(1)}, u32[]{:S(2)}, u32[]{:S(2)}) %collective-permute-start.11) | collective-permute-done | bytes 32800 | tf_op jit(solution)/shard_map/ppermute | solution.py:457
  115.8 10.2 %backward.1 = bf16[1536,384]{1,0:T(8,128)(2,1)} custom-call(s32[3]{0:T(128)S(1)} %pad_add_fusion.place_ref, f32[1,1]{1,0:T(1,128)} %bitcast.3.sigma_ref, f32[256,64]{1,0:T(8,128)S(1)} %get-tuple-element.39.sample_ref, f32[256,64]{1,0:T(8,128)S(1)} %bitcast.22, f32[256,64]{1,0:T(8,128)S(1)} %get-tuple-element.40.own_ref, ...), custom_call_target="tpu_custom_call" | custom-call | tf_op jit(solution)/shard_map/backward/pallas_call | solution.py:326
  126.0 6.4 %all-to-all-start.2 = ((bf16[64,24,384]{2,1,0:T(8,128)(2,1)}), bf16[64,24,384]{2,1,0:T(8,128)(2,1)S(1)}, u32[]{:S(2)}, u32[]{:S(2)}) async-start(bf16[64,24,384]{2,1,0:T(8,128)(2,1)} %bitcast.12), calls=%async_computation.2 | async-start | bytes 2359296 | tf_op jit(solution)/shard_map/all_to_all | solution.py:476
  132.4 0.7 copy.28
  133.1 18.8 %all-to-all-done.2 = bf16[64,24,384]{2,1,0:T(8,128)(2,1)S(1)} async-done(((bf16[64,24,384]{2,1,0:T(8,128)(2,1)}), bf16[64,24,384]{2,1,0:T(8,128)(2,1)S(1)}, u32[]{:S(2)}, u32[]{:S(2)}) %all-to-all-start.2) | async-done | bytes 1179680 | tf_op jit(solution)/shard_map/all_to_all | solution.py:476
  151.9 0.2 convert_reduce_fusion
  152.1 0.6 slice_bitcast_fusion
  152.7 0.1 broadcast_in_dim_reshape.3
  152.8 0.6 copy.29
  (29 shorter events, 0.1 us)
Async XLA Ops:
  2.4 0.9 copy-start.11
  3.3 0.7 copy-start.12
  4.0 0.7 copy-start.13
  5.6 1.5 copy-start
  7.1 9.5 %copy-start.3 = (bf16[1,128,1536]{2,1,0:T(8,128)(2,1)S(1)}, bf16[1,128,1536]{2,1,0:T(8,128)(2,1)}, u32[]{:S(2)}) copy-start(bf16[1,128,1536]{2,1,0:T(8,128)(2,1)} %param.14) | copy-start | bytes 1179652
  7.1 13.4 %copy-start.14 = (f32[1536]{0:T(1024)S(1)}, f32[1536]{0:T(1024)}, u32[]{:S(2)}) copy-start(f32[1536]{0:T(1024)} %param.18) | copy-start | bytes 18436
  7.1 45.0 %copy-start.2 = (bf16[64,1536]{1,0:T(8,128)(2,1)S(1)}, bf16[64,1536]{1,0:T(8,128)(2,1)}, u32[]{:S(2)}) copy-start(bf16[64,1536]{1,0:T(8,128)(2,1)} %latent_in_ref.3) | copy-start | bytes 589828
  7.2 45.0 %all-to-all-start = ((bf16[64,24,896]{2,1,0:T(8,128)(2,1)}), bf16[64,24,896]{2,1,0:T(8,128)(2,1)S(1)}, u32[]{:S(2)}, u32[]{:S(2)}) async-start(bf16[64,24,896]{2,1,0:T(8,128)(2,1)} %copy-done), calls=%async_computation | async-start | bytes 5505024 | tf_op jit(solution)/shard_map/all_to_all | solution.py:385
  16.7 13.0 %collective-permute-start.2 = (bf16[128,1536]{1,0:T(8,128)(2,1)S(1)}, bf16[128,1536]{1,0:T(8,128)(2,1)S(1)}, u32[]{:S(2)}, u32[]{:S(2)}) collective-permute-start(bf16[128,1536]{1,0:T(8,128)(2,1)S(1)} %bitcast.25), channel_id=1, source_target_pairs={{0,67},{1,66},{2,65},{3,64},{4,71},{5,70},{6,69},{7,68},{8,75},{9,... | collective-permute-start | bytes 1179656 | tf_op jit(solution)/shard_map/ppermute | solution.py:364
  20.2 18.1 %collective-permute-start.1 = (bf16[128,1536]{1,0:T(8,128)(2,1)S(1)}, bf16[128,1536]{1,0:T(8,128)(2,1)S(1)}, u32[]{:S(2)}, u32[]{:S(2)}) collective-permute-start(bf16[128,1536]{1,0:T(8,128)(2,1)S(1)} %bitcast.26), channel_id=1, source_target_pairs={{0,66},{1,67},{2,64},{3,65},{4,70},{5,71},{6,68},{7,69},{8,74},{9,... | collective-permute-start | bytes 1179656 | tf_op jit(solution)/shard_map/ppermute | solution.py:364
  20.5 18.5 %collective-permute-start = (bf16[128,1536]{1,0:T(8,128)(2,1)S(1)}, bf16[128,1536]{1,0:T(8,128)(2,1)S(1)}, u32[]{:S(2)}, u32[]{:S(2)}) collective-permute-start(bf16[128,1536]{1,0:T(8,128)(2,1)S(1)} %bitcast.27), channel_id=1, source_target_pairs={{0,1},{1,0},{2,3},{3,2},{4,5},{5,4},{6,7},{7,6},{8,9},{9,8},{10,11... | collective-permute-start | bytes 1179656 | tf_op jit(solution)/shard_map/ppermute | solution.py:364
  29.7 0.8 copy-start.5
  38.3 0.8 copy-start.7
  39.1 0.8 copy-start.9
  53.6 1.0 copy-start.1
  54.7 34.6 %collective-permute-start.10 = (bf16[1536,384]{1,0:T(8,128)(2,1)}, bf16[1536,384]{1,0:T(8,128)(2,1)}, u32[]{:S(2)}, u32[]{:S(2)}) collective-permute-start(bf16[1536,384]{1,0:T(8,128)(2,1)} %get-tuple-element.38.side_own_ref), channel_id=1, source_target_pairs={{0,1},{1,0},{2,3},{3,2},{4,5},{5,4},{6,7},{7,6},{8,9},{9,8},{10,11... | collective-permute-start | bytes 3538952 | tf_op jit(solution)/shard_map/ppermute | solution.py:364
  55.1 34.1 %all-to-all-start.1 = ((bf16[64,72,128]{2,1,0:T(8,128)(2,1)}), bf16[64,72,128]{2,1,0:T(8,128)(2,1)}, u32[]{:S(2)}, u32[]{:S(2)}) async-start(bf16[64,72,128]{2,1,0:T(8,128)(2,1)} %copy-done.1), calls=%async_computation.1 | async-start | bytes 2359296 | tf_op jit(solution)/shard_map/all_to_all | solution.py:398
  60.7 1.0 copy-start.4
  61.7 1.0 copy-start.6
  62.7 1.0 copy-start.8
  63.7 1.0 copy-start.10
  66.3 14.7 %collective-permute-start.6 = (bf16[128,384]{1,0:T(8,128)(2,1)S(1)}, bf16[128,384]{1,0:T(8,128)(2,1)S(1)}, u32[]{:S(2)}, u32[]{:S(2)}) collective-permute-start(bf16[128,384]{1,0:T(8,128)(2,1)S(1)} %get-tuple-element.34.text_0_ref), channel_id=1, source_target_pairs={{0,64},{1,65},{2,66},{3,67},{4,68},{5,69},{6,70},{7,71},{8,72},{9,... | collective-permute-start | bytes 294920 | tf_op jit(solution)/shard_map/ppermute | solution.py:364
  69.9 13.3 %collective-permute-start.7 = (bf16[128,384]{1,0:T(8,128)(2,1)S(1)}, bf16[128,384]{1,0:T(8,128)(2,1)S(1)}, u32[]{:S(2)}, u32[]{:S(2)}) collective-permute-start(bf16[128,384]{1,0:T(8,128)(2,1)S(1)} %get-tuple-element.35), channel_id=1, source_target_pairs={{0,65},{1,64},{2,67},{3,66},{4,69},{5,68},{6,71},{7,70},{8,73},{9,... | collective-permute-start | bytes 294920 | tf_op jit(solution)/shard_map/ppermute | solution.py:364
  69.9 14.0 %collective-permute-start.3 = (bf16[128,384]{1,0:T(8,128)(2,1)S(1)}, bf16[128,384]{1,0:T(8,128)(2,1)S(1)}, u32[]{:S(2)}, u32[]{:S(2)}) collective-permute-start(bf16[128,384]{1,0:T(8,128)(2,1)S(1)} %get-tuple-element.35), channel_id=1, source_target_pairs={{0,1},{1,0},{2,3},{3,2},{4,5},{5,4},{6,7},{7,6},{8,9},{9,8},{10,11... | collective-permute-start | bytes 294920 | tf_op jit(solution)/shard_map/ppermute | solution.py:364
  70.0 17.5 %collective-permute-start.8 = (bf16[128,384]{1,0:T(8,128)(2,1)}, bf16[128,384]{1,0:T(8,128)(2,1)S(1)}, u32[]{:S(2)}, u32[]{:S(2)}) collective-permute-start(bf16[128,384]{1,0:T(8,128)(2,1)} %get-tuple-element.36), channel_id=1, source_target_pairs={{0,66},{1,67},{2,64},{3,65},{4,70},{5,71},{6,68},{7,69},{8,74},{9,... | collective-permute-start | bytes 294920 | tf_op jit(solution)/shard_map/ppermute | solution.py:364
  81.1 6.5 %collective-permute-start.4 = (bf16[128,384]{1,0:T(8,128)(2,1)}, bf16[128,384]{1,0:T(8,128)(2,1)S(1)}, u32[]{:S(2)}, u32[]{:S(2)}) collective-permute-start(bf16[128,384]{1,0:T(8,128)(2,1)} %get-tuple-element.36), channel_id=1, source_target_pairs={{0,2},{1,3},{2,0},{3,1},{4,6},{5,7},{6,4},{7,5},{8,10},{9,11},{10,... | collective-permute-start | bytes 294920 | tf_op jit(solution)/shard_map/ppermute | solution.py:364
  83.2 6.0 %collective-permute-start.9 = (bf16[128,384]{1,0:T(8,128)(2,1)S(1)}, bf16[128,384]{1,0:T(8,128)(2,1)S(1)}, u32[]{:S(2)}, u32[]{:S(2)}) collective-permute-start(bf16[128,384]{1,0:T(8,128)(2,1)S(1)} %get-tuple-element.37), channel_id=1, source_target_pairs={{0,67},{1,66},{2,65},{3,64},{4,71},{5,70},{6,69},{7,68},{8,75},{9,... | collective-permute-start | bytes 294920 | tf_op jit(solution)/shard_map/ppermute | solution.py:364
  83.9 5.4 %collective-permute-start.5 = (bf16[128,384]{1,0:T(8,128)(2,1)S(1)}, bf16[128,384]{1,0:T(8,128)(2,1)S(1)}, u32[]{:S(2)}, u32[]{:S(2)}) collective-permute-start(bf16[128,384]{1,0:T(8,128)(2,1)S(1)} %get-tuple-element.37), channel_id=1, source_target_pairs={{0,3},{1,2},{2,1},{3,0},{4,7},{5,6},{6,5},{7,4},{8,11},{9,10},{10,... | collective-permute-start | bytes 294920 | tf_op jit(solution)/shard_map/ppermute | solution.py:364
  108.2 7.7 %collective-permute-start.11 = (bf16[256,64]{1,0:T(8,128)(2,1)S(1)}, bf16[256,64]{1,0:T(8,128)(2,1)S(1)}, u32[]{:S(2)}, u32[]{:S(2)}) collective-permute-start(bf16[256,64]{1,0:T(8,128)(2,1)S(1)} %get-tuple-element.41), channel_id=1, source_target_pairs={{64,0},{65,1},{66,2},{67,3},{68,4},{69,5},{70,6},{71,7},{72,8},{73... | collective-permute-start | bytes 98312 | tf_op jit(solution)/shard_map/ppermute | solution.py:457
  126.0 25.9 %all-to-all-start.2 = ((bf16[64,24,384]{2,1,0:T(8,128)(2,1)}), bf16[64,24,384]{2,1,0:T(8,128)(2,1)S(1)}, u32[]{:S(2)}, u32[]{:S(2)}) async-start(bf16[64,24,384]{2,1,0:T(8,128)(2,1)} %bitcast.12), calls=%async_computation.2 | async-start | bytes 2359296 | tf_op jit(solution)/shard_map/all_to_all | solution.py:476

commit v4 on v3

--- a/solution.py
+++ b/solution.py
@@ -19,6 +19,7 @@
 SIDE = 6 * RANK
 SHARE = 72
 PART = 128
+WRITES = 4
 MOVES = tuple((group, near) for group in range(2) for near in range(4))
 BF = jnp.bfloat16
 F32 = jnp.float32
@@ -44,32 +45,69 @@
     place_ref,
     base_ref,
     gen_down_ref,
+    critic_down_ref,
     gen_up_ref,
-    critic_down_ref,
     critic_up_ref,
     packed_ref,
+    base,
+    downs,
+    ups,
+    packed,
+    read_sem,
+    write_sem,
 ):
+    reads = [
+        pltpu.make_async_copy(base_ref, base, read_sem.at[0]),
+        pltpu.make_async_copy(gen_down_ref, downs.at[0], read_sem.at[1]),
+        pltpu.make_async_copy(critic_down_ref, downs.at[1], read_sem.at[2]),
+        pltpu.make_async_copy(gen_up_ref, ups.at[0], read_sem.at[3]),
+        pltpu.make_async_copy(critic_up_ref, ups.at[1], read_sem.at[4]),
+    ]
+    for read in reads:
+        read.start()
+    for read in reads:
+        read.wait()
     group = place_ref[0]
 
     def both(gen, critic):
         gen, critic = gen.astype(F32), critic.astype(F32)
         return jnp.concatenate([gen, jnp.where(group == 0, gen, critic)], axis=1).astype(BF)
 
-    sides = (
-        both(gen_down_ref[...], critic_down_ref[...]),
-        both(gen_up_ref[...].T, critic_up_ref[...].T),
-    )
-    rows = base_ref.shape[0]
+    up_rows = [jnp.concatenate([ups[role, block] for block in range(3)], axis=1) for role in range(2)]
+    sides = (both(downs[0], downs[1]), both(up_rows[0], up_rows[1]))
+    eighths = []
     for near in range(4):
         start = pl.multiple_of(HW + group * HW + near * EIGHTH, EIGHTH)
-        eighth = base_ref[:, pl.ds(start, EIGHTH)]
-        for device in range(near, packed_ref.shape[0], 4):
-            packed_ref[device, :, :EIGHTH] = eighth
-            packed_ref[device, :, EIGHTH : EIGHTH + SIDE] = sides[near % 2]
-            columns = base_ref[:, device * SHARE : (device + 1) * SHARE]
-            packed_ref[device, :, EIGHTH + SIDE :] = jnp.concatenate(
+        eighths.append(base[:, pl.ds(start, EIGHTH)])
+    rows = base.shape[0]
+    batch = packed.shape[0] // WRITES
+    writes = []
+    for step in range(WRITES):
+        for device in range(step * batch, (step + 1) * batch):
+            packed[device, :, :EIGHTH] = eighths[device % 4]
+            packed[device, :, EIGHTH : EIGHTH + SIDE] = sides[device % 2]
+            columns = base[:, device * SHARE : (device + 1) * SHARE]
+            packed[device, :, EIGHTH + SIDE :] = jnp.concatenate(
                 [columns, jnp.zeros((rows, PART - SHARE), BF)], axis=1
             )
+        span = pl.ds(step * batch, batch)
+        write = pltpu.make_async_copy(packed.at[span], packed_ref.at[span], write_sem.at[step])
+        write.start()
+        writes.append(write)
+    for write in writes:
+        write.wait()
+
+
+def prompt_kernel(text_0_ref, text_1_ref, text_2_ref, text_3_ref, prompts_ref):
+    for index, text_ref in enumerate((text_0_ref, text_1_ref, text_2_ref, text_3_ref)):
+        prompts_ref[index * TXT : (index + 1) * TXT, :] = unit_rows(text_ref[...])
+
+
+def sum_kernel(shares_ref, down_ref, up_ref):
+    total = jnp.sum(shares_ref[...].astype(F32), axis=0)
+    down_ref[...] = total[:, : 3 * RANK]
+    for block in range(3):
+        up_ref[block] = total[:, (3 + block) * RANK : (4 + block) * RANK]
 
 
 def fold_kernel(latent_in_ref, modulation_ref, packed_ref, share_ref, side_ref):
@@ -81,27 +119,10 @@
     side_ref[...] = packed_ref[:, EIGHTH : EIGHTH + SIDE]
 
 
-def mix_kernel(
-    text_0_ref,
-    text_1_ref,
-    text_2_ref,
-    text_3_ref,
-    packed_ref,
-    prompt_ref,
-    out_0_ref,
-    out_1_ref,
-    out_2_ref,
-    out_3_ref,
-):
-    prompt = unit_rows(text_0_ref[...])
-    prompt_ref[...] = prompt
-    out_0_ref[...] = dot(prompt, packed_ref[:, :EIGHTH]).astype(BF)
-    for text_ref, out_ref in (
-        (text_1_ref, out_1_ref),
-        (text_2_ref, out_2_ref),
-        (text_3_ref, out_3_ref),
-    ):
-        out_ref[...] = dot(unit_rows(text_ref[...]), packed_ref[:, :EIGHTH]).astype(BF)
+def mix_kernel(prompts_ref, packed_ref, out_0_ref, out_1_ref, out_2_ref, out_3_ref):
+    eighth = dot(prompts_ref[...], packed_ref[:, :EIGHTH]).astype(BF)
+    for index, out_ref in enumerate((out_0_ref, out_1_ref, out_2_ref, out_3_ref)):
+        out_ref[...] = eighth[index * TXT : (index + 1) * TXT]
 
 
 def forward_kernel(
@@ -125,6 +146,7 @@
     side_own_ref,
     side_core_ref,
     sample_ref,
+    sample_again_ref,
     velocity_ref,
     narrow_velocity_ref,
     q_ref,
@@ -175,12 +197,12 @@
 
     def readout(latent, noise_level, role, switch, save):
         base = role * 3 * RANK
-        narrow = latent.astype(BF)
+        narrow = latent.T.astype(BF)
         hidden = dot(narrow, latent_in_ref[...])
         inverse_rms = lax.rsqrt(jnp.mean(hidden * hidden, axis=-1, keepdims=True) + 1e-06)
         picture = (hidden * inverse_rms * (1.0 + noise_level * modulation_ref[...])).astype(BF)
         reduced_picture = dot(picture, downs[:, base : base + 3 * RANK]).astype(BF)
-        reduced_prompt = dot(prompt_ref[...], downs[:, base : base + 3 * RANK]).astype(BF)
+        reduced_prompt = dot(prompt_ref[:TXT, :], downs[:, base : base + 3 * RANK]).astype(BF)
 
         @save
         def _():
@@ -237,11 +259,12 @@
             return carry
 
         lax.fori_loop(0, HEADS, head, 0, unroll=2)
-        return dot(attended_now[...], velocity_out_ref[...])
+        return dot(velocity_out_ref[...], attended_now[...], 1, 1)
 
     latent = latent_ref[...]
     sample = latent - readout(latent, 1.0, 0, None, lambda f: f())
     sample_ref[...] = sample
+    sample_again_ref[...] = sample
     noised = (1.0 - sigma) * sample + sigma * fresh_ref[...]
     velocity = readout(noised, sigma, 1, group.astype(F32), pl.when(group == 1))
     velocity_ref[...] = velocity
@@ -282,13 +305,13 @@
     spread = distance * (1.0 / (IMG * CH)) + 1e-05
     cot_gen = -(clean_fake - clean_real) / spread
     cot_critic = 2.0 * (own - (fresh_ref[...] - sample)) / (IMG * CH)
-    cotangent = jnp.where(flag == 0, cot_gen, cot_critic).astype(BF)
+    cotangent = jnp.where(flag == 0, cot_gen, cot_critic).T.astype(BF)
 
     def head(index, carry):
         span = pl.ds(pl.multiple_of(index * HD, HD), HD)
         queries, keys, values = q_ref[:, span], k_ref[:, span], v_ref[:, span]
         weights = weights_ref[index]
-        upstream = dot(cotangent, velocity_out_ref[span, :], 1, 1) * inverse_ref[index]
+        upstream = dot(cotangent, velocity_out_ref[:, span]) * inverse_ref[index]
         inner = jnp.sum(upstream * attended_ref[:, span].astype(F32), axis=-1, keepdims=True)
         upstream = upstream.astype(BF)
         grad_v[:, span] = dot(weights, upstream, 0, 0).astype(BF)
@@ -305,7 +328,7 @@
     reduced_v = dot(grad_v[...], role_up_ref[:, spans[2]]).astype(BF)
     reduced_kv = jnp.concatenate([reduced_k, reduced_v], axis=1)
     down_q = dot(reduced_q, picture_ref[...], 0, 0)
-    down_kv = dot(reduced_kv[:TXT], prompt_ref[...], 0, 0) + dot(reduced_kv[TXT:], picture_ref[...], 0, 0)
+    down_kv = dot(reduced_kv[:TXT], prompt_ref[:TXT, :], 0, 0) + dot(reduced_kv[TXT:], picture_ref[...], 0, 0)
     up_q = dot(reduced_ref[TXT:, spans[0]], grad_q[...], 0, 0)
     up_k = dot(reduced_ref[:, spans[1]], grad_k[...], 0, 0)
     up_v = dot(reduced_ref[:, spans[2]], grad_v[...], 0, 0)
@@ -313,22 +336,18 @@
     grads_ref[...] = grads.T.astype(BF)
 
 
-def vmem():
-    return pl.BlockSpec(memory_space=pltpu.VMEM)
-
-
 def smem():
     return pl.BlockSpec(memory_space=pltpu.SMEM)
 
 
-def run(kernel, name, megabytes, scalars, outputs, scratch, *operands):
+def run(kernel, name, megabytes, scalars, outputs, scratch, *operands, space=pltpu.VMEM):
     shapes = tuple(jax.ShapeDtypeStruct(*output) for output in outputs)
     return pl.pallas_call(
         kernel,
         out_shape=shapes,
-        in_specs=[smem()] * scalars + [vmem()] * (len(operands) - scalars),
-        out_specs=tuple([vmem()] * len(outputs)),
-        scratch_shapes=[pltpu.VMEM(*buffer) for buffer in scratch],
+        in_specs=[smem()] * scalars + [pl.BlockSpec(memory_space=space)] * (len(operands) - scalars),
+        out_specs=tuple([pl.BlockSpec(memory_space=space)] * len(outputs)),
+        scratch_shapes=scratch,
         compiler_params=pltpu.CompilerParams(vmem_limit_bytes=megabytes * 2**20),
         name=name,
     )(*operands)
@@ -363,27 +382,38 @@
         ]
         return lax.ppermute(array, ("group", "fsdp"), pairs)
 
-    fresh = fresh_noise[0]
+    latent = latent_noise[0].T
+    fresh = fresh_noise[0].T
     text = text_states[0]
     gain = modulation.reshape(1, HW)
+    out_map = velocity_out.T
 
     texts = [text, move(text, 0, 1), move(text, 1, 2), move(text, 1, 3)]
     (packed,) = run(
         pack_kernel,
         "pack",
-        16,
+        60,
         1,
         [((devices, shard, EIGHTH + SIDE + PART), BF)],
-        [],
+        [
+            pltpu.VMEM((shard, 3 * HW), BF),
+            pltpu.VMEM((2, shard, 3 * RANK), BF),
+            pltpu.VMEM((2, 3, shard, RANK), BF),
+            pltpu.VMEM((devices, shard, EIGHTH + SIDE + PART), BF),
+            pltpu.SemaphoreType.DMA((5,)),
+            pltpu.SemaphoreType.DMA((WRITES,)),
+        ],
         place,
         base_qkv,
         gen_down,
-        gen_up.reshape(3 * RANK, shard),
         critic_down,
-        critic_up.reshape(3 * RANK, shard),
+        gen_up.transpose(0, 2, 1),
+        critic_up.transpose(0, 2, 1),
+        space=pl.ANY,
     )
     packed = lax.all_to_all(packed, "fsdp", 0, 0).reshape(HW, EIGHTH + SIDE + PART)
-    packed, *texts = lax.optimization_barrier((packed, *texts))
+    (prompts,) = run(prompt_kernel, "prompts", 16, 0, [((4 * TXT, HW), BF)], [], *texts)
+    packed, prompts = lax.optimization_barrier((packed, prompts))
     share, side_own = run(
         fold_kernel,
         "fold",
@@ -397,14 +427,15 @@
     )
     fold = lax.all_to_all(share, "fsdp", 0, 0).reshape(devices * SHARE, PART)
     side_core = move(side_own, 0, 1)
-    prompt, *parts = run(
+    prompts, side_core = lax.optimization_barrier((prompts, side_core))
+    parts = run(
         mix_kernel,
         "mix",
         16,
         0,
-        [((TXT, HW), BF)] + [((TXT, EIGHTH), BF)] * 4,
+        [((TXT, EIGHTH), BF)] * 4,
         [],
-        *texts,
+        prompts,
         packed,
     )
     pieces = [
@@ -412,15 +443,16 @@
         for across, near in MOVES
     ]
 
-    sample, velocity, narrow_velocity, *saved, role_up = run(
+    sample, sample_again, velocity, narrow_velocity, *saved, role_up = run(
         forward_kernel,
         "forward",
         32,
         2,
         [
-            ((IMG, CH), F32),
-            ((IMG, CH), F32),
-            ((IMG, CH), BF),
+            ((CH, IMG), F32),
+            ((CH, IMG), F32),
+            ((CH, IMG), F32),
+            ((CH, IMG), BF),
             ((IMG, HW), BF),
             ((ROWS, HW), BF),
             ((ROWS, HW), BF),
@@ -432,23 +464,23 @@
             ((HW, 3 * RANK), BF),
         ],
         [
-            ((CHUNK, 4 * CH), BF),
-            ((IMG, HW), BF),
-            ((ROWS, HW), BF),
-            ((ROWS, HW), BF),
-            ((IMG, HW), BF),
-            ((TXT, 2 * HW), BF),
-            ((HW, SIDE), BF),
-            ((HW, SIDE), BF),
+            pltpu.VMEM((CHUNK, 4 * CH), BF),
+            pltpu.VMEM((IMG, HW), BF),
+            pltpu.VMEM((ROWS, HW), BF),
+            pltpu.VMEM((ROWS, HW), BF),
+            pltpu.VMEM((IMG, HW), BF),
+            pltpu.VMEM((TXT, 2 * HW), BF),
+            pltpu.VMEM((HW, SIDE), BF),
+            pltpu.VMEM((HW, SIDE), BF),
         ],
         place,
         sigma,
-        latent_noise[0],
+        latent,
         fresh,
-        prompt,
+        prompts,
         latent_in,
         gain,
-        velocity_out,
+        out_map,
         fold,
         *pieces,
         side_own,
@@ -461,23 +493,29 @@
         24,
         2,
         [((HW, SIDE), BF)],
-        [((IMG, HW), BF), ((ROWS, HW), BF), ((ROWS, HW), BF)],
+        [pltpu.VMEM((IMG, HW), BF), pltpu.VMEM((ROWS, HW), BF), pltpu.VMEM((ROWS, HW), BF)],
         place,
         sigma,
-        sample,
+        sample_again,
         fresh,
         velocity,
         fake_velocity,
-        prompt,
-        velocity_out,
+        prompts,
+        out_map,
         role_up,
         *saved,
     )
     shares = lax.all_to_all(grads.reshape(devices, shard, SIDE), "fsdp", 0, 0)
-    total = jnp.sum(shares.astype(F32), axis=0)
-    share_down = total[:, : 3 * RANK]
-    share_up = total[:, 3 * RANK :].T.reshape(3, RANK, shard)
-    return (sample[None], share_down[None], share_up[None])
+    share_down, share_up = run(
+        sum_kernel,
+        "total",
+        16,
+        0,
+        [((shard, 3 * RANK), F32), ((3, shard, RANK), F32)],
+        [],
+        shares,
+    )
+    return (sample.T[None], share_down[None], share_up.transpose(0, 2, 1)[None])
 
 
 def solution(mesh):

time: 155 us -> 153 us (0.987)
  blocking collectives: 0 us -> 25.7 us
  local copies, waits for them, and re-layouts: 17.8 us -> 1.92 us
  waiting for transfers between devices: 65.4 us -> 53.4 us
  starting transfers between devices: 35.4 us -> 28 us
  Pallas kernels: 33.1 us -> 40 us
    all_to_all x0 -> x1, blocking collectives: none -> 25.7 us  [per_device(): shares = lax.all_to_all(grads.reshape(devices, shard, SIDE), 'fsdp', 0, 0)]
    all_to_all x1 -> x0, waiting for transfers between devices: 18.8 us -> none  [per_device(): shares = lax.all_to_all(grads.reshape(devices, shard, SIDE), 'fsdp', 0, 0)]
    unnamed x37 -> x16, local copies, waits for them, and re-layouts: 17.1 us -> 1.91 us
    pallas_call x5 -> x7, Pallas kernels: 33.1 us -> 40 us  [run(): pl.pallas_call(kernel, out_shape=shapes, in_specs=[smem()] * scalars + [p...]
    all_to_all x1 -> x0, starting transfers between devices: 6.41 us -> none  [per_device(): shares = lax.all_to_all(grads.reshape(devices, shard, SIDE), 'fsdp', 0, 0)]
    ppermute x11, waiting for transfers between devices: 27.9 us -> 34.1 us  [move(): return lax.ppermute(array, ('group', 'fsdp'), pairs)]
  transfers between devices with their start and end apart: 15 -> 14, of which waited for: 8 -> 8; matrix products, arithmetic and copies ran while one was open for 2% -> 0% of each run, Pallas kernels for 1% -> 3%
where the time goes in v4:
time: 153 us; the launch traced here: 151 us
  waiting for transfers between devices  53.4 us (35%)
  Pallas kernels  40 us (26%)
  starting transfers between devices  28 us (18%)
  blocking collectives  25.7 us (17%)
  local copies, waits for them, and re-layouts  1.92 us (1%)
    pallas_call x7, Pallas kernels, run(): pl.pallas_call(kernel, out_shape=shapes, in_specs=[smem()] * scalars + [p...  40 us
    ppermute x11, waiting for transfers between devices, move(): return lax.ppermute(array, ('group', 'fsdp'), pairs)  34.1 us
    all_to_all x1, blocking collectives, per_device(): shares = lax.all_to_all(grads.reshape(devices, shard, SIDE), 'fsdp', 0, 0)  25.7 us
    all_to_all x1, waiting for transfers between devices, per_device(): lax.all_to_all(packed, 'fsdp', 0, 0).reshape(HW, EIGHTH + SIDE + PART)  13.3 us
    ppermute x11, starting transfers between devices, move(): return lax.ppermute(array, ('group', 'fsdp'), pairs)  11.6 us
    all_to_all x1, starting transfers between devices, per_device(): lax.all_to_all(packed, 'fsdp', 0, 0).reshape(HW, EIGHTH + SIDE + PART)  9.75 us
    ppermute x1, waiting for transfers between devices, per_device(): fake_velocity = lax.ppermute(narrow_velocity, 'group', [(1, 0)])  6.01 us
    all_to_all x1, starting transfers between devices, per_device(): fold = lax.all_to_all(share, 'fsdp', 0, 0).reshape(devices * SHARE, PART)  5.36 us
  transfers between devices with their start and end apart: 14, of which 8 were waited for; matrix products, arithmetic and copies ran while one was open for 0% of the time, Pallas kernels for 3%

profile of v4, /device:TPU:0, one launch (start us, length us, event | category | flops | bytes accessed | tf_op | source)
XLA Modules:
  0.0 151.2 jit_solution(14683010249626221873)
XLA Ops:
  0.6 0.6 pad_add_fusion.place_ref
  1.3 3.4 %pack.1 = bf16[64,24,896]{2,1,0:T(8,128)(2,1)} custom-call(s32[3]{0:T(128)} %pad_add_fusion.place_ref, bf16[24,4608]{1,0:T(8,128)(2,1)} %base_ref.1, bf16[24,192]{1,0:T(8,128)(2,1)} %gen_down_ref.1, bf16[24,192]{1,0:T(8,128)(2,1)} %critic_down_ref.1, bf16[3,24,64]{2,1,0:T(8,128)(2,1)} %bitcast.35, bf16[3,24,64]{2,1,0:T(8,128)(2,1)} %bitcast.36), custom_call_target="tpu_custom_call" | custom-call | tf_op jit(solution)/shard_map/pack/pallas_call | solution.py:345
  4.7 0.0 copy-start.3
  4.7 0.0 copy-start.7
  4.7 9.8 %all-to-all-start = ((bf16[64,24,896]{2,1,0:T(8,128)(2,1)}), bf16[64,24,896]{2,1,0:T(8,128)(2,1)}, u32[]{:S(2)}, u32[]{:S(2)}) async-start(bf16[64,24,896]{2,1,0:T(8,128)(2,1)} %pack.1), calls=%async_computation | async-start | bytes 5505024 | tf_op jit(solution)/shard_map/all_to_all | solution.py:414
  14.5 0.0 copy-done.3
  14.5 3.5 %collective-permute-start.2 = (bf16[128,1536]{1,0:T(8,128)(2,1)S(1)}, bf16[128,1536]{1,0:T(8,128)(2,1)S(1)}, u32[]{:S(2)}, u32[]{:S(2)}) collective-permute-start(bf16[128,1536]{1,0:T(8,128)(2,1)S(1)} %bitcast.28), channel_id=1, source_target_pairs={{0,67},{1,66},{2,65},{3,64},{4,71},{5,70},{6,69},{7,68},{8,75},{9,... | collective-permute-start | bytes 1179656 | tf_op jit(solution)/shard_map/ppermute | solution.py:383
  17.9 0.3 collective-permute-start.1
  18.3 0.0 collective-permute-start
  18.3 0.0 copy-start.1
  18.3 9.1 %collective-permute-done.2.text_3_ref = bf16[128,1536]{1,0:T(8,128)(2,1)S(1)} collective-permute-done((bf16[128,1536]{1,0:T(8,128)(2,1)S(1)}, bf16[128,1536]{1,0:T(8,128)(2,1)S(1)}, u32[]{:S(2)}, u32[]{:S(2)}) %collective-permute-start.2) | collective-permute-done | bytes 393248 | tf_op jit(solution)/shard_map/ppermute | solution.py:383
  27.4 8.6 %collective-permute-done.1.text_2_ref = bf16[128,1536]{1,0:T(8,128)(2,1)S(1)} collective-permute-done((bf16[128,1536]{1,0:T(8,128)(2,1)S(1)}, bf16[128,1536]{1,0:T(8,128)(2,1)S(1)}, u32[]{:S(2)}, u32[]{:S(2)}) %collective-permute-start.1) | collective-permute-done | bytes 393248 | tf_op jit(solution)/shard_map/ppermute | solution.py:383
  36.0 0.0 collective-permute-done.text_1_ref
  36.0 0.5 prompts.1.prompts_ref.prompt_ref
  36.5 13.3 %all-to-all-done = bf16[64,24,896]{2,1,0:T(8,128)(2,1)} async-done(((bf16[64,24,896]{2,1,0:T(8,128)(2,1)}), bf16[64,24,896]{2,1,0:T(8,128)(2,1)}, u32[]{:S(2)}, u32[]{:S(2)}) %all-to-all-start) | async-done | bytes 2752544 | tf_op jit(solution)/shard_map/all_to_all | solution.py:414
  49.9 3.2 %fold.1 = (bf16[64,72,128]{2,1,0:T(8,128)(2,1)S(1)}, bf16[1536,384]{1,0:T(8,128)(2,1)}) custom-call(bf16[64,1536]{1,0:T(8,128)(2,1)S(1)} %copy-done.1, f32[1,1536]{1,0:T(1,128)S(1)} %reshape.23.modulation_ref, bf16[1536,896]{1,0:T(8,128)(2,1)} %bitcast.10.packed_ref), custom_call_target="tpu_custom_call" | custom-call | tf_op jit(solution)/shard_map/fold/pallas_call | solution.py:345
  53.1 1.0 copy-done
  54.1 0.4 collective-permute-start.3
  54.6 5.4 %all-to-all-start.1 = ((bf16[64,72,128]{2,1,0:T(8,128)(2,1)}), bf16[64,72,128]{2,1,0:T(8,128)(2,1)S(1)}, u32[]{:S(2)}, u32[]{:S(2)}) async-start(bf16[64,72,128]{2,1,0:T(8,128)(2,1)} %copy-done), calls=%async_computation.1 | async-start | bytes 2359296 | tf_op jit(solution)/shard_map/all_to_all | solution.py:428
  60.0 0.0 copy-start.2
  60.0 0.0 copy-start.4
  60.0 0.0 collective-permute-done.3.side_core_ref
  60.0 3.5 %mix.1 = (bf16[128,384]{1,0:T(8,128)(2,1)S(1)}, bf16[128,384]{1,0:T(8,128)(2,1)}, bf16[128,384]{1,0:T(8,128)(2,1)}, bf16[128,384]{1,0:T(8,128)(2,1)}) custom-call(bf16[512,1536]{1,0:T(8,128)(2,1)S(1)} %prompts.1.prompts_ref.prompt_ref, bf16[1536,896]{1,0:T(8,128)(2,1)} %bitcast.10.packed_ref), custom_call_target="tpu_custom_call" | custom-call | tf_op jit(solution)/shard_map/mix/pallas_call | solution.py:345
  63.5 3.6 %collective-permute-start.7 = (bf16[128,384]{1,0:T(8,128)(2,1)S(1)}, bf16[128,384]{1,0:T(8,128)(2,1)S(1)}, u32[]{:S(2)}, u32[]{:S(2)}) collective-permute-start(bf16[128,384]{1,0:T(8,128)(2,1)S(1)} %get-tuple-element.33.text_0_ref), channel_id=1, source_target_pairs={{0,64},{1,65},{2,66},{3,67},{4,68},{5,69},{6,70},{7,71},{8,72},{9,... | collective-permute-start | bytes 294920 | tf_op jit(solution)/shard_map/ppermute | solution.py:383
  67.1 0.0 collective-permute-start.8
  67.1 0.1 collective-permute-start.4
  67.2 3.6 %collective-permute-start.9 = (bf16[128,384]{1,0:T(8,128)(2,1)}, bf16[128,384]{1,0:T(8,128)(2,1)}, u32[]{:S(2)}, u32[]{:S(2)}) collective-permute-start(bf16[128,384]{1,0:T(8,128)(2,1)} %get-tuple-element.35), channel_id=1, source_target_pairs={{0,66},{1,67},{2,64},{3,65},{4,70},{5,71},{6,68},{7,69},{8,74},{9,... | collective-permute-start | bytes 294920 | tf_op jit(solution)/shard_map/ppermute | solution.py:383
  70.8 0.0 collective-permute-start.5
  70.8 9.8 %collective-permute-done.7.text_4_ref = bf16[128,384]{1,0:T(8,128)(2,1)S(1)} collective-permute-done((bf16[128,384]{1,0:T(8,128)(2,1)S(1)}, bf16[128,384]{1,0:T(8,128)(2,1)S(1)}, u32[]{:S(2)}, u32[]{:S(2)}) %collective-permute-start.7) | collective-permute-done | bytes 98336 | tf_op jit(solution)/shard_map/ppermute | solution.py:383
  80.6 0.0 collective-permute-start.10
  80.6 2.2 %collective-permute-done.8.text_5_ref = bf16[128,384]{1,0:T(8,128)(2,1)S(1)} collective-permute-done((bf16[128,384]{1,0:T(8,128)(2,1)}, bf16[128,384]{1,0:T(8,128)(2,1)S(1)}, u32[]{:S(2)}, u32[]{:S(2)}) %collective-permute-start.8) | collective-permute-done | bytes 98336 | tf_op jit(solution)/shard_map/ppermute | solution.py:383
  82.8 0.0 collective-permute-start.6
  83.5 0.0 all-to-all-done.1
  83.5 0.0 collective-permute-done.4.text_1_ref
  83.5 0.0 collective-permute-done.9.text_6_ref
  83.5 0.0 collective-permute-done.5.text_2_ref
  83.5 3.6 %collective-permute-done.10.text_7_ref = bf16[128,384]{1,0:T(8,128)(2,1)} collective-permute-done((bf16[128,384]{1,0:T(8,128)(2,1)}, bf16[128,384]{1,0:T(8,128)(2,1)}, u32[]{:S(2)}, u32[]{:S(2)}) %collective-permute-start.10) | collective-permute-done | bytes 98336 | tf_op jit(solution)/shard_map/ppermute | solution.py:383
  87.1 0.9 collective-permute-done.6.text_3_ref
  87.9 0.0 copy-done.2
  87.9 0.0 copy-done.6
  87.9 0.0 copy-start.5
  87.9 0.8 copy-done.5
  88.8 19.5 %forward.1 = (f32[64,256]{1,0:T(8,128)}, f32[64,256]{1,0:T(8,128)S(1)}, f32[64,256]{1,0:T(8,128)S(1)}, bf16[64,256]{1,0:T(8,128)(2,1)S(1)}, bf16[256,1536]{1,0:T...) custom-call(s32[3]{0:T(128)S(1)} %copy-done.6, ...), custom_call_target="tpu_custom_call" | custom-call | tf_op jit(solution)/shard_map/forward/pallas_call | solution.py:345
  108.2 1.3 collective-permute-start.11
  109.5 6.0 %collective-permute-done.11.fake_ref = bf16[64,256]{1,0:T(8,128)(2,1)S(1)} collective-permute-done((bf16[64,256]{1,0:T(8,128)(2,1)S(1)}, bf16[64,256]{1,0:T(8,128)(2,1)S(1)}, u32[]{:S(2)}, u32[]{:S(2)}) %collective-permute-start.11) | collective-permute-done | bytes 32800 | tf_op jit(solution)/shard_map/ppermute | solution.py:489
  115.5 9.1 %backward.1 = bf16[1536,384]{1,0:T(8,128)(2,1)S(1)} custom-call(s32[3]{0:T(128)S(1)} %copy-done.6, f32[1,1]{1,0:T(1,128)} %bitcast.3.sigma_ref, f32[64,256]{1,0:T(8,128)S(1)} %get-tuple-element.39.sample_ref, f32[64,256]{1,0:T(8,128)S(1)} %bitcast.33, f32[64,256]{1,0:T(8,128)S(1)} %get-tuple-element.40.own_ref, ...), custom_call_target="tpu_custom_call" | custom-call | tf_op jit(solution)/shard_map/backward/pallas_call | solution.py:345
  124.7 25.7 %all_to_all.15.shares_ref = bf16[64,24,384]{2,1,0:T(8,128)(2,1)S(1)} all-to-all(bf16[64,24,384]{2,1,0:T(8,128)(2,1)S(1)} %bitcast.24), channel_id=1, replica_groups=mesh['group'=2,'fsdp'=64] {'fsdp'}, dimensions={0} | all-to-all | bytes 2359296 | tf_op jit(solution)/shard_map/all_to_all | solution.py:508
  150.4 0.9 total.1
  (6 shorter events, 0.0 us)
Async XLA Ops:
  4.7 9.8 %copy-start.3 = (bf16[1,128,1536]{2,1,0:T(8,128)(2,1)S(1)}, bf16[1,128,1536]{2,1,0:T(8,128)(2,1)}, u32[]{:S(2)}) copy-start(bf16[1,128,1536]{2,1,0:T(8,128)(2,1)} %param.14) | copy-start | bytes 1179652
  4.7 13.6 %copy-start.7 = (f32[1536]{0:T(1024)S(1)}, f32[1536]{0:T(1024)}, u32[]{:S(2)}) copy-start(f32[1536]{0:T(1024)} %param.18) | copy-start | bytes 18436
  4.7 45.2 %all-to-all-start = ((bf16[64,24,896]{2,1,0:T(8,128)(2,1)}), bf16[64,24,896]{2,1,0:T(8,128)(2,1)}, u32[]{:S(2)}, u32[]{:S(2)}) async-start(bf16[64,24,896]{2,1,0:T(8,128)(2,1)} %pack.1), calls=%async_computation | async-start | bytes 5505024 | tf_op jit(solution)/shard_map/all_to_all | solution.py:414
  14.5 13.0 %collective-permute-start.2 = (bf16[128,1536]{1,0:T(8,128)(2,1)S(1)}, bf16[128,1536]{1,0:T(8,128)(2,1)S(1)}, u32[]{:S(2)}, u32[]{:S(2)}) collective-permute-start(bf16[128,1536]{1,0:T(8,128)(2,1)S(1)} %bitcast.28), channel_id=1, source_target_pairs={{0,67},{1,66},{2,65},{3,64},{4,71},{5,70},{6,69},{7,68},{8,75},{9,... | collective-permute-start | bytes 1179656 | tf_op jit(solution)/shard_map/ppermute | solution.py:383
  17.9 18.1 %collective-permute-start.1 = (bf16[128,1536]{1,0:T(8,128)(2,1)S(1)}, bf16[128,1536]{1,0:T(8,128)(2,1)S(1)}, u32[]{:S(2)}, u32[]{:S(2)}) collective-permute-start(bf16[128,1536]{1,0:T(8,128)(2,1)S(1)} %bitcast.29), channel_id=1, source_target_pairs={{0,66},{1,67},{2,64},{3,65},{4,70},{5,71},{6,68},{7,69},{8,74},{9,... | collective-permute-start | bytes 1179656 | tf_op jit(solution)/shard_map/ppermute | solution.py:383
  18.3 17.8 %collective-permute-start = (bf16[128,1536]{1,0:T(8,128)(2,1)S(1)}, bf16[128,1536]{1,0:T(8,128)(2,1)S(1)}, u32[]{:S(2)}, u32[]{:S(2)}) collective-permute-start(bf16[128,1536]{1,0:T(8,128)(2,1)S(1)} %bitcast.30), channel_id=1, source_target_pairs={{0,1},{1,0},{2,3},{3,2},{4,5},{5,4},{6,7},{7,6},{8,9},{9,8},{10,11... | collective-permute-start | bytes 1179656 | tf_op jit(solution)/shard_map/ppermute | solution.py:383
  18.3 31.6 %copy-start.1 = (bf16[64,1536]{1,0:T(8,128)(2,1)S(1)}, bf16[64,1536]{1,0:T(8,128)(2,1)}, u32[]{:S(2)}) copy-start(bf16[64,1536]{1,0:T(8,128)(2,1)} %latent_in_ref.3) | copy-start | bytes 589828
  53.1 1.0 copy-start
  54.1 5.9 %collective-permute-start.3 = (bf16[1536,384]{1,0:T(8,128)(2,1)}, bf16[1536,384]{1,0:T(8,128)(2,1)}, u32[]{:S(2)}, u32[]{:S(2)}) collective-permute-start(bf16[1536,384]{1,0:T(8,128)(2,1)} %get-tuple-element.30.side_own_ref), channel_id=1, source_target_pairs={{0,1},{1,0},{2,3},{3,2},{4,5},{5,4},{6,7},{7,6},{8,9},{9,8},{10,11... | collective-permute-start | bytes 3538952 | tf_op jit(solution)/shard_map/ppermute | solution.py:383
  54.6 28.9 %all-to-all-start.1 = ((bf16[64,72,128]{2,1,0:T(8,128)(2,1)}), bf16[64,72,128]{2,1,0:T(8,128)(2,1)S(1)}, u32[]{:S(2)}, u32[]{:S(2)}) async-start(bf16[64,72,128]{2,1,0:T(8,128)(2,1)} %copy-done), calls=%async_computation.1 | async-start | bytes 2359296 | tf_op jit(solution)/shard_map/all_to_all | solution.py:428
  60.0 27.9 %copy-start.2 = (bf16[1536,64]{0,1:T(8,128)(2,1)S(1)}, bf16[1536,64]{0,1:T(8,128)(2,1)}, u32[]{:S(2)}) copy-start(bf16[1536,64]{0,1:T(8,128)(2,1)} %param.19) | copy-start | bytes 589828
  60.0 27.9 %copy-start.4 = (f32[1,256,64]{1,2,0:T(8,128)S(1)}, f32[1,256,64]{1,2,0:T(8,128)}, u32[]{:S(2)}) copy-start(f32[1,256,64]{1,2,0:T(8,128)} %param.13) | copy-start | bytes 196612
  60.0 27.9 %copy-start.6 = (s32[3]{0:T(128)S(1)}, s32[3]{0:T(128)}, u32[]{:S(2)}) copy-start(s32[3]{0:T(128)} %pad_add_fusion.place_ref) | copy-start | bytes 40
  63.5 17.1 %collective-permute-start.7 = (bf16[128,384]{1,0:T(8,128)(2,1)S(1)}, bf16[128,384]{1,0:T(8,128)(2,1)S(1)}, u32[]{:S(2)}, u32[]{:S(2)}) collective-permute-start(bf16[128,384]{1,0:T(8,128)(2,1)S(1)} %get-tuple-element.33.text_0_ref), channel_id=1, source_target_pairs={{0,64},{1,65},{2,66},{3,67},{4,68},{5,69},{6,70},{7,71},{8,72},{9,... | collective-permute-start | bytes 294920 | tf_op jit(solution)/shard_map/ppermute | solution.py:383
  67.1 15.7 %collective-permute-start.8 = (bf16[128,384]{1,0:T(8,128)(2,1)}, bf16[128,384]{1,0:T(8,128)(2,1)S(1)}, u32[]{:S(2)}, u32[]{:S(2)}) collective-permute-start(bf16[128,384]{1,0:T(8,128)(2,1)} %get-tuple-element.34), channel_id=1, source_target_pairs={{0,65},{1,64},{2,67},{3,66},{4,69},{5,68},{6,71},{7,70},{8,73},{9,... | collective-permute-start | bytes 294920 | tf_op jit(solution)/shard_map/ppermute | solution.py:383
  67.1 16.4 %collective-permute-start.4 = (bf16[128,384]{1,0:T(8,128)(2,1)}, bf16[128,384]{1,0:T(8,128)(2,1)}, u32[]{:S(2)}, u32[]{:S(2)}) collective-permute-start(bf16[128,384]{1,0:T(8,128)(2,1)} %get-tuple-element.34), channel_id=1, source_target_pairs={{0,1},{1,0},{2,3},{3,2},{4,5},{5,4},{6,7},{7,6},{8,9},{9,8},{10,11... | collective-permute-start | bytes 294920 | tf_op jit(solution)/shard_map/ppermute | solution.py:383
  67.2 16.3 %collective-permute-start.9 = (bf16[128,384]{1,0:T(8,128)(2,1)}, bf16[128,384]{1,0:T(8,128)(2,1)}, u32[]{:S(2)}, u32[]{:S(2)}) collective-permute-start(bf16[128,384]{1,0:T(8,128)(2,1)} %get-tuple-element.35), channel_id=1, source_target_pairs={{0,66},{1,67},{2,64},{3,65},{4,70},{5,71},{6,68},{7,69},{8,74},{9,... | collective-permute-start | bytes 294920 | tf_op jit(solution)/shard_map/ppermute | solution.py:383
  70.8 12.7 %collective-permute-start.5 = (bf16[128,384]{1,0:T(8,128)(2,1)}, bf16[128,384]{1,0:T(8,128)(2,1)}, u32[]{:S(2)}, u32[]{:S(2)}) collective-permute-start(bf16[128,384]{1,0:T(8,128)(2,1)} %get-tuple-element.35), channel_id=1, source_target_pairs={{0,2},{1,3},{2,0},{3,1},{4,6},{5,7},{6,4},{7,5},{8,10},{9,11},{10,... | collective-permute-start | bytes 294920 | tf_op jit(solution)/shard_map/ppermute | solution.py:383
  80.6 6.4 %collective-permute-start.10 = (bf16[128,384]{1,0:T(8,128)(2,1)}, bf16[128,384]{1,0:T(8,128)(2,1)}, u32[]{:S(2)}, u32[]{:S(2)}) collective-permute-start(bf16[128,384]{1,0:T(8,128)(2,1)} %get-tuple-element.36), channel_id=1, source_target_pairs={{0,67},{1,66},{2,65},{3,64},{4,71},{5,70},{6,69},{7,68},{8,75},{9,... | collective-permute-start | bytes 294920 | tf_op jit(solution)/shard_map/ppermute | solution.py:383
  82.8 5.1 %collective-permute-start.6 = (bf16[128,384]{1,0:T(8,128)(2,1)}, bf16[128,384]{1,0:T(8,128)(2,1)}, u32[]{:S(2)}, u32[]{:S(2)}) collective-permute-start(bf16[128,384]{1,0:T(8,128)(2,1)} %get-tuple-element.36), channel_id=1, source_target_pairs={{0,3},{1,2},{2,1},{3,0},{4,7},{5,6},{6,5},{7,4},{8,11},{9,10},{10,... | collective-permute-start | bytes 294920 | tf_op jit(solution)/shard_map/ppermute | solution.py:383
  87.9 0.8 copy-start.5
  108.2 7.3 %collective-permute-start.11 = (bf16[64,256]{1,0:T(8,128)(2,1)S(1)}, bf16[64,256]{1,0:T(8,128)(2,1)S(1)}, u32[]{:S(2)}, u32[]{:S(2)}) collective-permute-start(bf16[64,256]{1,0:T(8,128)(2,1)S(1)} %get-tuple-element.41), channel_id=1, source_target_pairs={{64,0},{65,1},{66,2},{67,3},{68,4},{69,5},{70,6},{71,7},{72,8},{73... | collective-permute-start | bytes 98312 | tf_op jit(solution)/shard_map/ppermute | solution.py:489

commit v5 on v4

--- a/solution.py
+++ b/solution.py
@@ -20,7 +20,7 @@
 SHARE = 72
 PART = 128
 WRITES = 4
-MOVES = tuple((group, near) for group in range(2) for near in range(4))
+MOVES = ((0, 0), (1, 0), (0, 2), (1, 2))
 BF = jnp.bfloat16
 F32 = jnp.float32
 SCALE = HD ** (-0.5)
@@ -110,19 +110,46 @@
         up_ref[block] = total[:, (3 + block) * RANK : (4 + block) * RANK]
 
 
-def fold_kernel(latent_in_ref, modulation_ref, packed_ref, share_ref, side_ref):
+def fold_kernel(
+    latent_in_ref, modulation_ref, packed_ref, share_ref, side_ref, columns, shares, read_sem, write_sem
+):
+    read = pltpu.make_async_copy(packed_ref.at[:, EIGHTH + SIDE :], columns, read_sem.at[0])
+    read.start()
+    side = pltpu.make_async_copy(packed_ref.at[:, EIGHTH : EIGHTH + SIDE], side_ref, read_sem.at[1])
+    side.start()
     scaled_in = (latent_in_ref[...].astype(F32) * modulation_ref[...]).astype(BF)
     folds = jnp.concatenate([latent_in_ref[...], scaled_in], axis=0)
-    share = dot(folds, packed_ref[:, EIGHTH + SIDE :]).T[:SHARE].astype(BF)
-    for device in range(share_ref.shape[0]):
-        share_ref[device] = share
-    side_ref[...] = packed_ref[:, EIGHTH : EIGHTH + SIDE]
-
-
-def mix_kernel(prompts_ref, packed_ref, out_0_ref, out_1_ref, out_2_ref, out_3_ref):
-    eighth = dot(prompts_ref[...], packed_ref[:, :EIGHTH]).astype(BF)
-    for index, out_ref in enumerate((out_0_ref, out_1_ref, out_2_ref, out_3_ref)):
-        out_ref[...] = eighth[index * TXT : (index + 1) * TXT]
+    read.wait()
+    share = dot(folds, columns[...]).T[:SHARE].astype(BF)
+    batch = shares.shape[0]
+    for device in range(batch):
+        shares[device] = share
+    writes = [
+        pltpu.make_async_copy(shares, share_ref.at[pl.ds(step * batch, batch)], write_sem.at[step])
+        for step in range(share_ref.shape[0] // batch)
+    ]
+    for write in writes:
+        write.start()
+    for write in writes:
+        write.wait()
+    side.wait()
+
+
+def mix_kernel(prompts_ref, packed_ref, mine_ref, theirs_ref, columns, read_sem):
+    read = pltpu.make_async_copy(packed_ref.at[:, :EIGHTH], columns, read_sem.at[0])
+    read.start()
+    read.wait()
+    eighth = dot(prompts_ref[...], columns[...]).astype(BF)
+    mine_ref[:TXT, :] = eighth[:TXT]
+    theirs_ref[:TXT, :] = eighth[TXT : 2 * TXT]
+    mine_ref[TXT:, :] = eighth[2 * TXT : 3 * TXT]
+    theirs_ref[TXT:, :] = eighth[3 * TXT :]
+
+
+def pair_kernel(mine_ref, received_ref, own_ref, near_ref):
+    for place, part_ref in enumerate((mine_ref, received_ref)):
+        own_ref[place] = part_ref[:TXT, :]
+        near_ref[place] = part_ref[TXT:, :]
 
 
 def forward_kernel(
@@ -139,10 +166,6 @@
     text_1_ref,
     text_2_ref,
     text_3_ref,
-    text_4_ref,
-    text_5_ref,
-    text_6_ref,
-    text_7_ref,
     side_own_ref,
     side_core_ref,
     sample_ref,
@@ -169,19 +192,10 @@
 ):
     group, near, core = place_ref[0], place_ref[1], place_ref[2]
     sigma = sigma_ref[0, 0]
-    text_refs = (
-        text_0_ref,
-        text_1_ref,
-        text_2_ref,
-        text_3_ref,
-        text_4_ref,
-        text_5_ref,
-        text_6_ref,
-        text_7_ref,
-    )
-    for (across, move), text_ref in zip(MOVES, text_refs):
-        start = (group ^ across) * HW + (near ^ move) * EIGHTH
-        text[:, pl.ds(pl.multiple_of(start, EIGHTH), EIGHTH)] = text_ref[...]
+    for (across, move), text_ref in zip(MOVES, (text_0_ref, text_1_ref, text_2_ref, text_3_ref)):
+        for place in range(2):
+            start = (group ^ across) * HW + (near ^ move ^ place) * EIGHTH
+            text[:, pl.ds(pl.multiple_of(start, EIGHTH), EIGHTH)] = text_ref[place]
 
     @pl.when(core == 0)
     def _():
@@ -321,7 +335,7 @@
         grad_k[:, span] = dot(grad_scores, queries, 0, 0).astype(BF)
         return carry
 
-    lax.fori_loop(0, HEADS, head, 0, unroll=2)
+    lax.fori_loop(0, HEADS, head, 0, unroll=12)
     spans = [slice(block * RANK, (block + 1) * RANK) for block in range(3)]
     reduced_q = dot(grad_q[...], role_up_ref[:, spans[0]]).astype(BF)
     reduced_k = dot(grad_k[...], role_up_ref[:, spans[1]]).astype(BF)
@@ -336,17 +350,18 @@
     grads_ref[...] = grads.T.astype(BF)
 
 
-def smem():
-    return pl.BlockSpec(memory_space=pltpu.SMEM)
-
-
-def run(kernel, name, megabytes, scalars, outputs, scratch, *operands, space=pltpu.VMEM):
+def run(kernel, name, megabytes, scalars, outputs, scratch, *operands, far=(), out_space=pltpu.VMEM):
     shapes = tuple(jax.ShapeDtypeStruct(*output) for output in outputs)
     return pl.pallas_call(
         kernel,
         out_shape=shapes,
-        in_specs=[smem()] * scalars + [pl.BlockSpec(memory_space=space)] * (len(operands) - scalars),
-        out_specs=tuple([pl.BlockSpec(memory_space=space)] * len(outputs)),
+        in_specs=[
+            pl.BlockSpec(
+                memory_space=pltpu.SMEM if k < scalars else pl.ANY if k in far else pltpu.VMEM
+            )
+            for k in range(len(operands))
+        ],
+        out_specs=tuple([pl.BlockSpec(memory_space=out_space)] * len(outputs)),
         scratch_shapes=scratch,
         compiler_params=pltpu.CompilerParams(vmem_limit_bytes=megabytes * 2**20),
         name=name,
@@ -409,7 +424,8 @@
         critic_down,
         gen_up.transpose(0, 2, 1),
         critic_up.transpose(0, 2, 1),
-        space=pl.ANY,
+        far=(1, 2, 3, 4, 5),
+        out_space=pl.ANY,
     )
     packed = lax.all_to_all(packed, "fsdp", 0, 0).reshape(HW, EIGHTH + SIDE + PART)
     (prompts,) = run(prompt_kernel, "prompts", 16, 0, [((4 * TXT, HW), BF)], [], *texts)
@@ -420,28 +436,37 @@
         16,
         0,
         [((devices, SHARE, PART), BF), ((HW, SIDE), BF)],
-        [],
+        [
+            pltpu.VMEM((HW, PART), BF),
+            pltpu.VMEM((devices // 8, SHARE, PART), BF),
+            pltpu.SemaphoreType.DMA((2,)),
+            pltpu.SemaphoreType.DMA((8,)),
+        ],
         latent_in,
         gain,
         packed,
+        far=(2,),
+        out_space=pl.ANY,
     )
     fold = lax.all_to_all(share, "fsdp", 0, 0).reshape(devices * SHARE, PART)
     side_core = move(side_own, 0, 1)
     prompts, side_core = lax.optimization_barrier((prompts, side_core))
-    parts = run(
+    mine, theirs = run(
         mix_kernel,
         "mix",
         16,
         0,
-        [((TXT, EIGHTH), BF)] * 4,
-        [],
+        [((2 * TXT, EIGHTH), BF)] * 2,
+        [pltpu.VMEM((HW, EIGHTH), BF), pltpu.SemaphoreType.DMA((1,))],
         prompts,
         packed,
-    )
-    pieces = [
-        parts[near] if (across, near) == (0, 0) else move(parts[near], across, near)
-        for across, near in MOVES
-    ]
+        far=(1,),
+    )
+    received = move(theirs, 0, 1)
+    own_pair, near_pair = run(
+        pair_kernel, "pair", 16, 0, [((2, TXT, EIGHTH), BF)] * 2, [], mine, received
+    )
+    pieces = [own_pair, move(own_pair, 1, 0), move(near_pair, 0, 2), move(near_pair, 1, 2)]
 
     sample, sample_again, velocity, narrow_velocity, *saved, role_up = run(
         forward_kernel,

time: 153 us -> 181 us (1.18)
  Pallas kernels: 40 us -> 71.3 us
  starting transfers between devices: 28 us -> 25.4 us
    pallas_call x7 -> x8, Pallas kernels: 40 us -> 71.3 us  [run(): pl.pallas_call(kernel, out_shape=shapes, in_specs=[pl.BlockSpec(memory_sp...]
    all_to_all x1, waiting for transfers between devices: 0.01 us -> 9.63 us  [per_device(): fold = lax.all_to_all(share, 'fsdp', 0, 0).reshape(devices * SHARE, PART)]
    ppermute x11 -> x8, waiting for transfers between devices: 34.1 us -> 24.9 us  [move(): return lax.ppermute(array, ('group', 'fsdp'), pairs)]
    ppermute x11 -> x8, starting transfers between devices: 11.6 us -> 8.95 us  [move(): return lax.ppermute(array, ('group', 'fsdp'), pairs)]
  transfers between devices with their start and end apart: 14 -> 11, of which waited for: 8 -> 8; matrix products, arithmetic and copies ran while one was open for 0% -> 0% of each run, Pallas kernels for 3% -> 2%
where the time goes in v5:
time: 181 us; the launch traced here: 179 us
  Pallas kernels  71.3 us (39%)
  waiting for transfers between devices  53.9 us (30%)
  blocking collectives  25.6 us (14%)
  starting transfers between devices  25.4 us (14%)
    pallas_call x8, Pallas kernels, run(): pl.pallas_call(kernel, out_shape=shapes, in_specs=[pl.BlockSpec(memory_sp...  71.3 us
    all_to_all x1, blocking collectives, per_device(): shares = lax.all_to_all(grads.reshape(devices, shard, SIDE), 'fsdp', 0, 0)  25.6 us
    ppermute x8, waiting for transfers between devices, move(): return lax.ppermute(array, ('group', 'fsdp'), pairs)  24.9 us
    all_to_all x1, waiting for transfers between devices, per_device(): lax.all_to_all(packed, 'fsdp', 0, 0).reshape(HW, EIGHTH + SIDE + PART)  13.3 us
    all_to_all x1, starting transfers between devices, per_device(): lax.all_to_all(packed, 'fsdp', 0, 0).reshape(HW, EIGHTH + SIDE + PART)  9.75 us
    all_to_all x1, waiting for transfers between devices, per_device(): fold = lax.all_to_all(share, 'fsdp', 0, 0).reshape(devices * SHARE, PART)  9.63 us
    ppermute x8, starting transfers between devices, move(): return lax.ppermute(array, ('group', 'fsdp'), pairs)  8.95 us
    ppermute x1, waiting for transfers between devices, per_device(): fake_velocity = lax.ppermute(narrow_velocity, 'group', [(1, 0)])  6.01 us
  transfers between devices with their start and end apart: 11, of which 8 were waited for; matrix products, arithmetic and copies ran while one was open for 0% of the time, Pallas kernels for 2%

profile of v5, /device:TPU:0, one launch (start us, length us, event | category | flops | bytes accessed | tf_op | source)
XLA Modules:
  0.0 179.3 jit_solution(788769880410920434)
XLA Ops:
  0.6 0.6 pad_add_fusion.place_ref
  1.3 3.4 %pack.1 = bf16[64,24,896]{2,1,0:T(8,128)(2,1)} custom-call(s32[3]{0:T(128)} %pad_add_fusion.place_ref, bf16[24,4608]{1,0:T(8,128)(2,1)} %base_ref.1, bf16[24,192]{1,0:T(8,128)(2,1)} %gen_down_ref.1, bf16[24,192]{1,0:T(8,128)(2,1)} %critic_down_ref.1, bf16[3,24,64]{2,1,0:T(8,128)(2,1)} %bitcast.35, bf16[3,24,64]{2,1,0:T(8,128)(2,1)} %bitcast.36), custom_call_target="tpu_custom_call" | custom-call | tf_op jit(solution)/shard_map/pack/pallas_call | solution.py:355
  4.7 0.0 copy-start.3
  4.7 0.0 copy-start.7
  4.7 9.8 %all-to-all-start = ((bf16[64,24,896]{2,1,0:T(8,128)(2,1)}), bf16[64,24,896]{2,1,0:T(8,128)(2,1)}, u32[]{:S(2)}, u32[]{:S(2)}) async-start(bf16[64,24,896]{2,1,0:T(8,128)(2,1)} %pack.1), calls=%async_computation | async-start | bytes 5505024 | tf_op jit(solution)/shard_map/all_to_all | solution.py:430
  14.5 0.0 copy-done.3
  14.5 3.5 %collective-permute-start.2 = (bf16[128,1536]{1,0:T(8,128)(2,1)S(1)}, bf16[128,1536]{1,0:T(8,128)(2,1)S(1)}, u32[]{:S(2)}, u32[]{:S(2)}) collective-permute-start(bf16[128,1536]{1,0:T(8,128)(2,1)S(1)} %bitcast.28), channel_id=1, source_target_pairs={{0,67},{1,66},{2,65},{3,64},{4,71},{5,70},{6,69},{7,68},{8,75},{9,... | collective-permute-start | bytes 1179656 | tf_op jit(solution)/shard_map/ppermute | solution.py:398
  17.9 0.3 collective-permute-start.1
  18.3 0.0 collective-permute-start
  18.3 0.0 copy-done.7
  18.3 0.0 copy-start.1
  18.3 9.1 %collective-permute-done.2.text_3_ref = bf16[128,1536]{1,0:T(8,128)(2,1)S(1)} collective-permute-done((bf16[128,1536]{1,0:T(8,128)(2,1)S(1)}, bf16[128,1536]{1,0:T(8,128)(2,1)S(1)}, u32[]{:S(2)}, u32[]{:S(2)}) %collective-permute-start.2) | collective-permute-done | bytes 393248 | tf_op jit(solution)/shard_map/ppermute | solution.py:398
  27.4 8.6 %collective-permute-done.1.text_2_ref = bf16[128,1536]{1,0:T(8,128)(2,1)S(1)} collective-permute-done((bf16[128,1536]{1,0:T(8,128)(2,1)S(1)}, bf16[128,1536]{1,0:T(8,128)(2,1)S(1)}, u32[]{:S(2)}, u32[]{:S(2)}) %collective-permute-start.1) | collective-permute-done | bytes 393248 | tf_op jit(solution)/shard_map/ppermute | solution.py:398
  36.0 0.0 collective-permute-done.text_1_ref
  36.0 0.5 prompts.1.prompts_ref.prompt_ref
  36.5 13.3 %all-to-all-done = bf16[64,24,896]{2,1,0:T(8,128)(2,1)} async-done(((bf16[64,24,896]{2,1,0:T(8,128)(2,1)}), bf16[64,24,896]{2,1,0:T(8,128)(2,1)}, u32[]{:S(2)}, u32[]{:S(2)}) %all-to-all-start) | async-done | bytes 2752544 | tf_op jit(solution)/shard_map/all_to_all | solution.py:430
  49.9 0.0 copy-done.1
  49.9 36.9 %fold.1 = (bf16[64,72,128]{2,1,0:T(8,128)(2,1)S(1)}, bf16[1536,384]{1,0:T(8,128)(2,1)}) custom-call(bf16[64,1536]{1,0:T(8,128)(2,1)S(1)} %copy-done.1, f32[1,1536]{1,0:T(1,128)S(1)} %reshape.23.modulation_ref, bf16[1536,896]{1,0:T(8,128)(2,1)} %bitcast.10.packed_ref), custom_call_target="tpu_custom_call" | custom-call | tf_op jit(solution)/shard_map/fold/pallas_call | solution.py:355
  86.8 0.0 copy-start
  86.8 1.0 copy-done
  87.9 0.4 collective-permute-start.3
  88.3 5.4 %all-to-all-start.1 = ((bf16[64,72,128]{2,1,0:T(8,128)(2,1)}), bf16[64,72,128]{2,1,0:T(8,128)(2,1)S(1)}, u32[]{:S(2)}, u32[]{:S(2)}) async-start(bf16[64,72,128]{2,1,0:T(8,128)(2,1)} %copy-done), calls=%async_computation.1 | async-start | bytes 2359296 | tf_op jit(solution)/shard_map/all_to_all | solution.py:451
  93.7 0.0 copy-start.2
  93.7 0.0 copy-start.4
  93.7 0.0 copy-start.5
  93.7 0.0 copy-start.6
  93.7 0.0 collective-permute-done.3.side_core_ref
  93.7 2.3 %mix.1 = (bf16[256,384]{1,0:T(8,128)(2,1)S(1)}, bf16[256,384]{1,0:T(8,128)(2,1)S(1)}) custom-call(bf16[512,1536]{1,0:T(8,128)(2,1)S(1)} %prompts.1.prompts_ref.prompt_ref, bf16[1536,896]{1,0:T(8,128)(2,1)} %bitcast.10.packed_ref), custom_call_target="tpu_custom_call" | custom-call | tf_op jit(solution)/shard_map/mix/pallas_call | solution.py:355
  96.1 0.1 collective-permute-start.4
  96.2 1.4 collective-permute-done.4.received_ref
  97.6 0.7 pair.1
  98.3 3.6 %collective-permute-start.5 = (bf16[2,128,384]{2,1,0:T(8,128)(2,1)S(1)}, bf16[2,128,384]{2,1,0:T(8,128)(2,1)}, u32[]{:S(2)}, u32[]{:S(2)}) collective-permute-start(bf16[2,128,384]{2,1,0:T(8,128)(2,1)S(1)} %get-tuple-element.35.text_0_ref), channel_id=1, source_target_pairs={{0,64},{1,65},{2,66},{3,67},{4,68},{5,69},{6,70},{7,71},{8,72},{9,... | collective-permute-start | bytes 589832 | tf_op jit(solution)/shard_map/ppermute | solution.py:398
  101.9 0.7 collective-permute-start.7
  102.6 0.3 collective-permute-start.6
  103.5 9.6 %all-to-all-done.1 = bf16[64,72,128]{2,1,0:T(8,128)(2,1)S(1)} async-done(((bf16[64,72,128]{2,1,0:T(8,128)(2,1)}), bf16[64,72,128]{2,1,0:T(8,128)(2,1)S(1)}, u32[]{:S(2)}, u32[]{:S(2)}) %all-to-all-start.1) | async-done | bytes 1179680 | tf_op jit(solution)/shard_map/all_to_all | solution.py:451
  113.2 3.6 %collective-permute-done.5.text_1_ref = bf16[2,128,384]{2,1,0:T(8,128)(2,1)} collective-permute-done((bf16[2,128,384]{2,1,0:T(8,128)(2,1)S(1)}, bf16[2,128,384]{2,1,0:T(8,128)(2,1)}, u32[]{:S(2)}, u32[]{:S(2)}) %collective-permute-start.5) | collective-permute-done | bytes 196640 | tf_op jit(solution)/shard_map/ppermute | solution.py:398
  116.7 0.0 collective-permute-done.7.text_3_ref
  116.7 2.3 %collective-permute-done.6.text_2_ref = bf16[2,128,384]{2,1,0:T(8,128)(2,1)} collective-permute-done((bf16[2,128,384]{2,1,0:T(8,128)(2,1)}, bf16[2,128,384]{2,1,0:T(8,128)(2,1)}, u32[]{:S(2)}, u32[]{:S(2)}) %collective-permute-start.6) | collective-permute-done | bytes 196640 | tf_op jit(solution)/shard_map/ppermute | solution.py:398
  119.0 0.0 copy-done.2
  119.0 0.0 copy-done.4
  119.0 0.0 copy-done.5
  119.0 0.0 copy-done.6
  119.0 19.5 %forward.1 = (f32[64,256]{1,0:T(8,128)}, f32[64,256]{1,0:T(8,128)S(1)}, f32[64,256]{1,0:T(8,128)S(1)}, bf16[64,256]{1,0:T(8,128)(2,1)S(1)}, bf16[256,1536]{1,0:T...) custom-call(s32[3]{0:T(128)S(1)} %copy-done.6, ...), custom_call_target="tpu_custom_call" | custom-call | tf_op jit(solution)/shard_map/forward/pallas_call | solution.py:355
  138.5 1.3 collective-permute-start.8
  139.8 6.0 %collective-permute-done.8.fake_ref = bf16[64,256]{1,0:T(8,128)(2,1)S(1)} collective-permute-done((bf16[64,256]{1,0:T(8,128)(2,1)S(1)}, bf16[64,256]{1,0:T(8,128)(2,1)S(1)}, u32[]{:S(2)}, u32[]{:S(2)}) %collective-permute-start.8) | collective-permute-done | bytes 32800 | tf_op jit(solution)/shard_map/ppermute | solution.py:514
  145.8 7.1 %backward.1 = bf16[1536,384]{1,0:T(8,128)(2,1)S(1)} custom-call(s32[3]{0:T(128)S(1)} %copy-done.6, f32[1,1]{1,0:T(1,128)} %bitcast.3.sigma_ref, f32[64,256]{1,0:T(8,128)S(1)} %get-tuple-element.39.sample_ref, f32[64,256]{1,0:T(8,128)S(1)} %bitcast.33, f32[64,256]{1,0:T(8,128)S(1)} %get-tuple-element.40.own_ref, ...), custom_call_target="tpu_custom_call" | custom-call | tf_op jit(solution)/shard_map/backward/pallas_call | solution.py:355
  152.8 25.6 %all_to_all.15.shares_ref = bf16[64,24,384]{2,1,0:T(8,128)(2,1)S(1)} all-to-all(bf16[64,24,384]{2,1,0:T(8,128)(2,1)S(1)} %bitcast.24), channel_id=1, replica_groups=mesh['group'=2,'fsdp'=64] {'fsdp'}, dimensions={0} | all-to-all | bytes 2359296 | tf_op jit(solution)/shard_map/all_to_all | solution.py:533
  178.4 0.9 total.1
  (1 shorter events, 0.0 us)
Async XLA Ops:
  4.7 9.8 %copy-start.3 = (bf16[1,128,1536]{2,1,0:T(8,128)(2,1)S(1)}, bf16[1,128,1536]{2,1,0:T(8,128)(2,1)}, u32[]{:S(2)}) copy-start(bf16[1,128,1536]{2,1,0:T(8,128)(2,1)} %param.14) | copy-start | bytes 1179652
  4.7 13.6 %copy-start.7 = (f32[1536]{0:T(1024)S(1)}, f32[1536]{0:T(1024)}, u32[]{:S(2)}) copy-start(f32[1536]{0:T(1024)} %param.18) | copy-start | bytes 18436
  4.7 45.2 %all-to-all-start = ((bf16[64,24,896]{2,1,0:T(8,128)(2,1)}), bf16[64,24,896]{2,1,0:T(8,128)(2,1)}, u32[]{:S(2)}, u32[]{:S(2)}) async-start(bf16[64,24,896]{2,1,0:T(8,128)(2,1)} %pack.1), calls=%async_computation | async-start | bytes 5505024 | tf_op jit(solution)/shard_map/all_to_all | solution.py:430
  14.5 13.0 %collective-permute-start.2 = (bf16[128,1536]{1,0:T(8,128)(2,1)S(1)}, bf16[128,1536]{1,0:T(8,128)(2,1)S(1)}, u32[]{:S(2)}, u32[]{:S(2)}) collective-permute-start(bf16[128,1536]{1,0:T(8,128)(2,1)S(1)} %bitcast.28), channel_id=1, source_target_pairs={{0,67},{1,66},{2,65},{3,64},{4,71},{5,70},{6,69},{7,68},{8,75},{9,... | collective-permute-start | bytes 1179656 | tf_op jit(solution)/shard_map/ppermute | solution.py:398
  17.9 18.1 %collective-permute-start.1 = (bf16[128,1536]{1,0:T(8,128)(2,1)S(1)}, bf16[128,1536]{1,0:T(8,128)(2,1)S(1)}, u32[]{:S(2)}, u32[]{:S(2)}) collective-permute-start(bf16[128,1536]{1,0:T(8,128)(2,1)S(1)} %bitcast.29), channel_id=1, source_target_pairs={{0,66},{1,67},{2,64},{3,65},{4,70},{5,71},{6,68},{7,69},{8,74},{9,... | collective-permute-start | bytes 1179656 | tf_op jit(solution)/shard_map/ppermute | solution.py:398
  18.3 17.8 %collective-permute-start = (bf16[128,1536]{1,0:T(8,128)(2,1)S(1)}, bf16[128,1536]{1,0:T(8,128)(2,1)S(1)}, u32[]{:S(2)}, u32[]{:S(2)}) collective-permute-start(bf16[128,1536]{1,0:T(8,128)(2,1)S(1)} %bitcast.30), channel_id=1, source_target_pairs={{0,1},{1,0},{2,3},{3,2},{4,5},{5,4},{6,7},{7,6},{8,9},{9,8},{10,11... | collective-permute-start | bytes 1179656 | tf_op jit(solution)/shard_map/ppermute | solution.py:398
  18.3 31.6 %copy-start.1 = (bf16[64,1536]{1,0:T(8,128)(2,1)S(1)}, bf16[64,1536]{1,0:T(8,128)(2,1)}, u32[]{:S(2)}) copy-start(bf16[64,1536]{1,0:T(8,128)(2,1)} %latent_in_ref.3) | copy-start | bytes 589828
  86.8 1.1 copy-start
  87.9 5.9 %collective-permute-start.3 = (bf16[1536,384]{1,0:T(8,128)(2,1)}, bf16[1536,384]{1,0:T(8,128)(2,1)}, u32[]{:S(2)}, u32[]{:S(2)}) collective-permute-start(bf16[1536,384]{1,0:T(8,128)(2,1)} %get-tuple-element.30.side_own_ref), channel_id=1, source_target_pairs={{0,1},{1,0},{2,3},{3,2},{4,5},{5,4},{6,7},{7,6},{8,9},{9,8},{10,11... | collective-permute-start | bytes 3538952 | tf_op jit(solution)/shard_map/ppermute | solution.py:398
  88.3 24.8 %all-to-all-start.1 = ((bf16[64,72,128]{2,1,0:T(8,128)(2,1)}), bf16[64,72,128]{2,1,0:T(8,128)(2,1)S(1)}, u32[]{:S(2)}, u32[]{:S(2)}) async-start(bf16[64,72,128]{2,1,0:T(8,128)(2,1)} %copy-done), calls=%async_computation.1 | async-start | bytes 2359296 | tf_op jit(solution)/shard_map/all_to_all | solution.py:451
  93.7 25.3 %copy-start.2 = (bf16[1536,64]{0,1:T(8,128)(2,1)S(1)}, bf16[1536,64]{0,1:T(8,128)(2,1)}, u32[]{:S(2)}) copy-start(bf16[1536,64]{0,1:T(8,128)(2,1)} %param.19) | copy-start | bytes 589828
  93.7 25.3 %copy-start.4 = (f32[1,256,64]{1,2,0:T(8,128)S(1)}, f32[1,256,64]{1,2,0:T(8,128)}, u32[]{:S(2)}) copy-start(f32[1,256,64]{1,2,0:T(8,128)} %param.13) | copy-start | bytes 196612
  93.7 25.3 %copy-start.5 = (f32[1,256,64]{1,2,0:T(8,128)S(1)}, f32[1,256,64]{1,2,0:T(8,128)}, u32[]{:S(2)}) copy-start(f32[1,256,64]{1,2,0:T(8,128)} %param.12) | copy-start | bytes 196612
  93.7 25.3 %copy-start.6 = (s32[3]{0:T(128)S(1)}, s32[3]{0:T(128)}, u32[]{:S(2)}) copy-start(s32[3]{0:T(128)} %pad_add_fusion.place_ref) | copy-start | bytes 40
  96.1 1.5 collective-permute-start.4
  98.3 18.4 %collective-permute-start.5 = (bf16[2,128,384]{2,1,0:T(8,128)(2,1)S(1)}, bf16[2,128,384]{2,1,0:T(8,128)(2,1)}, u32[]{:S(2)}, u32[]{:S(2)}) collective-permute-start(bf16[2,128,384]{2,1,0:T(8,128)(2,1)S(1)} %get-tuple-element.35.text_0_ref), channel_id=1, source_target_pairs={{0,64},{1,65},{2,66},{3,67},{4,68},{5,69},{6,70},{7,71},{8,72},{9,... | collective-permute-start | bytes 589832 | tf_op jit(solution)/shard_map/ppermute | solution.py:398
  101.9 14.8 %collective-permute-start.7 = (bf16[2,128,384]{2,1,0:T(8,128)(2,1)}, bf16[2,128,384]{2,1,0:T(8,128)(2,1)}, u32[]{:S(2)}, u32[]{:S(2)}) collective-permute-start(bf16[2,128,384]{2,1,0:T(8,128)(2,1)} %get-tuple-element.36), channel_id=1, source_target_pairs={{0,66},{1,67},{2,64},{3,65},{4,70},{5,71},{6,68},{7,69},{8,74},{9,... | collective-permute-start | bytes 589832 | tf_op jit(solution)/shard_map/ppermute | solution.py:398
  102.6 16.4 %collective-permute-start.6 = (bf16[2,128,384]{2,1,0:T(8,128)(2,1)}, bf16[2,128,384]{2,1,0:T(8,128)(2,1)}, u32[]{:S(2)}, u32[]{:S(2)}) collective-permute-start(bf16[2,128,384]{2,1,0:T(8,128)(2,1)} %get-tuple-element.36), channel_id=1, source_target_pairs={{0,2},{1,3},{2,0},{3,1},{4,6},{5,7},{6,4},{7,5},{8,10},{9,11},{10,... | collective-permute-start | bytes 589832 | tf_op jit(solution)/shard_map/ppermute | solution.py:398
  138.5 7.3 %collective-permute-start.8 = (bf16[64,256]{1,0:T(8,128)(2,1)S(1)}, bf16[64,256]{1,0:T(8,128)(2,1)S(1)}, u32[]{:S(2)}, u32[]{:S(2)}) collective-permute-start(bf16[64,256]{1,0:T(8,128)(2,1)S(1)} %get-tuple-element.41), channel_id=1, source_target_pairs={{64,0},{65,1},{66,2},{67,3},{68,4},{69,5},{70,6},{71,7},{72,8},{73... | collective-permute-start | bytes 98312 | tf_op jit(solution)/shard_map/ppermute | solution.py:514

commit v6 on v5

--- a/solution.py
+++ b/solution.py
@@ -111,11 +111,20 @@
 
 
 def fold_kernel(
-    latent_in_ref, modulation_ref, packed_ref, share_ref, side_ref, columns, shares, read_sem, write_sem
+    latent_in_ref,
+    modulation_ref,
+    packed_ref,
+    share_ref,
+    side_ref,
+    columns,
+    sides,
+    shares,
+    read_sem,
+    write_sem,
 ):
     read = pltpu.make_async_copy(packed_ref.at[:, EIGHTH + SIDE :], columns, read_sem.at[0])
     read.start()
-    side = pltpu.make_async_copy(packed_ref.at[:, EIGHTH : EIGHTH + SIDE], side_ref, read_sem.at[1])
+    side = pltpu.make_async_copy(packed_ref.at[:, EIGHTH : EIGHTH + SIDE], sides, read_sem.at[1])
     side.start()
     scaled_in = (latent_in_ref[...].astype(F32) * modulation_ref[...]).astype(BF)
     folds = jnp.concatenate([latent_in_ref[...], scaled_in], axis=0)
@@ -130,6 +139,9 @@
     ]
     for write in writes:
         write.start()
+    side.wait()
+    side = pltpu.make_async_copy(sides, side_ref, read_sem.at[1])
+    side.start()
     for write in writes:
         write.wait()
     side.wait()
@@ -303,10 +315,12 @@
     attended_ref,
     reduced_ref,
     picture_ref,
-    grads_ref,
+    mine_ref,
+    theirs_ref,
     grad_q,
     grad_k,
     grad_v,
+    grads,
 ):
     flag = place_ref[0]
     sigma = sigma_ref[0, 0]
@@ -346,8 +360,18 @@
     up_q = dot(reduced_ref[TXT:, spans[0]], grad_q[...], 0, 0)
     up_k = dot(reduced_ref[:, spans[1]], grad_k[...], 0, 0)
     up_v = dot(reduced_ref[:, spans[2]], grad_v[...], 0, 0)
-    grads = jnp.concatenate([down_q, down_kv, up_q, up_k, up_v], axis=0)
-    grads_ref[...] = grads.T.astype(BF)
+    grads[...] = jnp.concatenate([down_q, down_kv, up_q, up_k, up_v], axis=0).T
+    core = place_ref[2]
+    pairs, rows, _ = mine_ref.shape
+    for pair in range(pairs):
+        mine = pl.ds(pl.multiple_of((2 * pair + core) * rows, 8), rows)
+        theirs = pl.ds(pl.multiple_of((2 * pair + 1 - core) * rows, 8), rows)
+        mine_ref[pair] = grads[mine, :]
+        theirs_ref[pair] = grads[theirs, :].astype(BF)
+
+
+def add_kernel(mine_ref, received_ref, sums_ref):
+    sums_ref[...] = (mine_ref[...] + received_ref[...].astype(F32)).astype(BF)
 
 
 def run(kernel, name, megabytes, scalars, outputs, scratch, *operands, far=(), out_space=pltpu.VMEM):
@@ -438,6 +462,7 @@
         [((devices, SHARE, PART), BF), ((HW, SIDE), BF)],
         [
             pltpu.VMEM((HW, PART), BF),
+            pltpu.VMEM((HW, SIDE), BF),
             pltpu.VMEM((devices // 8, SHARE, PART), BF),
             pltpu.SemaphoreType.DMA((2,)),
             pltpu.SemaphoreType.DMA((8,)),
@@ -512,13 +537,19 @@
         side_core,
     )
     fake_velocity = lax.ppermute(narrow_velocity, "group", [(1, 0)])
-    (grads,) = run(
+    half = (devices // 2, shard, SIDE)
+    mine, theirs = run(
         backward_kernel,
         "backward",
         24,
         2,
-        [((HW, SIDE), BF)],
-        [pltpu.VMEM((IMG, HW), BF), pltpu.VMEM((ROWS, HW), BF), pltpu.VMEM((ROWS, HW), BF)],
+        [(half, F32), (half, BF)],
+        [
+            pltpu.VMEM((IMG, HW), BF),
+            pltpu.VMEM((ROWS, HW), BF),
+            pltpu.VMEM((ROWS, HW), BF),
+            pltpu.VMEM((HW, SIDE), F32),
+        ],
         place,
         sigma,
         sample_again,
@@ -530,7 +561,9 @@
         role_up,
         *saved,
     )
-    shares = lax.all_to_all(grads.reshape(devices, shard, SIDE), "fsdp", 0, 0)
+    (sums,) = run(add_kernel, "add", 16, 0, [(half, BF)], [], mine, move(theirs, 0, 1))
+    parities = [list(range(core, devices, 2)) for core in range(2)]
+    shares = lax.all_to_all(sums, "fsdp", 0, 0, axis_index_groups=parities)
     share_down, share_up = run(
         sum_kernel,
         "total",

time: 181 us -> 142 us (0.78)
  Pallas kernels: 71.3 us -> 38.6 us
  blocking collectives: 25.6 us -> 18.7 us
  waiting for transfers between devices: 53.9 us -> 55.9 us
    pallas_call x8 -> x9, Pallas kernels: 71.3 us -> 38.6 us  [run(): pl.pallas_call(kernel, out_shape=shapes, in_specs=[pl.BlockSpec(memory_sp...]
    all_to_all x1, blocking collectives: 25.6 us -> 18.7 us  [per_device(): shares = lax.all_to_all(sums, 'fsdp', 0, 0, axis_index_groups=parities)]
    ppermute x8 -> x9, waiting for transfers between devices: 24.9 us -> 26.9 us  [move(): return lax.ppermute(array, ('group', 'fsdp'), pairs)]
    ppermute x8 -> x9, starting transfers between devices: 8.95 us -> 9.04 us  [move(): return lax.ppermute(array, ('group', 'fsdp'), pairs)]
  transfers between devices with their start and end apart: 11 -> 12, of which waited for: 8 -> 9; matrix products, arithmetic and copies ran while one was open for 0% -> 0% of each run, Pallas kernels for 2% -> 3%
where the time goes in v6:
time: 142 us
  waiting for transfers between devices  55.9 us (39%)
  Pallas kernels  38.6 us (27%)
  starting transfers between devices  25.4 us (18%)
  blocking collectives  18.7 us (13%)
  between operations  1.47 us (1%)
    pallas_call x9, Pallas kernels, run(): pl.pallas_call(kernel, out_shape=shapes, in_specs=[pl.BlockSpec(memory_sp...  38.6 us
    ppermute x9, waiting for transfers between devices, move(): return lax.ppermute(array, ('group', 'fsdp'), pairs)  26.9 us
    all_to_all x1, blocking collectives, per_device(): shares = lax.all_to_all(sums, 'fsdp', 0, 0, axis_index_groups=parities)  18.7 us
    all_to_all x1, waiting for transfers between devices, per_device(): lax.all_to_all(packed, 'fsdp', 0, 0).reshape(HW, EIGHTH + SIDE + PART)  13.3 us
    all_to_all x1, starting transfers between devices, per_device(): lax.all_to_all(packed, 'fsdp', 0, 0).reshape(HW, EIGHTH + SIDE + PART)  9.75 us
    all_to_all x1, waiting for transfers between devices, per_device(): fold = lax.all_to_all(share, 'fsdp', 0, 0).reshape(devices * SHARE, PART)  9.63 us
    ppermute x9, starting transfers between devices, move(): return lax.ppermute(array, ('group', 'fsdp'), pairs)  9.04 us
    ppermute x1, waiting for transfers between devices, per_device(): fake_velocity = lax.ppermute(narrow_velocity, 'group', [(1, 0)])  6.01 us
  transfers between devices with their start and end apart: 12, of which 9 were waited for; matrix products, arithmetic and copies ran while one was open for 0% of the time, Pallas kernels for 3%

profile of v6, /device:TPU:0, one launch (start us, length us, event | category | flops | bytes accessed | tf_op | source)
XLA Modules:
  0.0 141.7 jit_solution(9310551017261889292)
XLA Ops:
  0.6 0.6 pad_add_fusion.place_ref
  1.2 3.4 %pack.1 = bf16[64,24,896]{2,1,0:T(8,128)(2,1)} custom-call(s32[3]{0:T(128)} %pad_add_fusion.place_ref, bf16[24,4608]{1,0:T(8,128)(2,1)} %base_ref.1, bf16[24,192]{1,0:T(8,128)(2,1)} %gen_down_ref.1, bf16[24,192]{1,0:T(8,128)(2,1)} %critic_down_ref.1, bf16[3,24,64]{2,1,0:T(8,128)(2,1)} %bitcast.33, bf16[3,24,64]{2,1,0:T(8,128)(2,1)} %bitcast.34), custom_call_target="tpu_custom_call" | custom-call | tf_op jit(solution)/shard_map/pack/pallas_call | solution.py:379
  4.6 0.0 copy-start.3
  4.6 0.0 copy-start.7
  4.7 9.8 %all-to-all-start = ((bf16[64,24,896]{2,1,0:T(8,128)(2,1)}), bf16[64,24,896]{2,1,0:T(8,128)(2,1)}, u32[]{:S(2)}, u32[]{:S(2)}) async-start(bf16[64,24,896]{2,1,0:T(8,128)(2,1)} %pack.1), calls=%async_computation | async-start | bytes 5505024 | tf_op jit(solution)/shard_map/all_to_all | solution.py:454
  14.4 0.0 copy-done.3
  14.4 3.5 %collective-permute-start.2 = (bf16[128,1536]{1,0:T(8,128)(2,1)S(1)}, bf16[128,1536]{1,0:T(8,128)(2,1)S(1)}, u32[]{:S(2)}, u32[]{:S(2)}) collective-permute-start(bf16[128,1536]{1,0:T(8,128)(2,1)S(1)} %bitcast.26), channel_id=1, source_target_pairs={{0,67},{1,66},{2,65},{3,64},{4,71},{5,70},{6,69},{7,68},{8,75},{9,... | collective-permute-start | bytes 1179656 | tf_op jit(solution)/shard_map/ppermute | solution.py:422
  17.9 0.3 collective-permute-start.1
  18.2 0.0 collective-permute-start
  18.3 0.0 copy-done.7
  18.3 0.0 copy-start.1
  18.3 9.1 %collective-permute-done.2.text_3_ref = bf16[128,1536]{1,0:T(8,128)(2,1)S(1)} collective-permute-done((bf16[128,1536]{1,0:T(8,128)(2,1)S(1)}, bf16[128,1536]{1,0:T(8,128)(2,1)S(1)}, u32[]{:S(2)}, u32[]{:S(2)}) %collective-permute-start.2) | collective-permute-done | bytes 393248 | tf_op jit(solution)/shard_map/ppermute | solution.py:422
  27.4 8.6 %collective-permute-done.1.text_2_ref = bf16[128,1536]{1,0:T(8,128)(2,1)S(1)} collective-permute-done((bf16[128,1536]{1,0:T(8,128)(2,1)S(1)}, bf16[128,1536]{1,0:T(8,128)(2,1)S(1)}, u32[]{:S(2)}, u32[]{:S(2)}) %collective-permute-start.1) | collective-permute-done | bytes 393248 | tf_op jit(solution)/shard_map/ppermute | solution.py:422
  36.0 0.0 collective-permute-done.text_1_ref
  36.0 0.5 prompts.1.prompts_ref.prompt_ref
  36.5 13.3 %all-to-all-done = bf16[64,24,896]{2,1,0:T(8,128)(2,1)} async-done(((bf16[64,24,896]{2,1,0:T(8,128)(2,1)}), bf16[64,24,896]{2,1,0:T(8,128)(2,1)}, u32[]{:S(2)}, u32[]{:S(2)}) %all-to-all-start) | async-done | bytes 2752544 | tf_op jit(solution)/shard_map/all_to_all | solution.py:454
  49.8 0.0 copy-done.1
  49.8 4.0 %fold.1 = (bf16[64,72,128]{2,1,0:T(8,128)(2,1)S(1)}, bf16[1536,384]{1,0:T(8,128)(2,1)}) custom-call(bf16[64,1536]{1,0:T(8,128)(2,1)S(1)} %copy-done.1, f32[1,1536]{1,0:T(1,128)S(1)} %reshape.20.modulation_ref, bf16[1536,896]{1,0:T(8,128)(2,1)} %bitcast.10.packed_ref), custom_call_target="tpu_custom_call" | custom-call | tf_op jit(solution)/shard_map/fold/pallas_call | solution.py:379
  53.8 0.0 copy-start
  53.8 1.0 copy-done
  54.8 0.4 collective-permute-start.3
  55.3 5.4 %all-to-all-start.1 = ((bf16[64,72,128]{2,1,0:T(8,128)(2,1)}), bf16[64,72,128]{2,1,0:T(8,128)(2,1)S(1)}, u32[]{:S(2)}, u32[]{:S(2)}) async-start(bf16[64,72,128]{2,1,0:T(8,128)(2,1)} %copy-done), calls=%async_computation.1 | async-start | bytes 2359296 | tf_op jit(solution)/shard_map/all_to_all | solution.py:476
  60.6 0.0 copy-start.2
  60.7 0.0 copy-start.4
  60.7 0.0 copy-start.5
  60.7 0.0 collective-permute-done.3.side_core_ref
  60.7 2.3 %mix.1 = (bf16[256,384]{1,0:T(8,128)(2,1)S(1)}, bf16[256,384]{1,0:T(8,128)(2,1)S(1)}) custom-call(bf16[512,1536]{1,0:T(8,128)(2,1)S(1)} %prompts.1.prompts_ref.prompt_ref, bf16[1536,896]{1,0:T(8,128)(2,1)} %bitcast.10.packed_ref), custom_call_target="tpu_custom_call" | custom-call | tf_op jit(solution)/shard_map/mix/pallas_call | solution.py:379
  63.0 0.1 collective-permute-start.4
  63.2 1.4 collective-permute-done.4.received_ref
  64.6 0.7 pair.1
  65.3 3.6 %collective-permute-start.5 = (bf16[2,128,384]{2,1,0:T(8,128)(2,1)S(1)}, bf16[2,128,384]{2,1,0:T(8,128)(2,1)}, u32[]{:S(2)}, u32[]{:S(2)}) collective-permute-start(bf16[2,128,384]{2,1,0:T(8,128)(2,1)S(1)} %get-tuple-element.37.text_0_ref), channel_id=1, source_target_pairs={{0,64},{1,65},{2,66},{3,67},{4,68},{5,69},{6,70},{7,71},{8,72},{9,... | collective-permute-start | bytes 589832 | tf_op jit(solution)/shard_map/ppermute | solution.py:422
  68.9 0.7 collective-permute-start.7
  69.5 0.3 collective-permute-start.6
  70.5 9.6 %all-to-all-done.1 = bf16[64,72,128]{2,1,0:T(8,128)(2,1)S(1)} async-done(((bf16[64,72,128]{2,1,0:T(8,128)(2,1)}), bf16[64,72,128]{2,1,0:T(8,128)(2,1)S(1)}, u32[]{:S(2)}, u32[]{:S(2)}) %all-to-all-start.1) | async-done | bytes 1179680 | tf_op jit(solution)/shard_map/all_to_all | solution.py:476
  80.1 3.6 %collective-permute-done.5.text_1_ref = bf16[2,128,384]{2,1,0:T(8,128)(2,1)} collective-permute-done((bf16[2,128,384]{2,1,0:T(8,128)(2,1)S(1)}, bf16[2,128,384]{2,1,0:T(8,128)(2,1)}, u32[]{:S(2)}, u32[]{:S(2)}) %collective-permute-start.5) | collective-permute-done | bytes 196640 | tf_op jit(solution)/shard_map/ppermute | solution.py:422
  83.7 0.0 collective-permute-done.7.text_3_ref
  83.7 2.3 %collective-permute-done.6.text_2_ref = bf16[2,128,384]{2,1,0:T(8,128)(2,1)} collective-permute-done((bf16[2,128,384]{2,1,0:T(8,128)(2,1)}, bf16[2,128,384]{2,1,0:T(8,128)(2,1)}, u32[]{:S(2)}, u32[]{:S(2)}) %collective-permute-start.6) | collective-permute-done | bytes 196640 | tf_op jit(solution)/shard_map/ppermute | solution.py:422
  86.0 0.0 copy-done.5
  86.0 0.0 copy-done.6
  86.0 19.5 %forward.1 = (f32[64,256]{1,0:T(8,128)}, f32[64,256]{1,0:T(8,128)S(1)}, f32[64,256]{1,0:T(8,128)S(1)}, bf16[64,256]{1,0:T(8,128)(2,1)S(1)}, bf16[256,1536]{1,0:T...) custom-call(s32[3]{0:T(128)S(1)} %copy-done.6, ...), custom_call_target="tpu_custom_call" | custom-call | tf_op jit(solution)/shard_map/forward/pallas_call | solution.py:379
  105.5 1.3 collective-permute-start.8
  106.7 6.0 %collective-permute-done.8.fake_ref = bf16[64,256]{1,0:T(8,128)(2,1)S(1)} collective-permute-done((bf16[64,256]{1,0:T(8,128)(2,1)S(1)}, bf16[64,256]{1,0:T(8,128)(2,1)S(1)}, u32[]{:S(2)}, u32[]{:S(2)}) %collective-permute-start.8) | collective-permute-done | bytes 32800 | tf_op jit(solution)/shard_map/ppermute | solution.py:539
  112.8 7.3 %backward.1 = (f32[32,24,384]{2,1,0:T(8,128)S(1)}, bf16[32,24,384]{2,1,0:T(8,128)(2,1)S(1)}) custom-call(s32[3]{0:T(128)S(1)} %copy-done.6, f32[1,1]{1,0:T(1,128)} %bitcast.3.sigma_ref, f32[64,256]{1,0:T(8,128)S(1)} %get-tuple-element.41.sample_ref, f32[64,256]{1,0:T(8,128)S(1)} %bitcast.31, f32[64,256]{1,0:T(8,128)S(1)} %get-tuple-element.42.own_ref, ...), custom_call_target="tpu_custom_call" | custom-call | tf_op jit(solution)/shard_map/backward/pallas_call | solution.py:379
  120.1 0.1 collective-permute-start.9
  120.2 2.0 %collective-permute-done.9.received_ref = bf16[32,24,384]{2,1,0:T(8,128)(2,1)S(1)} collective-permute-done((bf16[32,24,384]{2,1,0:T(8,128)(2,1)S(1)}, bf16[32,24,384]{2,1,0:T(8,128)(2,1)S(1)}, u32[]{:S(2)}, u32[]{:S(2)}) %collective-permute-start.9) | collective-permute-done | bytes 589856 | tf_op jit(solution)/shard_map/ppermute | solution.py:422
  122.1 0.1 add.9
  122.3 18.7 %all_to_all.15.shares_ref = bf16[32,24,384]{2,1,0:T(8,128)(2,1)S(1)} all-to-all(bf16[32,24,384]{2,1,0:T(8,128)(2,1)S(1)} %add.9), channel_id=1, replica_groups={{0,2,4,6,8,10,12,14,16,18,20,22,24,26,28,30,32,34,36,38,40,42,44,46,48,..., dimensions={0} | all-to-all | bytes 1179648 | tf_op jit(solution)/shard_map/all_to_all | solution.py:566
  141.0 0.8 total.1
  (4 shorter events, 0.0 us)
Async XLA Ops:
  4.6 9.8 %copy-start.3 = (bf16[1,128,1536]{2,1,0:T(8,128)(2,1)S(1)}, bf16[1,128,1536]{2,1,0:T(8,128)(2,1)}, u32[]{:S(2)}) copy-start(bf16[1,128,1536]{2,1,0:T(8,128)(2,1)} %param.14) | copy-start | bytes 1179652
  4.6 13.6 %copy-start.7 = (f32[1536]{0:T(1024)S(1)}, f32[1536]{0:T(1024)}, u32[]{:S(2)}) copy-start(f32[1536]{0:T(1024)} %param.18) | copy-start | bytes 18436
  4.7 45.2 %all-to-all-start = ((bf16[64,24,896]{2,1,0:T(8,128)(2,1)}), bf16[64,24,896]{2,1,0:T(8,128)(2,1)}, u32[]{:S(2)}, u32[]{:S(2)}) async-start(bf16[64,24,896]{2,1,0:T(8,128)(2,1)} %pack.1), calls=%async_computation | async-start | bytes 5505024 | tf_op jit(solution)/shard_map/all_to_all | solution.py:454
  14.4 13.0 %collective-permute-start.2 = (bf16[128,1536]{1,0:T(8,128)(2,1)S(1)}, bf16[128,1536]{1,0:T(8,128)(2,1)S(1)}, u32[]{:S(2)}, u32[]{:S(2)}) collective-permute-start(bf16[128,1536]{1,0:T(8,128)(2,1)S(1)} %bitcast.26), channel_id=1, source_target_pairs={{0,67},{1,66},{2,65},{3,64},{4,71},{5,70},{6,69},{7,68},{8,75},{9,... | collective-permute-start | bytes 1179656 | tf_op jit(solution)/shard_map/ppermute | solution.py:422
  17.9 18.1 %collective-permute-start.1 = (bf16[128,1536]{1,0:T(8,128)(2,1)S(1)}, bf16[128,1536]{1,0:T(8,128)(2,1)S(1)}, u32[]{:S(2)}, u32[]{:S(2)}) collective-permute-start(bf16[128,1536]{1,0:T(8,128)(2,1)S(1)} %bitcast.27), channel_id=1, source_target_pairs={{0,66},{1,67},{2,64},{3,65},{4,70},{5,71},{6,68},{7,69},{8,74},{9,... | collective-permute-start | bytes 1179656 | tf_op jit(solution)/shard_map/ppermute | solution.py:422
  18.2 17.8 %collective-permute-start = (bf16[128,1536]{1,0:T(8,128)(2,1)S(1)}, bf16[128,1536]{1,0:T(8,128)(2,1)S(1)}, u32[]{:S(2)}, u32[]{:S(2)}) collective-permute-start(bf16[128,1536]{1,0:T(8,128)(2,1)S(1)} %bitcast.28), channel_id=1, source_target_pairs={{0,1},{1,0},{2,3},{3,2},{4,5},{5,4},{6,7},{7,6},{8,9},{9,8},{10,11... | collective-permute-start | bytes 1179656 | tf_op jit(solution)/shard_map/ppermute | solution.py:422
  18.3 31.6 %copy-start.1 = (bf16[64,1536]{1,0:T(8,128)(2,1)S(1)}, bf16[64,1536]{1,0:T(8,128)(2,1)}, u32[]{:S(2)}) copy-start(bf16[64,1536]{1,0:T(8,128)(2,1)} %latent_in_ref.3) | copy-start | bytes 589828
  53.8 1.0 copy-start
  54.8 5.9 %collective-permute-start.3 = (bf16[1536,384]{1,0:T(8,128)(2,1)}, bf16[1536,384]{1,0:T(8,128)(2,1)}, u32[]{:S(2)}, u32[]{:S(2)}) collective-permute-start(bf16[1536,384]{1,0:T(8,128)(2,1)} %get-tuple-element.32.side_own_ref), channel_id=1, source_target_pairs={{0,1},{1,0},{2,3},{3,2},{4,5},{5,4},{6,7},{7,6},{8,9},{9,8},{10,11... | collective-permute-start | bytes 3538952 | tf_op jit(solution)/shard_map/ppermute | solution.py:422
  55.3 24.8 %all-to-all-start.1 = ((bf16[64,72,128]{2,1,0:T(8,128)(2,1)}), bf16[64,72,128]{2,1,0:T(8,128)(2,1)S(1)}, u32[]{:S(2)}, u32[]{:S(2)}) async-start(bf16[64,72,128]{2,1,0:T(8,128)(2,1)} %copy-done), calls=%async_computation.1 | async-start | bytes 2359296 | tf_op jit(solution)/shard_map/all_to_all | solution.py:476
  60.6 25.3 %copy-start.2 = (bf16[1536,64]{0,1:T(8,128)(2,1)S(1)}, bf16[1536,64]{0,1:T(8,128)(2,1)}, u32[]{:S(2)}) copy-start(bf16[1536,64]{0,1:T(8,128)(2,1)} %param.19) | copy-start | bytes 589828
  60.7 25.3 %copy-start.4 = (f32[1,256,64]{1,2,0:T(8,128)S(1)}, f32[1,256,64]{1,2,0:T(8,128)}, u32[]{:S(2)}) copy-start(f32[1,256,64]{1,2,0:T(8,128)} %param.13) | copy-start | bytes 196612
  60.7 25.3 %copy-start.5 = (f32[1,256,64]{1,2,0:T(8,128)S(1)}, f32[1,256,64]{1,2,0:T(8,128)}, u32[]{:S(2)}) copy-start(f32[1,256,64]{1,2,0:T(8,128)} %param.12) | copy-start | bytes 196612
  60.7 25.3 %copy-start.6 = (s32[3]{0:T(128)S(1)}, s32[3]{0:T(128)}, u32[]{:S(2)}) copy-start(s32[3]{0:T(128)} %pad_add_fusion.place_ref) | copy-start | bytes 40
  63.0 1.5 %collective-permute-start.4 = (bf16[256,384]{1,0:T(8,128)(2,1)S(1)}, bf16[256,384]{1,0:T(8,128)(2,1)S(1)}, u32[]{:S(2)}, u32[]{:S(2)}) collective-permute-start(bf16[256,384]{1,0:T(8,128)(2,1)S(1)} %get-tuple-element.36), channel_id=1, source_target_pairs={{0,1},{1,0},{2,3},{3,2},{4,5},{5,4},{6,7},{7,6},{8,9},{9,8},{10,11... | collective-permute-start | bytes 589832 | tf_op jit(solution)/shard_map/ppermute | solution.py:422
  65.3 18.4 %collective-permute-start.5 = (bf16[2,128,384]{2,1,0:T(8,128)(2,1)S(1)}, bf16[2,128,384]{2,1,0:T(8,128)(2,1)}, u32[]{:S(2)}, u32[]{:S(2)}) collective-permute-start(bf16[2,128,384]{2,1,0:T(8,128)(2,1)S(1)} %get-tuple-element.37.text_0_ref), channel_id=1, source_target_pairs={{0,64},{1,65},{2,66},{3,67},{4,68},{5,69},{6,70},{7,71},{8,72},{9,... | collective-permute-start | bytes 589832 | tf_op jit(solution)/shard_map/ppermute | solution.py:422
  68.9 14.8 %collective-permute-start.7 = (bf16[2,128,384]{2,1,0:T(8,128)(2,1)}, bf16[2,128,384]{2,1,0:T(8,128)(2,1)}, u32[]{:S(2)}, u32[]{:S(2)}) collective-permute-start(bf16[2,128,384]{2,1,0:T(8,128)(2,1)} %get-tuple-element.38), channel_id=1, source_target_pairs={{0,66},{1,67},{2,64},{3,65},{4,70},{5,71},{6,68},{7,69},{8,74},{9,... | collective-permute-start | bytes 589832 | tf_op jit(solution)/shard_map/ppermute | solution.py:422
  69.5 16.4 %collective-permute-start.6 = (bf16[2,128,384]{2,1,0:T(8,128)(2,1)}, bf16[2,128,384]{2,1,0:T(8,128)(2,1)}, u32[]{:S(2)}, u32[]{:S(2)}) collective-permute-start(bf16[2,128,384]{2,1,0:T(8,128)(2,1)} %get-tuple-element.38), channel_id=1, source_target_pairs={{0,2},{1,3},{2,0},{3,1},{4,6},{5,7},{6,4},{7,5},{8,10},{9,11},{10,... | collective-permute-start | bytes 589832 | tf_op jit(solution)/shard_map/ppermute | solution.py:422
  105.5 7.3 %collective-permute-start.8 = (bf16[64,256]{1,0:T(8,128)(2,1)S(1)}, bf16[64,256]{1,0:T(8,128)(2,1)S(1)}, u32[]{:S(2)}, u32[]{:S(2)}) collective-permute-start(bf16[64,256]{1,0:T(8,128)(2,1)S(1)} %get-tuple-element.43), channel_id=1, source_target_pairs={{64,0},{65,1},{66,2},{67,3},{68,4},{69,5},{70,6},{71,7},{72,8},{73... | collective-permute-start | bytes 98312 | tf_op jit(solution)/shard_map/ppermute | solution.py:539
  120.1 2.1 %collective-permute-start.9 = (bf16[32,24,384]{2,1,0:T(8,128)(2,1)S(1)}, bf16[32,24,384]{2,1,0:T(8,128)(2,1)S(1)}, u32[]{:S(2)}, u32[]{:S(2)}) collective-permute-start(bf16[32,24,384]{2,1,0:T(8,128)(2,1)S(1)} %get-tuple-element.54), channel_id=1, source_target_pairs={{0,1},{1,0},{2,3},{3,2},{4,5},{5,4},{6,7},{7,6},{8,9},{9,8},{10,11... | collective-permute-start | bytes 1769480 | tf_op jit(solution)/shard_map/ppermute | solution.py:422

commit v7 on v6

--- a/solution.py
+++ b/solution.py
@@ -110,25 +110,32 @@
         up_ref[block] = total[:, (3 + block) * RANK : (4 + block) * RANK]
 
 
-def fold_kernel(
+def mix_kernel(
+    prompts_ref,
     latent_in_ref,
     modulation_ref,
     packed_ref,
+    mine_ref,
+    theirs_ref,
     share_ref,
     side_ref,
     columns,
+    eighths,
     sides,
     shares,
     read_sem,
     write_sem,
 ):
-    read = pltpu.make_async_copy(packed_ref.at[:, EIGHTH + SIDE :], columns, read_sem.at[0])
-    read.start()
-    side = pltpu.make_async_copy(packed_ref.at[:, EIGHTH : EIGHTH + SIDE], sides, read_sem.at[1])
-    side.start()
+    reads = [
+        pltpu.make_async_copy(packed_ref.at[:, EIGHTH + SIDE :], columns, read_sem.at[0]),
+        pltpu.make_async_copy(packed_ref.at[:, :EIGHTH], eighths, read_sem.at[1]),
+        pltpu.make_async_copy(packed_ref.at[:, EIGHTH : EIGHTH + SIDE], sides, read_sem.at[2]),
+    ]
+    for read in reads:
+        read.start()
     scaled_in = (latent_in_ref[...].astype(F32) * modulation_ref[...]).astype(BF)
     folds = jnp.concatenate([latent_in_ref[...], scaled_in], axis=0)
-    read.wait()
+    reads[0].wait()
     share = dot(folds, columns[...]).T[:SHARE].astype(BF)
     batch = shares.shape[0]
     for device in range(batch):
@@ -139,23 +146,18 @@
     ]
     for write in writes:
         write.start()
-    side.wait()
-    side = pltpu.make_async_copy(sides, side_ref, read_sem.at[1])
+    reads[1].wait()
+    eighth = dot(prompts_ref[...], eighths[...]).astype(BF)
+    reads[2].wait()
+    side = pltpu.make_async_copy(sides, side_ref, read_sem.at[2])
     side.start()
-    for write in writes:
-        write.wait()
-    side.wait()
-
-
-def mix_kernel(prompts_ref, packed_ref, mine_ref, theirs_ref, columns, read_sem):
-    read = pltpu.make_async_copy(packed_ref.at[:, :EIGHTH], columns, read_sem.at[0])
-    read.start()
-    read.wait()
-    eighth = dot(prompts_ref[...], columns[...]).astype(BF)
     mine_ref[:TXT, :] = eighth[:TXT]
     theirs_ref[:TXT, :] = eighth[TXT : 2 * TXT]
     mine_ref[TXT:, :] = eighth[2 * TXT : 3 * TXT]
     theirs_ref[TXT:, :] = eighth[3 * TXT :]
+    for write in writes:
+        write.wait()
+    side.wait()
 
 
 def pair_kernel(mine_ref, received_ref, own_ref, near_ref):
@@ -374,7 +376,7 @@
     sums_ref[...] = (mine_ref[...] + received_ref[...].astype(F32)).astype(BF)
 
 
-def run(kernel, name, megabytes, scalars, outputs, scratch, *operands, far=(), out_space=pltpu.VMEM):
+def run(kernel, name, megabytes, scalars, outputs, scratch, *operands, far=(), far_out=()):
     shapes = tuple(jax.ShapeDtypeStruct(*output) for output in outputs)
     return pl.pallas_call(
         kernel,
@@ -385,7 +387,10 @@
             )
             for k in range(len(operands))
         ],
-        out_specs=tuple([pl.BlockSpec(memory_space=out_space)] * len(outputs)),
+        out_specs=tuple(
+            pl.BlockSpec(memory_space=pl.ANY if k in far_out else pltpu.VMEM)
+            for k in range(len(outputs))
+        ),
         scratch_shapes=scratch,
         compiler_params=pltpu.CompilerParams(vmem_limit_bytes=megabytes * 2**20),
         name=name,
@@ -449,54 +454,49 @@
         gen_up.transpose(0, 2, 1),
         critic_up.transpose(0, 2, 1),
         far=(1, 2, 3, 4, 5),
-        out_space=pl.ANY,
+        far_out=(0,),
     )
     packed = lax.all_to_all(packed, "fsdp", 0, 0).reshape(HW, EIGHTH + SIDE + PART)
     (prompts,) = run(prompt_kernel, "prompts", 16, 0, [((4 * TXT, HW), BF)], [], *texts)
     packed, prompts = lax.optimization_barrier((packed, prompts))
-    share, side_own = run(
-        fold_kernel,
-        "fold",
-        16,
+    mine, theirs, share, side_own = run(
+        mix_kernel,
+        "mix",
+        52,
         0,
-        [((devices, SHARE, PART), BF), ((HW, SIDE), BF)],
+        [
+            ((2 * TXT, EIGHTH), BF),
+            ((2 * TXT, EIGHTH), BF),
+            ((devices, SHARE, PART), BF),
+            ((HW, SIDE), BF),
+        ],
         [
             pltpu.VMEM((HW, PART), BF),
+            pltpu.VMEM((HW, EIGHTH), BF),
             pltpu.VMEM((HW, SIDE), BF),
             pltpu.VMEM((devices // 8, SHARE, PART), BF),
-            pltpu.SemaphoreType.DMA((2,)),
+            pltpu.SemaphoreType.DMA((3,)),
             pltpu.SemaphoreType.DMA((8,)),
         ],
+        prompts,
         latent_in,
         gain,
         packed,
-        far=(2,),
-        out_space=pl.ANY,
-    )
+        far=(3,),
+        far_out=(2, 3),
+    )
+    received = move(theirs, 0, 1)
     fold = lax.all_to_all(share, "fsdp", 0, 0).reshape(devices * SHARE, PART)
     side_core = move(side_own, 0, 1)
-    prompts, side_core = lax.optimization_barrier((prompts, side_core))
-    mine, theirs = run(
-        mix_kernel,
-        "mix",
-        16,
-        0,
-        [((2 * TXT, EIGHTH), BF)] * 2,
-        [pltpu.VMEM((HW, EIGHTH), BF), pltpu.SemaphoreType.DMA((1,))],
-        prompts,
-        packed,
-        far=(1,),
-    )
-    received = move(theirs, 0, 1)
     own_pair, near_pair = run(
-        pair_kernel, "pair", 16, 0, [((2, TXT, EIGHTH), BF)] * 2, [], mine, received
+        pair_kernel, "pair", 52, 0, [((2, TXT, EIGHTH), BF)] * 2, [], mine, received
     )
     pieces = [own_pair, move(own_pair, 1, 0), move(near_pair, 0, 2), move(near_pair, 1, 2)]
 
     sample, sample_again, velocity, narrow_velocity, *saved, role_up = run(
         forward_kernel,
         "forward",
-        32,
+        46,
         2,
         [
             ((CH, IMG), F32),
@@ -541,7 +541,7 @@
     mine, theirs = run(
         backward_kernel,
         "backward",
-        24,
+        46,
         2,
         [(half, F32), (half, BF)],
         [

time: 142 us -> 147 us (1.035)
  Pallas kernels: 38.6 us -> 40.5 us
    ppermute x9, waiting for transfers between devices: 26.9 us -> 38.6 us  [move(): return lax.ppermute(array, ('group', 'fsdp'), pairs)]
    all_to_all x1, waiting for transfers between devices: 9.63 us -> 0.01 us  [per_device(): fold = lax.all_to_all(share, 'fsdp', 0, 0).reshape(devices * SHARE, PART)]
    pallas_call x9 -> x8, Pallas kernels: 38.6 us -> 40.5 us  [run(): pl.pallas_call(kernel, out_shape=shapes, in_specs=[pl.BlockSpec(memory_sp...]
  transfers between devices with their start and end apart: 12 -> 12, of which waited for: 9 -> 8; matrix products, arithmetic and copies ran while one was open for 0% -> 0% of each run, Pallas kernels for 3% -> 0%
where the time goes in v7:
time: 147 us
  waiting for transfers between devices  56.7 us (39%)
  Pallas kernels  40.5 us (28%)
  starting transfers between devices  25.7 us (17%)
  blocking collectives  19.6 us (13%)
  local copies, waits for them, and re-layouts  2.31 us (2%)
    pallas_call x8, Pallas kernels, run(): pl.pallas_call(kernel, out_shape=shapes, in_specs=[pl.BlockSpec(memory_sp...  40.5 us
    ppermute x9, waiting for transfers between devices, move(): return lax.ppermute(array, ('group', 'fsdp'), pairs)  38.6 us
    all_to_all x1, blocking collectives, per_device(): shares = lax.all_to_all(sums, 'fsdp', 0, 0, axis_index_groups=parities)  19.6 us
    all_to_all x1, waiting for transfers between devices, per_device(): lax.all_to_all(packed, 'fsdp', 0, 0).reshape(HW, EIGHTH + SIDE + PART)  12.1 us
    all_to_all x1, starting transfers between devices, per_device(): lax.all_to_all(packed, 'fsdp', 0, 0).reshape(HW, EIGHTH + SIDE + PART)  9.75 us
    ppermute x9, starting transfers between devices, move(): return lax.ppermute(array, ('group', 'fsdp'), pairs)  9.2 us
    ppermute x1, waiting for transfers between devices, per_device(): fake_velocity = lax.ppermute(narrow_velocity, 'group', [(1, 0)])  6.01 us
    all_to_all x1, starting transfers between devices, per_device(): fold = lax.all_to_all(share, 'fsdp', 0, 0).reshape(devices * SHARE, PART)  5.51 us
  transfers between devices with their start and end apart: 12, of which 8 were waited for; matrix products, arithmetic and copies ran while one was open for 0% of the time, Pallas kernels for 0%

profile of v7, /device:TPU:0, one launch (start us, length us, event | category | flops | bytes accessed | tf_op | source)
XLA Modules:
  0.0 146.9 jit_solution(4878048648704128138)
XLA Ops:
  0.6 0.6 pad_add_fusion.place_ref
  1.3 3.4 %pack.1 = bf16[64,24,896]{2,1,0:T(8,128)(2,1)} custom-call(s32[3]{0:T(128)} %pad_add_fusion.place_ref, bf16[24,4608]{1,0:T(8,128)(2,1)} %base_ref.1, bf16[24,192]{1,0:T(8,128)(2,1)} %gen_down_ref.1, bf16[24,192]{1,0:T(8,128)(2,1)} %critic_down_ref.1, bf16[3,24,64]{2,1,0:T(8,128)(2,1)} %bitcast.33, bf16[3,24,64]{2,1,0:T(8,128)(2,1)} %bitcast.34), custom_call_target="tpu_custom_call" | custom-call | tf_op jit(solution)/shard_map/pack/pallas_call | solution.py:381
  4.7 0.0 copy-start.3
  4.7 0.0 copy-start.8
  4.7 9.8 %all-to-all-start = ((bf16[64,24,896]{2,1,0:T(8,128)(2,1)}), bf16[64,24,896]{2,1,0:T(8,128)(2,1)}, u32[]{:S(2)}, u32[]{:S(2)}) async-start(bf16[64,24,896]{2,1,0:T(8,128)(2,1)} %pack.1), calls=%async_computation | async-start | bytes 5505024 | tf_op jit(solution)/shard_map/all_to_all | solution.py:459
  14.5 0.0 copy-done.3
  14.5 3.5 %collective-permute-start.2 = (bf16[128,1536]{1,0:T(8,128)(2,1)S(1)}, bf16[128,1536]{1,0:T(8,128)(2,1)S(1)}, u32[]{:S(2)}, u32[]{:S(2)}) collective-permute-start(bf16[128,1536]{1,0:T(8,128)(2,1)S(1)} %bitcast.25), channel_id=1, source_target_pairs={{0,67},{1,66},{2,65},{3,64},{4,71},{5,70},{6,69},{7,68},{8,75},{9,... | collective-permute-start | bytes 1179656 | tf_op jit(solution)/shard_map/ppermute | solution.py:427
  17.9 0.3 collective-permute-start.1
  18.3 0.0 collective-permute-start
  18.3 0.0 copy-done.8
  18.3 0.0 copy-start.1
  18.3 9.1 %collective-permute-done.2.text_3_ref = bf16[128,1536]{1,0:T(8,128)(2,1)S(1)} collective-permute-done((bf16[128,1536]{1,0:T(8,128)(2,1)S(1)}, bf16[128,1536]{1,0:T(8,128)(2,1)S(1)}, u32[]{:S(2)}, u32[]{:S(2)}) %collective-permute-start.2) | collective-permute-done | bytes 393248 | tf_op jit(solution)/shard_map/ppermute | solution.py:427
  27.4 8.6 %collective-permute-done.1.text_2_ref = bf16[128,1536]{1,0:T(8,128)(2,1)S(1)} collective-permute-done((bf16[128,1536]{1,0:T(8,128)(2,1)S(1)}, bf16[128,1536]{1,0:T(8,128)(2,1)S(1)}, u32[]{:S(2)}, u32[]{:S(2)}) %collective-permute-start.1) | collective-permute-done | bytes 393248 | tf_op jit(solution)/shard_map/ppermute | solution.py:427
  36.0 0.0 collective-permute-done.text_1_ref
  36.0 0.5 prompts.1.prompts_ref.prompt_ref
  36.5 0.0 copy-start
  36.6 1.2 copy-done
  37.7 12.1 %all-to-all-done = bf16[64,24,896]{2,1,0:T(8,128)(2,1)} async-done(((bf16[64,24,896]{2,1,0:T(8,128)(2,1)}), bf16[64,24,896]{2,1,0:T(8,128)(2,1)}, u32[]{:S(2)}, u32[]{:S(2)}) %all-to-all-start) | async-done | bytes 2752544 | tf_op jit(solution)/shard_map/all_to_all | solution.py:459
  49.9 0.0 copy-done.1
  49.9 4.9 %mix.1 = (bf16[256,384]{1,0:T(8,128)(2,1)S(1)}, bf16[256,384]{1,0:T(8,128)(2,1)S(1)}, bf16[64,72,128]{2,1,0:T(8,128)(2,1)}, bf16[1536,384]{1,0:T(8,128)(2,1)}) custom-call(bf16[512,1536]{1,0:T(8,128)(2,1)} %copy-done, bf16[64,1536]{1,0:T(8,128)(2,1)S(1)} %copy-done.1, f32[1,1536]{1,0:T(1,128)S(1)} %reshape.20.modulation_ref, ...), custom_call_target="tpu_custom_call" | custom-call | tf_op jit(solution)/shard_map/mix/pallas_call | solution.py:381
  54.8 0.5 collective-permute-start.7
  55.3 0.0 copy-start.2
  55.3 0.0 copy-start.4
  55.3 5.5 %all-to-all-start.1 = ((bf16[64,72,128]{2,1,0:T(8,128)(2,1)}), bf16[64,72,128]{2,1,0:T(8,128)(2,1)S(1)}, u32[]{:S(2)}, u32[]{:S(2)}) async-start(bf16[64,72,128]{2,1,0:T(8,128)(2,1)} %get-tuple-element.30), calls=%async_computation.1 | async-start | bytes 2359296 | tf_op jit(solution)/shard_map/all_to_all | solution.py:489
  60.9 0.1 collective-permute-start.3
  61.0 1.4 collective-permute-done.3.received_ref
  62.4 3.7 %collective-permute-start.4 = (bf16[2,128,384]{2,1,0:T(8,128)(2,1)S(1)}, bf16[2,128,384]{2,1,0:T(8,128)(2,1)S(1)}, u32[]{:S(2)}, u32[]{:S(2)}) collective-permute-start(bf16[2,128,384]{2,1,0:T(8,128)(2,1)S(1)} %get-tuple-element.33.text_0_ref), channel_id=1, source_target_pairs={{0,64},{1,65},{2,66},{3,67},{4,68},{5,69},{6,70},{7,71},{8,72},{9,... | collective-permute-start | bytes 589832 | tf_op jit(solution)/shard_map/ppermute | solution.py:427
  66.1 0.7 collective-permute-start.6
  66.7 0.3 collective-permute-start.5
  67.7 15.8 %collective-permute-done.4.text_1_ref = bf16[2,128,384]{2,1,0:T(8,128)(2,1)S(1)} collective-permute-done((bf16[2,128,384]{2,1,0:T(8,128)(2,1)S(1)}, bf16[2,128,384]{2,1,0:T(8,128)(2,1)S(1)}, u32[]{:S(2)}, u32[]{:S(2)}) %collective-permute-start.4) | collective-permute-done | bytes 196640 | tf_op jit(solution)/shard_map/ppermute | solution.py:427
  83.5 0.0 collective-permute-done.6.text_3_ref
  83.5 1.7 %collective-permute-done.5.text_2_ref = bf16[2,128,384]{2,1,0:T(8,128)(2,1)S(1)} collective-permute-done((bf16[2,128,384]{2,1,0:T(8,128)(2,1)S(1)}, bf16[2,128,384]{2,1,0:T(8,128)(2,1)S(1)}, u32[]{:S(2)}, u32[]{:S(2)}) %collective-permute-start.5) | collective-permute-done | bytes 196640 | tf_op jit(solution)/shard_map/ppermute | solution.py:427
  85.2 0.0 all-to-all-done.1
  85.2 0.0 collective-permute-done.7.side_core_ref
  85.2 1.1 copy-done.7
  86.3 0.0 copy-done.2
  86.3 0.0 copy-done.4
  86.3 0.0 copy-done.5
  86.3 0.0 copy-done.6
  86.3 21.4 %forward.1 = (f32[64,256]{1,0:T(8,128)}, f32[64,256]{1,0:T(8,128)S(1)}, f32[64,256]{1,0:T(8,128)S(1)}, bf16[64,256]{1,0:T(8,128)(2,1)S(1)}, bf16[256,1536]{1,0:T...) custom-call(s32[3]{0:T(128)S(1)} %copy-done.6, ...), custom_call_target="tpu_custom_call" | custom-call | tf_op jit(solution)/shard_map/forward/pallas_call | solution.py:381
  107.7 1.3 collective-permute-start.8
  109.0 6.0 %collective-permute-done.8.fake_ref = bf16[64,256]{1,0:T(8,128)(2,1)S(1)} collective-permute-done((bf16[64,256]{1,0:T(8,128)(2,1)S(1)}, bf16[64,256]{1,0:T(8,128)(2,1)S(1)}, u32[]{:S(2)}, u32[]{:S(2)}) %collective-permute-start.8) | collective-permute-done | bytes 32800 | tf_op jit(solution)/shard_map/ppermute | solution.py:539
  115.0 9.3 %backward.1 = (f32[32,24,384]{2,1,0:T(8,128)S(1)}, bf16[32,24,384]{2,1,0:T(8,128)(2,1)S(1)}) custom-call(s32[3]{0:T(128)S(1)} %copy-done.6, f32[1,1]{1,0:T(1,128)} %bitcast.3.sigma_ref, f32[64,256]{1,0:T(8,128)S(1)} %get-tuple-element.37.sample_ref, f32[64,256]{1,0:T(8,128)S(1)} %bitcast.30, f32[64,256]{1,0:T(8,128)S(1)} %get-tuple-element.38.own_ref, ...), custom_call_target="tpu_custom_call" | custom-call | tf_op jit(solution)/shard_map/backward/pallas_call | solution.py:381
  124.4 0.1 collective-permute-start.9
  124.5 2.0 %collective-permute-done.9.received_ref = bf16[32,24,384]{2,1,0:T(8,128)(2,1)S(1)} collective-permute-done((bf16[32,24,384]{2,1,0:T(8,128)(2,1)S(1)}, bf16[32,24,384]{2,1,0:T(8,128)(2,1)S(1)}, u32[]{:S(2)}, u32[]{:S(2)}) %collective-permute-start.9) | collective-permute-done | bytes 589856 | tf_op jit(solution)/shard_map/ppermute | solution.py:427
  126.5 0.1 add.9
  126.6 19.6 %all_to_all.15.shares_ref = bf16[32,24,384]{2,1,0:T(8,128)(2,1)S(1)} all-to-all(bf16[32,24,384]{2,1,0:T(8,128)(2,1)S(1)} %add.9), channel_id=1, replica_groups={{0,2,4,6,8,10,12,14,16,18,20,22,24,26,28,30,32,34,36,38,40,42,44,46,48,..., dimensions={0} | all-to-all | bytes 1179648 | tf_op jit(solution)/shard_map/all_to_all | solution.py:566
  146.1 0.8 total.1
  (5 shorter events, 0.0 us)
Async XLA Ops:
  4.7 9.8 %copy-start.3 = (bf16[1,128,1536]{2,1,0:T(8,128)(2,1)S(1)}, bf16[1,128,1536]{2,1,0:T(8,128)(2,1)}, u32[]{:S(2)}) copy-start(bf16[1,128,1536]{2,1,0:T(8,128)(2,1)} %param.14) | copy-start | bytes 1179652
  4.7 13.6 %copy-start.8 = (f32[1536]{0:T(1024)S(1)}, f32[1536]{0:T(1024)}, u32[]{:S(2)}) copy-start(f32[1536]{0:T(1024)} %param.18) | copy-start | bytes 18436
  4.7 45.2 %all-to-all-start = ((bf16[64,24,896]{2,1,0:T(8,128)(2,1)}), bf16[64,24,896]{2,1,0:T(8,128)(2,1)}, u32[]{:S(2)}, u32[]{:S(2)}) async-start(bf16[64,24,896]{2,1,0:T(8,128)(2,1)} %pack.1), calls=%async_computation | async-start | bytes 5505024 | tf_op jit(solution)/shard_map/all_to_all | solution.py:459
  14.5 13.0 %collective-permute-start.2 = (bf16[128,1536]{1,0:T(8,128)(2,1)S(1)}, bf16[128,1536]{1,0:T(8,128)(2,1)S(1)}, u32[]{:S(2)}, u32[]{:S(2)}) collective-permute-start(bf16[128,1536]{1,0:T(8,128)(2,1)S(1)} %bitcast.25), channel_id=1, source_target_pairs={{0,67},{1,66},{2,65},{3,64},{4,71},{5,70},{6,69},{7,68},{8,75},{9,... | collective-permute-start | bytes 1179656 | tf_op jit(solution)/shard_map/ppermute | solution.py:427
  17.9 18.1 %collective-permute-start.1 = (bf16[128,1536]{1,0:T(8,128)(2,1)S(1)}, bf16[128,1536]{1,0:T(8,128)(2,1)S(1)}, u32[]{:S(2)}, u32[]{:S(2)}) collective-permute-start(bf16[128,1536]{1,0:T(8,128)(2,1)S(1)} %bitcast.26), channel_id=1, source_target_pairs={{0,66},{1,67},{2,64},{3,65},{4,70},{5,71},{6,68},{7,69},{8,74},{9,... | collective-permute-start | bytes 1179656 | tf_op jit(solution)/shard_map/ppermute | solution.py:427
  18.3 17.8 %collective-permute-start = (bf16[128,1536]{1,0:T(8,128)(2,1)S(1)}, bf16[128,1536]{1,0:T(8,128)(2,1)S(1)}, u32[]{:S(2)}, u32[]{:S(2)}) collective-permute-start(bf16[128,1536]{1,0:T(8,128)(2,1)S(1)} %bitcast.27), channel_id=1, source_target_pairs={{0,1},{1,0},{2,3},{3,2},{4,5},{5,4},{6,7},{7,6},{8,9},{9,8},{10,11... | collective-permute-start | bytes 1179656 | tf_op jit(solution)/shard_map/ppermute | solution.py:427
  18.3 31.6 %copy-start.1 = (bf16[64,1536]{1,0:T(8,128)(2,1)S(1)}, bf16[64,1536]{1,0:T(8,128)(2,1)}, u32[]{:S(2)}) copy-start(bf16[64,1536]{1,0:T(8,128)(2,1)} %latent_in_ref.3) | copy-start | bytes 589828
  36.5 1.2 copy-start
  54.8 30.4 %collective-permute-start.7 = (bf16[1536,384]{1,0:T(8,128)(2,1)}, bf16[1536,384]{1,0:T(8,128)(2,1)}, u32[]{:S(2)}, u32[]{:S(2)}) collective-permute-start(bf16[1536,384]{1,0:T(8,128)(2,1)} %get-tuple-element.35.side_own_ref), channel_id=1, source_target_pairs={{0,1},{1,0},{2,3},{3,2},{4,5},{5,4},{6,7},{7,6},{8,9},{9,8},{10,11... | collective-permute-start | bytes 3538952 | tf_op jit(solution)/shard_map/ppermute | solution.py:427
  55.3 31.0 %copy-start.2 = (bf16[1536,64]{0,1:T(8,128)(2,1)S(1)}, bf16[1536,64]{0,1:T(8,128)(2,1)}, u32[]{:S(2)}) copy-start(bf16[1536,64]{0,1:T(8,128)(2,1)} %param.19) | copy-start | bytes 589828
  55.3 31.0 %copy-start.4 = (f32[1,256,64]{1,2,0:T(8,128)S(1)}, f32[1,256,64]{1,2,0:T(8,128)}, u32[]{:S(2)}) copy-start(f32[1,256,64]{1,2,0:T(8,128)} %param.13) | copy-start | bytes 196612
  55.3 31.0 %copy-start.5 = (f32[1,256,64]{1,2,0:T(8,128)S(1)}, f32[1,256,64]{1,2,0:T(8,128)}, u32[]{:S(2)}) copy-start(f32[1,256,64]{1,2,0:T(8,128)} %param.12) | copy-start | bytes 196612
  55.3 31.0 %copy-start.6 = (s32[3]{0:T(128)S(1)}, s32[3]{0:T(128)}, u32[]{:S(2)}) copy-start(s32[3]{0:T(128)} %pad_add_fusion.place_ref) | copy-start | bytes 40
  55.3 29.9 %all-to-all-start.1 = ((bf16[64,72,128]{2,1,0:T(8,128)(2,1)}), bf16[64,72,128]{2,1,0:T(8,128)(2,1)S(1)}, u32[]{:S(2)}, u32[]{:S(2)}) async-start(bf16[64,72,128]{2,1,0:T(8,128)(2,1)} %get-tuple-element.30), calls=%async_computation.1 | async-start | bytes 2359296 | tf_op jit(solution)/shard_map/all_to_all | solution.py:489
  60.9 1.5 %collective-permute-start.3 = (bf16[256,384]{1,0:T(8,128)(2,1)S(1)}, bf16[256,384]{1,0:T(8,128)(2,1)S(1)}, u32[]{:S(2)}, u32[]{:S(2)}) collective-permute-start(bf16[256,384]{1,0:T(8,128)(2,1)S(1)} %get-tuple-element.32), channel_id=1, source_target_pairs={{0,1},{1,0},{2,3},{3,2},{4,5},{5,4},{6,7},{7,6},{8,9},{9,8},{10,11... | collective-permute-start | bytes 589832 | tf_op jit(solution)/shard_map/ppermute | solution.py:427
  62.4 21.1 %collective-permute-start.4 = (bf16[2,128,384]{2,1,0:T(8,128)(2,1)S(1)}, bf16[2,128,384]{2,1,0:T(8,128)(2,1)S(1)}, u32[]{:S(2)}, u32[]{:S(2)}) collective-permute-start(bf16[2,128,384]{2,1,0:T(8,128)(2,1)S(1)} %get-tuple-element.33.text_0_ref), channel_id=1, source_target_pairs={{0,64},{1,65},{2,66},{3,67},{4,68},{5,69},{6,70},{7,71},{8,72},{9,... | collective-permute-start | bytes 589832 | tf_op jit(solution)/shard_map/ppermute | solution.py:427
  66.1 17.4 %collective-permute-start.6 = (bf16[2,128,384]{2,1,0:T(8,128)(2,1)S(1)}, bf16[2,128,384]{2,1,0:T(8,128)(2,1)S(1)}, u32[]{:S(2)}, u32[]{:S(2)}) collective-permute-start(bf16[2,128,384]{2,1,0:T(8,128)(2,1)S(1)} %get-tuple-element.34), channel_id=1, source_target_pairs={{0,66},{1,67},{2,64},{3,65},{4,70},{5,71},{6,68},{7,69},{8,74},{9,... | collective-permute-start | bytes 589832 | tf_op jit(solution)/shard_map/ppermute | solution.py:427
  66.7 18.5 %collective-permute-start.5 = (bf16[2,128,384]{2,1,0:T(8,128)(2,1)S(1)}, bf16[2,128,384]{2,1,0:T(8,128)(2,1)S(1)}, u32[]{:S(2)}, u32[]{:S(2)}) collective-permute-start(bf16[2,128,384]{2,1,0:T(8,128)(2,1)S(1)} %get-tuple-element.34), channel_id=1, source_target_pairs={{0,2},{1,3},{2,0},{3,1},{4,6},{5,7},{6,4},{7,5},{8,10},{9,11},{10,... | collective-permute-start | bytes 589832 | tf_op jit(solution)/shard_map/ppermute | solution.py:427
  85.2 1.1 copy-start.7
  107.7 7.3 %collective-permute-start.8 = (bf16[64,256]{1,0:T(8,128)(2,1)S(1)}, bf16[64,256]{1,0:T(8,128)(2,1)S(1)}, u32[]{:S(2)}, u32[]{:S(2)}) collective-permute-start(bf16[64,256]{1,0:T(8,128)(2,1)S(1)} %get-tuple-element.39), channel_id=1, source_target_pairs={{64,0},{65,1},{66,2},{67,3},{68,4},{69,5},{70,6},{71,7},{72,8},{73... | collective-permute-start | bytes 98312 | tf_op jit(solution)/shard_map/ppermute | solution.py:539
  124.4 2.1 %collective-permute-start.9 = (bf16[32,24,384]{2,1,0:T(8,128)(2,1)S(1)}, bf16[32,24,384]{2,1,0:T(8,128)(2,1)S(1)}, u32[]{:S(2)}, u32[]{:S(2)}) collective-permute-start(bf16[32,24,384]{2,1,0:T(8,128)(2,1)S(1)} %get-tuple-element.50), channel_id=1, source_target_pairs={{0,1},{1,0},{2,3},{3,2},{4,5},{5,4},{6,7},{7,6},{8,9},{9,8},{10,11... | collective-permute-start | bytes 1769480 | tf_op jit(solution)/shard_map/ppermute | solution.py:427

commit v8 on v6

--- a/solution.py
+++ b/solution.py
@@ -98,9 +98,10 @@
         write.wait()
 
 
-def prompt_kernel(text_0_ref, text_1_ref, text_2_ref, text_3_ref, prompts_ref):
+def prompt_kernel(text_0_ref, text_1_ref, text_2_ref, text_3_ref, prompts_ref, prompt_ref):
     for index, text_ref in enumerate((text_0_ref, text_1_ref, text_2_ref, text_3_ref)):
         prompts_ref[index * TXT : (index + 1) * TXT, :] = unit_rows(text_ref[...])
+    prompt_ref[...] = prompts_ref[:TXT, :]
 
 
 def sum_kernel(shares_ref, down_ref, up_ref):
@@ -111,21 +112,10 @@
 
 
 def fold_kernel(
-    latent_in_ref,
-    modulation_ref,
-    packed_ref,
-    share_ref,
-    side_ref,
-    columns,
-    sides,
-    shares,
-    read_sem,
-    write_sem,
+    latent_in_ref, modulation_ref, packed_ref, share_ref, columns, shares, read_sem, write_sem
 ):
     read = pltpu.make_async_copy(packed_ref.at[:, EIGHTH + SIDE :], columns, read_sem.at[0])
     read.start()
-    side = pltpu.make_async_copy(packed_ref.at[:, EIGHTH : EIGHTH + SIDE], sides, read_sem.at[1])
-    side.start()
     scaled_in = (latent_in_ref[...].astype(F32) * modulation_ref[...]).astype(BF)
     folds = jnp.concatenate([latent_in_ref[...], scaled_in], axis=0)
     read.wait()
@@ -139,12 +129,8 @@
     ]
     for write in writes:
         write.start()
-    side.wait()
-    side = pltpu.make_async_copy(sides, side_ref, read_sem.at[1])
-    side.start()
     for write in writes:
         write.wait()
-    side.wait()
 
 
 def mix_kernel(prompts_ref, packed_ref, mine_ref, theirs_ref, columns, read_sem):
@@ -178,8 +164,8 @@
     text_1_ref,
     text_2_ref,
     text_3_ref,
-    side_own_ref,
-    side_core_ref,
+    packed_own_ref,
+    packed_core_ref,
     sample_ref,
     sample_again_ref,
     velocity_ref,
@@ -199,27 +185,23 @@
     v_now,
     attended_now,
     text,
-    downs,
-    ups,
+    sides,
+    sem,
 ):
     group, near, core = place_ref[0], place_ref[1], place_ref[2]
     sigma = sigma_ref[0, 0]
+    lanes = slice(EIGHTH, EIGHTH + SIDE)
+    reads = [
+        pltpu.make_async_copy(packed_own_ref.at[:, lanes], sides.at[core], sem.at[0]),
+        pltpu.make_async_copy(packed_core_ref.at[:, lanes], sides.at[1 - core], sem.at[1]),
+    ]
+    for read in reads:
+        read.start()
+    downs, ups = sides.at[0], sides.at[1]
     for (across, move), text_ref in zip(MOVES, (text_0_ref, text_1_ref, text_2_ref, text_3_ref)):
         for place in range(2):
             start = (group ^ across) * HW + (near ^ move ^ place) * EIGHTH
             text[:, pl.ds(pl.multiple_of(start, EIGHTH), EIGHTH)] = text_ref[place]
-
-    @pl.when(core == 0)
-    def _():
-        downs[...] = side_own_ref[...]
-        ups[...] = side_core_ref[...]
-
-    @pl.when(core == 1)
-    def _():
-        downs[...] = side_core_ref[...]
-        ups[...] = side_own_ref[...]
-
-    role_up_ref[...] = ups[:, 3 * RANK :]
 
     def readout(latent, noise_level, role, switch, save):
         base = role * 3 * RANK
@@ -227,6 +209,10 @@
         hidden = dot(narrow, latent_in_ref[...])
         inverse_rms = lax.rsqrt(jnp.mean(hidden * hidden, axis=-1, keepdims=True) + 1e-06)
         picture = (hidden * inverse_rms * (1.0 + noise_level * modulation_ref[...])).astype(BF)
+        if role == 0:
+            for read in reads:
+                read.wait()
+            role_up_ref[...] = ups[:, 3 * RANK :]
         reduced_picture = dot(picture, downs[:, base : base + 3 * RANK]).astype(BF)
         reduced_prompt = dot(prompt_ref[:TXT, :], downs[:, base : base + 3 * RANK]).astype(BF)
 
@@ -374,7 +360,7 @@
     sums_ref[...] = (mine_ref[...] + received_ref[...].astype(F32)).astype(BF)
 
 
-def run(kernel, name, megabytes, scalars, outputs, scratch, *operands, far=(), out_space=pltpu.VMEM):
+def run(kernel, name, megabytes, scalars, outputs, scratch, *operands, far=(), far_out=()):
     shapes = tuple(jax.ShapeDtypeStruct(*output) for output in outputs)
     return pl.pallas_call(
         kernel,
@@ -385,7 +371,10 @@
             )
             for k in range(len(operands))
         ],
-        out_specs=tuple([pl.BlockSpec(memory_space=out_space)] * len(outputs)),
+        out_specs=tuple(
+            pl.BlockSpec(memory_space=pl.ANY if k in far_out else pltpu.VMEM)
+            for k in range(len(outputs))
+        ),
         scratch_shapes=scratch,
         compiler_params=pltpu.CompilerParams(vmem_limit_bytes=megabytes * 2**20),
         name=name,
@@ -449,33 +438,34 @@
         gen_up.transpose(0, 2, 1),
         critic_up.transpose(0, 2, 1),
         far=(1, 2, 3, 4, 5),
-        out_space=pl.ANY,
+        far_out=(0,),
     )
     packed = lax.all_to_all(packed, "fsdp", 0, 0).reshape(HW, EIGHTH + SIDE + PART)
-    (prompts,) = run(prompt_kernel, "prompts", 16, 0, [((4 * TXT, HW), BF)], [], *texts)
+    prompts, prompt = run(
+        prompt_kernel, "prompts", 16, 0, [((4 * TXT, HW), BF), ((TXT, HW), BF)], [], *texts
+    )
     packed, prompts = lax.optimization_barrier((packed, prompts))
-    share, side_own = run(
+    (share,) = run(
         fold_kernel,
         "fold",
         16,
         0,
-        [((devices, SHARE, PART), BF), ((HW, SIDE), BF)],
+        [((devices, SHARE, PART), BF)],
         [
             pltpu.VMEM((HW, PART), BF),
-            pltpu.VMEM((HW, SIDE), BF),
             pltpu.VMEM((devices // 8, SHARE, PART), BF),
-            pltpu.SemaphoreType.DMA((2,)),
+            pltpu.SemaphoreType.DMA((1,)),
             pltpu.SemaphoreType.DMA((8,)),
         ],
         latent_in,
         gain,
         packed,
         far=(2,),
-        out_space=pl.ANY,
+        far_out=(0,),
     )
     fold = lax.all_to_all(share, "fsdp", 0, 0).reshape(devices * SHARE, PART)
-    side_core = move(side_own, 0, 1)
-    prompts, side_core = lax.optimization_barrier((prompts, side_core))
+    packed_core = move(packed, 0, 1)
+    prompts, packed_core = lax.optimization_barrier((prompts, packed_core))
     mine, theirs = run(
         mix_kernel,
         "mix",
@@ -520,21 +510,22 @@
             pltpu.VMEM((ROWS, HW), BF),
             pltpu.VMEM((IMG, HW), BF),
             pltpu.VMEM((TXT, 2 * HW), BF),
-            pltpu.VMEM((HW, SIDE), BF),
-            pltpu.VMEM((HW, SIDE), BF),
+            pltpu.VMEM((2, HW, SIDE), BF),
+            pltpu.SemaphoreType.DMA((2,)),
         ],
         place,
         sigma,
         latent,
         fresh,
-        prompts,
+        prompt,
         latent_in,
         gain,
         out_map,
         fold,
         *pieces,
-        side_own,
-        side_core,
+        packed,
+        packed_core,
+        far=(13, 14),
     )
     fake_velocity = lax.ppermute(narrow_velocity, "group", [(1, 0)])
     half = (devices // 2, shard, SIDE)
@@ -556,7 +547,7 @@
         fresh,
         velocity,
         fake_velocity,
-        prompts,
+        prompt,
         out_map,
         role_up,
         *saved,

time: 142 us -> 143 us (level)
  local copies, waits for them, and re-layouts: 1.08 us -> 6.3 us
  Pallas kernels: 38.6 us -> 35.9 us
  waiting for transfers between devices: 55.9 us -> 53.6 us
    unnamed x16 -> x22, local copies, waits for them, and re-layouts: 1.08 us -> 6.29 us
    pallas_call x9, Pallas kernels: 38.6 us -> 35.9 us  [run(): pl.pallas_call(kernel, out_shape=shapes, in_specs=[pl.BlockSpec(memory_sp...]
    all_to_all x1, waiting for transfers between devices: 13.3 us -> 11.2 us  [per_device(): lax.all_to_all(packed, 'fsdp', 0, 0).reshape(HW, EIGHTH + SIDE + PART)]
where the time goes in v8:
time: 143 us; the launch traced here: 142 us
  waiting for transfers between devices  53.6 us (37%)
  Pallas kernels  35.9 us (25%)
  starting transfers between devices  25.4 us (18%)
  blocking collectives  18.6 us (13%)
  local copies, waits for them, and re-layouts  6.3 us (4%)
  between operations  1.47 us (1%)
    pallas_call x9, Pallas kernels, run(): pl.pallas_call(kernel, out_shape=shapes, in_specs=[pl.BlockSpec(memory_sp...  35.9 us
    ppermute x9, waiting for transfers between devices, move(): return lax.ppermute(array, ('group', 'fsdp'), pairs)  27 us
    all_to_all x1, blocking collectives, per_device(): shares = lax.all_to_all(sums, 'fsdp', 0, 0, axis_index_groups=parities)  18.6 us
    all_to_all x1, waiting for transfers between devices, per_device(): lax.all_to_all(packed, 'fsdp', 0, 0).reshape(HW, EIGHTH + SIDE + PART)  11.2 us
    all_to_all x1, starting transfers between devices, per_device(): lax.all_to_all(packed, 'fsdp', 0, 0).reshape(HW, EIGHTH + SIDE + PART)  9.52 us
    all_to_all x1, waiting for transfers between devices, per_device(): fold = lax.all_to_all(share, 'fsdp', 0, 0).reshape(devices * SHARE, PART)  9.35 us
    ppermute x9, starting transfers between devices, move(): return lax.ppermute(array, ('group', 'fsdp'), pairs)  8.99 us
    unnamed x22, local copies, waits for them, and re-layouts  6.29 us
  transfers between devices with their start and end apart: 12, of which 9 were waited for; matrix products, arithmetic and copies ran while one was open for 0% of the time, Pallas kernels for 3%

profile of v8, /device:TPU:0, one launch (start us, length us, event | category | flops | bytes accessed | tf_op | source)
XLA Modules:
  0.0 141.9 jit_solution(12136212764751629270)
XLA Ops:
  0.6 0.7 pad_add_fusion.place_ref
  1.3 3.4 %pack.1 = bf16[64,24,896]{2,1,0:T(8,128)(2,1)} custom-call(s32[3]{0:T(128)} %pad_add_fusion.place_ref, bf16[24,4608]{1,0:T(8,128)(2,1)} %base_ref.1, bf16[24,192]{1,0:T(8,128)(2,1)} %gen_down_ref.1, bf16[24,192]{1,0:T(8,128)(2,1)} %critic_down_ref.1, bf16[3,24,64]{2,1,0:T(8,128)(2,1)} %bitcast.36, bf16[3,24,64]{2,1,0:T(8,128)(2,1)} %bitcast.37), custom_call_target="tpu_custom_call" | custom-call | tf_op jit(solution)/shard_map/pack/pallas_call | solution.py:365
  4.7 0.0 copy-start.5
  4.7 0.0 copy-start.10
  4.7 9.5 %all-to-all-start = ((bf16[64,24,896]{2,1,0:T(8,128)(2,1)}), bf16[64,24,896]{2,1,0:T(8,128)(2,1)S(1)}, u32[]{:S(2)}, u32[]{:S(2)}) async-start(bf16[64,24,896]{2,1,0:T(8,128)(2,1)} %pack.1), calls=%async_computation | async-start | bytes 5505024 | tf_op jit(solution)/shard_map/all_to_all | solution.py:443
  14.2 0.0 copy-start.3
  14.2 0.0 copy-done.5
  14.2 3.5 %collective-permute-start.2 = (bf16[128,1536]{1,0:T(8,128)(2,1)S(1)}, bf16[128,1536]{1,0:T(8,128)(2,1)S(1)}, u32[]{:S(2)}, u32[]{:S(2)}) collective-permute-start(bf16[128,1536]{1,0:T(8,128)(2,1)S(1)} %bitcast.29), channel_id=1, source_target_pairs={{0,67},{1,66},{2,65},{3,64},{4,71},{5,70},{6,69},{7,68},{8,75},{9,... | collective-permute-start | bytes 1179656 | tf_op jit(solution)/shard_map/ppermute | solution.py:411
  17.8 0.3 collective-permute-start.1
  18.1 0.0 collective-permute-start
  18.1 9.1 %collective-permute-done.2.text_3_ref = bf16[128,1536]{1,0:T(8,128)(2,1)S(1)} collective-permute-done((bf16[128,1536]{1,0:T(8,128)(2,1)S(1)}, bf16[128,1536]{1,0:T(8,128)(2,1)S(1)}, u32[]{:S(2)}, u32[]{:S(2)}) %collective-permute-start.2) | collective-permute-done | bytes 393248 | tf_op jit(solution)/shard_map/ppermute | solution.py:411
  27.3 8.6 %collective-permute-done.1.text_2_ref = bf16[128,1536]{1,0:T(8,128)(2,1)S(1)} collective-permute-done((bf16[128,1536]{1,0:T(8,128)(2,1)S(1)}, bf16[128,1536]{1,0:T(8,128)(2,1)S(1)}, u32[]{:S(2)}, u32[]{:S(2)}) %collective-permute-start.1) | collective-permute-done | bytes 393248 | tf_op jit(solution)/shard_map/ppermute | solution.py:411
  35.9 0.0 collective-permute-done.text_1_ref
  35.9 1.0 copy-done.6
  36.9 0.5 prompts.1
  37.4 0.0 copy-start.1
  37.4 1.1 copy-done.1
  38.5 11.2 %all-to-all-done = bf16[64,24,896]{2,1,0:T(8,128)(2,1)S(1)} async-done(((bf16[64,24,896]{2,1,0:T(8,128)(2,1)}), bf16[64,24,896]{2,1,0:T(8,128)(2,1)S(1)}, u32[]{:S(2)}, u32[]{:S(2)}) %all-to-all-start) | async-done | bytes 2752544 | tf_op jit(solution)/shard_map/all_to_all | solution.py:443
  49.8 0.4 collective-permute-start.3
  50.2 2.0 %fold.1 = bf16[64,72,128]{2,1,0:T(8,128)(2,1)S(1)} custom-call(bf16[64,1536]{1,0:T(8,128)(2,1)S(1)} %copy-done.3, f32[1,1536]{1,0:T(1,128)S(1)} %reshape.19.modulation_ref, bf16[1536,896]{1,0:T(8,128)(2,1)S(1)} %bitcast.24), custom_call_target="tpu_custom_call" | custom-call | tf_op jit(solution)/shard_map/fold/pallas_call | solution.py:365
  52.3 1.0 copy-done
  53.3 5.6 %all-to-all-start.1 = ((bf16[64,72,128]{2,1,0:T(8,128)(2,1)}), bf16[64,72,128]{2,1,0:T(8,128)(2,1)}, u32[]{:S(2)}, u32[]{:S(2)}) async-start(bf16[64,72,128]{2,1,0:T(8,128)(2,1)} %copy-done), calls=%async_computation.1 | async-start | bytes 2359296 | tf_op jit(solution)/shard_map/all_to_all | solution.py:466
  58.9 0.0 collective-permute-done.3.packed_core_ref
  58.9 0.0 copy-start.2
  58.9 1.4 copy-done.2
  60.3 1.1 mix.1
  61.5 0.1 collective-permute-start.4
  61.6 1.4 %collective-permute-done.4.received_ref = bf16[256,384]{1,0:T(8,128)(2,1)S(1)} collective-permute-done((bf16[256,384]{1,0:T(8,128)(2,1)S(1)}, bf16[256,384]{1,0:T(8,128)(2,1)S(1)}, u32[]{:S(2)}, u32[]{:S(2)}) %collective-permute-start.4) | collective-permute-done | bytes 196640 | tf_op jit(solution)/shard_map/ppermute | solution.py:411
  63.0 0.8 pair.1
  63.8 3.6 %collective-permute-start.5 = (bf16[2,128,384]{2,1,0:T(8,128)(2,1)}, bf16[2,128,384]{2,1,0:T(8,128)(2,1)}, u32[]{:S(2)}, u32[]{:S(2)}) collective-permute-start(bf16[2,128,384]{2,1,0:T(8,128)(2,1)} %get-tuple-element.37.text_0_ref), channel_id=1, source_target_pairs={{0,64},{1,65},{2,66},{3,67},{4,68},{5,69},{6,70},{7,71},{8,72},{9,... | collective-permute-start | bytes 589832 | tf_op jit(solution)/shard_map/ppermute | solution.py:411
  67.4 0.6 collective-permute-start.7
  68.0 0.3 collective-permute-start.6
  68.9 9.4 %all-to-all-done.1 = bf16[64,72,128]{2,1,0:T(8,128)(2,1)} async-done(((bf16[64,72,128]{2,1,0:T(8,128)(2,1)}), bf16[64,72,128]{2,1,0:T(8,128)(2,1)}, u32[]{:S(2)}, u32[]{:S(2)}) %all-to-all-start.1) | async-done | bytes 1179680 | tf_op jit(solution)/shard_map/all_to_all | solution.py:466
  78.3 3.4 %collective-permute-done.5.text_1_ref = bf16[2,128,384]{2,1,0:T(8,128)(2,1)} collective-permute-done((bf16[2,128,384]{2,1,0:T(8,128)(2,1)}, bf16[2,128,384]{2,1,0:T(8,128)(2,1)}, u32[]{:S(2)}, u32[]{:S(2)}) %collective-permute-start.5) | collective-permute-done | bytes 196640 | tf_op jit(solution)/shard_map/ppermute | solution.py:411
  81.7 0.0 collective-permute-done.7.text_3_ref
  81.7 2.5 %collective-permute-done.6.text_2_ref = bf16[2,128,384]{2,1,0:T(8,128)(2,1)} collective-permute-done((bf16[2,128,384]{2,1,0:T(8,128)(2,1)}, bf16[2,128,384]{2,1,0:T(8,128)(2,1)}, u32[]{:S(2)}, u32[]{:S(2)}) %collective-permute-start.6) | collective-permute-done | bytes 196640 | tf_op jit(solution)/shard_map/ppermute | solution.py:411
  84.1 0.0 copy-done.4
  84.1 0.8 copy-done.7
  85.0 0.8 copy-done.8
  85.8 19.9 %forward.1 = (f32[64,256]{1,0:T(8,128)}, f32[64,256]{1,0:T(8,128)S(1)}, f32[64,256]{1,0:T(8,128)S(1)}, bf16[64,256]{1,0:T(8,128)(2,1)S(1)}, bf16[256,1536]{1,0:T...) custom-call(s32[3]{0:T(128)S(1)} %copy-done.9, ...), custom_call_target="tpu_custom_call" | custom-call | tf_op jit(solution)/shard_map/forward/pallas_call | solution.py:365
  105.8 1.3 collective-permute-start.8
  107.1 6.0 %collective-permute-done.8.fake_ref = bf16[64,256]{1,0:T(8,128)(2,1)S(1)} collective-permute-done((bf16[64,256]{1,0:T(8,128)(2,1)S(1)}, bf16[64,256]{1,0:T(8,128)(2,1)S(1)}, u32[]{:S(2)}, u32[]{:S(2)}) %collective-permute-start.8) | collective-permute-done | bytes 32800 | tf_op jit(solution)/shard_map/ppermute | solution.py:530
  113.1 7.3 %backward.1 = (f32[32,24,384]{2,1,0:T(8,128)S(1)}, bf16[32,24,384]{2,1,0:T(8,128)(2,1)S(1)}) custom-call(s32[3]{0:T(128)S(1)} %copy-done.9, f32[1,1]{1,0:T(1,128)} %bitcast.3.sigma_ref, f32[64,256]{1,0:T(8,128)S(1)} %get-tuple-element.41.sample_ref, f32[64,256]{1,0:T(8,128)S(1)} %bitcast.34, f32[64,256]{1,0:T(8,128)S(1)} %get-tuple-element.42.own_ref, ...), custom_call_target="tpu_custom_call" | custom-call | tf_op jit(solution)/shard_map/backward/pallas_call | solution.py:365
  120.4 0.1 collective-permute-start.9
  120.5 2.0 %collective-permute-done.9.received_ref = bf16[32,24,384]{2,1,0:T(8,128)(2,1)S(1)} collective-permute-done((bf16[32,24,384]{2,1,0:T(8,128)(2,1)S(1)}, bf16[32,24,384]{2,1,0:T(8,128)(2,1)S(1)}, u32[]{:S(2)}, u32[]{:S(2)}) %collective-permute-start.9) | collective-permute-done | bytes 589856 | tf_op jit(solution)/shard_map/ppermute | solution.py:411
  122.5 0.1 add.9
  122.6 18.6 %all_to_all.15.shares_ref = bf16[32,24,384]{2,1,0:T(8,128)(2,1)S(1)} all-to-all(bf16[32,24,384]{2,1,0:T(8,128)(2,1)S(1)} %add.9), channel_id=1, replica_groups={{0,2,4,6,8,10,12,14,16,18,20,22,24,26,28,30,32,34,36,38,40,42,44,46,48,..., dimensions={0} | all-to-all | bytes 1179648 | tf_op jit(solution)/shard_map/all_to_all | solution.py:557
  141.2 0.8 total.1
  (10 shorter events, 0.0 us)
Async XLA Ops:
  4.7 9.6 %copy-start.5 = (bf16[1,128,1536]{2,1,0:T(8,128)(2,1)S(1)}, bf16[1,128,1536]{2,1,0:T(8,128)(2,1)}, u32[]{:S(2)}) copy-start(bf16[1,128,1536]{2,1,0:T(8,128)(2,1)} %param.14) | copy-start | bytes 1179652
  4.7 45.5 %copy-start.10 = (f32[1536]{0:T(1024)S(1)}, f32[1536]{0:T(1024)}, u32[]{:S(2)}) copy-start(f32[1536]{0:T(1024)} %param.18) | copy-start | bytes 18436
  4.7 45.1 %all-to-all-start = ((bf16[64,24,896]{2,1,0:T(8,128)(2,1)}), bf16[64,24,896]{2,1,0:T(8,128)(2,1)S(1)}, u32[]{:S(2)}, u32[]{:S(2)}) async-start(bf16[64,24,896]{2,1,0:T(8,128)(2,1)} %pack.1), calls=%async_computation | async-start | bytes 5505024 | tf_op jit(solution)/shard_map/all_to_all | solution.py:443
  14.2 36.0 %copy-start.3 = (bf16[64,1536]{1,0:T(8,128)(2,1)S(1)}, bf16[64,1536]{1,0:T(8,128)(2,1)}, u32[]{:S(2)}) copy-start(bf16[64,1536]{1,0:T(8,128)(2,1)} %latent_in_ref.3) | copy-start | bytes 589828
  14.2 13.0 %collective-permute-start.2 = (bf16[128,1536]{1,0:T(8,128)(2,1)S(1)}, bf16[128,1536]{1,0:T(8,128)(2,1)S(1)}, u32[]{:S(2)}, u32[]{:S(2)}) collective-permute-start(bf16[128,1536]{1,0:T(8,128)(2,1)S(1)} %bitcast.29), channel_id=1, source_target_pairs={{0,67},{1,66},{2,65},{3,64},{4,71},{5,70},{6,69},{7,68},{8,75},{9,... | collective-permute-start | bytes 1179656 | tf_op jit(solution)/shard_map/ppermute | solution.py:411
  17.8 18.1 %collective-permute-start.1 = (bf16[128,1536]{1,0:T(8,128)(2,1)S(1)}, bf16[128,1536]{1,0:T(8,128)(2,1)S(1)}, u32[]{:S(2)}, u32[]{:S(2)}) collective-permute-start(bf16[128,1536]{1,0:T(8,128)(2,1)S(1)} %bitcast.30), channel_id=1, source_target_pairs={{0,66},{1,67},{2,64},{3,65},{4,70},{5,71},{6,68},{7,69},{8,74},{9,... | collective-permute-start | bytes 1179656 | tf_op jit(solution)/shard_map/ppermute | solution.py:411
  18.1 17.8 %collective-permute-start = (bf16[128,1536]{1,0:T(8,128)(2,1)S(1)}, bf16[128,1536]{1,0:T(8,128)(2,1)S(1)}, u32[]{:S(2)}, u32[]{:S(2)}) collective-permute-start(bf16[128,1536]{1,0:T(8,128)(2,1)S(1)} %bitcast.31), channel_id=1, source_target_pairs={{0,1},{1,0},{2,3},{3,2},{4,5},{5,4},{6,7},{7,6},{8,9},{9,8},{10,11... | collective-permute-start | bytes 1179656 | tf_op jit(solution)/shard_map/ppermute | solution.py:411
  35.9 1.0 copy-start.6
  37.4 1.2 copy-start.1
  49.8 9.2 %collective-permute-start.3 = (bf16[1536,896]{1,0:T(8,128)(2,1)S(1)}, bf16[1536,896]{1,0:T(8,128)(2,1)}, u32[]{:S(2)}, u32[]{:S(2)}) collective-permute-start(bf16[1536,896]{1,0:T(8,128)(2,1)S(1)} %bitcast.23), channel_id=1, source_target_pairs={{0,1},{1,0},{2,3},{3,2},{4,5},{5,4},{6,7},{7,6},{8,9},{9,8},{10,11... | collective-permute-start | bytes 8257544 | tf_op jit(solution)/shard_map/ppermute | solution.py:411
  52.3 1.0 copy-start
  53.3 25.0 %all-to-all-start.1 = ((bf16[64,72,128]{2,1,0:T(8,128)(2,1)}), bf16[64,72,128]{2,1,0:T(8,128)(2,1)}, u32[]{:S(2)}, u32[]{:S(2)}) async-start(bf16[64,72,128]{2,1,0:T(8,128)(2,1)} %copy-done), calls=%async_computation.1 | async-start | bytes 2359296 | tf_op jit(solution)/shard_map/all_to_all | solution.py:466
  58.9 1.4 copy-start.2
  60.3 23.8 %copy-start.4 = (bf16[1536,64]{0,1:T(8,128)(2,1)S(1)}, bf16[1536,64]{0,1:T(8,128)(2,1)}, u32[]{:S(2)}) copy-start(bf16[1536,64]{0,1:T(8,128)(2,1)} %param.19) | copy-start | bytes 589828
  60.3 23.8 %copy-start.9 = (s32[3]{0:T(128)S(1)}, s32[3]{0:T(128)}, u32[]{:S(2)}) copy-start(s32[3]{0:T(128)} %pad_add_fusion.place_ref) | copy-start | bytes 40
  61.5 1.5 %collective-permute-start.4 = (bf16[256,384]{1,0:T(8,128)(2,1)S(1)}, bf16[256,384]{1,0:T(8,128)(2,1)S(1)}, u32[]{:S(2)}, u32[]{:S(2)}) collective-permute-start(bf16[256,384]{1,0:T(8,128)(2,1)S(1)} %get-tuple-element.36), channel_id=1, source_target_pairs={{0,1},{1,0},{2,3},{3,2},{4,5},{5,4},{6,7},{7,6},{8,9},{9,8},{10,11... | collective-permute-start | bytes 589832 | tf_op jit(solution)/shard_map/ppermute | solution.py:411
  63.8 17.9 %collective-permute-start.5 = (bf16[2,128,384]{2,1,0:T(8,128)(2,1)}, bf16[2,128,384]{2,1,0:T(8,128)(2,1)}, u32[]{:S(2)}, u32[]{:S(2)}) collective-permute-start(bf16[2,128,384]{2,1,0:T(8,128)(2,1)} %get-tuple-element.37.text_0_ref), channel_id=1, source_target_pairs={{0,64},{1,65},{2,66},{3,67},{4,68},{5,69},{6,70},{7,71},{8,72},{9,... | collective-permute-start | bytes 589832 | tf_op jit(solution)/shard_map/ppermute | solution.py:411
  67.4 14.3 %collective-permute-start.7 = (bf16[2,128,384]{2,1,0:T(8,128)(2,1)}, bf16[2,128,384]{2,1,0:T(8,128)(2,1)}, u32[]{:S(2)}, u32[]{:S(2)}) collective-permute-start(bf16[2,128,384]{2,1,0:T(8,128)(2,1)} %get-tuple-element.38), channel_id=1, source_target_pairs={{0,66},{1,67},{2,64},{3,65},{4,70},{5,71},{6,68},{7,69},{8,74},{9,... | collective-permute-start | bytes 589832 | tf_op jit(solution)/shard_map/ppermute | solution.py:411
  68.0 16.2 %collective-permute-start.6 = (bf16[2,128,384]{2,1,0:T(8,128)(2,1)}, bf16[2,128,384]{2,1,0:T(8,128)(2,1)}, u32[]{:S(2)}, u32[]{:S(2)}) collective-permute-start(bf16[2,128,384]{2,1,0:T(8,128)(2,1)} %get-tuple-element.38), channel_id=1, source_target_pairs={{0,2},{1,3},{2,0},{3,1},{4,6},{5,7},{6,4},{7,5},{8,10},{9,11},{10,... | collective-permute-start | bytes 589832 | tf_op jit(solution)/shard_map/ppermute | solution.py:411
  84.1 0.8 copy-start.7
  85.0 0.8 copy-start.8
  105.8 7.3 %collective-permute-start.8 = (bf16[64,256]{1,0:T(8,128)(2,1)S(1)}, bf16[64,256]{1,0:T(8,128)(2,1)S(1)}, u32[]{:S(2)}, u32[]{:S(2)}) collective-permute-start(bf16[64,256]{1,0:T(8,128)(2,1)S(1)} %get-tuple-element.43), channel_id=1, source_target_pairs={{64,0},{65,1},{66,2},{67,3},{68,4},{69,5},{70,6},{71,7},{72,8},{73... | collective-permute-start | bytes 98312 | tf_op jit(solution)/shard_map/ppermute | solution.py:530
  120.4 2.1 %collective-permute-start.9 = (bf16[32,24,384]{2,1,0:T(8,128)(2,1)S(1)}, bf16[32,24,384]{2,1,0:T(8,128)(2,1)S(1)}, u32[]{:S(2)}, u32[]{:S(2)}) collective-permute-start(bf16[32,24,384]{2,1,0:T(8,128)(2,1)S(1)} %get-tuple-element.54), channel_id=1, source_target_pairs={{0,1},{1,0},{2,3},{3,2},{4,5},{5,4},{6,7},{7,6},{8,9},{9,8},{10,11... | collective-permute-start | bytes 1769480 | tf_op jit(solution)/shard_map/ppermute | solution.py:411

commit v9 on v8

--- a/solution.py
+++ b/solution.py
@@ -448,7 +448,7 @@
     (share,) = run(
         fold_kernel,
         "fold",
-        16,
+        60,
         0,
         [((devices, SHARE, PART), BF)],
         [
@@ -469,7 +469,7 @@
     mine, theirs = run(
         mix_kernel,
         "mix",
-        16,
+        60,
         0,
         [((2 * TXT, EIGHTH), BF)] * 2,
         [pltpu.VMEM((HW, EIGHTH), BF), pltpu.SemaphoreType.DMA((1,))],

time: 143 us -> 142 us (level)
  Pallas kernels: 35.9 us -> 39.7 us
  local copies, waits for them, and re-layouts: 6.3 us -> 2.73 us
    unnamed x22 -> x20, local copies, waits for them, and re-layouts: 6.29 us -> 2.13 us
    pallas_call x9, Pallas kernels: 35.9 us -> 39.7 us  [run(): pl.pallas_call(kernel, out_shape=shapes, in_specs=[pl.BlockSpec(memory_sp...]
    all_to_all x1, waiting for transfers between devices: 9.35 us -> 6.88 us  [per_device(): fold = lax.all_to_all(share, 'fsdp', 0, 0).reshape(devices * SHARE, PART)]
  transfers between devices with their start and end apart: 12 -> 12, of which waited for: 9 -> 9; matrix products, arithmetic and copies ran while one was open for 0% -> 0% of each run, Pallas kernels for 3% -> 6%
where the time goes in v9:
time: 142 us; the launch traced here: 141 us
  waiting for transfers between devices  52.6 us (37%)
  Pallas kernels  39.7 us (28%)
  starting transfers between devices  25.5 us (18%)
  blocking collectives  18.6 us (13%)
  local copies, waits for them, and re-layouts  2.73 us (2%)
  between operations  1.5 us (1%)
    pallas_call x9, Pallas kernels, run(): pl.pallas_call(kernel, out_shape=shapes, in_specs=[pl.BlockSpec(memory_sp...  39.7 us
    ppermute x9, waiting for transfers between devices, move(): return lax.ppermute(array, ('group', 'fsdp'), pairs)  27.6 us
    all_to_all x1, blocking collectives, per_device(): shares = lax.all_to_all(sums, 'fsdp', 0, 0, axis_index_groups=parities)  18.6 us
    all_to_all x1, waiting for transfers between devices, per_device(): lax.all_to_all(packed, 'fsdp', 0, 0).reshape(HW, EIGHTH + SIDE + PART)  12.1 us
    all_to_all x1, starting transfers between devices, per_device(): lax.all_to_all(packed, 'fsdp', 0, 0).reshape(HW, EIGHTH + SIDE + PART)  9.75 us
    ppermute x9, starting transfers between devices, move(): return lax.ppermute(array, ('group', 'fsdp'), pairs)  9.12 us
    all_to_all x1, waiting for transfers between devices, per_device(): fold = lax.all_to_all(share, 'fsdp', 0, 0).reshape(devices * SHARE, PART)  6.88 us
    ppermute x1, waiting for transfers between devices, per_device(): fake_velocity = lax.ppermute(narrow_velocity, 'group', [(1, 0)])  6.01 us
  transfers between devices with their start and end apart: 12, of which 9 were waited for; matrix products, arithmetic and copies ran while one was open for 0% of the time, Pallas kernels for 6%

profile of v9, /device:TPU:0, one launch (start us, length us, event | category | flops | bytes accessed | tf_op | source)
XLA Modules:
  0.0 141.3 jit_solution(623273917483957844)
XLA Ops:
  0.6 0.6 pad_add_fusion.place_ref
  1.2 3.4 %pack.1 = bf16[64,24,896]{2,1,0:T(8,128)(2,1)} custom-call(s32[3]{0:T(128)} %pad_add_fusion.place_ref, bf16[24,4608]{1,0:T(8,128)(2,1)} %base_ref.1, bf16[24,192]{1,0:T(8,128)(2,1)} %gen_down_ref.1, bf16[24,192]{1,0:T(8,128)(2,1)} %critic_down_ref.1, bf16[3,24,64]{2,1,0:T(8,128)(2,1)} %bitcast.33, bf16[3,24,64]{2,1,0:T(8,128)(2,1)} %bitcast.34), custom_call_target="tpu_custom_call" | custom-call | tf_op jit(solution)/shard_map/pack/pallas_call | solution.py:365
  4.6 0.0 copy-start.3
  4.6 9.8 %all-to-all-start = ((bf16[64,24,896]{2,1,0:T(8,128)(2,1)}), bf16[64,24,896]{2,1,0:T(8,128)(2,1)}, u32[]{:S(2)}, u32[]{:S(2)}) async-start(bf16[64,24,896]{2,1,0:T(8,128)(2,1)} %pack.1), calls=%async_computation | async-start | bytes 5505024 | tf_op jit(solution)/shard_map/all_to_all | solution.py:443
  14.4 0.0 copy-start.9
  14.4 3.5 %collective-permute-start.2 = (bf16[128,1536]{1,0:T(8,128)(2,1)S(1)}, bf16[128,1536]{1,0:T(8,128)(2,1)S(1)}, u32[]{:S(2)}, u32[]{:S(2)}) collective-permute-start(bf16[128,1536]{1,0:T(8,128)(2,1)S(1)} %bitcast.26), channel_id=1, source_target_pairs={{0,67},{1,66},{2,65},{3,64},{4,71},{5,70},{6,69},{7,68},{8,75},{9,... | collective-permute-start | bytes 1179656 | tf_op jit(solution)/shard_map/ppermute | solution.py:411
  17.8 0.3 collective-permute-start.1
  18.2 0.0 collective-permute-start
  18.2 9.1 %collective-permute-done.2.text_3_ref = bf16[128,1536]{1,0:T(8,128)(2,1)S(1)} collective-permute-done((bf16[128,1536]{1,0:T(8,128)(2,1)S(1)}, bf16[128,1536]{1,0:T(8,128)(2,1)S(1)}, u32[]{:S(2)}, u32[]{:S(2)}) %collective-permute-start.2) | collective-permute-done | bytes 393248 | tf_op jit(solution)/shard_map/ppermute | solution.py:411
  27.3 8.6 %collective-permute-done.1.text_2_ref = bf16[128,1536]{1,0:T(8,128)(2,1)S(1)} collective-permute-done((bf16[128,1536]{1,0:T(8,128)(2,1)S(1)}, bf16[128,1536]{1,0:T(8,128)(2,1)S(1)}, u32[]{:S(2)}, u32[]{:S(2)}) %collective-permute-start.1) | collective-permute-done | bytes 393248 | tf_op jit(solution)/shard_map/ppermute | solution.py:411
  35.9 0.0 collective-permute-done.text_1_ref
  35.9 0.5 prompts.1
  36.5 1.2 copy-done
  37.6 12.1 %all-to-all-done = bf16[64,24,896]{2,1,0:T(8,128)(2,1)} async-done(((bf16[64,24,896]{2,1,0:T(8,128)(2,1)}), bf16[64,24,896]{2,1,0:T(8,128)(2,1)}, u32[]{:S(2)}, u32[]{:S(2)}) %all-to-all-start) | async-done | bytes 2752544 | tf_op jit(solution)/shard_map/all_to_all | solution.py:443
  49.8 0.4 collective-permute-start.3
  50.2 0.6 reshape.19.modulation_ref
  50.8 3.4 %fold.1 = bf16[64,72,128]{2,1,0:T(8,128)(2,1)} custom-call(bf16[64,1536]{1,0:T(8,128)(2,1)} %latent_in_ref.3, f32[1,1536]{1,0:T(1,128)} %reshape.19.modulation_ref, bf16[1536,896]{1,0:T(8,128)(2,1)} %bitcast.12.packed_ref.packed_own_ref), custom_call_target="tpu_custom_call" | custom-call | tf_op jit(solution)/shard_map/fold/pallas_call | solution.py:365
  54.2 5.4 %all-to-all-start.1 = ((bf16[64,72,128]{2,1,0:T(8,128)(2,1)}), bf16[64,72,128]{2,1,0:T(8,128)(2,1)S(1)}, u32[]{:S(2)}, u32[]{:S(2)}) async-start(bf16[64,72,128]{2,1,0:T(8,128)(2,1)} %fold.1), calls=%async_computation.1 | async-start | bytes 2359296 | tf_op jit(solution)/shard_map/all_to_all | solution.py:466
  59.6 0.0 copy-start.1
  59.6 0.0 copy-start.2
  59.6 0.0 copy-start.4
  59.6 0.0 copy-start.6
  59.7 0.0 copy-start.7
  59.7 0.0 copy-start.8
  59.7 0.0 collective-permute-done.3.packed_core_ref
  59.7 4.5 %mix.1 = (bf16[256,384]{1,0:T(8,128)(2,1)}, bf16[256,384]{1,0:T(8,128)(2,1)}) custom-call(bf16[512,1536]{1,0:T(8,128)(2,1)} %copy-done, bf16[1536,896]{1,0:T(8,128)(2,1)} %bitcast.12.packed_ref.packed_own_ref), custom_call_target="tpu_custom_call" | custom-call | tf_op jit(solution)/shard_map/mix/pallas_call | solution.py:365
  64.2 0.1 collective-permute-start.4
  64.3 1.6 %collective-permute-done.4.received_ref = bf16[256,384]{1,0:T(8,128)(2,1)S(1)} collective-permute-done((bf16[256,384]{1,0:T(8,128)(2,1)}, bf16[256,384]{1,0:T(8,128)(2,1)S(1)}, u32[]{:S(2)}, u32[]{:S(2)}) %collective-permute-start.4) | collective-permute-done | bytes 196640 | tf_op jit(solution)/shard_map/ppermute | solution.py:411
  65.9 0.9 copy-done.5
  66.9 3.7 %collective-permute-start.5 = (bf16[2,128,384]{2,1,0:T(8,128)(2,1)S(1)}, bf16[2,128,384]{2,1,0:T(8,128)(2,1)S(1)}, u32[]{:S(2)}, u32[]{:S(2)}) collective-permute-start(bf16[2,128,384]{2,1,0:T(8,128)(2,1)S(1)} %get-tuple-element.37.text_0_ref), channel_id=1, source_target_pairs={{0,64},{1,65},{2,66},{3,67},{4,68},{5,69},{6,70},{7,71},{8,72},{9,... | collective-permute-start | bytes 589832 | tf_op jit(solution)/shard_map/ppermute | solution.py:411
  70.6 0.7 collective-permute-start.7
  71.2 0.3 collective-permute-start.6
  72.2 6.9 %all-to-all-done.1 = bf16[64,72,128]{2,1,0:T(8,128)(2,1)S(1)} async-done(((bf16[64,72,128]{2,1,0:T(8,128)(2,1)}), bf16[64,72,128]{2,1,0:T(8,128)(2,1)S(1)}, u32[]{:S(2)}, u32[]{:S(2)}) %all-to-all-start.1) | async-done | bytes 1179680 | tf_op jit(solution)/shard_map/all_to_all | solution.py:466
  79.1 3.5 %collective-permute-done.5.text_1_ref = bf16[2,128,384]{2,1,0:T(8,128)(2,1)S(1)} collective-permute-done((bf16[2,128,384]{2,1,0:T(8,128)(2,1)S(1)}, bf16[2,128,384]{2,1,0:T(8,128)(2,1)S(1)}, u32[]{:S(2)}, u32[]{:S(2)}) %collective-permute-start.5) | collective-permute-done | bytes 196640 | tf_op jit(solution)/shard_map/ppermute | solution.py:411
  82.5 0.0 collective-permute-done.7.text_3_ref
  82.5 2.8 %collective-permute-done.6.text_2_ref = bf16[2,128,384]{2,1,0:T(8,128)(2,1)S(1)} collective-permute-done((bf16[2,128,384]{2,1,0:T(8,128)(2,1)S(1)}, bf16[2,128,384]{2,1,0:T(8,128)(2,1)S(1)}, u32[]{:S(2)}, u32[]{:S(2)}) %collective-permute-start.6) | collective-permute-done | bytes 196640 | tf_op jit(solution)/shard_map/ppermute | solution.py:411
  85.4 0.0 copy-done.6
  85.4 0.0 copy-done.7
  85.4 0.0 copy-done.8
  85.4 19.7 %forward.1 = (f32[64,256]{1,0:T(8,128)}, f32[64,256]{1,0:T(8,128)S(1)}, f32[64,256]{1,0:T(8,128)S(1)}, bf16[64,256]{1,0:T(8,128)(2,1)S(1)}, bf16[256,1536]{1,0:T...) custom-call(s32[3]{0:T(128)S(1)} %copy-done.8, ...), custom_call_target="tpu_custom_call" | custom-call | tf_op jit(solution)/shard_map/forward/pallas_call | solution.py:365
  105.1 1.3 collective-permute-start.8
  106.4 6.0 %collective-permute-done.8.fake_ref = bf16[64,256]{1,0:T(8,128)(2,1)S(1)} collective-permute-done((bf16[64,256]{1,0:T(8,128)(2,1)S(1)}, bf16[64,256]{1,0:T(8,128)(2,1)S(1)}, u32[]{:S(2)}, u32[]{:S(2)}) %collective-permute-start.8) | collective-permute-done | bytes 32800 | tf_op jit(solution)/shard_map/ppermute | solution.py:530
  112.4 7.3 %backward.1 = (f32[32,24,384]{2,1,0:T(8,128)S(1)}, bf16[32,24,384]{2,1,0:T(8,128)(2,1)S(1)}) custom-call(s32[3]{0:T(128)S(1)} %copy-done.8, f32[1,1]{1,0:T(1,128)} %bitcast.3.sigma_ref, f32[64,256]{1,0:T(8,128)S(1)} %get-tuple-element.41.sample_ref, f32[64,256]{1,0:T(8,128)S(1)} %bitcast.31, f32[64,256]{1,0:T(8,128)S(1)} %get-tuple-element.42.own_ref, ...), custom_call_target="tpu_custom_call" | custom-call | tf_op jit(solution)/shard_map/backward/pallas_call | solution.py:365
  119.7 0.1 collective-permute-start.9
  119.8 2.0 %collective-permute-done.9.received_ref = bf16[32,24,384]{2,1,0:T(8,128)(2,1)S(1)} collective-permute-done((bf16[32,24,384]{2,1,0:T(8,128)(2,1)S(1)}, bf16[32,24,384]{2,1,0:T(8,128)(2,1)S(1)}, u32[]{:S(2)}, u32[]{:S(2)}) %collective-permute-start.9) | collective-permute-done | bytes 589856 | tf_op jit(solution)/shard_map/ppermute | solution.py:411
  121.8 0.1 add.9
  121.9 18.6 %all_to_all.15.shares_ref = bf16[32,24,384]{2,1,0:T(8,128)(2,1)S(1)} all-to-all(bf16[32,24,384]{2,1,0:T(8,128)(2,1)S(1)} %add.9), channel_id=1, replica_groups={{0,2,4,6,8,10,12,14,16,18,20,22,24,26,28,30,32,34,36,38,40,42,44,46,48,..., dimensions={0} | all-to-all | bytes 1179648 | tf_op jit(solution)/shard_map/all_to_all | solution.py:557
  140.5 0.8 total.1
  (8 shorter events, 0.0 us)
Async XLA Ops:
  4.6 9.8 %copy-start.3 = (bf16[1,128,1536]{2,1,0:T(8,128)(2,1)S(1)}, bf16[1,128,1536]{2,1,0:T(8,128)(2,1)}, u32[]{:S(2)}) copy-start(bf16[1,128,1536]{2,1,0:T(8,128)(2,1)} %param.14) | copy-start | bytes 1179652
  4.6 45.2 %all-to-all-start = ((bf16[64,24,896]{2,1,0:T(8,128)(2,1)}), bf16[64,24,896]{2,1,0:T(8,128)(2,1)}, u32[]{:S(2)}, u32[]{:S(2)}) async-start(bf16[64,24,896]{2,1,0:T(8,128)(2,1)} %pack.1), calls=%async_computation | async-start | bytes 5505024 | tf_op jit(solution)/shard_map/all_to_all | solution.py:443
  14.4 35.8 %copy-start.9 = (f32[1536]{0:T(1024)S(1)}, f32[1536]{0:T(1024)}, u32[]{:S(2)}) copy-start(f32[1536]{0:T(1024)} %param.18) | copy-start | bytes 18436
  14.4 13.0 %collective-permute-start.2 = (bf16[128,1536]{1,0:T(8,128)(2,1)S(1)}, bf16[128,1536]{1,0:T(8,128)(2,1)S(1)}, u32[]{:S(2)}, u32[]{:S(2)}) collective-permute-start(bf16[128,1536]{1,0:T(8,128)(2,1)S(1)} %bitcast.26), channel_id=1, source_target_pairs={{0,67},{1,66},{2,65},{3,64},{4,71},{5,70},{6,69},{7,68},{8,75},{9,... | collective-permute-start | bytes 1179656 | tf_op jit(solution)/shard_map/ppermute | solution.py:411
  17.8 18.1 %collective-permute-start.1 = (bf16[128,1536]{1,0:T(8,128)(2,1)S(1)}, bf16[128,1536]{1,0:T(8,128)(2,1)S(1)}, u32[]{:S(2)}, u32[]{:S(2)}) collective-permute-start(bf16[128,1536]{1,0:T(8,128)(2,1)S(1)} %bitcast.27), channel_id=1, source_target_pairs={{0,66},{1,67},{2,64},{3,65},{4,70},{5,71},{6,68},{7,69},{8,74},{9,... | collective-permute-start | bytes 1179656 | tf_op jit(solution)/shard_map/ppermute | solution.py:411
  18.2 17.8 %collective-permute-start = (bf16[128,1536]{1,0:T(8,128)(2,1)S(1)}, bf16[128,1536]{1,0:T(8,128)(2,1)S(1)}, u32[]{:S(2)}, u32[]{:S(2)}) collective-permute-start(bf16[128,1536]{1,0:T(8,128)(2,1)S(1)} %bitcast.28), channel_id=1, source_target_pairs={{0,1},{1,0},{2,3},{3,2},{4,5},{5,4},{6,7},{7,6},{8,9},{9,8},{10,11... | collective-permute-start | bytes 1179656 | tf_op jit(solution)/shard_map/ppermute | solution.py:411
  36.5 1.2 copy-start
  49.8 9.9 %collective-permute-start.3 = (bf16[1536,896]{1,0:T(8,128)(2,1)}, bf16[1536,896]{1,0:T(8,128)(2,1)}, u32[]{:S(2)}, u32[]{:S(2)}) collective-permute-start(bf16[1536,896]{1,0:T(8,128)(2,1)} %bitcast.12.packed_ref.packed_own_ref), channel_id=1, source_target_pairs={{0,1},{1,0},{2,3},{3,2},{4,5},{5,4},{6,7},{7,6},{8,9},{9,8},{10,11... | collective-permute-start | bytes 8257544 | tf_op jit(solution)/shard_map/ppermute | solution.py:411
  54.2 24.9 %all-to-all-start.1 = ((bf16[64,72,128]{2,1,0:T(8,128)(2,1)}), bf16[64,72,128]{2,1,0:T(8,128)(2,1)S(1)}, u32[]{:S(2)}, u32[]{:S(2)}) async-start(bf16[64,72,128]{2,1,0:T(8,128)(2,1)} %fold.1), calls=%async_computation.1 | async-start | bytes 2359296 | tf_op jit(solution)/shard_map/all_to_all | solution.py:466
  59.6 25.8 %copy-start.1 = (bf16[64,1536]{1,0:T(8,128)(2,1)S(1)}, bf16[64,1536]{1,0:T(8,128)(2,1)}, u32[]{:S(2)}) copy-start(bf16[64,1536]{1,0:T(8,128)(2,1)} %latent_in_ref.3) | copy-start | bytes 589828
  59.6 25.7 %copy-start.2 = (bf16[1536,64]{0,1:T(8,128)(2,1)S(1)}, bf16[1536,64]{0,1:T(8,128)(2,1)}, u32[]{:S(2)}) copy-start(bf16[1536,64]{0,1:T(8,128)(2,1)} %param.19) | copy-start | bytes 589828
  59.6 25.7 %copy-start.4 = (f32[1,256,64]{1,2,0:T(8,128)S(1)}, f32[1,256,64]{1,2,0:T(8,128)}, u32[]{:S(2)}) copy-start(f32[1,256,64]{1,2,0:T(8,128)} %param.13) | copy-start | bytes 196612
  59.6 25.7 %copy-start.6 = (f32[1,256,64]{1,2,0:T(8,128)S(1)}, f32[1,256,64]{1,2,0:T(8,128)}, u32[]{:S(2)}) copy-start(f32[1,256,64]{1,2,0:T(8,128)} %param.12) | copy-start | bytes 196612
  59.7 25.7 %copy-start.7 = (f32[1,1536]{1,0:T(1,128)S(1)}, f32[1,1536]{1,0:T(1,128)}, u32[]{:S(2)}) copy-start(f32[1,1536]{1,0:T(1,128)} %reshape.19.modulation_ref) | copy-start | bytes 18436
  59.7 25.7 %copy-start.8 = (s32[3]{0:T(128)S(1)}, s32[3]{0:T(128)}, u32[]{:S(2)}) copy-start(s32[3]{0:T(128)} %pad_add_fusion.place_ref) | copy-start | bytes 40
  64.2 1.7 %collective-permute-start.4 = (bf16[256,384]{1,0:T(8,128)(2,1)}, bf16[256,384]{1,0:T(8,128)(2,1)S(1)}, u32[]{:S(2)}, u32[]{:S(2)}) collective-permute-start(bf16[256,384]{1,0:T(8,128)(2,1)} %get-tuple-element.36), channel_id=1, source_target_pairs={{0,1},{1,0},{2,3},{3,2},{4,5},{5,4},{6,7},{7,6},{8,9},{9,8},{10,11... | collective-permute-start | bytes 589832 | tf_op jit(solution)/shard_map/ppermute | solution.py:411
  65.9 0.9 copy-start.5
  66.9 15.6 %collective-permute-start.5 = (bf16[2,128,384]{2,1,0:T(8,128)(2,1)S(1)}, bf16[2,128,384]{2,1,0:T(8,128)(2,1)S(1)}, u32[]{:S(2)}, u32[]{:S(2)}) collective-permute-start(bf16[2,128,384]{2,1,0:T(8,128)(2,1)S(1)} %get-tuple-element.37.text_0_ref), channel_id=1, source_target_pairs={{0,64},{1,65},{2,66},{3,67},{4,68},{5,69},{6,70},{7,71},{8,72},{9,... | collective-permute-start | bytes 589832 | tf_op jit(solution)/shard_map/ppermute | solution.py:411
  70.6 12.0 %collective-permute-start.7 = (bf16[2,128,384]{2,1,0:T(8,128)(2,1)S(1)}, bf16[2,128,384]{2,1,0:T(8,128)(2,1)S(1)}, u32[]{:S(2)}, u32[]{:S(2)}) collective-permute-start(bf16[2,128,384]{2,1,0:T(8,128)(2,1)S(1)} %get-tuple-element.38), channel_id=1, source_target_pairs={{0,66},{1,67},{2,64},{3,65},{4,70},{5,71},{6,68},{7,69},{8,74},{9,... | collective-permute-start | bytes 589832 | tf_op jit(solution)/shard_map/ppermute | solution.py:411
  71.2 14.1 %collective-permute-start.6 = (bf16[2,128,384]{2,1,0:T(8,128)(2,1)S(1)}, bf16[2,128,384]{2,1,0:T(8,128)(2,1)S(1)}, u32[]{:S(2)}, u32[]{:S(2)}) collective-permute-start(bf16[2,128,384]{2,1,0:T(8,128)(2,1)S(1)} %get-tuple-element.38), channel_id=1, source_target_pairs={{0,2},{1,3},{2,0},{3,1},{4,6},{5,7},{6,4},{7,5},{8,10},{9,11},{10,... | collective-permute-start | bytes 589832 | tf_op jit(solution)/shard_map/ppermute | solution.py:411
  105.1 7.3 %collective-permute-start.8 = (bf16[64,256]{1,0:T(8,128)(2,1)S(1)}, bf16[64,256]{1,0:T(8,128)(2,1)S(1)}, u32[]{:S(2)}, u32[]{:S(2)}) collective-permute-start(bf16[64,256]{1,0:T(8,128)(2,1)S(1)} %get-tuple-element.43), channel_id=1, source_target_pairs={{64,0},{65,1},{66,2},{67,3},{68,4},{69,5},{70,6},{71,7},{72,8},{73... | collective-permute-start | bytes 98312 | tf_op jit(solution)/shard_map/ppermute | solution.py:530
  119.7 2.1 %collective-permute-start.9 = (bf16[32,24,384]{2,1,0:T(8,128)(2,1)S(1)}, bf16[32,24,384]{2,1,0:T(8,128)(2,1)S(1)}, u32[]{:S(2)}, u32[]{:S(2)}) collective-permute-start(bf16[32,24,384]{2,1,0:T(8,128)(2,1)S(1)} %get-tuple-element.54), channel_id=1, source_target_pairs={{0,1},{1,0},{2,3},{3,2},{4,5},{5,4},{6,7},{7,6},{8,9},{9,8},{10,11... | collective-permute-start | bytes 1769480 | tf_op jit(solution)/shard_map/ppermute | solution.py:411

commit v10 on v8

--- a/solution.py
+++ b/solution.py
@@ -42,7 +42,6 @@
 
 
 def pack_kernel(
-    place_ref,
     base_ref,
     gen_down_ref,
     critic_down_ref,
@@ -67,7 +66,7 @@
         read.start()
     for read in reads:
         read.wait()
-    group = place_ref[0]
+    group = lax.axis_index("group")
 
     def both(gen, critic):
         gen, critic = gen.astype(F32), critic.astype(F32)
@@ -153,8 +152,7 @@
 def forward_kernel(
     place_ref,
     sigma_ref,
-    latent_ref,
-    fresh_ref,
+    latents_ref,
     prompt_ref,
     latent_in_ref,
     modulation_ref,
@@ -270,14 +268,14 @@
 
             return carry
 
-        lax.fori_loop(0, HEADS, head, 0, unroll=2)
+        lax.fori_loop(0, HEADS, head, 0, unroll=3)
         return dot(velocity_out_ref[...], attended_now[...], 1, 1)
 
-    latent = latent_ref[...]
+    latent = latents_ref[0]
     sample = latent - readout(latent, 1.0, 0, None, lambda f: f())
     sample_ref[...] = sample
     sample_again_ref[...] = sample
-    noised = (1.0 - sigma) * sample + sigma * fresh_ref[...]
+    noised = (1.0 - sigma) * sample + sigma * latents_ref[1]
     velocity = readout(noised, sigma, 1, group.astype(F32), pl.when(group == 1))
     velocity_ref[...] = velocity
     narrow_velocity_ref[...] = velocity.astype(BF)
@@ -287,7 +285,7 @@
     place_ref,
     sigma_ref,
     sample_ref,
-    fresh_ref,
+    latents_ref,
     own_ref,
     fake_ref,
     prompt_ref,
@@ -312,13 +310,13 @@
     sigma = sigma_ref[0, 0]
     sample = sample_ref[...]
     own = own_ref[...]
-    noised = (1.0 - sigma) * sample + sigma * fresh_ref[...]
+    noised = (1.0 - sigma) * sample + sigma * latents_ref[1]
     clean_real = noised - sigma * own
     clean_fake = noised - sigma * fake_ref[...].astype(F32)
     distance = jnp.sum(jnp.sum(jnp.abs(sample - clean_real), axis=1, keepdims=True), axis=0, keepdims=True)
     spread = distance * (1.0 / (IMG * CH)) + 1e-05
     cot_gen = -(clean_fake - clean_real) / spread
-    cot_critic = 2.0 * (own - (fresh_ref[...] - sample)) / (IMG * CH)
+    cot_critic = 2.0 * (own - (latents_ref[1] - sample)) / (IMG * CH)
     cotangent = jnp.where(flag == 0, cot_gen, cot_critic).T.astype(BF)
 
     def head(index, carry):
@@ -410,8 +408,7 @@
         ]
         return lax.ppermute(array, ("group", "fsdp"), pairs)
 
-    latent = latent_noise[0].T
-    fresh = fresh_noise[0].T
+    latents = jnp.stack([latent_noise[0].T, fresh_noise[0].T])
     text = text_states[0]
     gain = modulation.reshape(1, HW)
     out_map = velocity_out.T
@@ -421,7 +418,7 @@
         pack_kernel,
         "pack",
         60,
-        1,
+        0,
         [((devices, shard, EIGHTH + SIDE + PART), BF)],
         [
             pltpu.VMEM((shard, 3 * HW), BF),
@@ -431,13 +428,12 @@
             pltpu.SemaphoreType.DMA((5,)),
             pltpu.SemaphoreType.DMA((WRITES,)),
         ],
-        place,
         base_qkv,
         gen_down,
         critic_down,
         gen_up.transpose(0, 2, 1),
         critic_up.transpose(0, 2, 1),
-        far=(1, 2, 3, 4, 5),
+        far=(0, 1, 2, 3, 4),
         far_out=(0,),
     )
     packed = lax.all_to_all(packed, "fsdp", 0, 0).reshape(HW, EIGHTH + SIDE + PART)
@@ -515,8 +511,7 @@
         ],
         place,
         sigma,
-        latent,
-        fresh,
+        latents,
         prompt,
         latent_in,
         gain,
@@ -525,7 +520,7 @@
         *pieces,
         packed,
         packed_core,
-        far=(13, 14),
+        far=(12, 13),
     )
     fake_velocity = lax.ppermute(narrow_velocity, "group", [(1, 0)])
     half = (devices // 2, shard, SIDE)
@@ -544,7 +539,7 @@
         place,
         sigma,
         sample_again,
-        fresh,
+        latents,
         velocity,
         fake_velocity,
         prompt,

time: 143 us -> 143 us (level)
  waiting for transfers between devices: 53.6 us -> 51.1 us
    all_to_all x1, waiting for transfers between devices: 9.35 us -> 5.04 us  [per_device(): fold = lax.all_to_all(share, 'fsdp', 0, 0).reshape(devices * SHARE, PART)]
    ppermute x9, waiting for transfers between devices: 27 us -> 28.9 us  [move(): return lax.ppermute(array, ('group', 'fsdp'), pairs)]
  transfers between devices with their start and end apart: 12 -> 12, of which waited for: 9 -> 8; matrix products, arithmetic and copies ran while one was open for 0% -> 1% of each run, Pallas kernels for 3% -> 4%
where the time goes in v10:
time: 143 us; the launch traced here: 142 us
  waiting for transfers between devices  51.1 us (36%)
  Pallas kernels  36.5 us (26%)
  starting transfers between devices  25.9 us (18%)
  blocking collectives  19 us (13%)
  local copies, waits for them, and re-layouts  7.14 us (5%)
  between operations  1.47 us (1%)
    pallas_call x9, Pallas kernels, run(): pl.pallas_call(kernel, out_shape=shapes, in_specs=[pl.BlockSpec(memory_sp...  36.5 us
    ppermute x9, waiting for transfers between devices, move(): return lax.ppermute(array, ('group', 'fsdp'), pairs)  28.9 us
    all_to_all x1, blocking collectives, per_device(): shares = lax.all_to_all(sums, 'fsdp', 0, 0, axis_index_groups=parities)  19 us
    all_to_all x1, waiting for transfers between devices, per_device(): lax.all_to_all(packed, 'fsdp', 0, 0).reshape(HW, EIGHTH + SIDE + PART)  11.2 us
    all_to_all x1, starting transfers between devices, per_device(): lax.all_to_all(packed, 'fsdp', 0, 0).reshape(HW, EIGHTH + SIDE + PART)  9.52 us
    ppermute x9, starting transfers between devices, move(): return lax.ppermute(array, ('group', 'fsdp'), pairs)  9.51 us
    unnamed x22, local copies, waits for them, and re-layouts  7.13 us
    ppermute x1, waiting for transfers between devices, per_device(): fake_velocity = lax.ppermute(narrow_velocity, 'group', [(1, 0)])  6.01 us
  transfers between devices with their start and end apart: 12, of which 8 were waited for; matrix products, arithmetic and copies ran while one was open for 1% of the time, Pallas kernels for 4%

profile of v10, /device:TPU:0, one launch (start us, length us, event | category | flops | bytes accessed | tf_op | source)
XLA Modules:
  0.0 142.1 jit_solution(4034939648077957067)
XLA Ops:
  0.6 2.7 %pack.1 = bf16[64,24,896]{2,1,0:T(8,128)(2,1)} custom-call(bf16[24,4608]{1,0:T(8,128)(2,1)} %base_ref.1, bf16[24,192]{1,0:T(8,128)(2,1)} %gen_down_ref.1, bf16[24,192]{1,0:T(8,128)(2,1)} %critic_down_ref.1, bf16[3,24,64]{2,1,0:T(8,128)(2,1)} %bitcast.39, bf16[3,24,64]{2,1,0:T(8,128)(2,1)} %bitcast.40), custom_call_target="tpu_custom_call" | custom-call | tf_op jit(solution)/shard_map/pack/pallas_call | solution.py:363
  3.3 0.0 copy-start.5
  3.4 0.0 copy-start.10
  3.4 9.5 %all-to-all-start = ((bf16[64,24,896]{2,1,0:T(8,128)(2,1)}), bf16[64,24,896]{2,1,0:T(8,128)(2,1)S(1)}, u32[]{:S(2)}, u32[]{:S(2)}) async-start(bf16[64,24,896]{2,1,0:T(8,128)(2,1)} %pack.1), calls=%async_computation | async-start | bytes 5505024 | tf_op jit(solution)/shard_map/all_to_all | solution.py:439
  12.9 0.0 copy-start.3
  12.9 0.0 copy-done.5
  12.9 3.5 %collective-permute-start.2 = (bf16[128,1536]{1,0:T(8,128)(2,1)S(1)}, bf16[128,1536]{1,0:T(8,128)(2,1)S(1)}, u32[]{:S(2)}, u32[]{:S(2)}) collective-permute-start(bf16[128,1536]{1,0:T(8,128)(2,1)S(1)} %bitcast.33), channel_id=1, source_target_pairs={{0,67},{1,66},{2,65},{3,64},{4,71},{5,70},{6,69},{7,68},{8,75},{9,... | collective-permute-start | bytes 1179656 | tf_op jit(solution)/shard_map/ppermute | solution.py:409
  16.4 0.3 collective-permute-start.1
  16.8 0.0 collective-permute-start
  16.8 9.1 %collective-permute-done.2.text_3_ref = bf16[128,1536]{1,0:T(8,128)(2,1)S(1)} collective-permute-done((bf16[128,1536]{1,0:T(8,128)(2,1)S(1)}, bf16[128,1536]{1,0:T(8,128)(2,1)S(1)}, u32[]{:S(2)}, u32[]{:S(2)}) %collective-permute-start.2) | collective-permute-done | bytes 393248 | tf_op jit(solution)/shard_map/ppermute | solution.py:409
  26.0 8.6 %collective-permute-done.1.text_2_ref = bf16[128,1536]{1,0:T(8,128)(2,1)S(1)} collective-permute-done((bf16[128,1536]{1,0:T(8,128)(2,1)S(1)}, bf16[128,1536]{1,0:T(8,128)(2,1)S(1)}, u32[]{:S(2)}, u32[]{:S(2)}) %collective-permute-start.1) | collective-permute-done | bytes 393248 | tf_op jit(solution)/shard_map/ppermute | solution.py:409
  34.6 0.0 collective-permute-done.text_1_ref
  34.6 1.0 copy-done.6
  35.6 0.5 prompts.1
  36.1 1.1 copy-done.1
  37.2 11.2 %all-to-all-done = bf16[64,24,896]{2,1,0:T(8,128)(2,1)S(1)} async-done(((bf16[64,24,896]{2,1,0:T(8,128)(2,1)}), bf16[64,24,896]{2,1,0:T(8,128)(2,1)S(1)}, u32[]{:S(2)}, u32[]{:S(2)}) %all-to-all-start) | async-done | bytes 2752544 | tf_op jit(solution)/shard_map/all_to_all | solution.py:439
  48.4 0.4 collective-permute-start.3
  48.9 2.0 %fold.1 = bf16[64,72,128]{2,1,0:T(8,128)(2,1)S(1)} custom-call(bf16[64,1536]{1,0:T(8,128)(2,1)S(1)} %copy-done.3, f32[1,1536]{1,0:T(1,128)S(1)} %reshape.19.modulation_ref, bf16[1536,896]{1,0:T(8,128)(2,1)S(1)} %bitcast.28), custom_call_target="tpu_custom_call" | custom-call | tf_op jit(solution)/shard_map/fold/pallas_call | solution.py:363
  50.9 1.0 copy-done
  52.0 5.6 %all-to-all-start.1 = ((bf16[64,72,128]{2,1,0:T(8,128)(2,1)}), bf16[64,72,128]{2,1,0:T(8,128)(2,1)}, u32[]{:S(2)}, u32[]{:S(2)}) async-start(bf16[64,72,128]{2,1,0:T(8,128)(2,1)} %copy-done), calls=%async_computation.1 | async-start | bytes 2359296 | tf_op jit(solution)/shard_map/all_to_all | solution.py:462
  57.6 0.0 collective-permute-done.3.packed_core_ref
  57.6 0.0 copy-start.2
  57.6 1.4 copy-done.2
  59.0 1.8 %mix.1 = (bf16[256,384]{1,0:T(8,128)(2,1)S(1)}, bf16[256,384]{1,0:T(8,128)(2,1)}) custom-call(bf16[512,1536]{1,0:T(8,128)(2,1)S(1)} %copy-done.2, bf16[1536,896]{1,0:T(8,128)(2,1)S(1)} %bitcast.29), custom_call_target="tpu_custom_call" | custom-call | tf_op jit(solution)/shard_map/mix/pallas_call | solution.py:363
  60.8 0.7 copy-done.7
  61.5 0.0 collective-permute-start.4
  62.1 1.1 collective-permute-done.4.received_ref
  63.3 0.9 copy-done.8
  64.2 1.7 %pair.1 = (bf16[2,128,384]{2,1,0:T(8,128)(2,1)}, bf16[2,128,384]{2,1,0:T(8,128)(2,1)}) custom-call(bf16[256,384]{1,0:T(8,128)(2,1)S(1)} %copy-done.8, bf16[256,384]{1,0:T(8,128)(2,1)} %collective-permute-done.4.received_ref), custom_call_target="tpu_custom_call" | custom-call | tf_op jit(solution)/shard_map/pair/pallas_call | solution.py:363
  65.9 3.6 %collective-permute-start.7 = (bf16[2,128,384]{2,1,0:T(8,128)(2,1)}, bf16[2,128,384]{2,1,0:T(8,128)(2,1)}, u32[]{:S(2)}, u32[]{:S(2)}) collective-permute-start(bf16[2,128,384]{2,1,0:T(8,128)(2,1)} %get-tuple-element.38), channel_id=1, source_target_pairs={{0,66},{1,67},{2,64},{3,65},{4,70},{5,71},{6,68},{7,69},{8,74},{9,... | collective-permute-start | bytes 589832 | tf_op jit(solution)/shard_map/ppermute | solution.py:409
  69.5 0.0 collective-permute-start.6
  69.5 1.5 %collective-permute-start.5 = (bf16[2,128,384]{2,1,0:T(8,128)(2,1)}, bf16[2,128,384]{2,1,0:T(8,128)(2,1)}, u32[]{:S(2)}, u32[]{:S(2)}) collective-permute-start(bf16[2,128,384]{2,1,0:T(8,128)(2,1)} %get-tuple-element.37.text_0_ref), channel_id=1, source_target_pairs={{0,64},{1,65},{2,66},{3,67},{4,68},{5,69},{6,70},{7,71},{8,72},{9,... | collective-permute-start | bytes 589832 | tf_op jit(solution)/shard_map/ppermute | solution.py:409
  71.0 0.1 pad_add_fusion.place_ref
  71.1 0.8 pad_maximum_fusion.latents_ref
  71.9 5.0 %all-to-all-done.1 = bf16[64,72,128]{2,1,0:T(8,128)(2,1)} async-done(((bf16[64,72,128]{2,1,0:T(8,128)(2,1)}), bf16[64,72,128]{2,1,0:T(8,128)(2,1)}, u32[]{:S(2)}, u32[]{:S(2)}) %all-to-all-start.1) | async-done | bytes 1179680 | tf_op jit(solution)/shard_map/all_to_all | solution.py:462
  77.0 8.0 %collective-permute-done.5.text_1_ref = bf16[2,128,384]{2,1,0:T(8,128)(2,1)} collective-permute-done((bf16[2,128,384]{2,1,0:T(8,128)(2,1)}, bf16[2,128,384]{2,1,0:T(8,128)(2,1)}, u32[]{:S(2)}, u32[]{:S(2)}) %collective-permute-start.5) | collective-permute-done | bytes 196640 | tf_op jit(solution)/shard_map/ppermute | solution.py:409
  85.0 0.0 collective-permute-done.7.text_3_ref
  85.0 0.0 collective-permute-done.6.text_2_ref
  85.0 0.9 copy-done.4
  85.9 19.6 %forward.1 = (f32[64,256]{1,0:T(8,128)}, f32[64,256]{1,0:T(8,128)S(1)}, f32[64,256]{1,0:T(8,128)S(1)}, bf16[64,256]{1,0:T(8,128)(2,1)S(1)}, bf16[256,1536]{1,0:T...) custom-call(s32[3]{0:T(128)S(1)} %pad_add_fusion.place_ref, ...), custom_call_target="tpu_custom_call" | custom-call | tf_op jit(solution)/shard_map/forward/pallas_call | solution.py:363
  105.6 1.3 collective-permute-start.8
  106.9 6.0 %collective-permute-done.8.fake_ref = bf16[64,256]{1,0:T(8,128)(2,1)S(1)} collective-permute-done((bf16[64,256]{1,0:T(8,128)(2,1)S(1)}, bf16[64,256]{1,0:T(8,128)(2,1)S(1)}, u32[]{:S(2)}, u32[]{:S(2)}) %collective-permute-start.8) | collective-permute-done | bytes 32800 | tf_op jit(solution)/shard_map/ppermute | solution.py:525
  112.9 7.3 %backward.1 = (f32[32,24,384]{2,1,0:T(8,128)S(1)}, bf16[32,24,384]{2,1,0:T(8,128)(2,1)S(1)}) custom-call(s32[3]{0:T(128)S(1)} %pad_add_fusion.place_ref, f32[1,1]{1,0:T(1,128)} %bitcast.3.sigma_ref, f32[64,256]{1,0:T(8,128)S(1)} %get-tuple-element.41.sample_ref, f32[2,64,256]{2,1,0:T(8,128)S(1)} %pad_maximum_fusion.latents_ref, ...), custom_call_target="tpu_custom_call" | custom-call | tf_op jit(solution)/shard_map/backward/pallas_call | solution.py:363
  120.2 0.1 collective-permute-start.9
  120.3 2.0 %collective-permute-done.9.received_ref = bf16[32,24,384]{2,1,0:T(8,128)(2,1)S(1)} collective-permute-done((bf16[32,24,384]{2,1,0:T(8,128)(2,1)S(1)}, bf16[32,24,384]{2,1,0:T(8,128)(2,1)S(1)}, u32[]{:S(2)}, u32[]{:S(2)}) %collective-permute-start.9) | collective-permute-done | bytes 589856 | tf_op jit(solution)/shard_map/ppermute | solution.py:409
  122.3 0.1 add.9
  122.4 19.0 %all_to_all.15.shares_ref = bf16[32,24,384]{2,1,0:T(8,128)(2,1)S(1)} all-to-all(bf16[32,24,384]{2,1,0:T(8,128)(2,1)S(1)} %add.9), channel_id=1, replica_groups={{0,2,4,6,8,10,12,14,16,18,20,22,24,26,28,30,32,34,36,38,40,42,44,46,48,..., dimensions={0} | all-to-all | bytes 1179648 | tf_op jit(solution)/shard_map/all_to_all | solution.py:552
  141.3 0.8 total.1
  (11 shorter events, 0.0 us)
Async XLA Ops:
  3.3 9.6 %copy-start.5 = (bf16[1,128,1536]{2,1,0:T(8,128)(2,1)S(1)}, bf16[1,128,1536]{2,1,0:T(8,128)(2,1)}, u32[]{:S(2)}) copy-start(bf16[1,128,1536]{2,1,0:T(8,128)(2,1)} %param.14) | copy-start | bytes 1179652
  3.4 45.5 %copy-start.10 = (f32[1536]{0:T(1024)S(1)}, f32[1536]{0:T(1024)}, u32[]{:S(2)}) copy-start(f32[1536]{0:T(1024)} %param.18) | copy-start | bytes 18436
  3.4 45.1 %all-to-all-start = ((bf16[64,24,896]{2,1,0:T(8,128)(2,1)}), bf16[64,24,896]{2,1,0:T(8,128)(2,1)S(1)}, u32[]{:S(2)}, u32[]{:S(2)}) async-start(bf16[64,24,896]{2,1,0:T(8,128)(2,1)} %pack.1), calls=%async_computation | async-start | bytes 5505024 | tf_op jit(solution)/shard_map/all_to_all | solution.py:439
  12.9 36.0 %copy-start.3 = (bf16[64,1536]{1,0:T(8,128)(2,1)S(1)}, bf16[64,1536]{1,0:T(8,128)(2,1)}, u32[]{:S(2)}) copy-start(bf16[64,1536]{1,0:T(8,128)(2,1)} %latent_in_ref.3) | copy-start | bytes 589828
  12.9 13.0 %collective-permute-start.2 = (bf16[128,1536]{1,0:T(8,128)(2,1)S(1)}, bf16[128,1536]{1,0:T(8,128)(2,1)S(1)}, u32[]{:S(2)}, u32[]{:S(2)}) collective-permute-start(bf16[128,1536]{1,0:T(8,128)(2,1)S(1)} %bitcast.33), channel_id=1, source_target_pairs={{0,67},{1,66},{2,65},{3,64},{4,71},{5,70},{6,69},{7,68},{8,75},{9,... | collective-permute-start | bytes 1179656 | tf_op jit(solution)/shard_map/ppermute | solution.py:409
  16.4 18.1 %collective-permute-start.1 = (bf16[128,1536]{1,0:T(8,128)(2,1)S(1)}, bf16[128,1536]{1,0:T(8,128)(2,1)S(1)}, u32[]{:S(2)}, u32[]{:S(2)}) collective-permute-start(bf16[128,1536]{1,0:T(8,128)(2,1)S(1)} %bitcast.34), channel_id=1, source_target_pairs={{0,66},{1,67},{2,64},{3,65},{4,70},{5,71},{6,68},{7,69},{8,74},{9,... | collective-permute-start | bytes 1179656 | tf_op jit(solution)/shard_map/ppermute | solution.py:409
  16.8 17.8 %collective-permute-start = (bf16[128,1536]{1,0:T(8,128)(2,1)S(1)}, bf16[128,1536]{1,0:T(8,128)(2,1)S(1)}, u32[]{:S(2)}, u32[]{:S(2)}) collective-permute-start(bf16[128,1536]{1,0:T(8,128)(2,1)S(1)} %bitcast.35), channel_id=1, source_target_pairs={{0,1},{1,0},{2,3},{3,2},{4,5},{5,4},{6,7},{7,6},{8,9},{9,8},{10,11... | collective-permute-start | bytes 1179656 | tf_op jit(solution)/shard_map/ppermute | solution.py:409
  34.6 1.0 copy-start.6
  36.1 1.2 copy-start.1
  48.4 9.2 %collective-permute-start.3 = (bf16[1536,896]{1,0:T(8,128)(2,1)S(1)}, bf16[1536,896]{1,0:T(8,128)(2,1)}, u32[]{:S(2)}, u32[]{:S(2)}) collective-permute-start(bf16[1536,896]{1,0:T(8,128)(2,1)S(1)} %bitcast.27), channel_id=1, source_target_pairs={{0,1},{1,0},{2,3},{3,2},{4,5},{5,4},{6,7},{7,6},{8,9},{9,8},{10,11... | collective-permute-start | bytes 8257544 | tf_op jit(solution)/shard_map/ppermute | solution.py:409
  50.9 1.0 copy-start
  52.0 25.0 %all-to-all-start.1 = ((bf16[64,72,128]{2,1,0:T(8,128)(2,1)}), bf16[64,72,128]{2,1,0:T(8,128)(2,1)}, u32[]{:S(2)}, u32[]{:S(2)}) async-start(bf16[64,72,128]{2,1,0:T(8,128)(2,1)} %copy-done), calls=%async_computation.1 | async-start | bytes 2359296 | tf_op jit(solution)/shard_map/all_to_all | solution.py:462
  57.6 1.4 copy-start.2
  59.0 12.1 %copy-start.9 = (f32[1,256,64]{1,2,0:T(8,128)S(1)}, f32[1,256,64]{1,2,0:T(8,128)}, u32[]{:S(2)}) copy-start(f32[1,256,64]{1,2,0:T(8,128)} %param.13) | copy-start | bytes 196612
  60.8 0.7 copy-start.7
  61.5 1.8 %collective-permute-start.4 = (bf16[256,384]{1,0:T(8,128)(2,1)}, bf16[256,384]{1,0:T(8,128)(2,1)}, u32[]{:S(2)}, u32[]{:S(2)}) collective-permute-start(bf16[256,384]{1,0:T(8,128)(2,1)} %get-tuple-element.36), channel_id=1, source_target_pairs={{0,1},{1,0},{2,3},{3,2},{4,5},{5,4},{6,7},{7,6},{8,9},{9,8},{10,11... | collective-permute-start | bytes 589832 | tf_op jit(solution)/shard_map/ppermute | solution.py:409
  63.3 0.9 copy-start.8
  65.9 19.1 %collective-permute-start.7 = (bf16[2,128,384]{2,1,0:T(8,128)(2,1)}, bf16[2,128,384]{2,1,0:T(8,128)(2,1)}, u32[]{:S(2)}, u32[]{:S(2)}) collective-permute-start(bf16[2,128,384]{2,1,0:T(8,128)(2,1)} %get-tuple-element.38), channel_id=1, source_target_pairs={{0,66},{1,67},{2,64},{3,65},{4,70},{5,71},{6,68},{7,69},{8,74},{9,... | collective-permute-start | bytes 589832 | tf_op jit(solution)/shard_map/ppermute | solution.py:409
  69.5 15.5 %collective-permute-start.6 = (bf16[2,128,384]{2,1,0:T(8,128)(2,1)}, bf16[2,128,384]{2,1,0:T(8,128)(2,1)}, u32[]{:S(2)}, u32[]{:S(2)}) collective-permute-start(bf16[2,128,384]{2,1,0:T(8,128)(2,1)} %get-tuple-element.38), channel_id=1, source_target_pairs={{0,2},{1,3},{2,0},{3,1},{4,6},{5,7},{6,4},{7,5},{8,10},{9,11},{10,... | collective-permute-start | bytes 589832 | tf_op jit(solution)/shard_map/ppermute | solution.py:409
  69.5 15.5 %collective-permute-start.5 = (bf16[2,128,384]{2,1,0:T(8,128)(2,1)}, bf16[2,128,384]{2,1,0:T(8,128)(2,1)}, u32[]{:S(2)}, u32[]{:S(2)}) collective-permute-start(bf16[2,128,384]{2,1,0:T(8,128)(2,1)} %get-tuple-element.37.text_0_ref), channel_id=1, source_target_pairs={{0,64},{1,65},{2,66},{3,67},{4,68},{5,69},{6,70},{7,71},{8,72},{9,... | collective-permute-start | bytes 589832 | tf_op jit(solution)/shard_map/ppermute | solution.py:409
  85.0 0.9 copy-start.4
  105.6 7.3 %collective-permute-start.8 = (bf16[64,256]{1,0:T(8,128)(2,1)S(1)}, bf16[64,256]{1,0:T(8,128)(2,1)S(1)}, u32[]{:S(2)}, u32[]{:S(2)}) collective-permute-start(bf16[64,256]{1,0:T(8,128)(2,1)S(1)} %get-tuple-element.43), channel_id=1, source_target_pairs={{64,0},{65,1},{66,2},{67,3},{68,4},{69,5},{70,6},{71,7},{72,8},{73... | collective-permute-start | bytes 98312 | tf_op jit(solution)/shard_map/ppermute | solution.py:525
  120.2 2.1 %collective-permute-start.9 = (bf16[32,24,384]{2,1,0:T(8,128)(2,1)S(1)}, bf16[32,24,384]{2,1,0:T(8,128)(2,1)S(1)}, u32[]{:S(2)}, u32[]{:S(2)}) collective-permute-start(bf16[32,24,384]{2,1,0:T(8,128)(2,1)S(1)} %get-tuple-element.54), channel_id=1, source_target_pairs={{0,1},{1,0},{2,3},{3,2},{4,5},{5,4},{6,7},{7,6},{8,9},{9,8},{10,11... | collective-permute-start | bytes 1769480 | tf_op jit(solution)/shard_map/ppermute | solution.py:409

commit v11 on v6

--- a/solution.py
+++ b/solution.py
@@ -42,7 +42,6 @@
 
 
 def pack_kernel(
-    place_ref,
     base_ref,
     gen_down_ref,
     critic_down_ref,
@@ -67,7 +66,7 @@
         read.start()
     for read in reads:
         read.wait()
-    group = place_ref[0]
+    group = lax.axis_index("group")
 
     def both(gen, critic):
         gen, critic = gen.astype(F32), critic.astype(F32)
@@ -129,6 +128,9 @@
     scaled_in = (latent_in_ref[...].astype(F32) * modulation_ref[...]).astype(BF)
     folds = jnp.concatenate([latent_in_ref[...], scaled_in], axis=0)
     read.wait()
+    side.wait()
+    side = pltpu.make_async_copy(sides, side_ref, read_sem.at[1])
+    side.start()
     share = dot(folds, columns[...]).T[:SHARE].astype(BF)
     batch = shares.shape[0]
     for device in range(batch):
@@ -139,9 +141,6 @@
     ]
     for write in writes:
         write.start()
-    side.wait()
-    side = pltpu.make_async_copy(sides, side_ref, read_sem.at[1])
-    side.start()
     for write in writes:
         write.wait()
     side.wait()
@@ -432,7 +431,7 @@
         pack_kernel,
         "pack",
         60,
-        1,
+        0,
         [((devices, shard, EIGHTH + SIDE + PART), BF)],
         [
             pltpu.VMEM((shard, 3 * HW), BF),
@@ -442,13 +441,12 @@
             pltpu.SemaphoreType.DMA((5,)),
             pltpu.SemaphoreType.DMA((WRITES,)),
         ],
-        place,
         base_qkv,
         gen_down,
         critic_down,
         gen_up.transpose(0, 2, 1),
         critic_up.transpose(0, 2, 1),
-        far=(1, 2, 3, 4, 5),
+        far=(0, 1, 2, 3, 4),
         out_space=pl.ANY,
     )
     packed = lax.all_to_all(packed, "fsdp", 0, 0).reshape(HW, EIGHTH + SIDE + PART)

time: 142 us -> 140 us (0.986)
  no operation moved by 1% of the time
where the time goes in v11:
time: 140 us
  waiting for transfers between devices  55.8 us (40%)
  Pallas kernels  37.3 us (27%)
  starting transfers between devices  25.4 us (18%)
  blocking collectives  18.7 us (13%)
  between operations  1.45 us (1%)
    pallas_call x9, Pallas kernels, run(): pl.pallas_call(kernel, out_shape=shapes, in_specs=[pl.BlockSpec(memory_sp...  37.3 us
    ppermute x9, waiting for transfers between devices, move(): return lax.ppermute(array, ('group', 'fsdp'), pairs)  26.9 us
    all_to_all x1, blocking collectives, per_device(): shares = lax.all_to_all(sums, 'fsdp', 0, 0, axis_index_groups=parities)  18.7 us
    all_to_all x1, waiting for transfers between devices, per_device(): lax.all_to_all(packed, 'fsdp', 0, 0).reshape(HW, EIGHTH + SIDE + PART)  13.3 us
    all_to_all x1, starting transfers between devices, per_device(): lax.all_to_all(packed, 'fsdp', 0, 0).reshape(HW, EIGHTH + SIDE + PART)  9.75 us
    all_to_all x1, waiting for transfers between devices, per_device(): fold = lax.all_to_all(share, 'fsdp', 0, 0).reshape(devices * SHARE, PART)  9.58 us
    ppermute x9, starting transfers between devices, move(): return lax.ppermute(array, ('group', 'fsdp'), pairs)  9.04 us
    ppermute x1, waiting for transfers between devices, per_device(): fake_velocity = lax.ppermute(narrow_velocity, 'group', [(1, 0)])  6.01 us
  transfers between devices with their start and end apart: 12, of which 9 were waited for; matrix products, arithmetic and copies ran while one was open for 0% of the time, Pallas kernels for 3%

profile of v11, /device:TPU:0, one launch (start us, length us, event | category | flops | bytes accessed | tf_op | source)
XLA Modules:
  0.0 140.0 jit_solution(8519666858525958438)
XLA Ops:
  0.6 2.7 %pack.1 = bf16[64,24,896]{2,1,0:T(8,128)(2,1)} custom-call(bf16[24,4608]{1,0:T(8,128)(2,1)} %base_ref.1, bf16[24,192]{1,0:T(8,128)(2,1)} %gen_down_ref.1, bf16[24,192]{1,0:T(8,128)(2,1)} %critic_down_ref.1, bf16[3,24,64]{2,1,0:T(8,128)(2,1)} %bitcast.33, bf16[3,24,64]{2,1,0:T(8,128)(2,1)} %bitcast.34), custom_call_target="tpu_custom_call" | custom-call | tf_op jit(solution)/shard_map/pack/pallas_call | solution.py:378
  3.4 0.0 copy-start.3
  3.4 0.0 copy-start.6
  3.4 9.8 %all-to-all-start = ((bf16[64,24,896]{2,1,0:T(8,128)(2,1)}), bf16[64,24,896]{2,1,0:T(8,128)(2,1)}, u32[]{:S(2)}, u32[]{:S(2)}) async-start(bf16[64,24,896]{2,1,0:T(8,128)(2,1)} %pack.1), calls=%async_computation | async-start | bytes 5505024 | tf_op jit(solution)/shard_map/all_to_all | solution.py:452
  13.2 0.0 copy-done.3
  13.2 3.5 %collective-permute-start.2 = (bf16[128,1536]{1,0:T(8,128)(2,1)S(1)}, bf16[128,1536]{1,0:T(8,128)(2,1)S(1)}, u32[]{:S(2)}, u32[]{:S(2)}) collective-permute-start(bf16[128,1536]{1,0:T(8,128)(2,1)S(1)} %bitcast.26), channel_id=1, source_target_pairs={{0,67},{1,66},{2,65},{3,64},{4,71},{5,70},{6,69},{7,68},{8,75},{9,... | collective-permute-start | bytes 1179656 | tf_op jit(solution)/shard_map/ppermute | solution.py:421
  16.6 0.3 collective-permute-start.1
  17.0 0.0 collective-permute-start
  17.0 0.0 copy-done.6
  17.0 0.0 copy-start.1
  17.0 9.1 %collective-permute-done.2.text_3_ref = bf16[128,1536]{1,0:T(8,128)(2,1)S(1)} collective-permute-done((bf16[128,1536]{1,0:T(8,128)(2,1)S(1)}, bf16[128,1536]{1,0:T(8,128)(2,1)S(1)}, u32[]{:S(2)}, u32[]{:S(2)}) %collective-permute-start.2) | collective-permute-done | bytes 393248 | tf_op jit(solution)/shard_map/ppermute | solution.py:421
  26.1 8.6 %collective-permute-done.1.text_2_ref = bf16[128,1536]{1,0:T(8,128)(2,1)S(1)} collective-permute-done((bf16[128,1536]{1,0:T(8,128)(2,1)S(1)}, bf16[128,1536]{1,0:T(8,128)(2,1)S(1)}, u32[]{:S(2)}, u32[]{:S(2)}) %collective-permute-start.1) | collective-permute-done | bytes 393248 | tf_op jit(solution)/shard_map/ppermute | solution.py:421
  34.7 0.0 collective-permute-done.text_1_ref
  34.7 0.5 prompts.1.prompts_ref.prompt_ref
  35.2 13.3 %all-to-all-done = bf16[64,24,896]{2,1,0:T(8,128)(2,1)} async-done(((bf16[64,24,896]{2,1,0:T(8,128)(2,1)}), bf16[64,24,896]{2,1,0:T(8,128)(2,1)}, u32[]{:S(2)}, u32[]{:S(2)}) %all-to-all-start) | async-done | bytes 2752544 | tf_op jit(solution)/shard_map/all_to_all | solution.py:452
  48.6 0.0 copy-done.1
  48.6 3.3 %fold.1 = (bf16[64,72,128]{2,1,0:T(8,128)(2,1)S(1)}, bf16[1536,384]{1,0:T(8,128)(2,1)}) custom-call(bf16[64,1536]{1,0:T(8,128)(2,1)S(1)} %copy-done.1, f32[1,1536]{1,0:T(1,128)S(1)} %reshape.20.modulation_ref, bf16[1536,896]{1,0:T(8,128)(2,1)} %bitcast.10.packed_ref), custom_call_target="tpu_custom_call" | custom-call | tf_op jit(solution)/shard_map/fold/pallas_call | solution.py:378
  51.9 0.0 copy-start
  51.9 1.0 copy-done
  53.0 0.4 collective-permute-start.3
  53.4 5.4 %all-to-all-start.1 = ((bf16[64,72,128]{2,1,0:T(8,128)(2,1)}), bf16[64,72,128]{2,1,0:T(8,128)(2,1)S(1)}, u32[]{:S(2)}, u32[]{:S(2)}) async-start(bf16[64,72,128]{2,1,0:T(8,128)(2,1)} %copy-done), calls=%async_computation.1 | async-start | bytes 2359296 | tf_op jit(solution)/shard_map/all_to_all | solution.py:474
  58.8 0.0 copy-start.2
  58.8 0.0 copy-start.4
  58.8 0.0 copy-start.5
  58.8 0.0 collective-permute-done.3.side_core_ref
  58.8 2.3 %mix.1 = (bf16[256,384]{1,0:T(8,128)(2,1)S(1)}, bf16[256,384]{1,0:T(8,128)(2,1)S(1)}) custom-call(bf16[512,1536]{1,0:T(8,128)(2,1)S(1)} %prompts.1.prompts_ref.prompt_ref, bf16[1536,896]{1,0:T(8,128)(2,1)} %bitcast.10.packed_ref), custom_call_target="tpu_custom_call" | custom-call | tf_op jit(solution)/shard_map/mix/pallas_call | solution.py:378
  61.2 0.1 collective-permute-start.4
  61.3 1.4 collective-permute-done.4.received_ref
  62.7 0.7 pair.1
  63.4 3.6 %collective-permute-start.5 = (bf16[2,128,384]{2,1,0:T(8,128)(2,1)S(1)}, bf16[2,128,384]{2,1,0:T(8,128)(2,1)}, u32[]{:S(2)}, u32[]{:S(2)}) collective-permute-start(bf16[2,128,384]{2,1,0:T(8,128)(2,1)S(1)} %get-tuple-element.37.text_0_ref), channel_id=1, source_target_pairs={{0,64},{1,65},{2,66},{3,67},{4,68},{5,69},{6,70},{7,71},{8,72},{9,... | collective-permute-start | bytes 589832 | tf_op jit(solution)/shard_map/ppermute | solution.py:421
  67.0 0.7 collective-permute-start.7
  67.6 0.3 collective-permute-start.6
  68.6 0.1 pad_add_fusion.place_ref
  68.7 9.6 %all-to-all-done.1 = bf16[64,72,128]{2,1,0:T(8,128)(2,1)S(1)} async-done(((bf16[64,72,128]{2,1,0:T(8,128)(2,1)}), bf16[64,72,128]{2,1,0:T(8,128)(2,1)S(1)}, u32[]{:S(2)}, u32[]{:S(2)}) %all-to-all-start.1) | async-done | bytes 1179680 | tf_op jit(solution)/shard_map/all_to_all | solution.py:474
  78.2 3.6 %collective-permute-done.5.text_1_ref = bf16[2,128,384]{2,1,0:T(8,128)(2,1)} collective-permute-done((bf16[2,128,384]{2,1,0:T(8,128)(2,1)S(1)}, bf16[2,128,384]{2,1,0:T(8,128)(2,1)}, u32[]{:S(2)}, u32[]{:S(2)}) %collective-permute-start.5) | collective-permute-done | bytes 196640 | tf_op jit(solution)/shard_map/ppermute | solution.py:421
  81.8 0.0 collective-permute-done.7.text_3_ref
  81.8 2.3 %collective-permute-done.6.text_2_ref = bf16[2,128,384]{2,1,0:T(8,128)(2,1)} collective-permute-done((bf16[2,128,384]{2,1,0:T(8,128)(2,1)}, bf16[2,128,384]{2,1,0:T(8,128)(2,1)}, u32[]{:S(2)}, u32[]{:S(2)}) %collective-permute-start.6) | collective-permute-done | bytes 196640 | tf_op jit(solution)/shard_map/ppermute | solution.py:421
  84.1 0.0 copy-done.2
  84.1 0.0 copy-done.5
  84.1 19.5 %forward.1 = (f32[64,256]{1,0:T(8,128)}, f32[64,256]{1,0:T(8,128)S(1)}, f32[64,256]{1,0:T(8,128)S(1)}, bf16[64,256]{1,0:T(8,128)(2,1)S(1)}, bf16[256,1536]{1,0:T...) custom-call(s32[3]{0:T(128)S(1)} %pad_add_fusion.place_ref, ...), custom_call_target="tpu_custom_call" | custom-call | tf_op jit(solution)/shard_map/forward/pallas_call | solution.py:378
  103.6 1.3 collective-permute-start.8
  104.9 6.0 %collective-permute-done.8.fake_ref = bf16[64,256]{1,0:T(8,128)(2,1)S(1)} collective-permute-done((bf16[64,256]{1,0:T(8,128)(2,1)S(1)}, bf16[64,256]{1,0:T(8,128)(2,1)S(1)}, u32[]{:S(2)}, u32[]{:S(2)}) %collective-permute-start.8) | collective-permute-done | bytes 32800 | tf_op jit(solution)/shard_map/ppermute | solution.py:537
  110.9 7.3 %backward.1 = (f32[32,24,384]{2,1,0:T(8,128)S(1)}, bf16[32,24,384]{2,1,0:T(8,128)(2,1)S(1)}) custom-call(s32[3]{0:T(128)S(1)} %pad_add_fusion.place_ref, f32[1,1]{1,0:T(1,128)} %bitcast.3.sigma_ref, f32[64,256]{1,0:T(8,128)S(1)} %get-tuple-element.41.sample_ref, f32[64,256]{1,0:T(8,128)S(1)} %bitcast.31, f32[64,256]{1,0:T(8,128)S(1)} %get-tuple-element.42.own_ref, ...), custom_call_target="tpu_custom_call" | custom-call | tf_op jit(solution)/shard_map/backward/pallas_call | solution.py:378
  118.2 0.1 collective-permute-start.9
  118.3 2.0 %collective-permute-done.9.received_ref = bf16[32,24,384]{2,1,0:T(8,128)(2,1)S(1)} collective-permute-done((bf16[32,24,384]{2,1,0:T(8,128)(2,1)S(1)}, bf16[32,24,384]{2,1,0:T(8,128)(2,1)S(1)}, u32[]{:S(2)}, u32[]{:S(2)}) %collective-permute-start.9) | collective-permute-done | bytes 589856 | tf_op jit(solution)/shard_map/ppermute | solution.py:421
  120.3 0.2 add.9
  120.4 18.7 %all_to_all.15.shares_ref = bf16[32,24,384]{2,1,0:T(8,128)(2,1)S(1)} all-to-all(bf16[32,24,384]{2,1,0:T(8,128)(2,1)S(1)} %add.9), channel_id=1, replica_groups={{0,2,4,6,8,10,12,14,16,18,20,22,24,26,28,30,32,34,36,38,40,42,44,46,48,..., dimensions={0} | all-to-all | bytes 1179648 | tf_op jit(solution)/shard_map/all_to_all | solution.py:564
  139.2 0.8 total.1
  (2 shorter events, 0.0 us)
Async XLA Ops:
  3.4 9.8 %copy-start.3 = (bf16[1,128,1536]{2,1,0:T(8,128)(2,1)S(1)}, bf16[1,128,1536]{2,1,0:T(8,128)(2,1)}, u32[]{:S(2)}) copy-start(bf16[1,128,1536]{2,1,0:T(8,128)(2,1)} %param.14) | copy-start | bytes 1179652
  3.4 13.6 %copy-start.6 = (f32[1536]{0:T(1024)S(1)}, f32[1536]{0:T(1024)}, u32[]{:S(2)}) copy-start(f32[1536]{0:T(1024)} %param.18) | copy-start | bytes 18436
  3.4 45.2 %all-to-all-start = ((bf16[64,24,896]{2,1,0:T(8,128)(2,1)}), bf16[64,24,896]{2,1,0:T(8,128)(2,1)}, u32[]{:S(2)}, u32[]{:S(2)}) async-start(bf16[64,24,896]{2,1,0:T(8,128)(2,1)} %pack.1), calls=%async_computation | async-start | bytes 5505024 | tf_op jit(solution)/shard_map/all_to_all | solution.py:452
  13.2 13.0 %collective-permute-start.2 = (bf16[128,1536]{1,0:T(8,128)(2,1)S(1)}, bf16[128,1536]{1,0:T(8,128)(2,1)S(1)}, u32[]{:S(2)}, u32[]{:S(2)}) collective-permute-start(bf16[128,1536]{1,0:T(8,128)(2,1)S(1)} %bitcast.26), channel_id=1, source_target_pairs={{0,67},{1,66},{2,65},{3,64},{4,71},{5,70},{6,69},{7,68},{8,75},{9,... | collective-permute-start | bytes 1179656 | tf_op jit(solution)/shard_map/ppermute | solution.py:421
  16.6 18.1 %collective-permute-start.1 = (bf16[128,1536]{1,0:T(8,128)(2,1)S(1)}, bf16[128,1536]{1,0:T(8,128)(2,1)S(1)}, u32[]{:S(2)}, u32[]{:S(2)}) collective-permute-start(bf16[128,1536]{1,0:T(8,128)(2,1)S(1)} %bitcast.27), channel_id=1, source_target_pairs={{0,66},{1,67},{2,64},{3,65},{4,70},{5,71},{6,68},{7,69},{8,74},{9,... | collective-permute-start | bytes 1179656 | tf_op jit(solution)/shard_map/ppermute | solution.py:421
  17.0 17.8 %collective-permute-start = (bf16[128,1536]{1,0:T(8,128)(2,1)S(1)}, bf16[128,1536]{1,0:T(8,128)(2,1)S(1)}, u32[]{:S(2)}, u32[]{:S(2)}) collective-permute-start(bf16[128,1536]{1,0:T(8,128)(2,1)S(1)} %bitcast.28), channel_id=1, source_target_pairs={{0,1},{1,0},{2,3},{3,2},{4,5},{5,4},{6,7},{7,6},{8,9},{9,8},{10,11... | collective-permute-start | bytes 1179656 | tf_op jit(solution)/shard_map/ppermute | solution.py:421
  17.0 31.6 %copy-start.1 = (bf16[64,1536]{1,0:T(8,128)(2,1)S(1)}, bf16[64,1536]{1,0:T(8,128)(2,1)}, u32[]{:S(2)}) copy-start(bf16[64,1536]{1,0:T(8,128)(2,1)} %latent_in_ref.3) | copy-start | bytes 589828
  51.9 1.0 copy-start
  53.0 5.9 %collective-permute-start.3 = (bf16[1536,384]{1,0:T(8,128)(2,1)}, bf16[1536,384]{1,0:T(8,128)(2,1)}, u32[]{:S(2)}, u32[]{:S(2)}) collective-permute-start(bf16[1536,384]{1,0:T(8,128)(2,1)} %get-tuple-element.32.side_own_ref), channel_id=1, source_target_pairs={{0,1},{1,0},{2,3},{3,2},{4,5},{5,4},{6,7},{7,6},{8,9},{9,8},{10,11... | collective-permute-start | bytes 3538952 | tf_op jit(solution)/shard_map/ppermute | solution.py:421
  53.4 24.8 %all-to-all-start.1 = ((bf16[64,72,128]{2,1,0:T(8,128)(2,1)}), bf16[64,72,128]{2,1,0:T(8,128)(2,1)S(1)}, u32[]{:S(2)}, u32[]{:S(2)}) async-start(bf16[64,72,128]{2,1,0:T(8,128)(2,1)} %copy-done), calls=%async_computation.1 | async-start | bytes 2359296 | tf_op jit(solution)/shard_map/all_to_all | solution.py:474
  58.8 25.3 %copy-start.2 = (bf16[1536,64]{0,1:T(8,128)(2,1)S(1)}, bf16[1536,64]{0,1:T(8,128)(2,1)}, u32[]{:S(2)}) copy-start(bf16[1536,64]{0,1:T(8,128)(2,1)} %param.19) | copy-start | bytes 589828
  58.8 25.3 %copy-start.4 = (f32[1,256,64]{1,2,0:T(8,128)S(1)}, f32[1,256,64]{1,2,0:T(8,128)}, u32[]{:S(2)}) copy-start(f32[1,256,64]{1,2,0:T(8,128)} %param.13) | copy-start | bytes 196612
  58.8 25.3 %copy-start.5 = (f32[1,256,64]{1,2,0:T(8,128)S(1)}, f32[1,256,64]{1,2,0:T(8,128)}, u32[]{:S(2)}) copy-start(f32[1,256,64]{1,2,0:T(8,128)} %param.12) | copy-start | bytes 196612
  61.2 1.5 %collective-permute-start.4 = (bf16[256,384]{1,0:T(8,128)(2,1)S(1)}, bf16[256,384]{1,0:T(8,128)(2,1)S(1)}, u32[]{:S(2)}, u32[]{:S(2)}) collective-permute-start(bf16[256,384]{1,0:T(8,128)(2,1)S(1)} %get-tuple-element.36), channel_id=1, source_target_pairs={{0,1},{1,0},{2,3},{3,2},{4,5},{5,4},{6,7},{7,6},{8,9},{9,8},{10,11... | collective-permute-start | bytes 589832 | tf_op jit(solution)/shard_map/ppermute | solution.py:421
  63.4 18.4 %collective-permute-start.5 = (bf16[2,128,384]{2,1,0:T(8,128)(2,1)S(1)}, bf16[2,128,384]{2,1,0:T(8,128)(2,1)}, u32[]{:S(2)}, u32[]{:S(2)}) collective-permute-start(bf16[2,128,384]{2,1,0:T(8,128)(2,1)S(1)} %get-tuple-element.37.text_0_ref), channel_id=1, source_target_pairs={{0,64},{1,65},{2,66},{3,67},{4,68},{5,69},{6,70},{7,71},{8,72},{9,... | collective-permute-start | bytes 589832 | tf_op jit(solution)/shard_map/ppermute | solution.py:421
  67.0 14.8 %collective-permute-start.7 = (bf16[2,128,384]{2,1,0:T(8,128)(2,1)}, bf16[2,128,384]{2,1,0:T(8,128)(2,1)}, u32[]{:S(2)}, u32[]{:S(2)}) collective-permute-start(bf16[2,128,384]{2,1,0:T(8,128)(2,1)} %get-tuple-element.38), channel_id=1, source_target_pairs={{0,66},{1,67},{2,64},{3,65},{4,70},{5,71},{6,68},{7,69},{8,74},{9,... | collective-permute-start | bytes 589832 | tf_op jit(solution)/shard_map/ppermute | solution.py:421
  67.6 16.4 %collective-permute-start.6 = (bf16[2,128,384]{2,1,0:T(8,128)(2,1)}, bf16[2,128,384]{2,1,0:T(8,128)(2,1)}, u32[]{:S(2)}, u32[]{:S(2)}) collective-permute-start(bf16[2,128,384]{2,1,0:T(8,128)(2,1)} %get-tuple-element.38), channel_id=1, source_target_pairs={{0,2},{1,3},{2,0},{3,1},{4,6},{5,7},{6,4},{7,5},{8,10},{9,11},{10,... | collective-permute-start | bytes 589832 | tf_op jit(solution)/shard_map/ppermute | solution.py:421
  103.6 7.3 %collective-permute-start.8 = (bf16[64,256]{1,0:T(8,128)(2,1)S(1)}, bf16[64,256]{1,0:T(8,128)(2,1)S(1)}, u32[]{:S(2)}, u32[]{:S(2)}) collective-permute-start(bf16[64,256]{1,0:T(8,128)(2,1)S(1)} %get-tuple-element.43), channel_id=1, source_target_pairs={{64,0},{65,1},{66,2},{67,3},{68,4},{69,5},{70,6},{71,7},{72,8},{73... | collective-permute-start | bytes 98312 | tf_op jit(solution)/shard_map/ppermute | solution.py:537
  118.2 2.1 %collective-permute-start.9 = (bf16[32,24,384]{2,1,0:T(8,128)(2,1)S(1)}, bf16[32,24,384]{2,1,0:T(8,128)(2,1)S(1)}, u32[]{:S(2)}, u32[]{:S(2)}) collective-permute-start(bf16[32,24,384]{2,1,0:T(8,128)(2,1)S(1)} %get-tuple-element.54), channel_id=1, source_target_pairs={{0,1},{1,0},{2,3},{3,2},{4,5},{5,4},{6,7},{7,6},{8,9},{9,8},{10,11... | collective-permute-start | bytes 1769480 | tf_op jit(solution)/shard_map/ppermute | solution.py:421

commit v12 on v11

--- a/solution.py
+++ b/solution.py
@@ -455,7 +455,7 @@
     share, side_own = run(
         fold_kernel,
         "fold",
-        16,
+        60,
         0,
         [((devices, SHARE, PART), BF), ((HW, SIDE), BF)],
         [

time: 140 us -> 141 us (level)
  no operation moved by 1% of the time
where the time goes in v12:
time: 141 us; the launch traced here: 140 us
  waiting for transfers between devices  55.2 us (39%)
  Pallas kernels  37.5 us (27%)
  starting transfers between devices  25.5 us (18%)
  blocking collectives  18.7 us (13%)
  local copies, waits for them, and re-layouts  1.91 us (1%)
  between operations  1.47 us (1%)
    pallas_call x9, Pallas kernels, run(): pl.pallas_call(kernel, out_shape=shapes, in_specs=[pl.BlockSpec(memory_sp...  37.5 us
    ppermute x9, waiting for transfers between devices, move(): return lax.ppermute(array, ('group', 'fsdp'), pairs)  26.4 us
    all_to_all x1, blocking collectives, per_device(): shares = lax.all_to_all(sums, 'fsdp', 0, 0, axis_index_groups=parities)  18.7 us
    all_to_all x1, waiting for transfers between devices, per_device(): lax.all_to_all(packed, 'fsdp', 0, 0).reshape(HW, EIGHTH + SIDE + PART)  13.3 us
    all_to_all x1, starting transfers between devices, per_device(): lax.all_to_all(packed, 'fsdp', 0, 0).reshape(HW, EIGHTH + SIDE + PART)  9.75 us
    all_to_all x1, waiting for transfers between devices, per_device(): fold = lax.all_to_all(share, 'fsdp', 0, 0).reshape(devices * SHARE, PART)  9.52 us
    ppermute x9, starting transfers between devices, move(): return lax.ppermute(array, ('group', 'fsdp'), pairs)  9.12 us
    ppermute x1, waiting for transfers between devices, per_device(): fake_velocity = lax.ppermute(narrow_velocity, 'group', [(1, 0)])  6.01 us
  transfers between devices with their start and end apart: 12, of which 9 were waited for; matrix products, arithmetic and copies ran while one was open for 0% of the time, Pallas kernels for 3%

profile of v12, /device:TPU:0, one launch (start us, length us, event | category | flops | bytes accessed | tf_op | source)
XLA Modules:
  0.0 140.3 jit_solution(13591164609110328896)
XLA Ops:
  0.6 2.7 %pack.1 = bf16[64,24,896]{2,1,0:T(8,128)(2,1)} custom-call(bf16[24,4608]{1,0:T(8,128)(2,1)} %base_ref.1, bf16[24,192]{1,0:T(8,128)(2,1)} %gen_down_ref.1, bf16[24,192]{1,0:T(8,128)(2,1)} %critic_down_ref.1, bf16[3,24,64]{2,1,0:T(8,128)(2,1)} %bitcast.33, bf16[3,24,64]{2,1,0:T(8,128)(2,1)} %bitcast.34), custom_call_target="tpu_custom_call" | custom-call | tf_op jit(solution)/shard_map/pack/pallas_call | solution.py:378
  3.4 0.0 copy-start.3
  3.4 0.0 copy-start.7
  3.4 9.8 %all-to-all-start = ((bf16[64,24,896]{2,1,0:T(8,128)(2,1)}), bf16[64,24,896]{2,1,0:T(8,128)(2,1)}, u32[]{:S(2)}, u32[]{:S(2)}) async-start(bf16[64,24,896]{2,1,0:T(8,128)(2,1)} %pack.1), calls=%async_computation | async-start | bytes 5505024 | tf_op jit(solution)/shard_map/all_to_all | solution.py:452
  13.2 3.5 %collective-permute-start.2 = (bf16[128,1536]{1,0:T(8,128)(2,1)S(1)}, bf16[128,1536]{1,0:T(8,128)(2,1)S(1)}, u32[]{:S(2)}, u32[]{:S(2)}) collective-permute-start(bf16[128,1536]{1,0:T(8,128)(2,1)S(1)} %bitcast.26), channel_id=1, source_target_pairs={{0,67},{1,66},{2,65},{3,64},{4,71},{5,70},{6,69},{7,68},{8,75},{9,... | collective-permute-start | bytes 1179656 | tf_op jit(solution)/shard_map/ppermute | solution.py:421
  16.6 0.3 collective-permute-start.1
  17.0 0.0 collective-permute-start
  17.0 0.6 reshape.20.modulation_ref
  17.6 8.5 %collective-permute-done.2.text_3_ref = bf16[128,1536]{1,0:T(8,128)(2,1)S(1)} collective-permute-done((bf16[128,1536]{1,0:T(8,128)(2,1)S(1)}, bf16[128,1536]{1,0:T(8,128)(2,1)S(1)}, u32[]{:S(2)}, u32[]{:S(2)}) %collective-permute-start.2) | collective-permute-done | bytes 393248 | tf_op jit(solution)/shard_map/ppermute | solution.py:421
  26.1 8.6 %collective-permute-done.1.text_2_ref = bf16[128,1536]{1,0:T(8,128)(2,1)S(1)} collective-permute-done((bf16[128,1536]{1,0:T(8,128)(2,1)S(1)}, bf16[128,1536]{1,0:T(8,128)(2,1)S(1)}, u32[]{:S(2)}, u32[]{:S(2)}) %collective-permute-start.1) | collective-permute-done | bytes 393248 | tf_op jit(solution)/shard_map/ppermute | solution.py:421
  34.7 0.0 collective-permute-done.text_1_ref
  34.7 0.5 prompts.1.prompts_ref.prompt_ref
  35.2 13.3 %all-to-all-done = bf16[64,24,896]{2,1,0:T(8,128)(2,1)} async-done(((bf16[64,24,896]{2,1,0:T(8,128)(2,1)}), bf16[64,24,896]{2,1,0:T(8,128)(2,1)}, u32[]{:S(2)}, u32[]{:S(2)}) %all-to-all-start) | async-done | bytes 2752544 | tf_op jit(solution)/shard_map/all_to_all | solution.py:452
  48.6 3.9 %fold.1 = (bf16[64,72,128]{2,1,0:T(8,128)(2,1)}, bf16[1536,384]{1,0:T(8,128)(2,1)}) custom-call(bf16[64,1536]{1,0:T(8,128)(2,1)} %latent_in_ref.3, f32[1,1536]{1,0:T(1,128)} %reshape.20.modulation_ref, bf16[1536,896]{1,0:T(8,128)(2,1)} %bitcast.10.packed_ref), custom_call_target="tpu_custom_call" | custom-call | tf_op jit(solution)/shard_map/fold/pallas_call | solution.py:378
  52.4 0.5 collective-permute-start.3
  53.0 5.4 %all-to-all-start.1 = ((bf16[64,72,128]{2,1,0:T(8,128)(2,1)}), bf16[64,72,128]{2,1,0:T(8,128)(2,1)S(1)}, u32[]{:S(2)}, u32[]{:S(2)}) async-start(bf16[64,72,128]{2,1,0:T(8,128)(2,1)} %get-tuple-element.34), calls=%async_computation.1 | async-start | bytes 2359296 | tf_op jit(solution)/shard_map/all_to_all | solution.py:474
  58.3 0.0 copy-start.1
  58.3 0.0 copy-start.2
  58.4 0.0 copy-start.4
  58.4 0.0 copy-start.5
  58.4 0.0 copy-start.6
  58.4 0.0 collective-permute-done.3.side_core_ref
  58.4 2.4 %mix.1 = (bf16[256,384]{1,0:T(8,128)(2,1)S(1)}, bf16[256,384]{1,0:T(8,128)(2,1)S(1)}) custom-call(bf16[512,1536]{1,0:T(8,128)(2,1)S(1)} %prompts.1.prompts_ref.prompt_ref, bf16[1536,896]{1,0:T(8,128)(2,1)} %bitcast.10.packed_ref), custom_call_target="tpu_custom_call" | custom-call | tf_op jit(solution)/shard_map/mix/pallas_call | solution.py:378
  60.8 0.1 collective-permute-start.4
  60.9 1.4 collective-permute-done.4.received_ref
  62.3 0.7 pair.1
  63.0 3.6 %collective-permute-start.5 = (bf16[2,128,384]{2,1,0:T(8,128)(2,1)S(1)}, bf16[2,128,384]{2,1,0:T(8,128)(2,1)}, u32[]{:S(2)}, u32[]{:S(2)}) collective-permute-start(bf16[2,128,384]{2,1,0:T(8,128)(2,1)S(1)} %get-tuple-element.37.text_0_ref), channel_id=1, source_target_pairs={{0,64},{1,65},{2,66},{3,67},{4,68},{5,69},{6,70},{7,71},{8,72},{9,... | collective-permute-start | bytes 589832 | tf_op jit(solution)/shard_map/ppermute | solution.py:421
  66.6 0.7 collective-permute-start.7
  67.2 0.3 collective-permute-start.6
  68.2 0.1 pad_add_fusion.place_ref
  68.3 9.5 %all-to-all-done.1 = bf16[64,72,128]{2,1,0:T(8,128)(2,1)S(1)} async-done(((bf16[64,72,128]{2,1,0:T(8,128)(2,1)}), bf16[64,72,128]{2,1,0:T(8,128)(2,1)S(1)}, u32[]{:S(2)}, u32[]{:S(2)}) %all-to-all-start.1) | async-done | bytes 1179680 | tf_op jit(solution)/shard_map/all_to_all | solution.py:474
  77.8 3.6 %collective-permute-done.5.text_1_ref = bf16[2,128,384]{2,1,0:T(8,128)(2,1)} collective-permute-done((bf16[2,128,384]{2,1,0:T(8,128)(2,1)S(1)}, bf16[2,128,384]{2,1,0:T(8,128)(2,1)}, u32[]{:S(2)}, u32[]{:S(2)}) %collective-permute-start.5) | collective-permute-done | bytes 196640 | tf_op jit(solution)/shard_map/ppermute | solution.py:421
  81.4 0.0 collective-permute-done.7.text_3_ref
  81.4 2.3 %collective-permute-done.6.text_2_ref = bf16[2,128,384]{2,1,0:T(8,128)(2,1)} collective-permute-done((bf16[2,128,384]{2,1,0:T(8,128)(2,1)}, bf16[2,128,384]{2,1,0:T(8,128)(2,1)}, u32[]{:S(2)}, u32[]{:S(2)}) %collective-permute-start.6) | collective-permute-done | bytes 196640 | tf_op jit(solution)/shard_map/ppermute | solution.py:421
  83.7 0.0 copy-done.4
  83.7 0.0 copy-done.5
  83.7 0.0 copy-done.6
  83.7 0.0 copy-start
  83.7 1.3 copy-done
  85.0 19.1 %forward.1 = (f32[64,256]{1,0:T(8,128)}, f32[64,256]{1,0:T(8,128)S(1)}, f32[64,256]{1,0:T(8,128)S(1)}, bf16[64,256]{1,0:T(8,128)(2,1)S(1)}, bf16[256,1536]{1,0:T...) custom-call(s32[3]{0:T(128)S(1)} %pad_add_fusion.place_ref, ...), custom_call_target="tpu_custom_call" | custom-call | tf_op jit(solution)/shard_map/forward/pallas_call | solution.py:378
  104.1 1.3 collective-permute-start.8
  105.4 6.0 %collective-permute-done.8.fake_ref = bf16[64,256]{1,0:T(8,128)(2,1)S(1)} collective-permute-done((bf16[64,256]{1,0:T(8,128)(2,1)S(1)}, bf16[64,256]{1,0:T(8,128)(2,1)S(1)}, u32[]{:S(2)}, u32[]{:S(2)}) %collective-permute-start.8) | collective-permute-done | bytes 32800 | tf_op jit(solution)/shard_map/ppermute | solution.py:537
  111.4 7.3 %backward.1 = (f32[32,24,384]{2,1,0:T(8,128)S(1)}, bf16[32,24,384]{2,1,0:T(8,128)(2,1)S(1)}) custom-call(s32[3]{0:T(128)S(1)} %pad_add_fusion.place_ref, f32[1,1]{1,0:T(1,128)} %bitcast.3.sigma_ref, f32[64,256]{1,0:T(8,128)S(1)} %get-tuple-element.41.sample_ref, f32[64,256]{1,0:T(8,128)S(1)} %bitcast.31, f32[64,256]{1,0:T(8,128)S(1)} %get-tuple-element.42.own_ref, ...), custom_call_target="tpu_custom_call" | custom-call | tf_op jit(solution)/shard_map/backward/pallas_call | solution.py:378
  118.7 0.1 collective-permute-start.9
  118.8 2.0 %collective-permute-done.9.received_ref = bf16[32,24,384]{2,1,0:T(8,128)(2,1)S(1)} collective-permute-done((bf16[32,24,384]{2,1,0:T(8,128)(2,1)S(1)}, bf16[32,24,384]{2,1,0:T(8,128)(2,1)S(1)}, u32[]{:S(2)}, u32[]{:S(2)}) %collective-permute-start.9) | collective-permute-done | bytes 589856 | tf_op jit(solution)/shard_map/ppermute | solution.py:421
  120.8 0.1 add.9
  120.9 18.7 %all_to_all.15.shares_ref = bf16[32,24,384]{2,1,0:T(8,128)(2,1)S(1)} all-to-all(bf16[32,24,384]{2,1,0:T(8,128)(2,1)S(1)} %add.9), channel_id=1, replica_groups={{0,2,4,6,8,10,12,14,16,18,20,22,24,26,28,30,32,34,36,38,40,42,44,46,48,..., dimensions={0} | all-to-all | bytes 1179648 | tf_op jit(solution)/shard_map/all_to_all | solution.py:564
  139.6 0.8 total.1
  (4 shorter events, 0.0 us)
Async XLA Ops:
  3.4 9.8 %copy-start.3 = (bf16[1,128,1536]{2,1,0:T(8,128)(2,1)S(1)}, bf16[1,128,1536]{2,1,0:T(8,128)(2,1)}, u32[]{:S(2)}) copy-start(bf16[1,128,1536]{2,1,0:T(8,128)(2,1)} %param.14) | copy-start | bytes 1179652
  3.4 13.6 %copy-start.7 = (f32[1536]{0:T(1024)S(1)}, f32[1536]{0:T(1024)}, u32[]{:S(2)}) copy-start(f32[1536]{0:T(1024)} %param.18) | copy-start | bytes 18436
  3.4 45.2 %all-to-all-start = ((bf16[64,24,896]{2,1,0:T(8,128)(2,1)}), bf16[64,24,896]{2,1,0:T(8,128)(2,1)}, u32[]{:S(2)}, u32[]{:S(2)}) async-start(bf16[64,24,896]{2,1,0:T(8,128)(2,1)} %pack.1), calls=%async_computation | async-start | bytes 5505024 | tf_op jit(solution)/shard_map/all_to_all | solution.py:452
  13.2 13.0 %collective-permute-start.2 = (bf16[128,1536]{1,0:T(8,128)(2,1)S(1)}, bf16[128,1536]{1,0:T(8,128)(2,1)S(1)}, u32[]{:S(2)}, u32[]{:S(2)}) collective-permute-start(bf16[128,1536]{1,0:T(8,128)(2,1)S(1)} %bitcast.26), channel_id=1, source_target_pairs={{0,67},{1,66},{2,65},{3,64},{4,71},{5,70},{6,69},{7,68},{8,75},{9,... | collective-permute-start | bytes 1179656 | tf_op jit(solution)/shard_map/ppermute | solution.py:421
  16.6 18.1 %collective-permute-start.1 = (bf16[128,1536]{1,0:T(8,128)(2,1)S(1)}, bf16[128,1536]{1,0:T(8,128)(2,1)S(1)}, u32[]{:S(2)}, u32[]{:S(2)}) collective-permute-start(bf16[128,1536]{1,0:T(8,128)(2,1)S(1)} %bitcast.27), channel_id=1, source_target_pairs={{0,66},{1,67},{2,64},{3,65},{4,70},{5,71},{6,68},{7,69},{8,74},{9,... | collective-permute-start | bytes 1179656 | tf_op jit(solution)/shard_map/ppermute | solution.py:421
  17.0 17.8 %collective-permute-start = (bf16[128,1536]{1,0:T(8,128)(2,1)S(1)}, bf16[128,1536]{1,0:T(8,128)(2,1)S(1)}, u32[]{:S(2)}, u32[]{:S(2)}) collective-permute-start(bf16[128,1536]{1,0:T(8,128)(2,1)S(1)} %bitcast.28), channel_id=1, source_target_pairs={{0,1},{1,0},{2,3},{3,2},{4,5},{5,4},{6,7},{7,6},{8,9},{9,8},{10,11... | collective-permute-start | bytes 1179656 | tf_op jit(solution)/shard_map/ppermute | solution.py:421
  52.4 6.0 %collective-permute-start.3 = (bf16[1536,384]{1,0:T(8,128)(2,1)}, bf16[1536,384]{1,0:T(8,128)(2,1)}, u32[]{:S(2)}, u32[]{:S(2)}) collective-permute-start(bf16[1536,384]{1,0:T(8,128)(2,1)} %get-tuple-element.32.side_own_ref), channel_id=1, source_target_pairs={{0,1},{1,0},{2,3},{3,2},{4,5},{5,4},{6,7},{7,6},{8,9},{9,8},{10,11... | collective-permute-start | bytes 3538952 | tf_op jit(solution)/shard_map/ppermute | solution.py:421
  53.0 24.8 %all-to-all-start.1 = ((bf16[64,72,128]{2,1,0:T(8,128)(2,1)}), bf16[64,72,128]{2,1,0:T(8,128)(2,1)S(1)}, u32[]{:S(2)}, u32[]{:S(2)}) async-start(bf16[64,72,128]{2,1,0:T(8,128)(2,1)} %get-tuple-element.34), calls=%async_computation.1 | async-start | bytes 2359296 | tf_op jit(solution)/shard_map/all_to_all | solution.py:474
  58.3 25.3 %copy-start.1 = (bf16[64,1536]{1,0:T(8,128)(2,1)S(1)}, bf16[64,1536]{1,0:T(8,128)(2,1)}, u32[]{:S(2)}) copy-start(bf16[64,1536]{1,0:T(8,128)(2,1)} %latent_in_ref.3) | copy-start | bytes 589828
  58.3 25.3 %copy-start.2 = (bf16[1536,64]{0,1:T(8,128)(2,1)S(1)}, bf16[1536,64]{0,1:T(8,128)(2,1)}, u32[]{:S(2)}) copy-start(bf16[1536,64]{0,1:T(8,128)(2,1)} %param.19) | copy-start | bytes 589828
  58.4 25.3 %copy-start.4 = (f32[1,256,64]{1,2,0:T(8,128)S(1)}, f32[1,256,64]{1,2,0:T(8,128)}, u32[]{:S(2)}) copy-start(f32[1,256,64]{1,2,0:T(8,128)} %param.13) | copy-start | bytes 196612
  58.4 25.3 %copy-start.5 = (f32[1,256,64]{1,2,0:T(8,128)S(1)}, f32[1,256,64]{1,2,0:T(8,128)}, u32[]{:S(2)}) copy-start(f32[1,256,64]{1,2,0:T(8,128)} %param.12) | copy-start | bytes 196612
  58.4 25.3 %copy-start.6 = (f32[1,1536]{1,0:T(1,128)S(1)}, f32[1,1536]{1,0:T(1,128)}, u32[]{:S(2)}) copy-start(f32[1,1536]{1,0:T(1,128)} %reshape.20.modulation_ref) | copy-start | bytes 18436
  60.8 1.5 %collective-permute-start.4 = (bf16[256,384]{1,0:T(8,128)(2,1)S(1)}, bf16[256,384]{1,0:T(8,128)(2,1)S(1)}, u32[]{:S(2)}, u32[]{:S(2)}) collective-permute-start(bf16[256,384]{1,0:T(8,128)(2,1)S(1)} %get-tuple-element.36), channel_id=1, source_target_pairs={{0,1},{1,0},{2,3},{3,2},{4,5},{5,4},{6,7},{7,6},{8,9},{9,8},{10,11... | collective-permute-start | bytes 589832 | tf_op jit(solution)/shard_map/ppermute | solution.py:421
  63.0 18.4 %collective-permute-start.5 = (bf16[2,128,384]{2,1,0:T(8,128)(2,1)S(1)}, bf16[2,128,384]{2,1,0:T(8,128)(2,1)}, u32[]{:S(2)}, u32[]{:S(2)}) collective-permute-start(bf16[2,128,384]{2,1,0:T(8,128)(2,1)S(1)} %get-tuple-element.37.text_0_ref), channel_id=1, source_target_pairs={{0,64},{1,65},{2,66},{3,67},{4,68},{5,69},{6,70},{7,71},{8,72},{9,... | collective-permute-start | bytes 589832 | tf_op jit(solution)/shard_map/ppermute | solution.py:421
  66.6 14.8 %collective-permute-start.7 = (bf16[2,128,384]{2,1,0:T(8,128)(2,1)}, bf16[2,128,384]{2,1,0:T(8,128)(2,1)}, u32[]{:S(2)}, u32[]{:S(2)}) collective-permute-start(bf16[2,128,384]{2,1,0:T(8,128)(2,1)} %get-tuple-element.38), channel_id=1, source_target_pairs={{0,66},{1,67},{2,64},{3,65},{4,70},{5,71},{6,68},{7,69},{8,74},{9,... | collective-permute-start | bytes 589832 | tf_op jit(solution)/shard_map/ppermute | solution.py:421
  67.2 16.4 %collective-permute-start.6 = (bf16[2,128,384]{2,1,0:T(8,128)(2,1)}, bf16[2,128,384]{2,1,0:T(8,128)(2,1)}, u32[]{:S(2)}, u32[]{:S(2)}) collective-permute-start(bf16[2,128,384]{2,1,0:T(8,128)(2,1)} %get-tuple-element.38), channel_id=1, source_target_pairs={{0,2},{1,3},{2,0},{3,1},{4,6},{5,7},{6,4},{7,5},{8,10},{9,11},{10,... | collective-permute-start | bytes 589832 | tf_op jit(solution)/shard_map/ppermute | solution.py:421
  83.7 1.3 copy-start
  104.1 7.3 %collective-permute-start.8 = (bf16[64,256]{1,0:T(8,128)(2,1)S(1)}, bf16[64,256]{1,0:T(8,128)(2,1)S(1)}, u32[]{:S(2)}, u32[]{:S(2)}) collective-permute-start(bf16[64,256]{1,0:T(8,128)(2,1)S(1)} %get-tuple-element.43), channel_id=1, source_target_pairs={{64,0},{65,1},{66,2},{67,3},{68,4},{69,5},{70,6},{71,7},{72,8},{73... | collective-permute-start | bytes 98312 | tf_op jit(solution)/shard_map/ppermute | solution.py:537
  118.7 2.1 %collective-permute-start.9 = (bf16[32,24,384]{2,1,0:T(8,128)(2,1)S(1)}, bf16[32,24,384]{2,1,0:T(8,128)(2,1)S(1)}, u32[]{:S(2)}, u32[]{:S(2)}) collective-permute-start(bf16[32,24,384]{2,1,0:T(8,128)(2,1)S(1)} %get-tuple-element.54), channel_id=1, source_target_pairs={{0,1},{1,0},{2,3},{3,2},{4,5},{5,4},{6,7},{7,6},{8,9},{9,8},{10,11... | collective-permute-start | bytes 1769480 | tf_op jit(solution)/shard_map/ppermute | solution.py:421

commit v13 on v11

--- a/solution.py
+++ b/solution.py
@@ -245,6 +245,11 @@
             left = jnp.concatenate(
                 [scaled_high, scaled_low, scaled_high, reduced_picture[:, rank_span]], axis=1
             )
+            if block > 0:
+                prompt_left = jnp.concatenate(
+                    [jnp.zeros((TXT, 3 * CH), BF), reduced_prompt[:, rank_span]], axis=1
+                )
+                left = jnp.concatenate([prompt_left, left], axis=0)
             for start in range(0, HW, CHUNK):
                 own = slice(start, start + CHUNK)
                 wide = slice(block * HW + start, block * HW + start + CHUNK)
@@ -252,14 +257,13 @@
                 fold_high, fold_low = high_low(parts[:, :CH] + noise_level * parts[:, CH:])
                 up = ups[own, up_span]
                 stacked[...] = jnp.concatenate([fold_high, fold_high, fold_low, up], axis=1)
-                picture_part = dot(left, stacked[...], 1, 1).astype(BF)
+                part = dot(left, stacked[...], 1, 1)
                 if block == 0:
-                    now[:, own] = picture_part
+                    now[:, own] = part.astype(BF)
                 else:
-                    now[TXT:, own] = picture_part
                     text_span = slice((block - 1) * HW + start, (block - 1) * HW + start + CHUNK)
-                    adapter = dot(reduced_prompt[:, rank_span], up, 1, 1)
-                    now[:TXT, own] = (text[:, text_span].astype(F32) + adapter).astype(BF)
+                    now[TXT:, own] = part[TXT:].astype(BF)
+                    now[:TXT, own] = (text[:, text_span].astype(F32) + part[:TXT]).astype(BF)
 
         def head(index, carry):
             span = pl.ds(pl.multiple_of(index * HD, HD), HD)
@@ -283,7 +287,7 @@
 
             return carry
 
-        lax.fori_loop(0, HEADS, head, 0, unroll=2)
+        lax.fori_loop(0, HEADS, head, 0, unroll=12)
         return dot(velocity_out_ref[...], attended_now[...], 1, 1)
 
     latent = latent_ref[...]

time: 140 us -> 140 us (level)
  no operation moved by 1% of the time
where the time goes in v13:
time: 140 us; the launch traced here: 139 us
  waiting for transfers between devices  55.8 us (40%)
  Pallas kernels  36.5 us (26%)
  starting transfers between devices  25.4 us (18%)
  blocking collectives  18.7 us (13%)
  between operations  1.45 us (1%)
    pallas_call x9, Pallas kernels, run(): pl.pallas_call(kernel, out_shape=shapes, in_specs=[pl.BlockSpec(memory_sp...  36.5 us
    ppermute x9, waiting for transfers between devices, move(): return lax.ppermute(array, ('group', 'fsdp'), pairs)  26.9 us
    all_to_all x1, blocking collectives, per_device(): shares = lax.all_to_all(sums, 'fsdp', 0, 0, axis_index_groups=parities)  18.7 us
    all_to_all x1, waiting for transfers between devices, per_device(): lax.all_to_all(packed, 'fsdp', 0, 0).reshape(HW, EIGHTH + SIDE + PART)  13.3 us
    all_to_all x1, starting transfers between devices, per_device(): lax.all_to_all(packed, 'fsdp', 0, 0).reshape(HW, EIGHTH + SIDE + PART)  9.75 us
    all_to_all x1, waiting for transfers between devices, per_device(): fold = lax.all_to_all(share, 'fsdp', 0, 0).reshape(devices * SHARE, PART)  9.58 us
    ppermute x9, starting transfers between devices, move(): return lax.ppermute(array, ('group', 'fsdp'), pairs)  9.04 us
    ppermute x1, waiting for transfers between devices, per_device(): fake_velocity = lax.ppermute(narrow_velocity, 'group', [(1, 0)])  6.01 us
  transfers between devices with their start and end apart: 12, of which 9 were waited for; matrix products, arithmetic and copies ran while one was open for 0% of the time, Pallas kernels for 3%

profile of v13, /device:TPU:0, one launch (start us, length us, event | category | flops | bytes accessed | tf_op | source)
XLA Modules:
  0.0 139.1 jit_solution(1303643061297527318)
XLA Ops:
  0.6 2.7 %pack.1 = bf16[64,24,896]{2,1,0:T(8,128)(2,1)} custom-call(bf16[24,4608]{1,0:T(8,128)(2,1)} %base_ref.1, bf16[24,192]{1,0:T(8,128)(2,1)} %gen_down_ref.1, bf16[24,192]{1,0:T(8,128)(2,1)} %critic_down_ref.1, bf16[3,24,64]{2,1,0:T(8,128)(2,1)} %bitcast.33, bf16[3,24,64]{2,1,0:T(8,128)(2,1)} %bitcast.34), custom_call_target="tpu_custom_call" | custom-call | tf_op jit(solution)/shard_map/pack/pallas_call | solution.py:382
  3.4 0.0 copy-start.3
  3.4 0.0 copy-start.6
  3.4 9.8 %all-to-all-start = ((bf16[64,24,896]{2,1,0:T(8,128)(2,1)}), bf16[64,24,896]{2,1,0:T(8,128)(2,1)}, u32[]{:S(2)}, u32[]{:S(2)}) async-start(bf16[64,24,896]{2,1,0:T(8,128)(2,1)} %pack.1), calls=%async_computation | async-start | bytes 5505024 | tf_op jit(solution)/shard_map/all_to_all | solution.py:456
  13.2 0.0 copy-done.3
  13.2 3.5 %collective-permute-start.2 = (bf16[128,1536]{1,0:T(8,128)(2,1)S(1)}, bf16[128,1536]{1,0:T(8,128)(2,1)S(1)}, u32[]{:S(2)}, u32[]{:S(2)}) collective-permute-start(bf16[128,1536]{1,0:T(8,128)(2,1)S(1)} %bitcast.26), channel_id=1, source_target_pairs={{0,67},{1,66},{2,65},{3,64},{4,71},{5,70},{6,69},{7,68},{8,75},{9,... | collective-permute-start | bytes 1179656 | tf_op jit(solution)/shard_map/ppermute | solution.py:425
  16.6 0.3 collective-permute-start.1
  17.0 0.0 collective-permute-start
  17.0 0.0 copy-done.6
  17.0 0.0 copy-start.1
  17.0 9.1 %collective-permute-done.2.text_3_ref = bf16[128,1536]{1,0:T(8,128)(2,1)S(1)} collective-permute-done((bf16[128,1536]{1,0:T(8,128)(2,1)S(1)}, bf16[128,1536]{1,0:T(8,128)(2,1)S(1)}, u32[]{:S(2)}, u32[]{:S(2)}) %collective-permute-start.2) | collective-permute-done | bytes 393248 | tf_op jit(solution)/shard_map/ppermute | solution.py:425
  26.1 8.6 %collective-permute-done.1.text_2_ref = bf16[128,1536]{1,0:T(8,128)(2,1)S(1)} collective-permute-done((bf16[128,1536]{1,0:T(8,128)(2,1)S(1)}, bf16[128,1536]{1,0:T(8,128)(2,1)S(1)}, u32[]{:S(2)}, u32[]{:S(2)}) %collective-permute-start.1) | collective-permute-done | bytes 393248 | tf_op jit(solution)/shard_map/ppermute | solution.py:425
  34.7 0.0 collective-permute-done.text_1_ref
  34.7 0.5 prompts.1.prompts_ref.prompt_ref
  35.2 13.3 %all-to-all-done = bf16[64,24,896]{2,1,0:T(8,128)(2,1)} async-done(((bf16[64,24,896]{2,1,0:T(8,128)(2,1)}), bf16[64,24,896]{2,1,0:T(8,128)(2,1)}, u32[]{:S(2)}, u32[]{:S(2)}) %all-to-all-start) | async-done | bytes 2752544 | tf_op jit(solution)/shard_map/all_to_all | solution.py:456
  48.6 0.0 copy-done.1
  48.6 3.3 %fold.1 = (bf16[64,72,128]{2,1,0:T(8,128)(2,1)S(1)}, bf16[1536,384]{1,0:T(8,128)(2,1)}) custom-call(bf16[64,1536]{1,0:T(8,128)(2,1)S(1)} %copy-done.1, f32[1,1536]{1,0:T(1,128)S(1)} %reshape.20.modulation_ref, bf16[1536,896]{1,0:T(8,128)(2,1)} %bitcast.10.packed_ref), custom_call_target="tpu_custom_call" | custom-call | tf_op jit(solution)/shard_map/fold/pallas_call | solution.py:382
  51.9 0.0 copy-start
  51.9 1.0 copy-done
  53.0 0.4 collective-permute-start.3
  53.4 5.4 %all-to-all-start.1 = ((bf16[64,72,128]{2,1,0:T(8,128)(2,1)}), bf16[64,72,128]{2,1,0:T(8,128)(2,1)S(1)}, u32[]{:S(2)}, u32[]{:S(2)}) async-start(bf16[64,72,128]{2,1,0:T(8,128)(2,1)} %copy-done), calls=%async_computation.1 | async-start | bytes 2359296 | tf_op jit(solution)/shard_map/all_to_all | solution.py:478
  58.8 0.0 copy-start.2
  58.8 0.0 copy-start.4
  58.8 0.0 copy-start.5
  58.8 0.0 collective-permute-done.3.side_core_ref
  58.8 2.3 %mix.1 = (bf16[256,384]{1,0:T(8,128)(2,1)S(1)}, bf16[256,384]{1,0:T(8,128)(2,1)S(1)}) custom-call(bf16[512,1536]{1,0:T(8,128)(2,1)S(1)} %prompts.1.prompts_ref.prompt_ref, bf16[1536,896]{1,0:T(8,128)(2,1)} %bitcast.10.packed_ref), custom_call_target="tpu_custom_call" | custom-call | tf_op jit(solution)/shard_map/mix/pallas_call | solution.py:382
  61.2 0.1 collective-permute-start.4
  61.3 1.4 collective-permute-done.4.received_ref
  62.7 0.7 pair.1
  63.4 3.6 %collective-permute-start.5 = (bf16[2,128,384]{2,1,0:T(8,128)(2,1)S(1)}, bf16[2,128,384]{2,1,0:T(8,128)(2,1)}, u32[]{:S(2)}, u32[]{:S(2)}) collective-permute-start(bf16[2,128,384]{2,1,0:T(8,128)(2,1)S(1)} %get-tuple-element.37.text_0_ref), channel_id=1, source_target_pairs={{0,64},{1,65},{2,66},{3,67},{4,68},{5,69},{6,70},{7,71},{8,72},{9,... | collective-permute-start | bytes 589832 | tf_op jit(solution)/shard_map/ppermute | solution.py:425
  67.0 0.7 collective-permute-start.7
  67.6 0.3 collective-permute-start.6
  68.6 0.1 pad_add_fusion.place_ref
  68.7 9.6 %all-to-all-done.1 = bf16[64,72,128]{2,1,0:T(8,128)(2,1)S(1)} async-done(((bf16[64,72,128]{2,1,0:T(8,128)(2,1)}), bf16[64,72,128]{2,1,0:T(8,128)(2,1)S(1)}, u32[]{:S(2)}, u32[]{:S(2)}) %all-to-all-start.1) | async-done | bytes 1179680 | tf_op jit(solution)/shard_map/all_to_all | solution.py:478
  78.2 3.6 %collective-permute-done.5.text_1_ref = bf16[2,128,384]{2,1,0:T(8,128)(2,1)} collective-permute-done((bf16[2,128,384]{2,1,0:T(8,128)(2,1)S(1)}, bf16[2,128,384]{2,1,0:T(8,128)(2,1)}, u32[]{:S(2)}, u32[]{:S(2)}) %collective-permute-start.5) | collective-permute-done | bytes 196640 | tf_op jit(solution)/shard_map/ppermute | solution.py:425
  81.8 0.0 collective-permute-done.7.text_3_ref
  81.8 2.3 %collective-permute-done.6.text_2_ref = bf16[2,128,384]{2,1,0:T(8,128)(2,1)} collective-permute-done((bf16[2,128,384]{2,1,0:T(8,128)(2,1)}, bf16[2,128,384]{2,1,0:T(8,128)(2,1)}, u32[]{:S(2)}, u32[]{:S(2)}) %collective-permute-start.6) | collective-permute-done | bytes 196640 | tf_op jit(solution)/shard_map/ppermute | solution.py:425
  84.1 0.0 copy-done.2
  84.1 0.0 copy-done.5
  84.1 18.7 %forward.1 = (f32[64,256]{1,0:T(8,128)}, f32[64,256]{1,0:T(8,128)S(1)}, f32[64,256]{1,0:T(8,128)S(1)}, bf16[64,256]{1,0:T(8,128)(2,1)S(1)}, bf16[256,1536]{1,0:T...) custom-call(s32[3]{0:T(128)S(1)} %pad_add_fusion.place_ref, ...), custom_call_target="tpu_custom_call" | custom-call | tf_op jit(solution)/shard_map/forward/pallas_call | solution.py:382
  102.8 1.3 collective-permute-start.8
  104.1 6.0 %collective-permute-done.8.fake_ref = bf16[64,256]{1,0:T(8,128)(2,1)S(1)} collective-permute-done((bf16[64,256]{1,0:T(8,128)(2,1)S(1)}, bf16[64,256]{1,0:T(8,128)(2,1)S(1)}, u32[]{:S(2)}, u32[]{:S(2)}) %collective-permute-start.8) | collective-permute-done | bytes 32800 | tf_op jit(solution)/shard_map/ppermute | solution.py:541
  110.1 7.3 %backward.1 = (f32[32,24,384]{2,1,0:T(8,128)S(1)}, bf16[32,24,384]{2,1,0:T(8,128)(2,1)S(1)}) custom-call(s32[3]{0:T(128)S(1)} %pad_add_fusion.place_ref, f32[1,1]{1,0:T(1,128)} %bitcast.3.sigma_ref, f32[64,256]{1,0:T(8,128)S(1)} %get-tuple-element.41.sample_ref, f32[64,256]{1,0:T(8,128)S(1)} %bitcast.31, f32[64,256]{1,0:T(8,128)S(1)} %get-tuple-element.42.own_ref, ...), custom_call_target="tpu_custom_call" | custom-call | tf_op jit(solution)/shard_map/backward/pallas_call | solution.py:382
  117.4 0.1 collective-permute-start.9
  117.5 2.0 %collective-permute-done.9.received_ref = bf16[32,24,384]{2,1,0:T(8,128)(2,1)S(1)} collective-permute-done((bf16[32,24,384]{2,1,0:T(8,128)(2,1)S(1)}, bf16[32,24,384]{2,1,0:T(8,128)(2,1)S(1)}, u32[]{:S(2)}, u32[]{:S(2)}) %collective-permute-start.9) | collective-permute-done | bytes 589856 | tf_op jit(solution)/shard_map/ppermute | solution.py:425
  119.5 0.2 add.9
  119.6 18.7 %all_to_all.15.shares_ref = bf16[32,24,384]{2,1,0:T(8,128)(2,1)S(1)} all-to-all(bf16[32,24,384]{2,1,0:T(8,128)(2,1)S(1)} %add.9), channel_id=1, replica_groups={{0,2,4,6,8,10,12,14,16,18,20,22,24,26,28,30,32,34,36,38,40,42,44,46,48,..., dimensions={0} | all-to-all | bytes 1179648 | tf_op jit(solution)/shard_map/all_to_all | solution.py:568
  138.3 0.8 total.1
  (2 shorter events, 0.0 us)
Async XLA Ops:
  3.4 9.8 %copy-start.3 = (bf16[1,128,1536]{2,1,0:T(8,128)(2,1)S(1)}, bf16[1,128,1536]{2,1,0:T(8,128)(2,1)}, u32[]{:S(2)}) copy-start(bf16[1,128,1536]{2,1,0:T(8,128)(2,1)} %param.14) | copy-start | bytes 1179652
  3.4 13.6 %copy-start.6 = (f32[1536]{0:T(1024)S(1)}, f32[1536]{0:T(1024)}, u32[]{:S(2)}) copy-start(f32[1536]{0:T(1024)} %param.18) | copy-start | bytes 18436
  3.4 45.2 %all-to-all-start = ((bf16[64,24,896]{2,1,0:T(8,128)(2,1)}), bf16[64,24,896]{2,1,0:T(8,128)(2,1)}, u32[]{:S(2)}, u32[]{:S(2)}) async-start(bf16[64,24,896]{2,1,0:T(8,128)(2,1)} %pack.1), calls=%async_computation | async-start | bytes 5505024 | tf_op jit(solution)/shard_map/all_to_all | solution.py:456
  13.2 13.0 %collective-permute-start.2 = (bf16[128,1536]{1,0:T(8,128)(2,1)S(1)}, bf16[128,1536]{1,0:T(8,128)(2,1)S(1)}, u32[]{:S(2)}, u32[]{:S(2)}) collective-permute-start(bf16[128,1536]{1,0:T(8,128)(2,1)S(1)} %bitcast.26), channel_id=1, source_target_pairs={{0,67},{1,66},{2,65},{3,64},{4,71},{5,70},{6,69},{7,68},{8,75},{9,... | collective-permute-start | bytes 1179656 | tf_op jit(solution)/shard_map/ppermute | solution.py:425
  16.6 18.1 %collective-permute-start.1 = (bf16[128,1536]{1,0:T(8,128)(2,1)S(1)}, bf16[128,1536]{1,0:T(8,128)(2,1)S(1)}, u32[]{:S(2)}, u32[]{:S(2)}) collective-permute-start(bf16[128,1536]{1,0:T(8,128)(2,1)S(1)} %bitcast.27), channel_id=1, source_target_pairs={{0,66},{1,67},{2,64},{3,65},{4,70},{5,71},{6,68},{7,69},{8,74},{9,... | collective-permute-start | bytes 1179656 | tf_op jit(solution)/shard_map/ppermute | solution.py:425
  17.0 17.8 %collective-permute-start = (bf16[128,1536]{1,0:T(8,128)(2,1)S(1)}, bf16[128,1536]{1,0:T(8,128)(2,1)S(1)}, u32[]{:S(2)}, u32[]{:S(2)}) collective-permute-start(bf16[128,1536]{1,0:T(8,128)(2,1)S(1)} %bitcast.28), channel_id=1, source_target_pairs={{0,1},{1,0},{2,3},{3,2},{4,5},{5,4},{6,7},{7,6},{8,9},{9,8},{10,11... | collective-permute-start | bytes 1179656 | tf_op jit(solution)/shard_map/ppermute | solution.py:425
  17.0 31.6 %copy-start.1 = (bf16[64,1536]{1,0:T(8,128)(2,1)S(1)}, bf16[64,1536]{1,0:T(8,128)(2,1)}, u32[]{:S(2)}) copy-start(bf16[64,1536]{1,0:T(8,128)(2,1)} %latent_in_ref.3) | copy-start | bytes 589828
  51.9 1.0 copy-start
  53.0 5.9 %collective-permute-start.3 = (bf16[1536,384]{1,0:T(8,128)(2,1)}, bf16[1536,384]{1,0:T(8,128)(2,1)}, u32[]{:S(2)}, u32[]{:S(2)}) collective-permute-start(bf16[1536,384]{1,0:T(8,128)(2,1)} %get-tuple-element.32.side_own_ref), channel_id=1, source_target_pairs={{0,1},{1,0},{2,3},{3,2},{4,5},{5,4},{6,7},{7,6},{8,9},{9,8},{10,11... | collective-permute-start | bytes 3538952 | tf_op jit(solution)/shard_map/ppermute | solution.py:425
  53.4 24.8 %all-to-all-start.1 = ((bf16[64,72,128]{2,1,0:T(8,128)(2,1)}), bf16[64,72,128]{2,1,0:T(8,128)(2,1)S(1)}, u32[]{:S(2)}, u32[]{:S(2)}) async-start(bf16[64,72,128]{2,1,0:T(8,128)(2,1)} %copy-done), calls=%async_computation.1 | async-start | bytes 2359296 | tf_op jit(solution)/shard_map/all_to_all | solution.py:478
  58.8 25.3 %copy-start.2 = (bf16[1536,64]{0,1:T(8,128)(2,1)S(1)}, bf16[1536,64]{0,1:T(8,128)(2,1)}, u32[]{:S(2)}) copy-start(bf16[1536,64]{0,1:T(8,128)(2,1)} %param.19) | copy-start | bytes 589828
  58.8 25.3 %copy-start.4 = (f32[1,256,64]{1,2,0:T(8,128)S(1)}, f32[1,256,64]{1,2,0:T(8,128)}, u32[]{:S(2)}) copy-start(f32[1,256,64]{1,2,0:T(8,128)} %param.13) | copy-start | bytes 196612
  58.8 25.3 %copy-start.5 = (f32[1,256,64]{1,2,0:T(8,128)S(1)}, f32[1,256,64]{1,2,0:T(8,128)}, u32[]{:S(2)}) copy-start(f32[1,256,64]{1,2,0:T(8,128)} %param.12) | copy-start | bytes 196612
  61.2 1.5 %collective-permute-start.4 = (bf16[256,384]{1,0:T(8,128)(2,1)S(1)}, bf16[256,384]{1,0:T(8,128)(2,1)S(1)}, u32[]{:S(2)}, u32[]{:S(2)}) collective-permute-start(bf16[256,384]{1,0:T(8,128)(2,1)S(1)} %get-tuple-element.36), channel_id=1, source_target_pairs={{0,1},{1,0},{2,3},{3,2},{4,5},{5,4},{6,7},{7,6},{8,9},{9,8},{10,11... | collective-permute-start | bytes 589832 | tf_op jit(solution)/shard_map/ppermute | solution.py:425
  63.4 18.4 %collective-permute-start.5 = (bf16[2,128,384]{2,1,0:T(8,128)(2,1)S(1)}, bf16[2,128,384]{2,1,0:T(8,128)(2,1)}, u32[]{:S(2)}, u32[]{:S(2)}) collective-permute-start(bf16[2,128,384]{2,1,0:T(8,128)(2,1)S(1)} %get-tuple-element.37.text_0_ref), channel_id=1, source_target_pairs={{0,64},{1,65},{2,66},{3,67},{4,68},{5,69},{6,70},{7,71},{8,72},{9,... | collective-permute-start | bytes 589832 | tf_op jit(solution)/shard_map/ppermute | solution.py:425
  67.0 14.8 %collective-permute-start.7 = (bf16[2,128,384]{2,1,0:T(8,128)(2,1)}, bf16[2,128,384]{2,1,0:T(8,128)(2,1)}, u32[]{:S(2)}, u32[]{:S(2)}) collective-permute-start(bf16[2,128,384]{2,1,0:T(8,128)(2,1)} %get-tuple-element.38), channel_id=1, source_target_pairs={{0,66},{1,67},{2,64},{3,65},{4,70},{5,71},{6,68},{7,69},{8,74},{9,... | collective-permute-start | bytes 589832 | tf_op jit(solution)/shard_map/ppermute | solution.py:425
  67.6 16.4 %collective-permute-start.6 = (bf16[2,128,384]{2,1,0:T(8,128)(2,1)}, bf16[2,128,384]{2,1,0:T(8,128)(2,1)}, u32[]{:S(2)}, u32[]{:S(2)}) collective-permute-start(bf16[2,128,384]{2,1,0:T(8,128)(2,1)} %get-tuple-element.38), channel_id=1, source_target_pairs={{0,2},{1,3},{2,0},{3,1},{4,6},{5,7},{6,4},{7,5},{8,10},{9,11},{10,... | collective-permute-start | bytes 589832 | tf_op jit(solution)/shard_map/ppermute | solution.py:425
  102.8 7.3 %collective-permute-start.8 = (bf16[64,256]{1,0:T(8,128)(2,1)S(1)}, bf16[64,256]{1,0:T(8,128)(2,1)S(1)}, u32[]{:S(2)}, u32[]{:S(2)}) collective-permute-start(bf16[64,256]{1,0:T(8,128)(2,1)S(1)} %get-tuple-element.43), channel_id=1, source_target_pairs={{64,0},{65,1},{66,2},{67,3},{68,4},{69,5},{70,6},{71,7},{72,8},{73... | collective-permute-start | bytes 98312 | tf_op jit(solution)/shard_map/ppermute | solution.py:541
  117.4 2.1 %collective-permute-start.9 = (bf16[32,24,384]{2,1,0:T(8,128)(2,1)S(1)}, bf16[32,24,384]{2,1,0:T(8,128)(2,1)S(1)}, u32[]{:S(2)}, u32[]{:S(2)}) collective-permute-start(bf16[32,24,384]{2,1,0:T(8,128)(2,1)S(1)} %get-tuple-element.54), channel_id=1, source_target_pairs={{0,1},{1,0},{2,3},{3,2},{4,5},{5,4},{6,7},{7,6},{8,9},{9,8},{10,11... | collective-permute-start | bytes 1769480 | tf_op jit(solution)/shard_map/ppermute | solution.py:425
